TPU v7x, 32 devices: a whole 2x2x4 slice. The times are simulated.
32 devices in a mesh: dp: 8 (over z, y), ctx: 4 (over x, core).
Axes of the slice: x: 2, y: 2, z: 4, core: 2. Of those that a mesh axis runs over, the one named last changes fastest.
Arguments:
- frames: bfloat16 [8, 512, 1024], P('dp', 'ctx'), may hold values from -6.5 to 6.5
- utt_lengths: int32 [8, 8], P('dp'), may hold values from 1 to 384, 512 in all within a row
- cotangent: bfloat16 [8, 512, 1024], P('dp', 'ctx'), may hold values from -6 to 6
- w_dw: float32 [31, 1024], replicated, may hold values from -1 to 1
- w_kv: bfloat16 [1024, 2048], replicated
Outputs:
- output: bfloat16 [8, 512, 1024], P('dp', 'ctx')
- dframes: bfloat16 [8, 512, 1024], P('dp', 'ctx')
- grad_kv: float32 [1024, 2048], P(('dp', 'ctx'))
- grad_dw: float32 [1024, 31], P(('dp', 'ctx'))
Inputs may be any that keep to these rules, and one draw needn't show every extreme that they name: `utt_lengths`: each row lists the frame counts of the utterances packed one after another into that sequence; they sum to 512 and the longest is exactly 384.
All inputs are finite; a program needn't handle non-finite values.
Results may differ from a plain program's by a relative error of at most 0.018.
Values may be sent and summed in bfloat16 or wider, within the bound.
No kernel may reach another device: no remote copies, remote signals or barrier semaphores. Data moves between devices by JAX's collectives and lax.ppermute only.
A program may use at most 128 MiB of HBM per device.

v0:
```python
import math

import jax
import jax.numpy as jnp
from jax import lax
from jax.sharding import PartitionSpec as P

H = 16
KERNEL = 31


def extended(block, sides, width):
    for axis, dim in sides:
        count = lax.axis_size(axis)
        forward = [(i, i + 1) for i in range(count - 1)]
        backward = [(target, source) for source, target in forward]
        low = lax.ppermute(
            lax.slice_in_dim(block, block.shape[dim] - width, None, axis=dim), axis, forward
        )
        high = lax.ppermute(lax.slice_in_dim(block, 0, width, axis=dim), axis, backward)
        block = jnp.concatenate([low, block, high], axis=dim)
    return block


def segment_index(lengths, frame_pos, seq_total):
    utt_ends = jnp.cumsum(lengths)
    counted = jnp.sum((utt_ends[None, :] <= frame_pos[:, None]).astype(jnp.int32), axis=1)
    inside = (frame_pos >= 0) & (frame_pos < seq_total)
    return jnp.where(inside, counted, -1)


def tap_sum(source, wide_seg, own_seg, weight_rows, row_count):
    result = jnp.zeros((row_count, source.shape[1]), jnp.float32)
    for tap_pos in range(weight_rows.shape[0]):
        same_utt = wide_seg[tap_pos : tap_pos + row_count] == own_seg
        result = (
            result
            + jnp.where(same_utt[:, None], source[tap_pos : tap_pos + row_count], 0.0)
            * weight_rows[tap_pos]
        )
    return result


def tap_grads(source, wide_seg, own_seg, grad_rows, row_count, tap_count):
    columns = []
    for tap_pos in range(tap_count):
        same_utt = wide_seg[tap_pos : tap_pos + row_count] == own_seg
        columns.append(
            jnp.sum(
                jnp.where(same_utt[:, None], source[tap_pos : tap_pos + row_count], 0.0)
                * grad_rows,
                axis=0,
            )
        )
    return jnp.stack(columns, axis=1)


def silu_slope(pre_act):
    sigmoid_v = jax.nn.sigmoid(pre_act)
    return sigmoid_v * (1.0 + pre_act * (1.0 - sigmoid_v))


def head_terms(query_rows, key_rows, value_rows, grad_rows, same_utt, score_scale):
    contract_last = (((1,), (1,)), ((), ()))
    contract_first = (((0,), (0,)), ((), ()))
    scores = (
        lax.dot_general(query_rows, key_rows, contract_last, preferred_element_type=jnp.float32)
        * score_scale
    )
    scores = jnp.where(same_utt, scores, -jnp.inf)
    row_top = jnp.max(scores, axis=1, keepdims=True)
    exp_scores = jnp.where(same_utt, jnp.exp(scores - row_top), 0.0)
    row_total = jnp.sum(exp_scores, axis=1, keepdims=True)
    attn_probs = exp_scores / row_total
    probs_low = attn_probs.astype(jnp.bfloat16)
    attended = jnp.dot(probs_low, value_rows, preferred_element_type=jnp.float32)
    dprobs = lax.dot_general(
        grad_rows, value_rows, contract_last, preferred_element_type=jnp.float32
    )
    rowdot = jnp.sum(grad_rows.astype(jnp.float32) * attended, axis=1, keepdims=True)
    dscores = (attn_probs * (dprobs - rowdot)).astype(jnp.bfloat16)
    dquery = jnp.dot(dscores, key_rows, preferred_element_type=jnp.float32) * score_scale
    dkeys = (
        lax.dot_general(dscores, query_rows, contract_first, preferred_element_type=jnp.float32)
        * score_scale
    )
    dvalues = lax.dot_general(
        probs_low, grad_rows, contract_first, preferred_element_type=jnp.float32
    )
    return (attended, dquery, dkeys, dvalues, row_top[:, 0], row_total[:, 0], rowdot[:, 0])


def on_device(frames, utt_lengths, cotangent, w_dw, w_kv):
    row_count = frames.shape[1]
    feat_width = frames.shape[2]
    head_count = H
    head_width = feat_width // head_count
    seq_total = row_count * lax.axis_size("ctx")
    rim_width = KERNEL // 2
    score_scale = 1.0 / math.sqrt(head_width)
    contract_first = (((0,), (0,)), ((), ()))
    contract_last = (((1,), (1,)), ((), ()))
    first_row = lax.axis_index("ctx") * row_count
    lengths = utt_lengths[0]
    local_pos = first_row + jnp.arange(row_count, dtype=jnp.int32)
    own_seg = segment_index(lengths, local_pos, seq_total)
    wide_seg = segment_index(
        lengths,
        first_row - rim_width + jnp.arange(row_count + 2 * rim_width, dtype=jnp.int32),
        seq_total,
    )
    frame_rows = frames[0]
    grad_out = cotangent[0]
    padded = extended(frame_rows, (("ctx", 0),), rim_width).astype(jnp.float32)
    conv_out = tap_sum(padded, wide_seg, own_seg, w_dw, row_count)
    hidden = (frame_rows.astype(jnp.float32) + jax.nn.silu(conv_out)).astype(jnp.bfloat16)
    kv_local = jnp.dot(hidden, w_kv, preferred_element_type=jnp.float32).astype(jnp.bfloat16)
    kv_rows_all = lax.all_gather(kv_local, "ctx", axis=0, tiled=True)
    key_count = kv_rows_all.shape[0]
    key_seg = segment_index(lengths, jnp.arange(key_count, dtype=jnp.int32), seq_total)
    key_heads = jnp.moveaxis(
        kv_rows_all[:, :feat_width].reshape(key_count, head_count, head_width), 1, 0
    )
    value_heads = jnp.moveaxis(
        kv_rows_all[:, feat_width:].reshape(key_count, head_count, head_width), 1, 0
    )
    query_heads = jnp.moveaxis(hidden.reshape(row_count, head_count, head_width), 1, 0)
    grad_heads = jnp.moveaxis(grad_out.reshape(row_count, head_count, head_width), 1, 0)
    same_utt = own_seg[:, None] == key_seg[None, :]

    def per_head(inputs):
        return head_terms(inputs[0], inputs[1], inputs[2], inputs[3], same_utt, score_scale)

    attended, dquery, dkeys, dvalues, row_top, row_total, rowdot = lax.map(
        per_head, (query_heads, key_heads, value_heads, grad_heads)
    )
    attended = jnp.moveaxis(attended, 0, 1).reshape(row_count, feat_width)
    dquery = jnp.moveaxis(dquery, 0, 1).reshape(row_count, feat_width)
    key_terms = jnp.concatenate(
        [
            jnp.moveaxis(dkeys, 0, 1).reshape(key_count, feat_width),
            jnp.moveaxis(dvalues, 0, 1).reshape(key_count, feat_width),
        ],
        axis=1,
    )
    kv_grad = lax.psum_scatter(
        key_terms.astype(jnp.bfloat16), "ctx", scatter_dimension=0, tiled=True
    )
    output = (hidden.astype(jnp.float32) + attended).astype(jnp.bfloat16)
    dhidden = (
        grad_out.astype(jnp.float32)
        + dquery
        + lax.dot_general(kv_grad, w_kv, contract_last, preferred_element_type=jnp.float32)
    )
    dconv = (dhidden * silu_slope(conv_out)).astype(jnp.bfloat16)
    dconv_pad = extended(dconv, (("ctx", 0),), rim_width).astype(jnp.float32)
    dframes = (dhidden + tap_sum(dconv_pad, wide_seg, own_seg, w_dw[::-1], row_count)).astype(
        jnp.bfloat16
    )
    part_dw = tap_grads(padded, wide_seg, own_seg, dconv.astype(jnp.float32), row_count, KERNEL)
    part_kv = lax.dot_general(hidden, kv_grad, contract_first, preferred_element_type=jnp.float32)
    grad_kv, grad_dw = (
        lax.psum_scatter(part_kv, ("dp", "ctx"), scatter_dimension=0, tiled=True),
        lax.psum_scatter(part_dw, ("dp", "ctx"), scatter_dimension=0, tiled=True),
    )
    return (output[None], dframes[None], grad_kv, grad_dw)


def solution(mesh):
    placed = (P("dp", "ctx", None), P("dp", None), P("dp", "ctx", None), P(), P())
    return jax.shard_map(
        on_device,
        mesh=mesh,
        in_specs=placed,
        out_specs=(
            P("dp", "ctx", None),
            P("dp", "ctx", None),
            P(("dp", "ctx"), None),
            P(("dp", "ctx"), None),
        ),
        check_vma=False,
    )
```

profile of v0, /device:TPU:0, one launch (start us, length us, event | category | flops | bytes accessed | tf_op | source)
XLA Modules:
  0.0 528.5 jit_solution(159612549304523741)
XLA Ops:
  8.0 2.4 collective-permute-start
  18.5 4.3 add_convert_fusion.1
  26.3 25.5 %all-gather.2.cloned.1.call-done = bf16[512,2048]{1,0:T(8,128)(2,1)} async-done(((bf16[128,2048]{1,0:T(8,128)(2,1)}), bf16[512,2048]{1,0:T(8,128)(2,1)}) %all-gather.2.cloned.1.call-update) | async-done | bytes 2097168 | tf_op jit(solution)/shard_map/all_gather | solution.py:118
  55.4 138.0 %while.17 = (s32[]{:T(128)}, f32[16,128,64]{1,2,0:T(8,128)}, f32[16,128,64]{1,2,0:T(8,128)}, bf16[16,512,64]{1,2,0:T(8,128)(2,1)}, bf16[16,512,64]{1,2,0:T(8,128...) while((s32[]{:T(128)}, f32[16,128,64]{1,2,0:T(8,128)}, ...), condition=%wide.region_8.9_spmd.clone, body=%wide.region_4.8_spmd.clone.sunk | while | flops 52035200 | bytes 2465921 | solution.py:134
  56.6 1.7 bitcast_dynamic-update-slice_fusion.2
  65.2 1.7 bitcast_dynamic-update-slice_fusion.2
  73.9 1.7 bitcast_dynamic-update-slice_fusion.2
  82.5 1.7 bitcast_dynamic-update-slice_fusion.2
  99.7 1.7 bitcast_dynamic-update-slice_fusion.2
  108.3 1.7 bitcast_dynamic-update-slice_fusion.2
  125.6 1.7 bitcast_dynamic-update-slice_fusion.2
  134.2 1.7 bitcast_dynamic-update-slice_fusion.2
  151.4 1.7 bitcast_dynamic-update-slice_fusion.2
  160.1 1.7 bitcast_dynamic-update-slice_fusion.2
  168.7 1.7 bitcast_dynamic-update-slice_fusion.2
  195.0 2.5 copy.45
  198.9 30.3 %reduce-scatter.10.cloned.1.call-done = bf16[128,2048]{1,0:T(8,128)(2,1)} async-done(((bf16[512,2048]{1,0:T(8,128)(2,1)}), bf16[128,2048]{1,0:T(8,128)(2,1)}) %reduce-scatter.10.cloned.1.call-update) | async-done | bytes 524304
  229.2 3.9 convolution_add_fusion
  237.3 1.7 fusion.68
  240.6 4.5 fusion.141
  246.4 1.8 collective-permute-start.2
  251.7 4.6 fusion.134
  256.3 118.2 %reduce-scatter.12.cloned.1.call-done = f32[32,31]{1,0:T(8,128)} async-done(((f32[1024,31]{1,0:T(8,128)}), f32[32,31]{1,0:T(8,128)}) %reduce-scatter.12.cloned.1.call-update) | async-done | bytes 3984
  374.5 147.5 %reduce-scatter.8.cloned.1.call-done = f32[32,2048]{1,0:T(8,128)} async-done(((f32[1024,2048]{1,0:T(8,128)}), f32[32,2048]{1,0:T(8,128)}) %reduce-scatter.8.cloned.1.call-update) | async-done | bytes 262160 | tf_op jit(solution)/shard_map/reduce_scatter | solution.py:163
  (331 shorter events, 147.1 us)
Async XLA Ops:
  7.2 44.6 %all-gather.2.cloned.1.call-start = ((), (), s32[]{:S(2)}) async-start(), calls=%async_computation.3 | async-start | bytes 2621440 | tf_op jit(solution)/shard_map/all_gather | solution.py:118
  8.0 9.0 %collective-permute-start = (bf16[15,1024]{1,0:T(8,128)(2,1)S(1)}, bf16[15,1024]{1,0:T(8,128)(2,1)S(1)}, u32[]{:S(2)}, u32[]{:S(2)}) collective-permute-start(bf16[15,1024]{1,0:T(8,128)(2,1)S(1)} %get-tuple-element.200), channel_id=1, source_target_pairs={{0,1},{1,2},{2,3},{4,5},{5,6},{6,7},{8,9},{9,10},{10,11},{12,13},{... | collective-permute-start | bytes 92168 | tf_op jit(solution)/shard_map/ppermute | solution.py:17
  10.4 6.7 %collective-permute-start.1 = (bf16[15,1024]{1,0:T(8,128)(2,1)S(1)}, bf16[15,1024]{1,0:T(8,128)(2,1)S(1)}, u32[]{:S(2)}, u32[]{:S(2)}) collective-permute-start(bf16[15,1024]{1,0:T(8,128)(2,1)S(1)} %get-tuple-element.201), channel_id=1, source_target_pairs={{1,0},{2,1},{3,2},{5,4},{6,5},{7,6},{9,8},{10,9},{11,10},{13,12},{... | collective-permute-start | bytes 92168 | tf_op jit(solution)/shard_map/ppermute | solution.py:20
  12.9 9.9 %copy-start.4 = (f32[1,1024]{1,0:T(1,128)}, f32[1,1024]{1,0:T(1,128)S(1)}, u32[]{:S(2)}) copy-start(f32[1,1024]{1,0:T(1,128)S(1)} %get-tuple-element.223) | copy-start | bytes 12292
  24.4 204.8 %reduce-scatter.10.cloned.1.call-start = ((), (), s32[]{:S(2)}) async-start(), calls=%async_computation.5 | async-start | bytes 2621440
  197.5 35.6 %copy-start.63 = (pred[128]{0:T(512)(128)(4,1)S(1)}, pred[128]{0:T(512)(128)(4,1)}, u32[]{:S(2)}) copy-start(pred[128]{0:T(512)(128)(4,1)} %copy-done.62) | copy-start | bytes 388
  197.5 35.6 %copy-start.65 = (pred[128]{0:T(512)(128)(4,1)S(1)}, pred[128]{0:T(512)(128)(4,1)}, u32[]{:S(2)}) copy-start(pred[128]{0:T(512)(128)(4,1)} %copy-done.64) | copy-start | bytes 388
  197.5 35.6 %copy-start.67 = (pred[128]{0:T(512)(128)(4,1)S(1)}, pred[128]{0:T(512)(128)(4,1)}, u32[]{:S(2)}) copy-start(pred[128]{0:T(512)(128)(4,1)} %copy-done.66) | copy-start | bytes 388
  197.5 35.6 %copy-start.69 = (pred[128]{0:T(512)(128)(4,1)S(1)}, pred[128]{0:T(512)(128)(4,1)}, u32[]{:S(2)}) copy-start(pred[128]{0:T(512)(128)(4,1)} %copy-done.68) | copy-start | bytes 388
  197.5 35.6 %copy-start.71 = (pred[128]{0:T(512)(128)(4,1)S(1)}, pred[128]{0:T(512)(128)(4,1)}, u32[]{:S(2)}) copy-start(pred[128]{0:T(512)(128)(4,1)} %copy-done.70) | copy-start | bytes 388
  197.5 35.6 %copy-start.73 = (pred[128]{0:T(512)(128)(4,1)S(1)}, pred[128]{0:T(512)(128)(4,1)}, u32[]{:S(2)}) copy-start(pred[128]{0:T(512)(128)(4,1)} %copy-done.72) | copy-start | bytes 388
  197.5 35.6 %copy-start.75 = (pred[128]{0:T(512)(128)(4,1)S(1)}, pred[128]{0:T(512)(128)(4,1)}, u32[]{:S(2)}) copy-start(pred[128]{0:T(512)(128)(4,1)} %copy-done.74) | copy-start | bytes 388
  197.6 35.6 %copy-start.77 = (pred[128]{0:T(512)(128)(4,1)S(1)}, pred[128]{0:T(512)(128)(4,1)}, u32[]{:S(2)}) copy-start(pred[128]{0:T(512)(128)(4,1)} %copy-done.76) | copy-start | bytes 388
  197.6 35.6 %copy-start.79 = (pred[128]{0:T(512)(128)(4,1)S(1)}, pred[128]{0:T(512)(128)(4,1)}, u32[]{:S(2)}) copy-start(pred[128]{0:T(512)(128)(4,1)} %copy-done.78) | copy-start | bytes 388
  197.6 176.9 %reduce-scatter.12.cloned.1.call-start = ((), (), s32[]{:S(2)}) async-start(), calls=%async_computation.6 | async-start | bytes 540672
  240.4 281.6 %reduce-scatter.8.cloned.1.call-start = ((), (), s32[]{:S(2)}) async-start(), calls=%async_computation.4 | async-start | bytes 8650752 | tf_op jit(solution)/shard_map/reduce_scatter | solution.py:163
  245.1 6.3 %copy-start.11 = (f32[1,1024]{1,0:T(1,128)S(1)}, f32[1,1024]{1,0:T(1,128)}, u32[]{:S(2)}) copy-start(f32[1,1024]{1,0:T(1,128)} %copy-done.10) | copy-start | bytes 12292
  245.1 6.3 %copy-start.13 = (f32[1,1024]{1,0:T(1,128)S(1)}, f32[1,1024]{1,0:T(1,128)}, u32[]{:S(2)}) copy-start(f32[1,1024]{1,0:T(1,128)} %copy-done.12) | copy-start | bytes 12292
  245.1 6.3 %copy-start.15 = (f32[1,1024]{1,0:T(1,128)S(1)}, f32[1,1024]{1,0:T(1,128)}, u32[]{:S(2)}) copy-start(f32[1,1024]{1,0:T(1,128)} %copy-done.14) | copy-start | bytes 12292
  245.1 6.3 %copy-start.17 = (f32[1,1024]{1,0:T(1,128)S(1)}, f32[1,1024]{1,0:T(1,128)}, u32[]{:S(2)}) copy-start(f32[1,1024]{1,0:T(1,128)} %copy-done.16) | copy-start | bytes 12292
  245.2 6.3 %copy-start.19 = (f32[1,1024]{1,0:T(1,128)S(1)}, f32[1,1024]{1,0:T(1,128)}, u32[]{:S(2)}) copy-start(f32[1,1024]{1,0:T(1,128)} %copy-done.18) | copy-start | bytes 12292
  245.2 6.3 %copy-start.21 = (f32[1,1024]{1,0:T(1,128)S(1)}, f32[1,1024]{1,0:T(1,128)}, u32[]{:S(2)}) copy-start(f32[1,1024]{1,0:T(1,128)} %copy-done.20) | copy-start | bytes 12292
  246.4 3.8 collective-permute-start.2
  248.1 3.2 collective-permute-start.3
  (66 other events, 300.9 us)
Sparse Core Ops, SparseCore 0:
  24.5 27.1 all-gather.1
  197.7 31.4 reduce-scatter.9
  240.5 133.9 reduce-scatter.11
  377.2 144.7 reduce-scatter.7
where the time goes:
time: 536 us; the launch traced here: 528 us
  waiting for transfers between devices  323 us (60%)
  matrix products  132 us (25%)
  other arithmetic  36 us (7%)
  between operations  15.2 us (3%)
  local copies, waits for them, and re-layouts  14.9 us (3%)
  starting transfers between devices  7.04 us (1%)
    unnamed x6, waiting for transfers between devices  149 us
    reduce_scatter x1, waiting for transfers between devices, on_device(): lax.psum_scatter(part_kv, ('dp', 'ctx'), scatter_dimension=0, tiled=True)  148 us
    dot_general x16, matrix products, head_terms(): jnp.dot(probs_low, value_rows, preferred_element_type=jnp.float32)  27.5 us
    dot_general x16, matrix products, head_terms(): lax.dot_general(probs_low, grad_rows, contract_first, preferred_element_t...  25.7 us
    all_gather x1, waiting for transfers between devices, on_device(): kv_rows_all = lax.all_gather(kv_local, 'ctx', axis=0, tiled=True)  25.5 us
    dot_general x16, matrix products, head_terms(): lax.dot_general(dscores, query_rows, contract_first, preferred_element_ty...  23.8 us
    dot_general x16, matrix products, head_terms(): lax.dot_general(grad_rows, value_rows, contract_last, preferred_element_t...  17.1 us
    dot_general x16, matrix products, head_terms(): lax.dot_general(query_rows, key_rows, contract_last, preferred_element_ty...  16.1 us
  transfers between devices with their start and end apart: 8, of which 5 were waited for; matrix products, arithmetic and copies ran while one was open for 3% of the time, Pallas kernels for 0%

commit v1 on v0

--- a/solution.py
+++ b/solution.py
@@ -1,12 +1,20 @@
+import functools
 import math
 
 import jax
 import jax.numpy as jnp
 from jax import lax
+from jax.experimental import pallas as pl
+from jax.experimental.pallas import tpu as pltpu
 from jax.sharding import PartitionSpec as P
 
 H = 16
 KERNEL = 31
+RIM = KERNEL // 2
+SUB = 8
+CHUNK = 6
+SWAP = (0, 2, 1, 3)
+VMEM_LIMIT = 56 * 1024 * 1024
 
 
 def extended(block, sides, width):
@@ -90,7 +98,7 @@
     return (attended, dquery, dkeys, dvalues, row_top[:, 0], row_total[:, 0], rowdot[:, 0])
 
 
-def on_device(frames, utt_lengths, cotangent, w_dw, w_kv):
+def on_device_any(frames, utt_lengths, cotangent, w_dw, w_kv):
     row_count = frames.shape[1]
     feat_width = frames.shape[2]
     head_count = H
@@ -166,6 +174,463 @@
     return (output[None], dframes[None], grad_kv, grad_dw)
 
 
+def nt_dot(left, right):
+    return lax.dot_general(left, right, (((1,), (1,)), ((), ())), preferred_element_type=jnp.float32)
+
+
+def tn_dot(left, right):
+    return lax.dot_general(left, right, (((0,), (0,)), ((), ())), preferred_element_type=jnp.float32)
+
+
+def utt_index(len_ref, frame_pos):
+    end = jnp.int32(0)
+    counted = jnp.zeros(frame_pos.shape, jnp.int32)
+    for utt in range(len_ref.shape[1]):
+        end = end + len_ref[0, utt]
+        counted = counted + (frame_pos >= end).astype(jnp.int32)
+    return counted
+
+
+def frame_at(row, own_index, row_count):
+    shift = row_count.bit_length() - 1
+    return ((own_index ^ (row >> shift)) << shift) + (row & (row_count - 1))
+
+
+def spaced_pos(len_ref, row, own_index, row_count):
+    frame_pos = frame_at(row, own_index, row_count)
+    return frame_pos + RIM * utt_index(len_ref, frame_pos)
+
+
+def spaced_steps(seq_total, utt_count):
+    rows = seq_total + RIM * (utt_count - 1)
+    return -(-rows // (SUB * CHUNK)) * CHUNK
+
+
+def spread_matrix(len_ref, own_index, row_count, seq_total, steps):
+    slot = lax.broadcasted_iota(jnp.int32, (steps * SUB, seq_total), 0)
+    slot_pos = (slot & (SUB - 1)) * steps + (slot >> 3)
+    row = lax.broadcasted_iota(jnp.int32, (1, seq_total), 1)
+    return (slot_pos == spaced_pos(len_ref, row, own_index, row_count)).astype(jnp.float32).astype(jnp.bfloat16)
+
+
+def gather_matrix(len_ref, own_index, row_count, seq_total, steps):
+    slot = lax.broadcasted_iota(jnp.int32, (1, steps * SUB), 1)
+    slot_pos = (slot & (SUB - 1)) * steps + (slot >> 3)
+    row = lax.broadcasted_iota(jnp.int32, (seq_total, 1), 0)
+    return (slot_pos == spaced_pos(len_ref, row, own_index, row_count)).astype(jnp.float32).astype(jnp.bfloat16)
+
+
+def write_extended(ext_ref, spaced, steps):
+    width = spaced.shape[1]
+    blocks = spaced.reshape(steps, SUB, width)
+    ext_ref[RIM : RIM + steps] = blocks
+    sub = lax.broadcasted_iota(jnp.int32, (RIM, SUB, width), 1)
+    ext_ref[0:RIM] = jnp.where(sub == 0, 0.0, pltpu.roll(blocks[steps - RIM :], 1, 1))
+    ext_ref[RIM + steps :] = jnp.where(sub == SUB - 1, 0.0, pltpu.roll(blocks[:RIM], SUB - 1, 1))
+
+
+def conv_loop(ext_ref, taps_ref, lanes, steps, flipped, finish):
+    def body(chunk, carry):
+        start = chunk * CHUNK
+        window = [ext_ref[start + m, :, lanes] for m in range(CHUNK + KERNEL - 1)]
+        sums = [None] * CHUNK
+        for tap in range(KERNEL):
+            weight = taps_ref[tap, :, lanes]
+            shift = KERNEL - 1 - tap if flipped else tap
+            for a in range(CHUNK):
+                term = window[a + shift] * weight
+                sums[a] = term if sums[a] is None else sums[a] + term
+        for a in range(CHUNK):
+            finish(start + a, sums[a], window[a + RIM])
+        return carry
+
+    lax.fori_loop(0, steps // CHUNK, body, 0)
+
+
+def pack_kernel(meta_ref, frames_ref, cot_ref, *outs):
+    group = meta_ref[1]
+    width = outs[4].shape[1]
+    for j in range(4):
+        target = group ^ SWAP[j]
+        for part in range(2):
+            start = pl.multiple_of((target ^ part) * width, width)
+            outs[j][:, part * width : (part + 1) * width] = frames_ref[:, pl.ds(start, width)]
+        start = pl.multiple_of(target * width, width)
+        outs[4 + j][...] = cot_ref[:, pl.ds(start, width)]
+
+
+def forward_conv_kernel(
+    meta_ref, len_ref, f0, f1, f2, f3, w_own_ref, w_oth_ref, hid_ref, xext_ref, conv_ref, ext_ref, taps_ref, hid_sp_ref
+):
+    own_index = meta_ref[0]
+    row_count = f0.shape[0]
+    seq_total = 4 * row_count
+    width = f0.shape[1]
+    half = width // 2
+    steps = conv_ref.shape[0]
+    rows = jnp.concatenate([f0[...], f1[...], f2[...], f3[...]], axis=0)
+    spread = spread_matrix(len_ref, own_index, row_count, seq_total, steps)
+    spaced = jnp.dot(spread, rows, preferred_element_type=jnp.float32)
+    write_extended(ext_ref, spaced, steps)
+    for tap in range(KERNEL):
+        taps_ref[tap, :, :half] = jnp.broadcast_to(w_own_ref[tap : tap + 1, :], (SUB, half))
+        taps_ref[tap, :, half:] = jnp.broadcast_to(w_oth_ref[tap : tap + 1, :], (SUB, half))
+    for lane in range(0, width, 128):
+        lanes = slice(lane, lane + 128)
+
+        def finish(step, conv, center, lane=lane, lanes=lanes):
+            hid_sp_ref[step, :, lanes] = center + conv / (1.0 + jnp.exp(-conv))
+            if lane < half:
+                conv_ref[step, :, lanes] = conv
+
+        conv_loop(ext_ref, taps_ref, lanes, steps, False, finish)
+    xext_ref[...] = ext_ref[:, :, :half]
+    hid_low = hid_sp_ref[...].reshape(steps * SUB, width).astype(jnp.bfloat16)
+    gather = gather_matrix(len_ref, own_index, row_count, seq_total, steps)
+    hid_ref[...] = jnp.dot(gather, hid_low, preferred_element_type=jnp.float32).astype(jnp.bfloat16)
+
+
+def swapped(array, order, row_count):
+    return jnp.concatenate([array[b * row_count : (b + 1) * row_count] for b in order], axis=0)
+
+
+def attention_kernel(
+    meta_ref, len_ref, hid_ref, sib_ref, c0, c1, c2, c3, wk_ref, wv_ref,
+    out_ref, keep_ref, send_ref, kvg_ref,
+    k_ref, v_ref, kt_ref, vt_ref, cot_ref, cott_ref, attt_ref, dqt_ref, dk_ref, dv_ref, bias_ref,
+):
+    own_index, group = meta_ref[0], meta_ref[1]
+    row_count = c0.shape[0]
+    seq_total = 4 * row_count
+    width = c0.shape[1]
+    head_width = 64
+    scale = 1.0 / math.sqrt(head_width)
+    bf16, f32 = jnp.bfloat16, jnp.float32
+    parts = [
+        hid_ref[:, :width],
+        hid_ref[:, width:],
+        swapped(sib_ref[:, :width], (1, 0, 3, 2), row_count),
+        swapped(sib_ref[:, width:], (1, 0, 3, 2), row_count),
+    ]
+
+    def w_rows(ref, j):
+        return ref[pl.ds(pl.multiple_of((group ^ j) * width, width), width), :]
+
+    keys = sum(jnp.dot(parts[j], w_rows(wk_ref, j), preferred_element_type=f32) for j in range(4)).astype(bf16)
+    values = sum(jnp.dot(parts[j], w_rows(wv_ref, j), preferred_element_type=f32) for j in range(4)).astype(bf16)
+    k_ref[...] = keys
+    v_ref[...] = values
+    kt_ref[...] = keys.T
+    vt_ref[...] = values.T
+    cot = jnp.concatenate([c0[...], c1[...], c2[...], c3[...]], axis=0)
+    cot_ref[...] = cot
+    cott_ref[...] = cot.T.astype(f32)
+    key_row = lax.broadcasted_iota(jnp.int32, (seq_total, 1), 0)
+    query_row = lax.broadcasted_iota(jnp.int32, (1, seq_total), 1)
+    key_utt = utt_index(len_ref, frame_at(key_row, own_index, row_count))
+    query_utt = utt_index(len_ref, frame_at(query_row, own_index, row_count))
+    bias_ref[...] = jnp.where(key_utt == query_utt, 0.0, -jnp.inf).astype(f32)
+    dk_ref[...] = jnp.zeros_like(dk_ref)
+    dv_ref[...] = jnp.zeros_like(dv_ref)
+    lane = lax.broadcasted_iota(jnp.int32, (1, 128), 1)
+    masks = [(lane < head_width).astype(f32).astype(bf16), (lane >= head_width).astype(f32).astype(bf16)]
+    query_block = min(256, seq_total)
+    blocks = seq_total // query_block
+    exp_scale = scale * math.log2(math.e)
+
+    def step(it, carry):
+        pair = it // blocks
+        q0 = pl.multiple_of((it % blocks) * query_block, query_block)
+        l0 = pl.multiple_of(pair * 128, 128)
+        qrows = pl.ds(q0, query_block)
+        lanes = pl.ds(l0, 128)
+        query = hid_ref[qrows, lanes]
+        grad = cot_ref[qrows, lanes]
+        k_pair = k_ref[:, lanes]
+        v_pair = v_ref[:, lanes]
+        dk_sum = dk_ref[:, lanes]
+        dv_sum = dv_ref[:, lanes]
+        for head in range(2):
+            mask = masks[head]
+            hrows = pl.ds(pl.multiple_of(l0 + head * head_width, head_width), head_width)
+            scores = nt_dot(k_pair * mask, query) + bias_ref[:, qrows]
+            top = jnp.max(scores, axis=0, keepdims=True)
+            expd = jnp.exp2((scores - top) * exp_scale)
+            probs = expd * (1.0 / jnp.sum(expd, axis=0, keepdims=True))
+            probs_low = probs.astype(bf16)
+            attended = jnp.dot(vt_ref[hrows, :], probs_low, preferred_element_type=f32)
+            dprobs = nt_dot(v_pair * mask, grad)
+            rowdot = jnp.sum(cott_ref[hrows, qrows] * attended, axis=0, keepdims=True)
+            dscores = (probs * (dprobs - rowdot)).astype(bf16)
+            attt_ref[hrows, qrows] = attended
+            dqt_ref[hrows, qrows] = jnp.dot(kt_ref[hrows, :], dscores, preferred_element_type=f32) * scale
+            dk_sum = dk_sum + jnp.dot(dscores, query * mask, preferred_element_type=f32)
+            dv_sum = dv_sum + jnp.dot(probs_low, grad * mask, preferred_element_type=f32)
+        dk_ref[:, lanes] = dk_sum
+        dv_ref[:, lanes] = dv_sum
+        return carry
+
+    lax.fori_loop(0, (width // 128) * blocks, step, 0)
+    out_ref[...] = (parts[0].astype(f32) + attt_ref[...].T).astype(bf16)
+    grad_k = (dk_ref[...] * scale).astype(bf16)
+    grad_v = dv_ref[...].astype(bf16)
+    kvg_ref[:, :width] = grad_k
+    kvg_ref[:, width:] = grad_v
+
+    def partial(j):
+        return nt_dot(grad_k, w_rows(wk_ref, j)) + nt_dot(grad_v, w_rows(wv_ref, j))
+
+    send_ref[:, :width] = partial(2).astype(bf16)
+    send_ref[:, width:] = partial(3).astype(bf16)
+    keep_ref[:, :width] = partial(0) + dqt_ref[...].T + cot.astype(f32)
+    keep_ref[:, width:] = partial(1)
+
+
+def weight_grad_kernel(meta_ref, hid_ref, sib_ref, kvg_ref, *refs):
+    outs, all_ref = refs[:-1], refs[-1]
+    group, dp_index = meta_ref[1], meta_ref[2]
+    width = hid_ref.shape[1] // 2
+    row_count = hid_ref.shape[0] // 4
+    kvg = kvg_ref[...]
+    parts = [
+        hid_ref[:, :width],
+        hid_ref[:, width:],
+        swapped(sib_ref[:, :width], (1, 0, 3, 2), row_count),
+        swapped(sib_ref[:, width:], (1, 0, 3, 2), row_count),
+    ]
+    for j in range(4):
+        start = pl.multiple_of((group ^ j) * width, width)
+        all_ref[pl.ds(start, width), :] = tn_dot(parts[j], kvg).astype(jnp.bfloat16)
+    block = outs[0].shape[0]
+    for k in range(len(outs)):
+        start = pl.multiple_of((dp_index ^ k) * block, block)
+        outs[k][...] = all_ref[pl.ds(start, block), :]
+
+
+def chip_sum_kernel(keep_ref, recv_ref, own_ref, send_ref):
+    width = keep_ref.shape[1] // 2
+    row_count = keep_ref.shape[0] // 4
+    total = keep_ref[...] + swapped(recv_ref[...], (1, 0, 3, 2), row_count).astype(jnp.float32)
+    own_ref[...] = total[:, :width]
+    send_ref[...] = total[:, width:].astype(jnp.bfloat16)
+
+
+def backward_conv_kernel(
+    meta_ref, len_ref, own_ref, recv_ref, xext_ref, conv_ref, w_ref, dframes_ref, gdw_ref,
+    ext_ref, taps_ref, dh_ref, df_ref,
+):
+    own_index = meta_ref[0]
+    seq_total, width = own_ref.shape
+    row_count = seq_total // 4
+    steps = conv_ref.shape[0]
+    bf16, f32 = jnp.bfloat16, jnp.float32
+    dhidden = own_ref[...] + swapped(recv_ref[...], (2, 3, 0, 1), row_count).astype(f32)
+    high = dhidden.astype(bf16)
+    low = (dhidden - high.astype(f32)).astype(bf16)
+    spread = spread_matrix(len_ref, own_index, row_count, seq_total, steps)
+    both = jnp.dot(spread, jnp.concatenate([high, low], axis=1), preferred_element_type=f32)
+    spaced = both[:, :width] + both[:, width:]
+    dh_ref[...] = spaced.reshape(steps, SUB, width)
+    conv = conv_ref[...].reshape(steps * SUB, width)
+    gate = 1.0 / (1.0 + jnp.exp(-conv))
+    dconv = (spaced * (gate * (1.0 + conv * (1.0 - gate)))).astype(bf16).astype(f32)
+    write_extended(ext_ref, dconv, steps)
+    for tap in range(KERNEL):
+        taps_ref[tap] = jnp.broadcast_to(w_ref[tap : tap + 1, :], (SUB, width))
+    half_taps = (KERNEL + 1) // 2
+    for lane in range(0, width, 128):
+        lanes = slice(lane, lane + 128)
+
+        def finish(step, conv, center, lanes=lanes):
+            df_ref[step, :, lanes] = dh_ref[step, :, lanes] + conv
+
+        conv_loop(ext_ref, taps_ref, lanes, steps, True, finish)
+        for first in range(0, KERNEL, half_taps):
+            count = min(half_taps, KERNEL - first)
+
+            def body(chunk, sums, lanes=lanes, first=first, count=count):
+                start = chunk * CHUNK
+                window = [xext_ref[start + first + m, :, lanes] for m in range(CHUNK + count - 1)]
+                grads = [ext_ref[start + RIM + a, :, lanes] for a in range(CHUNK)]
+                return tuple(
+                    functools.reduce(lambda x, y: x + y, [grads[a] * window[a + t] for a in range(CHUNK)], sums[t])
+                    for t in range(count)
+                )
+
+            zero = tuple(jnp.zeros((SUB, 128), f32) for _ in range(count))
+            sums = lax.fori_loop(0, steps // CHUNK, body, zero)
+            for t in range(count):
+                gdw_ref[first + t : first + t + 1, lanes] = jnp.sum(sums[t], axis=0, keepdims=True)
+    gdw_ref[KERNEL:, :] = jnp.zeros((gdw_ref.shape[0] - KERNEL, width), f32)
+    gather = gather_matrix(len_ref, own_index, row_count, seq_total, steps)
+    df_low = df_ref[...].reshape(steps * SUB, width).astype(bf16)
+    dframes_ref[...] = jnp.dot(gather, df_low, preferred_element_type=f32).astype(bf16)
+
+
+def place_kernel(meta_ref, own_ref, r1, r2, r3, out_ref, dframes_ref):
+    group = meta_ref[1]
+    row_count = out_ref.shape[0]
+    width = own_ref.shape[1] // 2
+    for j, ref in enumerate((own_ref, r1, r2, r3)):
+        start = pl.multiple_of((group ^ SWAP[j]) * width, width)
+        out_ref[:, pl.ds(start, width)] = ref[:row_count, :width]
+        dframes_ref[:, pl.ds(start, width)] = ref[:row_count, width:]
+
+
+def dp_sum_kernel(meta_ref, *refs):
+    ins, outs, total_ref = refs[:8], refs[8:12], refs[12]
+    own_index = meta_ref[0]
+    total = ins[0][...].astype(jnp.float32)
+    for ref in ins[1:]:
+        total = total + ref[...].astype(jnp.float32)
+    total_ref[...] = total
+    block = outs[0].shape[0]
+    for j in range(4):
+        start = pl.multiple_of((own_index ^ j) * block, block)
+        outs[j][...] = total_ref[pl.ds(start, block), :].astype(outs[j].dtype)
+
+
+def place_grad_kernel(meta_ref, own_ref, r1, r2, r3, out_ref):
+    group = meta_ref[1]
+    width = own_ref.shape[1] // 2
+    full = out_ref.shape[1] // 2
+    for j, ref in enumerate((own_ref, r1, r2, r3)):
+        start = pl.multiple_of((group ^ SWAP[j]) * width, width)
+        out_ref[:, pl.ds(start, width)] = ref[:, :width].astype(jnp.float32)
+        out_ref[:, pl.ds(full + start, width)] = ref[:, width:].astype(jnp.float32)
+
+
+def call(kernel, scalars, args, in_specs, outs, scratch=()):
+    def whole(shape):
+        zeros = (0,) * len(shape)
+        return pl.BlockSpec(shape, lambda *_: zeros)
+
+    specs = [whole(arg.shape) if spec is None else spec for arg, spec in zip(args, in_specs, strict=True)]
+    return pl.pallas_call(
+        kernel,
+        out_shape=[jax.ShapeDtypeStruct(shape, dtype) for shape, dtype in outs],
+        grid_spec=pltpu.PrefetchScalarGridSpec(
+            num_scalar_prefetch=len(scalars),
+            grid=(1,),
+            in_specs=specs,
+            out_specs=[whole(shape) for shape, _ in outs],
+            scratch_shapes=list(scratch),
+        ),
+        compiler_params=pltpu.CompilerParams(vmem_limit_bytes=VMEM_LIMIT),
+    )(*scalars, *args)
+
+
+def swap_ctx(array, j):
+    return lax.ppermute(array, "ctx", [(i, i ^ j) for i in range(4)])
+
+
+def on_device_pairs(frames, utt_lengths, cotangent, w_dw, w_kv):
+    row_count, feat_width = frames.shape[1:]
+    width = feat_width // 4
+    seq_total = 4 * row_count
+    steps = spaced_steps(seq_total, utt_lengths.shape[1])
+    bf16, f32 = jnp.bfloat16, jnp.float32
+    ctx_index, dp_index = lax.axis_index("ctx"), lax.axis_index("dp")
+    dp_size = lax.axis_size("dp")
+    group = 2 * (ctx_index & 1) + (ctx_index >> 1)
+    meta = jnp.stack([ctx_index, group, dp_index]).astype(jnp.int32)
+    lengths = utt_lengths
+
+    packed = call(
+        pack_kernel, (meta,), (frames[0], cotangent[0]), (None, None),
+        [((row_count, 2 * width), bf16)] * 4 + [((row_count, width), bf16)] * 4,
+    )
+    frame_blocks = [packed[0]] + [swap_ctx(packed[j], j) for j in (1, 2, 3)]
+    cot_blocks = [packed[4]] + [swap_ctx(packed[4 + j], j) for j in (1, 2, 3)]
+
+    tap_specs = [
+        pl.BlockSpec((KERNEL, width), lambda i, meta, lens, part=part: (0, meta[1] ^ part)) for part in range(2)
+    ]
+    hidden, frames_ext, conv_own = call(
+        forward_conv_kernel, (meta, lengths), (*frame_blocks, w_dw, w_dw), (None,) * 4 + tuple(tap_specs),
+        [((seq_total, 2 * width), bf16), ((steps + 2 * RIM, SUB, width), f32), ((steps, SUB, width), f32)],
+        [
+            pltpu.VMEM((steps + 2 * RIM, SUB, 2 * width), f32),
+            pltpu.VMEM((KERNEL, SUB, 2 * width), f32),
+            pltpu.VMEM((steps, SUB, 2 * width), f32),
+        ],
+    )
+    hidden_sib = swap_ctx(hidden, 1)
+
+    wide = (seq_total, width)
+    both = (seq_total, 2 * width)
+    kv_specs = [
+        pl.BlockSpec((feat_width, width), lambda i, meta, lens, part=part: (0, meta[1] + 4 * part))
+        for part in range(2)
+    ]
+    out_own, keep, send, kv_grad = call(
+        attention_kernel, (meta, lengths), (hidden, hidden_sib, *cot_blocks, w_kv, w_kv),
+        (None,) * 6 + tuple(kv_specs),
+        [(wide, bf16), (both, f32), (both, bf16), (both, bf16)],
+        [
+            pltpu.VMEM(wide, bf16), pltpu.VMEM(wide, bf16), pltpu.VMEM(wide[::-1], bf16), pltpu.VMEM(wide[::-1], bf16),
+            pltpu.VMEM(wide, bf16), pltpu.VMEM(wide[::-1], f32), pltpu.VMEM(wide[::-1], f32),
+            pltpu.VMEM(wide[::-1], f32), pltpu.VMEM(wide, f32), pltpu.VMEM(wide, f32),
+            pltpu.VMEM((seq_total, seq_total), f32),
+        ],
+    )
+    from_sib = swap_ctx(send, 1)
+    grad_blocks = call(
+        weight_grad_kernel, (meta,), (hidden, hidden_sib, kv_grad), (None,) * 3,
+        [((feat_width // dp_size, 2 * width), bf16)] * dp_size,
+        [pltpu.VMEM((feat_width, 2 * width), bf16)],
+    )
+    part_own, part_send = call(
+        chip_sum_kernel, (), (keep, from_sib), (None,) * 2, [(wide, f32), (wide, bf16)]
+    )
+    from_chip = swap_ctx(part_send, 2)
+    grad_recv = [grad_blocks[0]] + [
+        lax.ppermute(grad_blocks[k], "dp", [(i, i ^ k) for i in range(dp_size)]) for k in range(1, dp_size)
+    ]
+    dframes, part_dw = call(
+        backward_conv_kernel, (meta, lengths), (part_own, from_chip, frames_ext, conv_own, w_dw),
+        (None,) * 4 + (tap_specs[0],),
+        [(wide, bf16), ((KERNEL + 1, width), f32)],
+        [
+            pltpu.VMEM((steps + 2 * RIM, SUB, width), f32),
+            pltpu.VMEM((KERNEL, SUB, width), f32),
+            pltpu.VMEM((steps, SUB, width), f32),
+            pltpu.VMEM((steps, SUB, width), f32),
+        ],
+    )
+    results = jnp.concatenate([out_own, dframes], axis=1)
+    result_blocks = [results] + [
+        swap_ctx(results[j * row_count : (j + 1) * row_count], j) for j in (1, 2, 3)
+    ]
+    output, dframes_rows = call(
+        place_kernel, (meta,), tuple(result_blocks), (None,) * 4, [((row_count, feat_width), bf16)] * 2
+    )
+    piece = feat_width // dp_size // 4
+    sums = call(
+        dp_sum_kernel, (meta,), tuple(grad_recv), (None,) * 8,
+        [((piece, 2 * width), f32)] + [((piece, 2 * width), bf16)] * 3,
+        [pltpu.VMEM((4 * piece, 2 * width), f32)],
+    )
+    sum_blocks = [sums[0]] + [swap_ctx(sums[j], j) for j in (1, 2, 3)]
+    (grad_kv,) = call(
+        place_grad_kernel, (meta,), tuple(sum_blocks), (None,) * 4, [((piece, 2 * feat_width), f32)]
+    )
+    owners = width // piece
+    by_owner = jnp.moveaxis(part_dw.reshape(KERNEL + 1, owners, piece), 1, 0).reshape(owners, -1, 128)
+    spread_dw = lax.dynamic_update_slice_in_dim(
+        jnp.zeros((4 * owners,) + by_owner.shape[1:], f32), by_owner, group * owners, axis=0
+    )
+    all_dw = lax.all_to_all(spread_dw, ("dp", "ctx"), 0, 0)
+    grad_dw = jnp.sum(all_dw, axis=0).reshape(KERNEL + 1, piece).T[:, :KERNEL]
+    return (output[None], dframes_rows[None], grad_kv, grad_dw)
+
+
+def on_device(frames, utt_lengths, cotangent, w_dw, w_kv):
+    if lax.axis_size("ctx") == 4 and lax.axis_size("dp") == 8:
+        return on_device_pairs(frames, utt_lengths, cotangent, w_dw, w_kv)
+    return on_device_any(frames, utt_lengths, cotangent, w_dw, w_kv)
+
+
 def solution(mesh):
     placed = (P("dp", "ctx", None), P("dp", None), P("dp", "ctx", None), P(), P())
     return jax.shard_map(

time: 536 us -> 110 us (0.21)
  the two profiles are of different devices: /device:TPU:0 before, /device:TPU:9 now
where the time goes in v1:
time: 110 us
  Pallas kernels  46.5 us (42%)
  starting transfers between devices  26.7 us (24%)
  waiting for transfers between devices  25.4 us (23%)
  local copies, waits for them, and re-layouts  9.8 us (9%)
    pallas_call x9, Pallas kernels, call(): pl.pallas_call(kernel, out_shape=[jax.ShapeDtypeStruct(shape, dtype) for...  46.5 us
    ppermute x15, waiting for transfers between devices, swap_ctx(): return lax.ppermute(array, 'ctx', [(i, i ^ j) for i in range(4)])  14.4 us
    ppermute x15, starting transfers between devices, swap_ctx(): return lax.ppermute(array, 'ctx', [(i, i ^ j) for i in range(4)])  11.9 us
    ppermute x7, waiting for transfers between devices, on_device_pairs(): lax.ppermute(grad_blocks[k], 'dp', [(i, i ^ k) for i in range(dp_size)])  10.9 us
    ppermute x7, starting transfers between devices, on_device_pairs(): lax.ppermute(grad_blocks[k], 'dp', [(i, i ^ k) for i in range(dp_size)])  8.58 us
    unnamed x52, local copies, waits for them, and re-layouts  6.51 us
    all_to_all x1, starting transfers between devices, on_device_pairs(): all_dw = lax.all_to_all(spread_dw, ('dp', 'ctx'), 0, 0)  6.18 us
  transfers between devices with their start and end apart: 23, of which 9 were waited for; matrix products, arithmetic and copies ran while one was open for 4% of the time, Pallas kernels for 18%

profile of v1, /device:TPU:9, one launch (start us, length us, event | category | flops | bytes accessed | tf_op | source)
XLA Modules:
  0.0 109.8 jit_solution(7403090331765318248)
XLA Ops:
  1.3 2.6 %shard_map.84 = (bf16[128,512]{1,0:T(8,128)(2,1)}, bf16[128,512]{1,0:T(8,128)(2,1)}, bf16[128,512]{1,0:T(8,128)(2,1)}, bf16[128,512]{1,0:T(8,128)(2,1)}, bf16[12...) custom-call(s32[3]{0:T(128)} %pad_add_fusion.meta_ref, ...), custom_call_target="tpu_custom_call" | custom-call | tf_op jit(solution)/shard_map/pallas_call | solution.py:509
  6.2 3.6 %collective-permute-done.1.f2 = bf16[128,512]{1,0:T(8,128)(2,1)S(1)} collective-permute-done((bf16[128,512]{1,0:T(8,128)(2,1)}, bf16[128,512]{1,0:T(8,128)(2,1)S(1)}, u32[]{:S(2)}, u32[]{:S(2)}) %collective-permute-start.1) | collective-permute-done | bytes 131104 | tf_op jit(solution)/shard_map/ppermute | solution.py:524
  9.8 3.0 %collective-permute-done.2.f3 = bf16[128,512]{1,0:T(8,128)(2,1)S(1)} collective-permute-done((bf16[128,512]{1,0:T(8,128)(2,1)}, bf16[128,512]{1,0:T(8,128)(2,1)S(1)}, u32[]{:S(2)}, u32[]{:S(2)}) %collective-permute-start.2) | collective-permute-done | bytes 131104 | tf_op jit(solution)/shard_map/ppermute | solution.py:524
  13.5 8.4 %shard_map.85 = (bf16[512,512]{1,0:T(8,128)(2,1)}, f32[108,8,256]{2,1,0:T(8,128)}, f32[78,8,256]{2,1,0:T(8,128)}) custom-call(s32[3]{0:T(128)} %pad_add_fusion.meta_ref, s32[1,8]{1,0:T(1,128)} %len_ref.5, bf16[128,512]{1,0:T(8,128)(2,1)} %get-tuple-element.37.f0, bf16[128,512]{1,0:T(8,128)(2,1)} %copy-done.7, bf16[128,512]{1,0:T(8,128)(2,1)} %copy-done.8, ...), custom_call_target="tpu_custom_call" | custom-call | tf_op jit(solution)/shard_map/pallas_call | solution.py:509
  24.2 1.4 %collective-permute-done.5.c2 = bf16[128,256]{1,0:T(8,128)(2,1)S(1)} collective-permute-done((bf16[128,256]{1,0:T(8,128)(2,1)}, bf16[128,256]{1,0:T(8,128)(2,1)S(1)}, u32[]{:S(2)}, u32[]{:S(2)}) %collective-permute-start.5) | collective-permute-done | bytes 65568 | tf_op jit(solution)/shard_map/ppermute | solution.py:524
  25.7 2.4 %collective-permute-done.6.c3 = bf16[128,256]{1,0:T(8,128)(2,1)S(1)} collective-permute-done((bf16[128,256]{1,0:T(8,128)(2,1)}, bf16[128,256]{1,0:T(8,128)(2,1)S(1)}, u32[]{:S(2)}, u32[]{:S(2)}) %collective-permute-start.6) | collective-permute-done | bytes 65568 | tf_op jit(solution)/shard_map/ppermute | solution.py:524
  28.9 13.3 %shard_map.86 = (bf16[512,256]{1,0:T(8,128)(2,1)}, f32[512,512]{1,0:T(8,128)}, bf16[512,512]{1,0:T(8,128)(2,1)}, bf16[512,512]{1,0:T(8,128)(2,1)}) custom-call(s32[3]{0:T(128)} %pad_add_fusion.meta_ref, s32[1,8]{1,0:T(1,128)} %len_ref.5, bf16[512,512]{1,0:T(8,128)(2,1)} %get-tuple-element.41.hid_ref, bf16[512,512]{1,0:T(8,128)(2,1)} %copy-done.1, ...), custom_call_target="tpu_custom_call" | custom-call | tf_op jit(solution)/shard_map/pallas_call | solution.py:509
  42.7 1.7 %collective-permute-done.7.recv_ref = bf16[512,512]{1,0:T(8,128)(2,1)S(1)} collective-permute-done((bf16[512,512]{1,0:T(8,128)(2,1)}, bf16[512,512]{1,0:T(8,128)(2,1)S(1)}, u32[]{:S(2)}, u32[]{:S(2)}) %collective-permute-start.7) | collective-permute-done | bytes 524320 | tf_op jit(solution)/shard_map/ppermute | solution.py:524
  45.2 2.3 %shard_map.87 = (f32[512,256]{1,0:T(8,128)}, bf16[512,256]{1,0:T(8,128)(2,1)}) custom-call(f32[512,512]{1,0:T(8,128)} %get-tuple-element.47.keep_ref, bf16[512,512]{1,0:T(8,128)(2,1)} %copy-done.2), custom_call_target="tpu_custom_call" | custom-call | tf_op jit(solution)/shard_map/pallas_call | solution.py:509
  48.4 3.7 %shard_map.90 = (bf16[128,512]{1,0:T(8,128)(2,1)}, bf16[128,512]{1,0:T(8,128)(2,1)}, bf16[128,512]{1,0:T(8,128)(2,1)}, bf16[128,512]{1,0:T(8,128)(2,1)}, bf16[12...) custom-call(s32[3]{0:T(128)} %pad_add_fusion.meta_ref, ...), custom_call_target="tpu_custom_call" | custom-call | tf_op jit(solution)/shard_map/pallas_call | solution.py:509
  52.1 1.3 %collective-permute-start.12 = (bf16[128,512]{1,0:T(8,128)(2,1)}, bf16[128,512]{1,0:T(8,128)(2,1)S(1)}, u32[]{:S(2)}, u32[]{:S(2)}) collective-permute-start(bf16[128,512]{1,0:T(8,128)(2,1)} %get-tuple-element.58), channel_id=1, source_target_pairs={{0,4},{4,0},{8,12},{12,8},{16,20},{20,16},{24,28},{28,24},{1,5},{5... | collective-permute-start | bytes 393224 | tf_op jit(solution)/shard_map/ppermute | solution.py:588
  54.8 2.3 %collective-permute-start.15 = (bf16[128,512]{1,0:T(8,128)(2,1)}, bf16[128,512]{1,0:T(8,128)(2,1)S(1)}, u32[]{:S(2)}, u32[]{:S(2)}) collective-permute-start(bf16[128,512]{1,0:T(8,128)(2,1)} %get-tuple-element.61), channel_id=1, source_target_pairs={{0,16},{4,20},{8,24},{12,28},{16,0},{20,4},{24,8},{28,12},{1,17},{... | collective-permute-start | bytes 393224 | tf_op jit(solution)/shard_map/ppermute | solution.py:588
  59.2 8.4 %shard_map.88 = (bf16[512,256]{1,0:T(8,128)(2,1)}, f32[32,256]{1,0:T(8,128)}) custom-call(s32[3]{0:T(128)} %pad_add_fusion.meta_ref, s32[1,8]{1,0:T(1,128)} %len_ref.5, f32[512,256]{1,0:T(8,128)} %get-tuple-element.49.own_ref, bf16[512,256]{1,0:T(8,128)(2,1)} %copy-done.3, f32[108,8,256]{2,1,0:T(8,128)} %get-tuple-element.51.xext_ref, ...), custom_call_target="tpu_custom_call" | custom-call | tf_op jit(solution)/shard_map/pallas_call | solution.py:509
  69.8 6.2 %all-to-all-start = ((f32[32,8,128]{2,1,0:T(8,128)}), f32[32,8,128]{2,1,0:T(8,128)S(1)}, u32[]{:S(2)}, u32[]{:S(2)}) async-start(f32[32,8,128]{2,1,0:T(8,128)} %constant_dynamic-update-slice_fusion.2), calls=%async_computation | async-start | bytes 262144 | tf_op jit(solution)/shard_map/all_to_all | solution.py:623
  77.0 1.3 %collective-permute-start.17 = (bf16[128,512]{1,0:T(8,128)(2,1)S(1)}, bf16[128,512]{1,0:T(8,128)(2,1)S(1)}, u32[]{:S(2)}, u32[]{:S(2)}) collective-permute-start(bf16[128,512]{1,0:T(8,128)(2,1)S(1)} %copy-done.24), channel_id=1, source_target_pairs={{0,24},{4,28},{8,16},{12,20},{16,8},{20,12},{24,0},{28,4},{1,25},{... | collective-permute-start | bytes 393224 | tf_op jit(solution)/shard_map/ppermute | solution.py:588
  79.6 1.2 %collective-permute-start.10 = (bf16[128,512]{1,0:T(8,128)(2,1)S(1)}, bf16[128,512]{1,0:T(8,128)(2,1)S(1)}, u32[]{:S(2)}, u32[]{:S(2)}) collective-permute-start(bf16[128,512]{1,0:T(8,128)(2,1)S(1)} %get-tuple-element.75), channel_id=1, source_target_pairs={{0,2},{1,3},{2,0},{3,1},{4,6},{5,7},{6,4},{7,5},{8,10},{9,11},{10,... | collective-permute-start | bytes 393224 | tf_op jit(solution)/shard_map/ppermute | solution.py:524
  80.8 1.4 %collective-permute-start.11 = (bf16[128,512]{1,0:T(8,128)(2,1)S(1)}, bf16[128,512]{1,0:T(8,128)(2,1)S(1)}, u32[]{:S(2)}, u32[]{:S(2)}) collective-permute-start(bf16[128,512]{1,0:T(8,128)(2,1)S(1)} %get-tuple-element.74), channel_id=1, source_target_pairs={{0,3},{1,2},{2,1},{3,0},{4,7},{5,6},{6,5},{7,4},{8,11},{9,10},{10,... | collective-permute-start | bytes 393224 | tf_op jit(solution)/shard_map/ppermute | solution.py:524
  82.2 7.2 %collective-permute-done.17.refs_6_ = bf16[128,512]{1,0:T(8,128)(2,1)S(1)} collective-permute-done((bf16[128,512]{1,0:T(8,128)(2,1)S(1)}, bf16[128,512]{1,0:T(8,128)(2,1)S(1)}, u32[]{:S(2)}, u32[]{:S(2)}) %collective-permute-start.17) | collective-permute-done | bytes 131104 | tf_op jit(solution)/shard_map/ppermute | solution.py:588
  89.4 3.7 %collective-permute-done.18.refs_7_ = bf16[128,512]{1,0:T(8,128)(2,1)S(1)} collective-permute-done((bf16[128,512]{1,0:T(8,128)(2,1)S(1)}, bf16[128,512]{1,0:T(8,128)(2,1)S(1)}, u32[]{:S(2)}, u32[]{:S(2)}) %collective-permute-start.18) | collective-permute-done | bytes 131104 | tf_op jit(solution)/shard_map/ppermute | solution.py:588
  93.8 2.8 %shard_map.91 = (f32[32,512]{1,0:T(8,128)}, bf16[32,512]{1,0:T(8,128)(2,1)}, bf16[32,512]{1,0:T(8,128)(2,1)}, bf16[32,512]{1,0:T(8,128)(2,1)}) custom-call(s32[3]{0:T(128)} %pad_add_fusion.meta_ref, bf16[128,512]{1,0:T(8,128)(2,1)} %get-tuple-element.57.refs_0_, bf16[128,512]{1,0:T(8,128)(2,1)} %copy-done.10, bf16[128,512]{1,0:T(8,128)(2,1)} %copy-done.11, ...), custom_call_target="tpu_custom_call" | custom-call | tf_op jit(solution)/shard_map/pallas_call | solution.py:509
  98.5 1.3 %collective-permute-start.21 = (bf16[32,512]{1,0:T(8,128)(2,1)}, bf16[32,512]{1,0:T(8,128)(2,1)S(1)}, u32[]{:S(2)}, u32[]{:S(2)}) collective-permute-start(bf16[32,512]{1,0:T(8,128)(2,1)} %get-tuple-element.68), channel_id=1, source_target_pairs={{0,3},{1,2},{2,1},{3,0},{4,7},{5,6},{6,5},{7,4},{8,11},{9,10},{10,... | collective-permute-start | bytes 98312 | tf_op jit(solution)/shard_map/ppermute | solution.py:524
  100.3 1.8 %collective-permute-done.21.r3 = bf16[32,512]{1,0:T(8,128)(2,1)S(1)} collective-permute-done((bf16[32,512]{1,0:T(8,128)(2,1)}, bf16[32,512]{1,0:T(8,128)(2,1)S(1)}, u32[]{:S(2)}, u32[]{:S(2)}) %collective-permute-start.21) | collective-permute-done | bytes 32800 | tf_op jit(solution)/shard_map/ppermute | solution.py:524
  102.7 2.2 %shard_map.92 = f32[32,2048]{1,0:T(8,128)} custom-call(s32[3]{0:T(128)} %pad_add_fusion.meta_ref, f32[32,512]{1,0:T(8,128)} %get-tuple-element.65.own_ref, bf16[32,512]{1,0:T(8,128)(2,1)} %copy-done.20, bf16[32,512]{1,0:T(8,128)(2,1)} %copy-done.21, bf16[32,512]{1,0:T(8,128)(2,1)} %copy-done.22), custom_call_target="tpu_custom_call" | custom-call | tf_op jit(solution)/shard_map/pallas_call | solution.py:509
  106.3 2.7 %shard_map.89 = (bf16[128,1024]{1,0:T(8,128)(2,1)}, bf16[128,1024]{1,0:T(8,128)(2,1)}) custom-call(s32[3]{0:T(128)} %pad_add_fusion.meta_ref, bf16[512,512]{1,0:T(8,128)(2,1)} %copy-done, bf16[128,512]{1,0:T(8,128)(2,1)} %copy-done.6, bf16[128,512]{1,0:T(8,128)(2,1)} %copy-done.4, bf16[128,512]{1,0:T(8,128)(2,1)} %copy-done.5), custom_call_target="tpu_custom_call" | custom-call | tf_op jit(solution)/shard_map/pallas_call | solution.py:509
  (93 shorter events, 22.7 us)
Async XLA Ops:
  3.9 2.4 %collective-permute-start = (bf16[128,512]{1,0:T(8,128)(2,1)}, bf16[128,512]{1,0:T(8,128)(2,1)S(1)}, u32[]{:S(2)}, u32[]{:S(2)}) collective-permute-start(bf16[128,512]{1,0:T(8,128)(2,1)} %get-tuple-element.38), channel_id=1, source_target_pairs={{0,1},{1,0},{2,3},{3,2},{4,5},{5,4},{6,7},{7,6},{8,9},{9,8},{10,11... | collective-permute-start | bytes 393224 | tf_op jit(solution)/shard_map/ppermute | solution.py:524
  4.5 5.3 %collective-permute-start.1 = (bf16[128,512]{1,0:T(8,128)(2,1)}, bf16[128,512]{1,0:T(8,128)(2,1)S(1)}, u32[]{:S(2)}, u32[]{:S(2)}) collective-permute-start(bf16[128,512]{1,0:T(8,128)(2,1)} %get-tuple-element.39), channel_id=1, source_target_pairs={{0,2},{1,3},{2,0},{3,1},{4,6},{5,7},{6,4},{7,5},{8,10},{9,11},{10,... | collective-permute-start | bytes 393224 | tf_op jit(solution)/shard_map/ppermute | solution.py:524
  5.8 7.0 %collective-permute-start.2 = (bf16[128,512]{1,0:T(8,128)(2,1)}, bf16[128,512]{1,0:T(8,128)(2,1)S(1)}, u32[]{:S(2)}, u32[]{:S(2)}) collective-permute-start(bf16[128,512]{1,0:T(8,128)(2,1)} %get-tuple-element.40), channel_id=1, source_target_pairs={{0,3},{1,2},{2,1},{3,0},{4,7},{5,6},{6,5},{7,4},{8,11},{9,10},{10,... | collective-permute-start | bytes 393224 | tf_op jit(solution)/shard_map/ppermute | solution.py:524
  21.8 6.3 %collective-permute-start.3 = (bf16[512,512]{1,0:T(8,128)(2,1)}, bf16[512,512]{1,0:T(8,128)(2,1)S(1)}, u32[]{:S(2)}, u32[]{:S(2)}) collective-permute-start(bf16[512,512]{1,0:T(8,128)(2,1)} %get-tuple-element.41.hid_ref), channel_id=1, source_target_pairs={{0,1},{1,0},{2,3},{3,2},{4,5},{5,4},{6,7},{7,6},{8,9},{9,8},{10,11... | collective-permute-start | bytes 1572872 | tf_op jit(solution)/shard_map/ppermute | solution.py:524
  22.1 2.1 %collective-permute-start.4 = (bf16[128,256]{1,0:T(8,128)(2,1)}, bf16[128,256]{1,0:T(8,128)(2,1)S(1)}, u32[]{:S(2)}, u32[]{:S(2)}) collective-permute-start(bf16[128,256]{1,0:T(8,128)(2,1)} %get-tuple-element.43), channel_id=1, source_target_pairs={{0,1},{1,0},{2,3},{3,2},{4,5},{5,4},{6,7},{7,6},{8,9},{9,8},{10,11... | collective-permute-start | bytes 196616 | tf_op jit(solution)/shard_map/ppermute | solution.py:524
  22.4 3.3 %collective-permute-start.5 = (bf16[128,256]{1,0:T(8,128)(2,1)}, bf16[128,256]{1,0:T(8,128)(2,1)S(1)}, u32[]{:S(2)}, u32[]{:S(2)}) collective-permute-start(bf16[128,256]{1,0:T(8,128)(2,1)} %get-tuple-element.44), channel_id=1, source_target_pairs={{0,2},{1,3},{2,0},{3,1},{4,6},{5,7},{6,4},{7,5},{8,10},{9,11},{10,... | collective-permute-start | bytes 196616 | tf_op jit(solution)/shard_map/ppermute | solution.py:524
  23.6 4.6 %collective-permute-start.6 = (bf16[128,256]{1,0:T(8,128)(2,1)}, bf16[128,256]{1,0:T(8,128)(2,1)S(1)}, u32[]{:S(2)}, u32[]{:S(2)}) collective-permute-start(bf16[128,256]{1,0:T(8,128)(2,1)} %get-tuple-element.45), channel_id=1, source_target_pairs={{0,3},{1,2},{2,1},{3,0},{4,7},{5,6},{6,5},{7,4},{8,11},{9,10},{10,... | collective-permute-start | bytes 196616 | tf_op jit(solution)/shard_map/ppermute | solution.py:524
  42.3 2.1 %collective-permute-start.7 = (bf16[512,512]{1,0:T(8,128)(2,1)}, bf16[512,512]{1,0:T(8,128)(2,1)S(1)}, u32[]{:S(2)}, u32[]{:S(2)}) collective-permute-start(bf16[512,512]{1,0:T(8,128)(2,1)} %get-tuple-element.48), channel_id=1, source_target_pairs={{0,1},{1,0},{2,3},{3,2},{4,5},{5,4},{6,7},{7,6},{8,9},{9,8},{10,11... | collective-permute-start | bytes 1572872 | tf_op jit(solution)/shard_map/ppermute | solution.py:524
  47.5 10.6 %collective-permute-start.8 = (bf16[512,256]{1,0:T(8,128)(2,1)}, bf16[512,256]{1,0:T(8,128)(2,1)S(1)}, u32[]{:S(2)}, u32[]{:S(2)}) collective-permute-start(bf16[512,256]{1,0:T(8,128)(2,1)} %get-tuple-element.50), channel_id=1, source_target_pairs={{0,2},{1,3},{2,0},{3,1},{4,6},{5,7},{6,4},{7,5},{8,10},{9,11},{10,... | collective-permute-start | bytes 786440 | tf_op jit(solution)/shard_map/ppermute | solution.py:524
  52.1 24.9 %collective-permute-start.12 = (bf16[128,512]{1,0:T(8,128)(2,1)}, bf16[128,512]{1,0:T(8,128)(2,1)S(1)}, u32[]{:S(2)}, u32[]{:S(2)}) collective-permute-start(bf16[128,512]{1,0:T(8,128)(2,1)} %get-tuple-element.58), channel_id=1, source_target_pairs={{0,4},{4,0},{8,12},{12,8},{16,20},{20,16},{24,28},{28,24},{1,5},{5... | collective-permute-start | bytes 393224 | tf_op jit(solution)/shard_map/ppermute | solution.py:588
  53.4 24.9 %collective-permute-start.13 = (bf16[128,512]{1,0:T(8,128)(2,1)}, bf16[128,512]{1,0:T(8,128)(2,1)S(1)}, u32[]{:S(2)}, u32[]{:S(2)}) collective-permute-start(bf16[128,512]{1,0:T(8,128)(2,1)} %get-tuple-element.59), channel_id=1, source_target_pairs={{0,8},{4,12},{8,0},{12,4},{16,24},{20,28},{24,16},{28,20},{1,9},{5... | collective-permute-start | bytes 393224 | tf_op jit(solution)/shard_map/ppermute | solution.py:588
  53.6 26.0 %collective-permute-start.14 = (bf16[128,512]{1,0:T(8,128)(2,1)}, bf16[128,512]{1,0:T(8,128)(2,1)S(1)}, u32[]{:S(2)}, u32[]{:S(2)}) collective-permute-start(bf16[128,512]{1,0:T(8,128)(2,1)} %get-tuple-element.60), channel_id=1, source_target_pairs={{0,12},{4,8},{8,4},{12,0},{16,28},{20,24},{24,20},{28,16},{1,13},{... | collective-permute-start | bytes 393224 | tf_op jit(solution)/shard_map/ppermute | solution.py:588
  54.8 26.0 %collective-permute-start.15 = (bf16[128,512]{1,0:T(8,128)(2,1)}, bf16[128,512]{1,0:T(8,128)(2,1)S(1)}, u32[]{:S(2)}, u32[]{:S(2)}) collective-permute-start(bf16[128,512]{1,0:T(8,128)(2,1)} %get-tuple-element.61), channel_id=1, source_target_pairs={{0,16},{4,20},{8,24},{12,28},{16,0},{20,4},{24,8},{28,12},{1,17},{... | collective-permute-start | bytes 393224 | tf_op jit(solution)/shard_map/ppermute | solution.py:588
  58.1 24.1 %collective-permute-start.16 = (bf16[128,512]{1,0:T(8,128)(2,1)}, bf16[128,512]{1,0:T(8,128)(2,1)S(1)}, u32[]{:S(2)}, u32[]{:S(2)}) collective-permute-start(bf16[128,512]{1,0:T(8,128)(2,1)} %get-tuple-element.62), channel_id=1, source_target_pairs={{0,20},{4,16},{8,28},{12,24},{16,4},{20,0},{24,12},{28,8},{1,21},{... | collective-permute-start | bytes 393224 | tf_op jit(solution)/shard_map/ppermute | solution.py:588
  69.8 39.2 %all-to-all-start = ((f32[32,8,128]{2,1,0:T(8,128)}), f32[32,8,128]{2,1,0:T(8,128)S(1)}, u32[]{:S(2)}, u32[]{:S(2)}) async-start(f32[32,8,128]{2,1,0:T(8,128)} %constant_dynamic-update-slice_fusion.2), calls=%async_computation | async-start | bytes 262144 | tf_op jit(solution)/shard_map/all_to_all | solution.py:623
  77.0 28.0 %copy-start = (bf16[512,512]{1,0:T(8,128)(2,1)}, bf16[512,512]{1,0:T(8,128)(2,1)S(1)}, u32[]{:S(2)}) copy-start(bf16[512,512]{1,0:T(8,128)(2,1)S(1)} %constant_dynamic-update-slice_fusion.own_ref) | copy-start | bytes 1572868
  77.0 12.4 %collective-permute-start.17 = (bf16[128,512]{1,0:T(8,128)(2,1)S(1)}, bf16[128,512]{1,0:T(8,128)(2,1)S(1)}, u32[]{:S(2)}, u32[]{:S(2)}) collective-permute-start(bf16[128,512]{1,0:T(8,128)(2,1)S(1)} %copy-done.24), channel_id=1, source_target_pairs={{0,24},{4,28},{8,16},{12,20},{16,8},{20,12},{24,0},{28,4},{1,25},{... | collective-permute-start | bytes 393224 | tf_op jit(solution)/shard_map/ppermute | solution.py:588
  78.3 14.8 %collective-permute-start.18 = (bf16[128,512]{1,0:T(8,128)(2,1)S(1)}, bf16[128,512]{1,0:T(8,128)(2,1)S(1)}, u32[]{:S(2)}, u32[]{:S(2)}) collective-permute-start(bf16[128,512]{1,0:T(8,128)(2,1)S(1)} %copy-done.23), channel_id=1, source_target_pairs={{0,28},{4,24},{8,20},{12,16},{16,12},{20,8},{24,4},{28,0},{1,29},{... | collective-permute-start | bytes 393224 | tf_op jit(solution)/shard_map/ppermute | solution.py:588
  79.6 25.4 %collective-permute-start.10 = (bf16[128,512]{1,0:T(8,128)(2,1)S(1)}, bf16[128,512]{1,0:T(8,128)(2,1)S(1)}, u32[]{:S(2)}, u32[]{:S(2)}) collective-permute-start(bf16[128,512]{1,0:T(8,128)(2,1)S(1)} %get-tuple-element.75), channel_id=1, source_target_pairs={{0,2},{1,3},{2,0},{3,1},{4,6},{5,7},{6,4},{7,5},{8,10},{9,11},{10,... | collective-permute-start | bytes 393224 | tf_op jit(solution)/shard_map/ppermute | solution.py:524
  80.8 24.1 %collective-permute-start.11 = (bf16[128,512]{1,0:T(8,128)(2,1)S(1)}, bf16[128,512]{1,0:T(8,128)(2,1)S(1)}, u32[]{:S(2)}, u32[]{:S(2)}) collective-permute-start(bf16[128,512]{1,0:T(8,128)(2,1)S(1)} %get-tuple-element.74), channel_id=1, source_target_pairs={{0,3},{1,2},{2,1},{3,0},{4,7},{5,6},{6,5},{7,4},{8,11},{9,10},{10,... | collective-permute-start | bytes 393224 | tf_op jit(solution)/shard_map/ppermute | solution.py:524
  82.2 22.8 %collective-permute-start.9 = (bf16[128,512]{1,0:T(8,128)(2,1)S(1)}, bf16[128,512]{1,0:T(8,128)(2,1)S(1)}, u32[]{:S(2)}, u32[]{:S(2)}) collective-permute-start(bf16[128,512]{1,0:T(8,128)(2,1)S(1)} %get-tuple-element.76), channel_id=1, source_target_pairs={{0,1},{1,0},{2,3},{3,2},{4,5},{5,4},{6,7},{7,6},{8,9},{9,8},{10,11... | collective-permute-start | bytes 393224 | tf_op jit(solution)/shard_map/ppermute | solution.py:524
  96.6 2.0 %collective-permute-start.19 = (bf16[32,512]{1,0:T(8,128)(2,1)}, bf16[32,512]{1,0:T(8,128)(2,1)S(1)}, u32[]{:S(2)}, u32[]{:S(2)}) collective-permute-start(bf16[32,512]{1,0:T(8,128)(2,1)} %get-tuple-element.66), channel_id=1, source_target_pairs={{0,1},{1,0},{2,3},{3,2},{4,5},{5,4},{6,7},{7,6},{8,9},{9,8},{10,11... | collective-permute-start | bytes 98312 | tf_op jit(solution)/shard_map/ppermute | solution.py:524
  97.3 3.0 %collective-permute-start.20 = (bf16[32,512]{1,0:T(8,128)(2,1)}, bf16[32,512]{1,0:T(8,128)(2,1)S(1)}, u32[]{:S(2)}, u32[]{:S(2)}) collective-permute-start(bf16[32,512]{1,0:T(8,128)(2,1)} %get-tuple-element.67), channel_id=1, source_target_pairs={{0,2},{1,3},{2,0},{3,1},{4,6},{5,7},{6,4},{7,5},{8,10},{9,11},{10,... | collective-permute-start | bytes 98312 | tf_op jit(solution)/shard_map/ppermute | solution.py:524
  98.5 3.6 %collective-permute-start.21 = (bf16[32,512]{1,0:T(8,128)(2,1)}, bf16[32,512]{1,0:T(8,128)(2,1)S(1)}, u32[]{:S(2)}, u32[]{:S(2)}) collective-permute-start(bf16[32,512]{1,0:T(8,128)(2,1)} %get-tuple-element.68), channel_id=1, source_target_pairs={{0,3},{1,2},{2,1},{3,0},{4,7},{5,6},{6,5},{7,4},{8,11},{9,10},{10,... | collective-permute-start | bytes 98312 | tf_op jit(solution)/shard_map/ppermute | solution.py:524
  (24 other events, 151.1 us)

commit v2 on v1

--- a/solution.py
+++ b/solution.py
@@ -13,8 +13,8 @@
 RIM = KERNEL // 2
 SUB = 8
 CHUNK = 6
+META_LENGTHS = 3
 SWAP = (0, 2, 1, 3)
-VMEM_LIMIT = 56 * 1024 * 1024
 
 
 def extended(block, sides, width):
@@ -182,11 +182,11 @@
     return lax.dot_general(left, right, (((0,), (0,)), ((), ())), preferred_element_type=jnp.float32)
 
 
-def utt_index(len_ref, frame_pos):
+def utt_index(meta_ref, frame_pos):
     end = jnp.int32(0)
     counted = jnp.zeros(frame_pos.shape, jnp.int32)
-    for utt in range(len_ref.shape[1]):
-        end = end + len_ref[0, utt]
+    for utt in range(META_LENGTHS, meta_ref.shape[0]):
+        end = end + meta_ref[utt]
         counted = counted + (frame_pos >= end).astype(jnp.int32)
     return counted
 
@@ -196,9 +196,9 @@
     return ((own_index ^ (row >> shift)) << shift) + (row & (row_count - 1))
 
 
-def spaced_pos(len_ref, row, own_index, row_count):
+def spaced_pos(meta_ref, row, own_index, row_count):
     frame_pos = frame_at(row, own_index, row_count)
-    return frame_pos + RIM * utt_index(len_ref, frame_pos)
+    return frame_pos + RIM * utt_index(meta_ref, frame_pos)
 
 
 def spaced_steps(seq_total, utt_count):
@@ -206,18 +206,18 @@
     return -(-rows // (SUB * CHUNK)) * CHUNK
 
 
-def spread_matrix(len_ref, own_index, row_count, seq_total, steps):
+def spread_matrix(meta_ref, own_index, row_count, seq_total, steps):
     slot = lax.broadcasted_iota(jnp.int32, (steps * SUB, seq_total), 0)
     slot_pos = (slot & (SUB - 1)) * steps + (slot >> 3)
     row = lax.broadcasted_iota(jnp.int32, (1, seq_total), 1)
-    return (slot_pos == spaced_pos(len_ref, row, own_index, row_count)).astype(jnp.float32).astype(jnp.bfloat16)
-
-
-def gather_matrix(len_ref, own_index, row_count, seq_total, steps):
+    return (slot_pos == spaced_pos(meta_ref, row, own_index, row_count)).astype(jnp.float32).astype(jnp.bfloat16)
+
+
+def gather_matrix(meta_ref, own_index, row_count, seq_total, steps):
     slot = lax.broadcasted_iota(jnp.int32, (1, steps * SUB), 1)
     slot_pos = (slot & (SUB - 1)) * steps + (slot >> 3)
     row = lax.broadcasted_iota(jnp.int32, (seq_total, 1), 0)
-    return (slot_pos == spaced_pos(len_ref, row, own_index, row_count)).astype(jnp.float32).astype(jnp.bfloat16)
+    return (slot_pos == spaced_pos(meta_ref, row, own_index, row_count)).astype(jnp.float32).astype(jnp.bfloat16)
 
 
 def write_extended(ext_ref, spaced, steps):
@@ -229,13 +229,13 @@
     ext_ref[RIM + steps :] = jnp.where(sub == SUB - 1, 0.0, pltpu.roll(blocks[:RIM], SUB - 1, 1))
 
 
-def conv_loop(ext_ref, taps_ref, lanes, steps, flipped, finish):
+def conv_loop(ext_ref, taps_ref, lanes, tap_lanes, steps, flipped, finish):
     def body(chunk, carry):
         start = chunk * CHUNK
         window = [ext_ref[start + m, :, lanes] for m in range(CHUNK + KERNEL - 1)]
         sums = [None] * CHUNK
         for tap in range(KERNEL):
-            weight = taps_ref[tap, :, lanes]
+            weight = taps_ref[tap, :, tap_lanes]
             shift = KERNEL - 1 - tap if flipped else tap
             for a in range(CHUNK):
                 term = window[a + shift] * weight
@@ -247,47 +247,53 @@
     lax.fori_loop(0, steps // CHUNK, body, 0)
 
 
-def pack_kernel(meta_ref, frames_ref, cot_ref, *outs):
-    group = meta_ref[1]
-    width = outs[4].shape[1]
-    for j in range(4):
-        target = group ^ SWAP[j]
-        for part in range(2):
-            start = pl.multiple_of((target ^ part) * width, width)
-            outs[j][:, part * width : (part + 1) * width] = frames_ref[:, pl.ds(start, width)]
-        start = pl.multiple_of(target * width, width)
-        outs[4 + j][...] = cot_ref[:, pl.ds(start, width)]
-
-
 def forward_conv_kernel(
-    meta_ref, len_ref, f0, f1, f2, f3, w_own_ref, w_oth_ref, hid_ref, xext_ref, conv_ref, ext_ref, taps_ref, hid_sp_ref
+    meta_ref, frames_hbm, f1, f2, f3, w_hbm, hid_ref, xext_hbm, conv_hbm,
+    f0_ref, w_ref, ext_ref, oth_ref, conv_ref, taps_ref, hid_sp_ref, sems,
 ):
-    own_index = meta_ref[0]
-    row_count = f0.shape[0]
+    own_index, group = meta_ref[0], meta_ref[1]
+    row_count = f1.shape[0]
+    width = ext_ref.shape[2]
     seq_total = 4 * row_count
-    width = f0.shape[1]
-    half = width // 2
     steps = conv_ref.shape[0]
-    rows = jnp.concatenate([f0[...], f1[...], f2[...], f3[...]], axis=0)
-    spread = spread_matrix(len_ref, own_index, row_count, seq_total, steps)
-    spaced = jnp.dot(spread, rows, preferred_element_type=jnp.float32)
-    write_extended(ext_ref, spaced, steps)
+    loads = []
+    for part in range(2):
+        start = pl.multiple_of((group ^ part) * width, width)
+        lanes = pl.ds(part * width, width)
+        loads.append(pltpu.make_async_copy(frames_hbm.at[:, pl.ds(start, width)], f0_ref.at[:, lanes], sems.at[part]))
+        loads.append(pltpu.make_async_copy(w_hbm.at[:, pl.ds(start, width)], w_ref.at[:, lanes], sems.at[2 + part]))
+    for load in loads:
+        load.start()
+    spread = spread_matrix(meta_ref, own_index, row_count, seq_total, steps)
+    for load in loads:
+        load.wait()
+    halves = (slice(0, width), slice(width, 2 * width))
+    for lanes, ref in zip(halves, (ext_ref, oth_ref), strict=True):
+        rows = jnp.concatenate([f0_ref[:, lanes], f1[:, lanes], f2[:, lanes], f3[:, lanes]], axis=0)
+        write_extended(ref, jnp.dot(spread, rows, preferred_element_type=jnp.float32), steps)
+    save_ext = pltpu.make_async_copy(ext_ref, xext_hbm, sems.at[0])
+    save_conv = pltpu.make_async_copy(conv_ref, conv_hbm, sems.at[1])
+    save_ext.start()
     for tap in range(KERNEL):
-        taps_ref[tap, :, :half] = jnp.broadcast_to(w_own_ref[tap : tap + 1, :], (SUB, half))
-        taps_ref[tap, :, half:] = jnp.broadcast_to(w_oth_ref[tap : tap + 1, :], (SUB, half))
-    for lane in range(0, width, 128):
-        lanes = slice(lane, lane + 128)
-
-        def finish(step, conv, center, lane=lane, lanes=lanes):
-            hid_sp_ref[step, :, lanes] = center + conv / (1.0 + jnp.exp(-conv))
-            if lane < half:
-                conv_ref[step, :, lanes] = conv
-
-        conv_loop(ext_ref, taps_ref, lanes, steps, False, finish)
-    xext_ref[...] = ext_ref[:, :, :half]
-    hid_low = hid_sp_ref[...].reshape(steps * SUB, width).astype(jnp.bfloat16)
-    gather = gather_matrix(len_ref, own_index, row_count, seq_total, steps)
+        taps_ref[tap] = jnp.broadcast_to(w_ref[tap : tap + 1, :], (SUB, 2 * width))
+    for part, ref in enumerate((ext_ref, oth_ref)):
+        for lane in range(0, width, 128):
+            lanes = slice(lane, lane + 128)
+            outer = slice(part * width + lane, part * width + lane + 128)
+
+            def finish(step, conv, center, part=part, lanes=lanes, outer=outer):
+                hid_sp_ref[step, :, outer] = center + conv / (1.0 + jnp.exp(-conv))
+                if part == 0:
+                    conv_ref[step, :, lanes] = conv
+
+            conv_loop(ref, taps_ref, lanes, outer, steps, False, finish)
+        if part == 0:
+            save_conv.start()
+    hid_low = hid_sp_ref[...].reshape(steps * SUB, 2 * width).astype(jnp.bfloat16)
+    gather = gather_matrix(meta_ref, own_index, row_count, seq_total, steps)
     hid_ref[...] = jnp.dot(gather, hid_low, preferred_element_type=jnp.float32).astype(jnp.bfloat16)
+    save_ext.wait()
+    save_conv.wait()
 
 
 def swapped(array, order, row_count):
@@ -295,17 +301,31 @@
 
 
 def attention_kernel(
-    meta_ref, len_ref, hid_ref, sib_ref, c0, c1, c2, c3, wk_ref, wv_ref,
+    meta_ref, hid_ref, sib_ref, cot_hbm, f1, f2, f3, w_hbm,
     out_ref, keep_ref, send_ref, kvg_ref,
-    k_ref, v_ref, kt_ref, vt_ref, cot_ref, cott_ref, attt_ref, dqt_ref, dk_ref, dv_ref, bias_ref,
+    c0, wk_ref, wv_ref, sems, k_ref, v_ref, kt_ref, vt_ref, cot_ref, cott_ref, attt_ref, dqt_ref, dk_ref, dv_ref, bias_ref,
 ):
     own_index, group = meta_ref[0], meta_ref[1]
-    row_count = c0.shape[0]
+    row_count, width = c0.shape
     seq_total = 4 * row_count
-    width = c0.shape[1]
+    own = pl.multiple_of(group * width, width)
+    loads = [
+        pltpu.make_async_copy(w_hbm.at[:, pl.ds(own, width)], wk_ref, sems.at[0]),
+        pltpu.make_async_copy(w_hbm.at[:, pl.ds(4 * width + own, width)], wv_ref, sems.at[1]),
+        pltpu.make_async_copy(cot_hbm.at[:, pl.ds(own, width)], c0, sems.at[2]),
+    ]
+    for load in loads:
+        load.start()
     head_width = 64
     scale = 1.0 / math.sqrt(head_width)
     bf16, f32 = jnp.bfloat16, jnp.float32
+    key_row = lax.broadcasted_iota(jnp.int32, (seq_total, 1), 0)
+    query_row = lax.broadcasted_iota(jnp.int32, (1, seq_total), 1)
+    key_utt = utt_index(meta_ref, frame_at(key_row, own_index, row_count))
+    query_utt = utt_index(meta_ref, frame_at(query_row, own_index, row_count))
+    bias_ref[...] = jnp.where(key_utt == query_utt, 0.0, -jnp.inf).astype(f32)
+    for load in loads:
+        load.wait()
     parts = [
         hid_ref[:, :width],
         hid_ref[:, width:],
@@ -322,14 +342,10 @@
     v_ref[...] = values
     kt_ref[...] = keys.T
     vt_ref[...] = values.T
-    cot = jnp.concatenate([c0[...], c1[...], c2[...], c3[...]], axis=0)
+    tail = slice(2 * width, 3 * width)
+    cot = jnp.concatenate([c0[...], f1[:, tail], f2[:, tail], f3[:, tail]], axis=0)
     cot_ref[...] = cot
     cott_ref[...] = cot.T.astype(f32)
-    key_row = lax.broadcasted_iota(jnp.int32, (seq_total, 1), 0)
-    query_row = lax.broadcasted_iota(jnp.int32, (1, seq_total), 1)
-    key_utt = utt_index(len_ref, frame_at(key_row, own_index, row_count))
-    query_utt = utt_index(len_ref, frame_at(query_row, own_index, row_count))
-    bias_ref[...] = jnp.where(key_utt == query_utt, 0.0, -jnp.inf).astype(f32)
     dk_ref[...] = jnp.zeros_like(dk_ref)
     dv_ref[...] = jnp.zeros_like(dv_ref)
     lane = lax.broadcasted_iota(jnp.int32, (1, 128), 1)
@@ -386,9 +402,8 @@
     keep_ref[:, width:] = partial(1)
 
 
-def weight_grad_kernel(meta_ref, hid_ref, sib_ref, kvg_ref, *refs):
-    outs, all_ref = refs[:-1], refs[-1]
-    group, dp_index = meta_ref[1], meta_ref[2]
+def weight_grad_kernel(meta_ref, hid_ref, sib_ref, kvg_ref, out_ref):
+    group = meta_ref[1]
     width = hid_ref.shape[1] // 2
     row_count = hid_ref.shape[0] // 4
     kvg = kvg_ref[...]
@@ -400,11 +415,7 @@
     ]
     for j in range(4):
         start = pl.multiple_of((group ^ j) * width, width)
-        all_ref[pl.ds(start, width), :] = tn_dot(parts[j], kvg).astype(jnp.bfloat16)
-    block = outs[0].shape[0]
-    for k in range(len(outs)):
-        start = pl.multiple_of((dp_index ^ k) * block, block)
-        outs[k][...] = all_ref[pl.ds(start, block), :]
+        out_ref[pl.ds(start, width), :] = tn_dot(parts[j], kvg).astype(jnp.bfloat16)
 
 
 def chip_sum_kernel(keep_ref, recv_ref, own_ref, send_ref):
@@ -416,21 +427,31 @@
 
 
 def backward_conv_kernel(
-    meta_ref, len_ref, own_ref, recv_ref, xext_ref, conv_ref, w_ref, dframes_ref, gdw_ref,
-    ext_ref, taps_ref, dh_ref, df_ref,
+    meta_ref, own_ref, recv_ref, xext_hbm, conv_hbm, w_hbm, dframes_ref, gdw_ref,
+    xext_ref, conv_ref, w_ref, ext_ref, taps_ref, dh_ref, df_ref, sems,
 ):
-    own_index = meta_ref[0]
+    own_index, group = meta_ref[0], meta_ref[1]
     seq_total, width = own_ref.shape
     row_count = seq_total // 4
     steps = conv_ref.shape[0]
     bf16, f32 = jnp.bfloat16, jnp.float32
+    start = pl.multiple_of(group * width, width)
+    loads = [
+        pltpu.make_async_copy(conv_hbm, conv_ref, sems.at[0]),
+        pltpu.make_async_copy(w_hbm.at[:, pl.ds(start, width)], w_ref, sems.at[1]),
+        pltpu.make_async_copy(xext_hbm, xext_ref, sems.at[2]),
+    ]
+    for load in loads:
+        load.start()
     dhidden = own_ref[...] + swapped(recv_ref[...], (2, 3, 0, 1), row_count).astype(f32)
     high = dhidden.astype(bf16)
     low = (dhidden - high.astype(f32)).astype(bf16)
-    spread = spread_matrix(len_ref, own_index, row_count, seq_total, steps)
+    spread = spread_matrix(meta_ref, own_index, row_count, seq_total, steps)
     both = jnp.dot(spread, jnp.concatenate([high, low], axis=1), preferred_element_type=f32)
     spaced = both[:, :width] + both[:, width:]
     dh_ref[...] = spaced.reshape(steps, SUB, width)
+    for load in loads:
+        load.wait()
     conv = conv_ref[...].reshape(steps * SUB, width)
     gate = 1.0 / (1.0 + jnp.exp(-conv))
     dconv = (spaced * (gate * (1.0 + conv * (1.0 - gate)))).astype(bf16).astype(f32)
@@ -444,7 +465,7 @@
         def finish(step, conv, center, lanes=lanes):
             df_ref[step, :, lanes] = dh_ref[step, :, lanes] + conv
 
-        conv_loop(ext_ref, taps_ref, lanes, steps, True, finish)
+        conv_loop(ext_ref, taps_ref, lanes, lanes, steps, True, finish)
         for first in range(0, KERNEL, half_taps):
             count = min(half_taps, KERNEL - first)
 
@@ -462,7 +483,7 @@
             for t in range(count):
                 gdw_ref[first + t : first + t + 1, lanes] = jnp.sum(sums[t], axis=0, keepdims=True)
     gdw_ref[KERNEL:, :] = jnp.zeros((gdw_ref.shape[0] - KERNEL, width), f32)
-    gather = gather_matrix(len_ref, own_index, row_count, seq_total, steps)
+    gather = gather_matrix(meta_ref, own_index, row_count, seq_total, steps)
     df_low = df_ref[...].reshape(steps * SUB, width).astype(bf16)
     dframes_ref[...] = jnp.dot(gather, df_low, preferred_element_type=f32).astype(bf16)
 
@@ -477,47 +498,40 @@
         dframes_ref[:, pl.ds(start, width)] = ref[:row_count, width:]
 
 
-def dp_sum_kernel(meta_ref, *refs):
-    ins, outs, total_ref = refs[:8], refs[8:12], refs[12]
-    own_index = meta_ref[0]
-    total = ins[0][...].astype(jnp.float32)
-    for ref in ins[1:]:
-        total = total + ref[...].astype(jnp.float32)
-    total_ref[...] = total
-    block = outs[0].shape[0]
+def place_grad_kernel(blocks_ref, out_ref):
+    piece, wide = blocks_ref.shape[1:]
+    width = wide // 2
+    full = out_ref.shape[1] // 2
     for j in range(4):
-        start = pl.multiple_of((own_index ^ j) * block, block)
-        outs[j][...] = total_ref[pl.ds(start, block), :].astype(outs[j].dtype)
-
-
-def place_grad_kernel(meta_ref, own_ref, r1, r2, r3, out_ref):
-    group = meta_ref[1]
-    width = own_ref.shape[1] // 2
-    full = out_ref.shape[1] // 2
-    for j, ref in enumerate((own_ref, r1, r2, r3)):
-        start = pl.multiple_of((group ^ SWAP[j]) * width, width)
-        out_ref[:, pl.ds(start, width)] = ref[:, :width].astype(jnp.float32)
-        out_ref[:, pl.ds(full + start, width)] = ref[:, width:].astype(jnp.float32)
-
-
-def call(kernel, scalars, args, in_specs, outs, scratch=()):
+        total = blocks_ref[j].astype(jnp.float32)
+        for d in range(1, blocks_ref.shape[0] // 4):
+            total = total + blocks_ref[4 * d + j].astype(jnp.float32)
+        start = SWAP[j] * width
+        out_ref[:, start : start + width] = total[:, :width]
+        out_ref[:, full + start : full + start + width] = total[:, width:]
+
+
+def call(kernel, scalars, args, outs, scratch=(), hbm_in=(), hbm_out=(), vmem_mib=16, cost_us=2):
     def whole(shape):
         zeros = (0,) * len(shape)
         return pl.BlockSpec(shape, lambda *_: zeros)
 
-    specs = [whole(arg.shape) if spec is None else spec for arg, spec in zip(args, in_specs, strict=True)]
+    def placed(shape, in_hbm):
+        return pl.BlockSpec(memory_space=pltpu.HBM) if in_hbm else whole(shape)
+
     return pl.pallas_call(
         kernel,
-        out_shape=[jax.ShapeDtypeStruct(shape, dtype) for shape, dtype in outs],
+        out_shape=[pltpu.HBM(s, t) if i in hbm_out else jax.ShapeDtypeStruct(s, t) for i, (s, t) in enumerate(outs)],
         grid_spec=pltpu.PrefetchScalarGridSpec(
             num_scalar_prefetch=len(scalars),
             grid=(1,),
-            in_specs=specs,
-            out_specs=[whole(shape) for shape, _ in outs],
+            in_specs=[placed(arg.shape, i in hbm_in) for i, arg in enumerate(args)],
+            out_specs=[placed(shape, i in hbm_out) for i, (shape, _) in enumerate(outs)],
             scratch_shapes=list(scratch),
         ),
-        compiler_params=pltpu.CompilerParams(vmem_limit_bytes=VMEM_LIMIT),
-    )(*scalars, *args)
+        compiler_params=pltpu.CompilerParams(vmem_limit_bytes=vmem_mib * 1024 * 1024),
+        cost_estimate=pl.CostEstimate(flops=cost_us * 10**9, bytes_accessed=cost_us * 3 * 10**6, transcendentals=0),
+    )(*scalars, *(pltpu.with_memory_space_constraint(a, pltpu.HBM) if i in hbm_in else a for i, a in enumerate(args)))
 
 
 def swap_ctx(array, j):
@@ -533,95 +547,79 @@
     ctx_index, dp_index = lax.axis_index("ctx"), lax.axis_index("dp")
     dp_size = lax.axis_size("dp")
     group = 2 * (ctx_index & 1) + (ctx_index >> 1)
-    meta = jnp.stack([ctx_index, group, dp_index]).astype(jnp.int32)
-    lengths = utt_lengths
-
-    packed = call(
-        pack_kernel, (meta,), (frames[0], cotangent[0]), (None, None),
-        [((row_count, 2 * width), bf16)] * 4 + [((row_count, width), bf16)] * 4,
-    )
-    frame_blocks = [packed[0]] + [swap_ctx(packed[j], j) for j in (1, 2, 3)]
-    cot_blocks = [packed[4]] + [swap_ctx(packed[4 + j], j) for j in (1, 2, 3)]
-
-    tap_specs = [
-        pl.BlockSpec((KERNEL, width), lambda i, meta, lens, part=part: (0, meta[1] ^ part)) for part in range(2)
-    ]
-    hidden, frames_ext, conv_own = call(
-        forward_conv_kernel, (meta, lengths), (*frame_blocks, w_dw, w_dw), (None,) * 4 + tuple(tap_specs),
-        [((seq_total, 2 * width), bf16), ((steps + 2 * RIM, SUB, width), f32), ((steps, SUB, width), f32)],
-        [
-            pltpu.VMEM((steps + 2 * RIM, SUB, 2 * width), f32),
-            pltpu.VMEM((KERNEL, SUB, 2 * width), f32),
-            pltpu.VMEM((steps, SUB, 2 * width), f32),
-        ],
-    )
-    hidden_sib = swap_ctx(hidden, 1)
-
+    meta = jnp.concatenate([jnp.stack([ctx_index, group, dp_index]).astype(jnp.int32), utt_lengths[0]])
+
+    rows, grads = frames[0], cotangent[0]
+
+    def columns(array, owner):
+        return lax.dynamic_slice_in_dim(array, owner * width, width, axis=1)
+
+    def parcel(owner):
+        return jnp.concatenate([columns(rows, owner), columns(rows, owner ^ 1), columns(grads, owner)], axis=1)
+
+    blocks = [swap_ctx(parcel(group ^ SWAP[j]), j) for j in (1, 2, 3)]
     wide = (seq_total, width)
     both = (seq_total, 2 * width)
-    kv_specs = [
-        pl.BlockSpec((feat_width, width), lambda i, meta, lens, part=part: (0, meta[1] + 4 * part))
-        for part in range(2)
-    ]
+    tall = wide[::-1]
+    long = (steps + 2 * RIM, SUB, width)
+    short = (steps, SUB, width)
+    taps = (KERNEL, SUB, width)
+    dma = pltpu.SemaphoreType.DMA
+    hidden, frames_ext, conv_own = call(
+        forward_conv_kernel, (meta,), (rows, *blocks, w_dw), [(both, bf16), (long, f32), (short, f32)],
+        [
+            pltpu.VMEM((row_count, 2 * width), bf16), pltpu.VMEM((KERNEL, 2 * width), f32),
+            pltpu.VMEM(long, f32), pltpu.VMEM(long, f32), pltpu.VMEM(short, f32),
+            pltpu.VMEM((KERNEL, SUB, 2 * width), f32), pltpu.VMEM((steps, SUB, 2 * width), f32), dma((4,)),
+        ],
+        hbm_in=(0, 4), hbm_out=(1, 2), cost_us=6,
+    )
+    hidden_sib = swap_ctx(hidden, 1)
     out_own, keep, send, kv_grad = call(
-        attention_kernel, (meta, lengths), (hidden, hidden_sib, *cot_blocks, w_kv, w_kv),
-        (None,) * 6 + tuple(kv_specs),
+        attention_kernel, (meta,), (hidden, hidden_sib, grads, *blocks, w_kv),
         [(wide, bf16), (both, f32), (both, bf16), (both, bf16)],
         [
-            pltpu.VMEM(wide, bf16), pltpu.VMEM(wide, bf16), pltpu.VMEM(wide[::-1], bf16), pltpu.VMEM(wide[::-1], bf16),
-            pltpu.VMEM(wide, bf16), pltpu.VMEM(wide[::-1], f32), pltpu.VMEM(wide[::-1], f32),
-            pltpu.VMEM(wide[::-1], f32), pltpu.VMEM(wide, f32), pltpu.VMEM(wide, f32),
+            pltpu.VMEM((row_count, width), bf16), pltpu.VMEM((feat_width, width), bf16),
+            pltpu.VMEM((feat_width, width), bf16), dma((3,)),
+            pltpu.VMEM(wide, bf16), pltpu.VMEM(wide, bf16), pltpu.VMEM(tall, bf16), pltpu.VMEM(tall, bf16),
+            pltpu.VMEM(wide, bf16), pltpu.VMEM(tall, f32), pltpu.VMEM(tall, f32),
+            pltpu.VMEM(tall, f32), pltpu.VMEM(wide, f32), pltpu.VMEM(wide, f32),
             pltpu.VMEM((seq_total, seq_total), f32),
         ],
-    )
+        hbm_in=(2, 6), vmem_mib=24, cost_us=11,
+    )
+    (part_kv,) = call(
+        weight_grad_kernel, (meta,), (hidden, hidden_sib, kv_grad), [((feat_width, 2 * width), bf16)], cost_us=2
+    )
+    piece = feat_width // (4 * dp_size)
     from_sib = swap_ctx(send, 1)
-    grad_blocks = call(
-        weight_grad_kernel, (meta,), (hidden, hidden_sib, kv_grad), (None,) * 3,
-        [((feat_width // dp_size, 2 * width), bf16)] * dp_size,
-        [pltpu.VMEM((feat_width, 2 * width), bf16)],
-    )
-    part_own, part_send = call(
-        chip_sum_kernel, (), (keep, from_sib), (None,) * 2, [(wide, f32), (wide, bf16)]
-    )
+    part_own, part_send = call(chip_sum_kernel, (), (keep, from_sib), [(wide, f32), (wide, bf16)], cost_us=1)
+    part_send, part_kv = lax.optimization_barrier((part_send, part_kv))
     from_chip = swap_ctx(part_send, 2)
-    grad_recv = [grad_blocks[0]] + [
-        lax.ppermute(grad_blocks[k], "dp", [(i, i ^ k) for i in range(dp_size)]) for k in range(1, dp_size)
-    ]
+    all_kv = lax.all_to_all(part_kv.reshape(4 * dp_size, piece, 2 * width), ("dp", "ctx"), 0, 0)
     dframes, part_dw = call(
-        backward_conv_kernel, (meta, lengths), (part_own, from_chip, frames_ext, conv_own, w_dw),
-        (None,) * 4 + (tap_specs[0],),
+        backward_conv_kernel, (meta,), (part_own, from_chip, frames_ext, conv_own, w_dw),
         [(wide, bf16), ((KERNEL + 1, width), f32)],
         [
-            pltpu.VMEM((steps + 2 * RIM, SUB, width), f32),
-            pltpu.VMEM((KERNEL, SUB, width), f32),
-            pltpu.VMEM((steps, SUB, width), f32),
-            pltpu.VMEM((steps, SUB, width), f32),
+            pltpu.VMEM(long, f32), pltpu.VMEM(short, f32), pltpu.VMEM((KERNEL, width), f32),
+            pltpu.VMEM(long, f32), pltpu.VMEM(taps, f32), pltpu.VMEM(short, f32), pltpu.VMEM(short, f32), dma((3,)),
         ],
+        hbm_in=(2, 3, 4), cost_us=100,
     )
     results = jnp.concatenate([out_own, dframes], axis=1)
-    result_blocks = [results] + [
-        swap_ctx(results[j * row_count : (j + 1) * row_count], j) for j in (1, 2, 3)
-    ]
+    result_blocks = [results] + [swap_ctx(results[j * row_count : (j + 1) * row_count], j) for j in (1, 2, 3)]
     output, dframes_rows = call(
-        place_kernel, (meta,), tuple(result_blocks), (None,) * 4, [((row_count, feat_width), bf16)] * 2
-    )
-    piece = feat_width // dp_size // 4
-    sums = call(
-        dp_sum_kernel, (meta,), tuple(grad_recv), (None,) * 8,
-        [((piece, 2 * width), f32)] + [((piece, 2 * width), bf16)] * 3,
-        [pltpu.VMEM((4 * piece, 2 * width), f32)],
-    )
-    sum_blocks = [sums[0]] + [swap_ctx(sums[j], j) for j in (1, 2, 3)]
-    (grad_kv,) = call(
-        place_grad_kernel, (meta,), tuple(sum_blocks), (None,) * 4, [((piece, 2 * feat_width), f32)]
-    )
-    owners = width // piece
-    by_owner = jnp.moveaxis(part_dw.reshape(KERNEL + 1, owners, piece), 1, 0).reshape(owners, -1, 128)
-    spread_dw = lax.dynamic_update_slice_in_dim(
-        jnp.zeros((4 * owners,) + by_owner.shape[1:], f32), by_owner, group * owners, axis=0
-    )
-    all_dw = lax.all_to_all(spread_dw, ("dp", "ctx"), 0, 0)
-    grad_dw = jnp.sum(all_dw, axis=0).reshape(KERNEL + 1, piece).T[:, :KERNEL]
+        place_kernel, (meta,), tuple(result_blocks), [((row_count, feat_width), bf16)] * 2, cost_us=1
+    )
+    by_owner = jnp.moveaxis(part_dw.reshape(KERNEL + 1, dp_size, piece), 1, 0).reshape(dp_size, -1, 128)
+    dw_sends = [lax.dynamic_index_in_dim(by_owner, dp_index ^ k, 0, keepdims=False) for k in range(dp_size)]
+    sum_dw = dw_sends[0]
+    for k in range(1, dp_size):
+        sum_dw = sum_dw + lax.ppermute(dw_sends[k], "dp", [(i, i ^ k) for i in range(dp_size)])
+    sources = [(4 * d + 2 * (g & 1) + (g >> 1), dp_size * g + d) for d in range(dp_size) for g in range(4)]
+    all_dw = lax.ppermute(sum_dw, ("dp", "ctx"), sources)
+    (grad_kv,) = call(place_grad_kernel, (), (all_kv,), [((piece, 2 * feat_width), f32)], cost_us=1)
+    grad_dw = all_dw.reshape(KERNEL + 1, piece).T[:, :KERNEL]
     return (output[None], dframes_rows[None], grad_kv, grad_dw)
 
 

time: 110 us -> 83.8 us (0.76)
  the two profiles are of different devices: /device:TPU:9 before, /device:TPU:6 now
where the time goes in v2:
time: 83.8 us; the launch traced here: 83.4 us
  Pallas kernels  29.7 us (35%)
  starting transfers between devices  26.3 us (31%)
  waiting for transfers between devices  23.6 us (28%)
  local copies, waits for them, and re-layouts  2.2 us (3%)
    pallas_call x7, Pallas kernels, call(): pl.pallas_call(kernel, out_shape=[pltpu.HBM(s, t) if i in hbm_out else ja...  29.7 us
    ppermute x7, starting transfers between devices, on_device_pairs(): lax.ppermute(dw_sends[k], 'dp', [(i, i ^ k) for i in range(dp_size)])  13.4 us
    ppermute x9, waiting for transfers between devices, swap_ctx(): return lax.ppermute(array, 'ctx', [(i, i ^ j) for i in range(4)])  12.6 us
    ppermute x1, waiting for transfers between devices, on_device_pairs(): all_dw = lax.ppermute(sum_dw, ('dp', 'ctx'), sources)  7.17 us
    all_to_all x1, starting transfers between devices, on_device_pairs(): lax.all_to_all(part_kv.reshape(4 * dp_size, piece, 2 * width), ('dp', 'ct...  6.11 us
    ppermute x9, starting transfers between devices, swap_ctx(): return lax.ppermute(array, 'ctx', [(i, i ^ j) for i in range(4)])  4.88 us
    ppermute x7, waiting for transfers between devices, on_device_pairs(): lax.ppermute(dw_sends[k], 'dp', [(i, i ^ k) for i in range(dp_size)])  3.88 us
    ppermute x1, starting transfers between devices, on_device_pairs(): all_dw = lax.ppermute(sum_dw, ('dp', 'ctx'), sources)  1.92 us
  transfers between devices with their start and end apart: 18, of which 6 were waited for; matrix products, arithmetic and copies ran while one was open for 2% of the time, Pallas kernels for 13%

profile of v2, /device:TPU:6, one launch (start us, length us, event | category | flops | bytes accessed | tf_op | source)
XLA Modules:
  0.0 83.4 jit_solution(17018438032167472370)
XLA Ops:
  0.7 1.2 %dynamic-slice_bitcast_fusion = (bf16[128,256]{1,0:T(8,128)(2,1)S(1)}, bf16[128,256]{1,0:T(8,128)(2,1)S(1)}, bf16[128,256]{1,0:T(8,128)(2,1)S(1)}, bf16[128,256]...) fusion(bf16[1,128,1024]{2,1,0:T(8,128)(2,1)} %param.7, ...), kind=kLoop, calls=%fused_computation.4 | loop fusion | bytes 1179672 | tf_op jit(solution)/shard_map/dynamic_slice | solution.py:555
  2.0 1.5 %collective-permute-start.1 = (bf16[128,768]{1,0:T(8,128)(2,1)S(1)}, bf16[128,768]{1,0:T(8,128)(2,1)S(1)}, u32[]{:S(2)}, u32[]{:S(2)}) collective-permute-start(bf16[128,768]{1,0:T(8,128)(2,1)S(1)} %pad_maximum_fusion.1), channel_id=1, source_target_pairs={{0,2},{1,3},{2,0},{3,1},{4,6},{5,7},{6,4},{7,5},{8,10},{9,11},{10,... | collective-permute-start | bytes 589832 | tf_op jit(solution)/shard_map/ppermute | solution.py:538
  3.9 0.7 pad_add_fusion.meta_ref
  4.7 4.4 %collective-permute-done.2.f3 = bf16[128,768]{1,0:T(8,128)(2,1)S(1)} collective-permute-done((bf16[128,768]{1,0:T(8,128)(2,1)S(1)}, bf16[128,768]{1,0:T(8,128)(2,1)S(1)}, u32[]{:S(2)}, u32[]{:S(2)}) %collective-permute-start.2) | collective-permute-done | bytes 196640 | tf_op jit(solution)/shard_map/ppermute | solution.py:538
  9.1 4.2 %collective-permute-done.1.f2 = bf16[128,768]{1,0:T(8,128)(2,1)S(1)} collective-permute-done((bf16[128,768]{1,0:T(8,128)(2,1)S(1)}, bf16[128,768]{1,0:T(8,128)(2,1)S(1)}, u32[]{:S(2)}, u32[]{:S(2)}) %collective-permute-start.1) | collective-permute-done | bytes 196640 | tf_op jit(solution)/shard_map/ppermute | solution.py:538
  13.3 6.8 %shard_map.84 = (bf16[512,512]{1,0:T(8,128)(2,1)S(1)}, f32[108,8,256]{2,1,0:T(8,128)}, f32[78,8,256]{2,1,0:T(8,128)}) custom-call(s32[11]{0:T(128)S(1)} %pad_add_fusion.meta_ref, bf16[128,1024]{1,0:T(8,128)(2,1)} %bitcast.62, bf16[128,768]{1,0:T(8,128)(2,1)S(1)} %collective-permute-done.f1, bf16[128,768]{1,0:T(8,128)(2,1)S(1)} %collective-permute-done.1.f2, ...), custom_call_target="tpu_custom_call" | custom-call | flops 6000000000 | bytes 18000000 | tf_op jit(solution)/shard_map/pallas_call | solution.py:522
  20.3 1.8 %collective-permute-done.3.sib_ref = bf16[512,512]{1,0:T(8,128)(2,1)S(1)} collective-permute-done((bf16[512,512]{1,0:T(8,128)(2,1)S(1)}, bf16[512,512]{1,0:T(8,128)(2,1)S(1)}, u32[]{:S(2)}, u32[]{:S(2)}) %collective-permute-start.3) | collective-permute-done | bytes 524320 | tf_op jit(solution)/shard_map/ppermute | solution.py:538
  22.1 11.4 %shard_map.85 = (bf16[512,256]{1,0:T(8,128)(2,1)S(1)}, f32[512,512]{1,0:T(8,128)S(1)}, bf16[512,512]{1,0:T(8,128)(2,1)S(1)}, bf16[512,512]{1,0:T(8,128)(2,1)S(1)}) custom-call(s32[11]{0:T(128)S(1)} %pad_add_fusion.meta_ref, bf16[512,512]{1,0:T(8,128)(2,1)S(1)} %get-tuple-element.19.hid_ref, bf16[512,512]{1,0:T(8,128)(2,1)S(1)} %collective-permute-done.3.sib_ref, ...), custom_call_target="tpu_custom_call" | custom-call | flops 11000000512 | bytes 33000000 | tf_op jit(solution)/shard_map/pallas_call | solution.py:522
  33.7 2.3 %shard_map.87 = bf16[1024,512]{1,0:T(8,128)(2,1)} custom-call(s32[11]{0:T(128)S(1)} %pad_add_fusion.meta_ref, bf16[512,512]{1,0:T(8,128)(2,1)S(1)} %get-tuple-element.19.hid_ref, bf16[512,512]{1,0:T(8,128)(2,1)S(1)} %collective-permute-done.3.sib_ref, bf16[512,512]{1,0:T(8,128)(2,1)S(1)} %get-tuple-element.25.kvg_ref), custom_call_target="tpu_custom_call" | custom-call | flops 2000000000 | bytes 6000000 | tf_op jit(solution)/shard_map/pallas_call | solution.py:522
  36.7 6.1 %all-to-all-start = ((bf16[32,32,512]{2,1,0:T(8,128)(2,1)}), bf16[32,32,512]{2,1,0:T(8,128)(2,1)S(1)}, u32[]{:S(2)}, u32[]{:S(2)}) async-start(bf16[32,32,512]{2,1,0:T(8,128)(2,1)} %bitcast.17), calls=%async_computation | async-start | bytes 2097152 | tf_op jit(solution)/shard_map/all_to_all | solution.py:599
  42.8 2.1 %collective-permute-done.5.recv_ref = bf16[512,256]{1,0:T(8,128)(2,1)S(1)} collective-permute-done((bf16[512,256]{1,0:T(8,128)(2,1)S(1)}, bf16[512,256]{1,0:T(8,128)(2,1)S(1)}, u32[]{:S(2)}, u32[]{:S(2)}) %collective-permute-start.5) | collective-permute-done | bytes 262176 | tf_op jit(solution)/shard_map/ppermute | solution.py:538
  44.9 6.9 %shard_map.88 = (bf16[512,256]{1,0:T(8,128)(2,1)S(1)}, f32[32,256]{1,0:T(8,128)S(1)}) custom-call(s32[11]{0:T(128)S(1)} %pad_add_fusion.meta_ref, f32[512,256]{1,0:T(8,128)S(1)} %get-tuple-element.23.own_ref, bf16[512,256]{1,0:T(8,128)(2,1)S(1)} %collective-permute-done.5.recv_ref, f32[108,8,256]{2,1,0:T(8,128)} %get-tuple-element.27.xext_hbm, ...), custom_call_target="tpu_custom_call" | custom-call | flops 99999997952 | bytes 300000000 | tf_op jit(solution)/shard_map/pallas_call | solution.py:522
  52.1 1.8 %collective-permute-start.10 = (f32[8,128]{1,0:T(8,128)S(1)}, f32[8,128]{1,0:T(8,128)S(1)}, u32[]{:S(2)}, u32[]{:S(2)}) collective-permute-start(f32[8,128]{1,0:T(8,128)S(1)} %get-tuple-element.56), channel_id=1, source_target_pairs={{0,8},{4,12},{8,0},{12,4},{16,24},{20,28},{24,16},{28,20},{1,9},{5... | collective-permute-start | bytes 12296 | tf_op jit(solution)/shard_map/ppermute | solution.py:618
  54.3 3.2 %collective-permute-start.12 = (f32[8,128]{1,0:T(8,128)S(1)}, f32[8,128]{1,0:T(8,128)S(1)}, u32[]{:S(2)}, u32[]{:S(2)}) collective-permute-start(f32[8,128]{1,0:T(8,128)S(1)} %get-tuple-element.54), channel_id=1, source_target_pairs={{0,16},{4,20},{8,24},{12,28},{16,0},{20,4},{24,8},{28,12},{1,17},{... | collective-permute-start | bytes 12296 | tf_op jit(solution)/shard_map/ppermute | solution.py:618
  57.4 0.8 collective-permute-start.13
  58.3 4.3 %collective-permute-start.14 = (f32[8,128]{1,0:T(8,128)S(1)}, f32[8,128]{1,0:T(8,128)S(1)}, u32[]{:S(2)}, u32[]{:S(2)}) collective-permute-start(f32[8,128]{1,0:T(8,128)S(1)} %get-tuple-element.52), channel_id=1, source_target_pairs={{0,24},{4,28},{8,16},{12,20},{16,8},{20,12},{24,0},{28,4},{1,25},{... | collective-permute-start | bytes 12296 | tf_op jit(solution)/shard_map/ppermute | solution.py:618
  62.6 1.4 %collective-permute-start.15 = (f32[8,128]{1,0:T(8,128)S(1)}, f32[8,128]{1,0:T(8,128)S(1)}, u32[]{:S(2)}, u32[]{:S(2)}) collective-permute-start(f32[8,128]{1,0:T(8,128)S(1)} %get-tuple-element.51), channel_id=1, source_target_pairs={{0,28},{4,24},{8,20},{12,16},{16,12},{20,8},{24,4},{28,0},{1,29},{... | collective-permute-start | bytes 12296 | tf_op jit(solution)/shard_map/ppermute | solution.py:618
  64.0 1.5 %collective-permute-start.9 = (f32[8,128]{1,0:T(8,128)S(1)}, f32[8,128]{1,0:T(8,128)S(1)}, u32[]{:S(2)}, u32[]{:S(2)}) collective-permute-start(f32[8,128]{1,0:T(8,128)S(1)} %get-tuple-element.50), channel_id=1, source_target_pairs={{0,4},{4,0},{8,12},{12,8},{16,20},{20,16},{24,28},{28,24},{1,5},{5... | collective-permute-start | bytes 12296 | tf_op jit(solution)/shard_map/ppermute | solution.py:618
  65.5 3.9 %collective-permute-done.12 = f32[8,128]{1,0:T(8,128)S(1)} collective-permute-done((f32[8,128]{1,0:T(8,128)S(1)}, f32[8,128]{1,0:T(8,128)S(1)}, u32[]{:S(2)}, u32[]{:S(2)}) %collective-permute-start.12) | collective-permute-done | bytes 4128 | tf_op jit(solution)/shard_map/ppermute | solution.py:618
  70.0 1.3 %collective-permute-start.8 = (bf16[128,512]{1,0:T(8,128)(2,1)S(1)}, bf16[128,512]{1,0:T(8,128)(2,1)S(1)}, u32[]{:S(2)}, u32[]{:S(2)}) collective-permute-start(bf16[128,512]{1,0:T(8,128)(2,1)S(1)} %get-tuple-element.38), channel_id=1, source_target_pairs={{0,3},{1,2},{2,1},{3,0},{4,7},{5,6},{6,5},{7,4},{8,11},{9,10},{10,... | collective-permute-start | bytes 393224 | tf_op jit(solution)/shard_map/ppermute | solution.py:538
  71.3 1.9 %collective-permute-start.16 = (f32[8,128]{1,0:T(8,128)S(1)}, f32[8,128]{1,0:T(8,128)S(1)}, u32[]{:S(2)}, u32[]{:S(2)}) collective-permute-start(f32[8,128]{1,0:T(8,128)S(1)} %fusion.7), channel_id=1, source_target_pairs={{0,0},{2,8},{1,16},{3,24},{4,1},{6,9},{5,17},{7,25},{8,2},{10,10},... | collective-permute-start | bytes 12296 | tf_op jit(solution)/shard_map/ppermute | solution.py:620
  73.2 7.2 %collective-permute-done.16 = f32[8,128]{1,0:T(8,128)S(1)} collective-permute-done((f32[8,128]{1,0:T(8,128)S(1)}, f32[8,128]{1,0:T(8,128)S(1)}, u32[]{:S(2)}, u32[]{:S(2)}) %collective-permute-start.16) | collective-permute-done | bytes 4128 | tf_op jit(solution)/shard_map/ppermute | solution.py:620
  81.1 1.4 %shard_map.89 = (bf16[128,1024]{1,0:T(8,128)(2,1)}, bf16[128,1024]{1,0:T(8,128)(2,1)}) custom-call(s32[11]{0:T(128)S(1)} %pad_add_fusion.meta_ref, bf16[512,512]{1,0:T(8,128)(2,1)S(1)} %constant_dynamic-update-slice_fusion.own_ref, bf16[128,512]{1,0:T(8,128)(2,1)S(1)} %collective-permute-done.6.r1, bf16[128,512]{1,0:T(8,128)(2,1)S(1)} %collective-permute-done.7.r2, ...), custom_call_target="tpu_custom_call" | custom-call | flops 1000000000 | bytes 3000000 | tf_op jit(solution)/shard_map/pallas_call | solution.py:522
  82.5 0.8 %shard_map.90 = f32[32,2048]{1,0:T(8,128)} custom-call(bf16[32,32,512]{2,1,0:T(8,128)(2,1)S(1)} %all-to-all-done.blocks_ref), custom_call_target="tpu_custom_call" | custom-call | flops 1000000000 | bytes 3000000 | tf_op jit(solution)/shard_map/pallas_call | solution.py:522
  (34 shorter events, 3.8 us)
Async XLA Ops:
  1.9 7.3 %collective-permute-start.2 = (bf16[128,768]{1,0:T(8,128)(2,1)S(1)}, bf16[128,768]{1,0:T(8,128)(2,1)S(1)}, u32[]{:S(2)}, u32[]{:S(2)}) collective-permute-start(bf16[128,768]{1,0:T(8,128)(2,1)S(1)} %pad_maximum_fusion.2), channel_id=1, source_target_pairs={{0,3},{1,2},{2,1},{3,0},{4,7},{5,6},{6,5},{7,4},{8,11},{9,10},{10,... | collective-permute-start | bytes 589832 | tf_op jit(solution)/shard_map/ppermute | solution.py:538
  2.0 11.4 %collective-permute-start.1 = (bf16[128,768]{1,0:T(8,128)(2,1)S(1)}, bf16[128,768]{1,0:T(8,128)(2,1)S(1)}, u32[]{:S(2)}, u32[]{:S(2)}) collective-permute-start(bf16[128,768]{1,0:T(8,128)(2,1)S(1)} %pad_maximum_fusion.1), channel_id=1, source_target_pairs={{0,2},{1,3},{2,0},{3,1},{4,6},{5,7},{6,4},{7,5},{8,10},{9,11},{10,... | collective-permute-start | bytes 589832 | tf_op jit(solution)/shard_map/ppermute | solution.py:538
  3.5 9.9 %collective-permute-start = (bf16[128,768]{1,0:T(8,128)(2,1)S(1)}, bf16[128,768]{1,0:T(8,128)(2,1)S(1)}, u32[]{:S(2)}, u32[]{:S(2)}) collective-permute-start(bf16[128,768]{1,0:T(8,128)(2,1)S(1)} %pad_maximum_fusion), channel_id=1, source_target_pairs={{0,1},{1,0},{2,3},{3,2},{4,5},{5,4},{6,7},{7,6},{8,9},{9,8},{10,11... | collective-permute-start | bytes 589832 | tf_op jit(solution)/shard_map/ppermute | solution.py:538
  20.1 2.0 %collective-permute-start.3 = (bf16[512,512]{1,0:T(8,128)(2,1)S(1)}, bf16[512,512]{1,0:T(8,128)(2,1)S(1)}, u32[]{:S(2)}, u32[]{:S(2)}) collective-permute-start(bf16[512,512]{1,0:T(8,128)(2,1)S(1)} %get-tuple-element.19.hid_ref), channel_id=1, source_target_pairs={{0,1},{1,0},{2,3},{3,2},{4,5},{5,4},{6,7},{7,6},{8,9},{9,8},{10,11... | collective-permute-start | bytes 1572872 | tf_op jit(solution)/shard_map/ppermute | solution.py:538
  33.5 2.5 %collective-permute-start.4 = (bf16[512,512]{1,0:T(8,128)(2,1)S(1)}, bf16[512,512]{1,0:T(8,128)(2,1)S(1)}, u32[]{:S(2)}, u32[]{:S(2)}) collective-permute-start(bf16[512,512]{1,0:T(8,128)(2,1)S(1)} %get-tuple-element.22), channel_id=1, source_target_pairs={{0,1},{1,0},{2,3},{3,2},{4,5},{5,4},{6,7},{7,6},{8,9},{9,8},{10,11... | collective-permute-start | bytes 1572872 | tf_op jit(solution)/shard_map/ppermute | solution.py:538
  36.1 8.8 %collective-permute-start.5 = (bf16[512,256]{1,0:T(8,128)(2,1)S(1)}, bf16[512,256]{1,0:T(8,128)(2,1)S(1)}, u32[]{:S(2)}, u32[]{:S(2)}) collective-permute-start(bf16[512,256]{1,0:T(8,128)(2,1)S(1)} %get-tuple-element.26), channel_id=1, source_target_pairs={{0,2},{1,3},{2,0},{3,1},{4,6},{5,7},{6,4},{7,5},{8,10},{9,11},{10,... | collective-permute-start | bytes 786440 | tf_op jit(solution)/shard_map/ppermute | solution.py:538
  36.7 45.8 %all-to-all-start = ((bf16[32,32,512]{2,1,0:T(8,128)(2,1)}), bf16[32,32,512]{2,1,0:T(8,128)(2,1)S(1)}, u32[]{:S(2)}, u32[]{:S(2)}) async-start(bf16[32,32,512]{2,1,0:T(8,128)(2,1)} %bitcast.17), calls=%async_computation | async-start | bytes 2097152 | tf_op jit(solution)/shard_map/all_to_all | solution.py:599
  52.1 10.5 %collective-permute-start.10 = (f32[8,128]{1,0:T(8,128)S(1)}, f32[8,128]{1,0:T(8,128)S(1)}, u32[]{:S(2)}, u32[]{:S(2)}) collective-permute-start(f32[8,128]{1,0:T(8,128)S(1)} %get-tuple-element.56), channel_id=1, source_target_pairs={{0,8},{4,12},{8,0},{12,4},{16,24},{20,28},{24,16},{28,20},{1,9},{5... | collective-permute-start | bytes 12296 | tf_op jit(solution)/shard_map/ppermute | solution.py:618
  53.9 10.1 %collective-permute-start.11 = (f32[8,128]{1,0:T(8,128)S(1)}, f32[8,128]{1,0:T(8,128)S(1)}, u32[]{:S(2)}, u32[]{:S(2)}) collective-permute-start(f32[8,128]{1,0:T(8,128)S(1)} %get-tuple-element.55), channel_id=1, source_target_pairs={{0,12},{4,8},{8,4},{12,0},{16,28},{20,24},{24,20},{28,16},{1,13},{... | collective-permute-start | bytes 12296 | tf_op jit(solution)/shard_map/ppermute | solution.py:618
  54.3 15.1 %collective-permute-start.12 = (f32[8,128]{1,0:T(8,128)S(1)}, f32[8,128]{1,0:T(8,128)S(1)}, u32[]{:S(2)}, u32[]{:S(2)}) collective-permute-start(f32[8,128]{1,0:T(8,128)S(1)} %get-tuple-element.54), channel_id=1, source_target_pairs={{0,16},{4,20},{8,24},{12,28},{16,0},{20,4},{24,8},{28,12},{1,17},{... | collective-permute-start | bytes 12296 | tf_op jit(solution)/shard_map/ppermute | solution.py:618
  57.4 12.0 %collective-permute-start.13 = (f32[8,128]{1,0:T(8,128)S(1)}, f32[8,128]{1,0:T(8,128)S(1)}, u32[]{:S(2)}, u32[]{:S(2)}) collective-permute-start(f32[8,128]{1,0:T(8,128)S(1)} %get-tuple-element.53), channel_id=1, source_target_pairs={{0,20},{4,16},{8,28},{12,24},{16,4},{20,0},{24,12},{28,8},{1,21},{... | collective-permute-start | bytes 12296 | tf_op jit(solution)/shard_map/ppermute | solution.py:618
  58.3 11.7 %collective-permute-start.14 = (f32[8,128]{1,0:T(8,128)S(1)}, f32[8,128]{1,0:T(8,128)S(1)}, u32[]{:S(2)}, u32[]{:S(2)}) collective-permute-start(f32[8,128]{1,0:T(8,128)S(1)} %get-tuple-element.52), channel_id=1, source_target_pairs={{0,24},{4,28},{8,16},{12,20},{16,8},{20,12},{24,0},{28,4},{1,25},{... | collective-permute-start | bytes 12296 | tf_op jit(solution)/shard_map/ppermute | solution.py:618
  62.6 8.7 %collective-permute-start.15 = (f32[8,128]{1,0:T(8,128)S(1)}, f32[8,128]{1,0:T(8,128)S(1)}, u32[]{:S(2)}, u32[]{:S(2)}) collective-permute-start(f32[8,128]{1,0:T(8,128)S(1)} %get-tuple-element.51), channel_id=1, source_target_pairs={{0,28},{4,24},{8,20},{12,16},{16,12},{20,8},{24,4},{28,0},{1,29},{... | collective-permute-start | bytes 12296 | tf_op jit(solution)/shard_map/ppermute | solution.py:618
  64.0 7.3 %collective-permute-start.9 = (f32[8,128]{1,0:T(8,128)S(1)}, f32[8,128]{1,0:T(8,128)S(1)}, u32[]{:S(2)}, u32[]{:S(2)}) collective-permute-start(f32[8,128]{1,0:T(8,128)S(1)} %get-tuple-element.50), channel_id=1, source_target_pairs={{0,4},{4,0},{8,12},{12,8},{16,20},{20,16},{24,28},{28,24},{1,5},{5... | collective-permute-start | bytes 12296 | tf_op jit(solution)/shard_map/ppermute | solution.py:618
  69.4 11.8 %collective-permute-start.6 = (bf16[128,512]{1,0:T(8,128)(2,1)S(1)}, bf16[128,512]{1,0:T(8,128)(2,1)S(1)}, u32[]{:S(2)}, u32[]{:S(2)}) collective-permute-start(bf16[128,512]{1,0:T(8,128)(2,1)S(1)} %get-tuple-element.40), channel_id=1, source_target_pairs={{0,1},{1,0},{2,3},{3,2},{4,5},{5,4},{6,7},{7,6},{8,9},{9,8},{10,11... | collective-permute-start | bytes 393224 | tf_op jit(solution)/shard_map/ppermute | solution.py:538
  69.4 11.7 %collective-permute-start.7 = (bf16[128,512]{1,0:T(8,128)(2,1)S(1)}, bf16[128,512]{1,0:T(8,128)(2,1)S(1)}, u32[]{:S(2)}, u32[]{:S(2)}) collective-permute-start(bf16[128,512]{1,0:T(8,128)(2,1)S(1)} %get-tuple-element.39), channel_id=1, source_target_pairs={{0,2},{1,3},{2,0},{3,1},{4,6},{5,7},{6,4},{7,5},{8,10},{9,11},{10,... | collective-permute-start | bytes 393224 | tf_op jit(solution)/shard_map/ppermute | solution.py:538
  70.0 11.2 %collective-permute-start.8 = (bf16[128,512]{1,0:T(8,128)(2,1)S(1)}, bf16[128,512]{1,0:T(8,128)(2,1)S(1)}, u32[]{:S(2)}, u32[]{:S(2)}) collective-permute-start(bf16[128,512]{1,0:T(8,128)(2,1)S(1)} %get-tuple-element.38), channel_id=1, source_target_pairs={{0,3},{1,2},{2,1},{3,0},{4,7},{5,6},{6,5},{7,4},{8,11},{9,10},{10,... | collective-permute-start | bytes 393224 | tf_op jit(solution)/shard_map/ppermute | solution.py:538
  71.3 9.1 %collective-permute-start.16 = (f32[8,128]{1,0:T(8,128)S(1)}, f32[8,128]{1,0:T(8,128)S(1)}, u32[]{:S(2)}, u32[]{:S(2)}) collective-permute-start(f32[8,128]{1,0:T(8,128)S(1)} %fusion.7), channel_id=1, source_target_pairs={{0,0},{2,8},{1,16},{3,24},{4,1},{6,9},{5,17},{7,25},{8,2},{10,10},... | collective-permute-start | bytes 12296 | tf_op jit(solution)/shard_map/ppermute | solution.py:620

commit v3 on v2

--- a/solution.py
+++ b/solution.py
@@ -248,32 +248,20 @@
 
 
 def forward_conv_kernel(
-    meta_ref, frames_hbm, f1, f2, f3, w_hbm, hid_ref, xext_hbm, conv_hbm,
-    f0_ref, w_ref, ext_ref, oth_ref, conv_ref, taps_ref, hid_sp_ref, sems,
+    meta_ref, f0, f1, f2, f3, w_ref, hid_ref, ext_hbm, conv_ref, ext_ref, oth_ref, taps_ref, hid_sp_ref, sem
 ):
-    own_index, group = meta_ref[0], meta_ref[1]
+    own_index = meta_ref[0]
     row_count = f1.shape[0]
     width = ext_ref.shape[2]
     seq_total = 4 * row_count
     steps = conv_ref.shape[0]
-    loads = []
-    for part in range(2):
-        start = pl.multiple_of((group ^ part) * width, width)
-        lanes = pl.ds(part * width, width)
-        loads.append(pltpu.make_async_copy(frames_hbm.at[:, pl.ds(start, width)], f0_ref.at[:, lanes], sems.at[part]))
-        loads.append(pltpu.make_async_copy(w_hbm.at[:, pl.ds(start, width)], w_ref.at[:, lanes], sems.at[2 + part]))
-    for load in loads:
-        load.start()
     spread = spread_matrix(meta_ref, own_index, row_count, seq_total, steps)
-    for load in loads:
-        load.wait()
     halves = (slice(0, width), slice(width, 2 * width))
     for lanes, ref in zip(halves, (ext_ref, oth_ref), strict=True):
-        rows = jnp.concatenate([f0_ref[:, lanes], f1[:, lanes], f2[:, lanes], f3[:, lanes]], axis=0)
+        rows = jnp.concatenate([f0[:, lanes], f1[:, lanes], f2[:, lanes], f3[:, lanes]], axis=0)
         write_extended(ref, jnp.dot(spread, rows, preferred_element_type=jnp.float32), steps)
-    save_ext = pltpu.make_async_copy(ext_ref, xext_hbm, sems.at[0])
-    save_conv = pltpu.make_async_copy(conv_ref, conv_hbm, sems.at[1])
-    save_ext.start()
+    save = pltpu.make_async_copy(ext_ref, ext_hbm, sem)
+    save.start()
     for tap in range(KERNEL):
         taps_ref[tap] = jnp.broadcast_to(w_ref[tap : tap + 1, :], (SUB, 2 * width))
     for part, ref in enumerate((ext_ref, oth_ref)):
@@ -282,18 +270,16 @@
             outer = slice(part * width + lane, part * width + lane + 128)
 
             def finish(step, conv, center, part=part, lanes=lanes, outer=outer):
-                hid_sp_ref[step, :, outer] = center + conv / (1.0 + jnp.exp(-conv))
+                half = 0.5 * conv
+                hid_sp_ref[step, :, outer] = center + (half + half * jnp.tanh(half))
                 if part == 0:
                     conv_ref[step, :, lanes] = conv
 
             conv_loop(ref, taps_ref, lanes, outer, steps, False, finish)
-        if part == 0:
-            save_conv.start()
     hid_low = hid_sp_ref[...].reshape(steps * SUB, 2 * width).astype(jnp.bfloat16)
     gather = gather_matrix(meta_ref, own_index, row_count, seq_total, steps)
     hid_ref[...] = jnp.dot(gather, hid_low, preferred_element_type=jnp.float32).astype(jnp.bfloat16)
-    save_ext.wait()
-    save_conv.wait()
+    save.wait()
 
 
 def swapped(array, order, row_count):
@@ -301,21 +287,12 @@
 
 
 def attention_kernel(
-    meta_ref, hid_ref, sib_ref, cot_hbm, f1, f2, f3, w_hbm,
-    out_ref, keep_ref, send_ref, kvg_ref,
-    c0, wk_ref, wv_ref, sems, k_ref, v_ref, kt_ref, vt_ref, cot_ref, cott_ref, attt_ref, dqt_ref, dk_ref, dv_ref, bias_ref,
+    meta_ref, hid_ref, sib_ref, f0, f1, f2, f3, wk_ref, wv_ref, out_ref, keep_ref, send_ref, kvg_ref,
+    k_ref, v_ref, kt_ref, vt_ref, cot_ref, cott_ref, attt_ref, dqt_ref, dk_ref, dv_ref, bias_ref,
 ):
     own_index, group = meta_ref[0], meta_ref[1]
-    row_count, width = c0.shape
-    seq_total = 4 * row_count
-    own = pl.multiple_of(group * width, width)
-    loads = [
-        pltpu.make_async_copy(w_hbm.at[:, pl.ds(own, width)], wk_ref, sems.at[0]),
-        pltpu.make_async_copy(w_hbm.at[:, pl.ds(4 * width + own, width)], wv_ref, sems.at[1]),
-        pltpu.make_async_copy(cot_hbm.at[:, pl.ds(own, width)], c0, sems.at[2]),
-    ]
-    for load in loads:
-        load.start()
+    row_count = f0.shape[0]
+    seq_total, width = out_ref.shape
     head_width = 64
     scale = 1.0 / math.sqrt(head_width)
     bf16, f32 = jnp.bfloat16, jnp.float32
@@ -324,8 +301,6 @@
     key_utt = utt_index(meta_ref, frame_at(key_row, own_index, row_count))
     query_utt = utt_index(meta_ref, frame_at(query_row, own_index, row_count))
     bias_ref[...] = jnp.where(key_utt == query_utt, 0.0, -jnp.inf).astype(f32)
-    for load in loads:
-        load.wait()
     parts = [
         hid_ref[:, :width],
         hid_ref[:, width:],
@@ -343,50 +318,40 @@
     kt_ref[...] = keys.T
     vt_ref[...] = values.T
     tail = slice(2 * width, 3 * width)
-    cot = jnp.concatenate([c0[...], f1[:, tail], f2[:, tail], f3[:, tail]], axis=0)
+    cot = jnp.concatenate([f0[:, tail], f1[:, tail], f2[:, tail], f3[:, tail]], axis=0)
     cot_ref[...] = cot
     cott_ref[...] = cot.T.astype(f32)
-    dk_ref[...] = jnp.zeros_like(dk_ref)
-    dv_ref[...] = jnp.zeros_like(dv_ref)
     lane = lax.broadcasted_iota(jnp.int32, (1, 128), 1)
     masks = [(lane < head_width).astype(f32).astype(bf16), (lane >= head_width).astype(f32).astype(bf16)]
-    query_block = min(256, seq_total)
-    blocks = seq_total // query_block
     exp_scale = scale * math.log2(math.e)
-
-    def step(it, carry):
-        pair = it // blocks
-        q0 = pl.multiple_of((it % blocks) * query_block, query_block)
-        l0 = pl.multiple_of(pair * 128, 128)
-        qrows = pl.ds(q0, query_block)
-        lanes = pl.ds(l0, 128)
-        query = hid_ref[qrows, lanes]
-        grad = cot_ref[qrows, lanes]
+    for first in range(0, width, 128):
+        lanes = slice(first, first + 128)
+        query = hid_ref[:, lanes]
+        grad = cot_ref[:, lanes]
         k_pair = k_ref[:, lanes]
         v_pair = v_ref[:, lanes]
-        dk_sum = dk_ref[:, lanes]
-        dv_sum = dv_ref[:, lanes]
+        dk_pair = None
+        dv_pair = None
         for head in range(2):
             mask = masks[head]
-            hrows = pl.ds(pl.multiple_of(l0 + head * head_width, head_width), head_width)
-            scores = nt_dot(k_pair * mask, query) + bias_ref[:, qrows]
+            hrows = slice(first + head * head_width, first + (head + 1) * head_width)
+            scores = nt_dot(k_pair * mask, query) + bias_ref[...]
             top = jnp.max(scores, axis=0, keepdims=True)
             expd = jnp.exp2((scores - top) * exp_scale)
             probs = expd * (1.0 / jnp.sum(expd, axis=0, keepdims=True))
             probs_low = probs.astype(bf16)
             attended = jnp.dot(vt_ref[hrows, :], probs_low, preferred_element_type=f32)
             dprobs = nt_dot(v_pair * mask, grad)
-            rowdot = jnp.sum(cott_ref[hrows, qrows] * attended, axis=0, keepdims=True)
+            rowdot = jnp.sum(cott_ref[hrows, :] * attended, axis=0, keepdims=True)
             dscores = (probs * (dprobs - rowdot)).astype(bf16)
-            attt_ref[hrows, qrows] = attended
-            dqt_ref[hrows, qrows] = jnp.dot(kt_ref[hrows, :], dscores, preferred_element_type=f32) * scale
-            dk_sum = dk_sum + jnp.dot(dscores, query * mask, preferred_element_type=f32)
-            dv_sum = dv_sum + jnp.dot(probs_low, grad * mask, preferred_element_type=f32)
-        dk_ref[:, lanes] = dk_sum
-        dv_ref[:, lanes] = dv_sum
-        return carry
-
-    lax.fori_loop(0, (width // 128) * blocks, step, 0)
+            attt_ref[hrows, :] = attended
+            dqt_ref[hrows, :] = jnp.dot(kt_ref[hrows, :], dscores, preferred_element_type=f32) * scale
+            dk_head = jnp.dot(dscores, query * mask, preferred_element_type=f32)
+            dv_head = jnp.dot(probs_low, grad * mask, preferred_element_type=f32)
+            dk_pair = dk_head if head == 0 else dk_pair + dk_head
+            dv_pair = dv_head if head == 0 else dv_pair + dv_head
+        dk_ref[:, lanes] = dk_pair
+        dv_ref[:, lanes] = dv_pair
     out_ref[...] = (parts[0].astype(f32) + attt_ref[...].T).astype(bf16)
     grad_k = (dk_ref[...] * scale).astype(bf16)
     grad_v = dv_ref[...].astype(bf16)
@@ -402,7 +367,7 @@
     keep_ref[:, width:] = partial(1)
 
 
-def weight_grad_kernel(meta_ref, hid_ref, sib_ref, kvg_ref, out_ref):
+def weight_grad_kernel(meta_ref, hid_ref, sib_ref, kvg_ref, out_hbm, all_ref, sems):
     group = meta_ref[1]
     width = hid_ref.shape[1] // 2
     row_count = hid_ref.shape[0] // 4
@@ -413,9 +378,14 @@
         swapped(sib_ref[:, :width], (1, 0, 3, 2), row_count),
         swapped(sib_ref[:, width:], (1, 0, 3, 2), row_count),
     ]
+    saves = []
     for j in range(4):
+        all_ref[j] = tn_dot(parts[j], kvg).astype(jnp.bfloat16)
         start = pl.multiple_of((group ^ j) * width, width)
-        out_ref[pl.ds(start, width), :] = tn_dot(parts[j], kvg).astype(jnp.bfloat16)
+        saves.append(pltpu.make_async_copy(all_ref.at[j], out_hbm.at[pl.ds(start, width), :], sems.at[j]))
+        saves[j].start()
+    for save in saves:
+        save.wait()
 
 
 def chip_sum_kernel(keep_ref, recv_ref, own_ref, send_ref):
@@ -426,23 +396,16 @@
     send_ref[...] = total[:, width:].astype(jnp.bfloat16)
 
 
-def backward_conv_kernel(
-    meta_ref, own_ref, recv_ref, xext_hbm, conv_hbm, w_hbm, dframes_ref, gdw_ref,
-    xext_ref, conv_ref, w_ref, ext_ref, taps_ref, dh_ref, df_ref, sems,
+def tap_grad_kernel(
+    meta_ref, own_ref, recv_ref, xext_hbm, conv_ref, dh_ref, ext_ref, dw_keep_ref, dw_send_ref, xext_ref, gdw_ref, sem
 ):
-    own_index, group = meta_ref[0], meta_ref[1]
+    own_index, dp_index = meta_ref[0], meta_ref[2]
     seq_total, width = own_ref.shape
     row_count = seq_total // 4
     steps = conv_ref.shape[0]
     bf16, f32 = jnp.bfloat16, jnp.float32
-    start = pl.multiple_of(group * width, width)
-    loads = [
-        pltpu.make_async_copy(conv_hbm, conv_ref, sems.at[0]),
-        pltpu.make_async_copy(w_hbm.at[:, pl.ds(start, width)], w_ref, sems.at[1]),
-        pltpu.make_async_copy(xext_hbm, xext_ref, sems.at[2]),
-    ]
-    for load in loads:
-        load.start()
+    load = pltpu.make_async_copy(xext_hbm, xext_ref, sem)
+    load.start()
     dhidden = own_ref[...] + swapped(recv_ref[...], (2, 3, 0, 1), row_count).astype(f32)
     high = dhidden.astype(bf16)
     low = (dhidden - high.astype(f32)).astype(bf16)
@@ -450,22 +413,14 @@
     both = jnp.dot(spread, jnp.concatenate([high, low], axis=1), preferred_element_type=f32)
     spaced = both[:, :width] + both[:, width:]
     dh_ref[...] = spaced.reshape(steps, SUB, width)
-    for load in loads:
-        load.wait()
     conv = conv_ref[...].reshape(steps * SUB, width)
-    gate = 1.0 / (1.0 + jnp.exp(-conv))
+    gate = 0.5 + 0.5 * jnp.tanh(0.5 * conv)
     dconv = (spaced * (gate * (1.0 + conv * (1.0 - gate)))).astype(bf16).astype(f32)
     write_extended(ext_ref, dconv, steps)
-    for tap in range(KERNEL):
-        taps_ref[tap] = jnp.broadcast_to(w_ref[tap : tap + 1, :], (SUB, width))
+    load.wait()
     half_taps = (KERNEL + 1) // 2
     for lane in range(0, width, 128):
         lanes = slice(lane, lane + 128)
-
-        def finish(step, conv, center, lanes=lanes):
-            df_ref[step, :, lanes] = dh_ref[step, :, lanes] + conv
-
-        conv_loop(ext_ref, taps_ref, lanes, lanes, steps, True, finish)
         for first in range(0, KERNEL, half_taps):
             count = min(half_taps, KERNEL - first)
 
@@ -483,9 +438,28 @@
             for t in range(count):
                 gdw_ref[first + t : first + t + 1, lanes] = jnp.sum(sums[t], axis=0, keepdims=True)
     gdw_ref[KERNEL:, :] = jnp.zeros((gdw_ref.shape[0] - KERNEL, width), f32)
-    gather = gather_matrix(meta_ref, own_index, row_count, seq_total, steps)
-    df_low = df_ref[...].reshape(steps * SUB, width).astype(bf16)
-    dframes_ref[...] = jnp.dot(gather, df_low, preferred_element_type=f32).astype(bf16)
+    half = width // 2
+    side = dp_index & 1
+    dw_keep_ref[...] = gdw_ref[:, pl.ds(pl.multiple_of(side * half, half), half)].T
+    dw_send_ref[...] = gdw_ref[:, pl.ds(pl.multiple_of((1 - side) * half, half), half)].T
+
+
+def frame_grad_kernel(meta_ref, dh_ref, ext_ref, w_ref, dframes_ref, taps_ref, df_ref):
+    own_index = meta_ref[0]
+    seq_total, width = dframes_ref.shape
+    steps = dh_ref.shape[0]
+    for tap in range(KERNEL):
+        taps_ref[tap] = jnp.broadcast_to(w_ref[tap : tap + 1, :width], (SUB, width))
+    for lane in range(0, width, 128):
+        lanes = slice(lane, lane + 128)
+
+        def finish(step, conv, center, lanes=lanes):
+            df_ref[step, :, lanes] = dh_ref[step, :, lanes] + conv
+
+        conv_loop(ext_ref, taps_ref, lanes, lanes, steps, True, finish)
+    gather = gather_matrix(meta_ref, own_index, seq_total // 4, seq_total, steps)
+    df_low = df_ref[...].reshape(steps * SUB, width).astype(jnp.bfloat16)
+    dframes_ref[...] = jnp.dot(gather, df_low, preferred_element_type=jnp.float32).astype(jnp.bfloat16)
 
 
 def place_kernel(meta_ref, own_ref, r1, r2, r3, out_ref, dframes_ref):
@@ -511,27 +485,24 @@
         out_ref[:, full + start : full + start + width] = total[:, width:]
 
 
-def call(kernel, scalars, args, outs, scratch=(), hbm_in=(), hbm_out=(), vmem_mib=16, cost_us=2):
-    def whole(shape):
-        zeros = (0,) * len(shape)
-        return pl.BlockSpec(shape, lambda *_: zeros)
-
-    def placed(shape, in_hbm):
-        return pl.BlockSpec(memory_space=pltpu.HBM) if in_hbm else whole(shape)
-
+def call(kernel, scalars, args, outs, scratch=(), hbm_in=(), hbm_out=(), to_hbm=False, vmem_mib=16, cost_us=2):
+    vmem, hbm = pl.BlockSpec(memory_space=pltpu.VMEM), pl.BlockSpec(memory_space=pltpu.HBM)
+    colours = [pltpu.HBM if i in hbm_out else pltpu.VMEM for i in range(len(outs))]
     return pl.pallas_call(
         kernel,
-        out_shape=[pltpu.HBM(s, t) if i in hbm_out else jax.ShapeDtypeStruct(s, t) for i, (s, t) in enumerate(outs)],
+        out_shape=[jax.ShapeDtypeStruct(*o) if to_hbm else c(*o) for c, o in zip(colours, outs, strict=True)],
         grid_spec=pltpu.PrefetchScalarGridSpec(
             num_scalar_prefetch=len(scalars),
-            grid=(1,),
-            in_specs=[placed(arg.shape, i in hbm_in) for i, arg in enumerate(args)],
-            out_specs=[placed(shape, i in hbm_out) for i, (shape, _) in enumerate(outs)],
+            in_specs=[hbm if i in hbm_in else vmem for i in range(len(args))],
+            out_specs=[hbm if i in hbm_out else vmem for i in range(len(outs))],
             scratch_shapes=list(scratch),
         ),
         compiler_params=pltpu.CompilerParams(vmem_limit_bytes=vmem_mib * 1024 * 1024),
         cost_estimate=pl.CostEstimate(flops=cost_us * 10**9, bytes_accessed=cost_us * 3 * 10**6, transcendentals=0),
-    )(*scalars, *(pltpu.with_memory_space_constraint(a, pltpu.HBM) if i in hbm_in else a for i, a in enumerate(args)))
+    )(
+        *scalars,
+        *(pltpu.with_memory_space_constraint(a, pltpu.HBM if i in hbm_in else pltpu.VMEM) for i, a in enumerate(args)),
+    )
 
 
 def swap_ctx(array, j):
@@ -557,39 +528,38 @@
     def parcel(owner):
         return jnp.concatenate([columns(rows, owner), columns(rows, owner ^ 1), columns(grads, owner)], axis=1)
 
-    blocks = [swap_ctx(parcel(group ^ SWAP[j]), j) for j in (1, 2, 3)]
+    blocks = [parcel(group)] + [swap_ctx(parcel(group ^ SWAP[j]), j) for j in (1, 2, 3)]
+    w_taps = jnp.concatenate([columns(w_dw, group), columns(w_dw, group ^ 1)], axis=1)
+    w_keys, w_values = columns(w_kv, group), columns(w_kv, group + 4)
+    blocks, w_keys, w_values = lax.optimization_barrier((blocks, w_keys, w_values))
     wide = (seq_total, width)
     both = (seq_total, 2 * width)
     tall = wide[::-1]
     long = (steps + 2 * RIM, SUB, width)
     short = (steps, SUB, width)
-    taps = (KERNEL, SUB, width)
-    dma = pltpu.SemaphoreType.DMA
     hidden, frames_ext, conv_own = call(
-        forward_conv_kernel, (meta,), (rows, *blocks, w_dw), [(both, bf16), (long, f32), (short, f32)],
+        forward_conv_kernel, (meta,), (*blocks, w_taps), [(both, bf16), (long, f32), (short, f32)],
         [
-            pltpu.VMEM((row_count, 2 * width), bf16), pltpu.VMEM((KERNEL, 2 * width), f32),
-            pltpu.VMEM(long, f32), pltpu.VMEM(long, f32), pltpu.VMEM(short, f32),
-            pltpu.VMEM((KERNEL, SUB, 2 * width), f32), pltpu.VMEM((steps, SUB, 2 * width), f32), dma((4,)),
+            pltpu.VMEM(long, f32), pltpu.VMEM(long, f32), pltpu.VMEM((KERNEL, SUB, 2 * width), f32),
+            pltpu.VMEM((steps, SUB, 2 * width), f32), pltpu.SemaphoreType.DMA,
         ],
-        hbm_in=(0, 4), hbm_out=(1, 2), cost_us=6,
+        hbm_out=(1,), cost_us=6,
     )
     hidden_sib = swap_ctx(hidden, 1)
     out_own, keep, send, kv_grad = call(
-        attention_kernel, (meta,), (hidden, hidden_sib, grads, *blocks, w_kv),
+        attention_kernel, (meta,), (hidden, hidden_sib, *blocks, w_keys, w_values),
         [(wide, bf16), (both, f32), (both, bf16), (both, bf16)],
         [
-            pltpu.VMEM((row_count, width), bf16), pltpu.VMEM((feat_width, width), bf16),
-            pltpu.VMEM((feat_width, width), bf16), dma((3,)),
             pltpu.VMEM(wide, bf16), pltpu.VMEM(wide, bf16), pltpu.VMEM(tall, bf16), pltpu.VMEM(tall, bf16),
             pltpu.VMEM(wide, bf16), pltpu.VMEM(tall, f32), pltpu.VMEM(tall, f32),
             pltpu.VMEM(tall, f32), pltpu.VMEM(wide, f32), pltpu.VMEM(wide, f32),
             pltpu.VMEM((seq_total, seq_total), f32),
         ],
-        hbm_in=(2, 6), vmem_mib=24, cost_us=11,
+        vmem_mib=20, cost_us=8,
     )
     (part_kv,) = call(
-        weight_grad_kernel, (meta,), (hidden, hidden_sib, kv_grad), [((feat_width, 2 * width), bf16)], cost_us=2
+        weight_grad_kernel, (meta,), (hidden, hidden_sib, kv_grad), [((feat_width, 2 * width), bf16)],
+        [pltpu.VMEM((4, width, 2 * width), bf16), pltpu.SemaphoreType.DMA((4,))], hbm_out=(0,), cost_us=2,
     )
     piece = feat_width // (4 * dp_size)
     from_sib = swap_ctx(send, 1)
@@ -597,34 +567,42 @@
     part_send, part_kv = lax.optimization_barrier((part_send, part_kv))
     from_chip = swap_ctx(part_send, 2)
     all_kv = lax.all_to_all(part_kv.reshape(4 * dp_size, piece, 2 * width), ("dp", "ctx"), 0, 0)
-    dframes, part_dw = call(
-        backward_conv_kernel, (meta,), (part_own, from_chip, frames_ext, conv_own, w_dw),
-        [(wide, bf16), ((KERNEL + 1, width), f32)],
-        [
-            pltpu.VMEM(long, f32), pltpu.VMEM(short, f32), pltpu.VMEM((KERNEL, width), f32),
-            pltpu.VMEM(long, f32), pltpu.VMEM(taps, f32), pltpu.VMEM(short, f32), pltpu.VMEM(short, f32), dma((3,)),
-        ],
-        hbm_in=(2, 3, 4), cost_us=100,
-    )
+    dhidden, dconv_ext, dw_keep, dw_send = call(
+        tap_grad_kernel, (meta,), (part_own, from_chip, frames_ext, conv_own),
+        [(short, f32), (long, f32), ((width // 2, KERNEL + 1), f32), ((width // 2, KERNEL + 1), f32)],
+        [pltpu.VMEM(long, f32), pltpu.VMEM((KERNEL + 1, width), f32), pltpu.SemaphoreType.DMA],
+        hbm_in=(2,), cost_us=100,
+    )
+    (dframes,) = call(
+        frame_grad_kernel, (meta,), (dhidden, dconv_ext, w_taps), [(wide, bf16)],
+        [pltpu.VMEM((KERNEL, SUB, width), f32), pltpu.VMEM(short, f32)], cost_us=20,
+    )
+    dw_half = dw_keep + lax.ppermute(dw_send, "dp", [(i, i ^ 1) for i in range(dp_size)])
     results = jnp.concatenate([out_own, dframes], axis=1)
     result_blocks = [results] + [swap_ctx(results[j * row_count : (j + 1) * row_count], j) for j in (1, 2, 3)]
+    dw_half, result_blocks[1] = lax.optimization_barrier((dw_half, result_blocks[1]))
+    grad_dw = None
+    for turn in range(4):
+        pairs = []
+        for d in range(dp_size):
+            for c in range(4):
+                target = 2 * (2 * (c & 1) + (c >> 1)) + (d & 1)
+                pairs.append((4 * d + c, 4 * target + ((d >> 1) ^ turn)))
+        quarter = lax.dynamic_slice_in_dim(dw_half, ((dp_index >> 1) ^ turn) * piece, piece, axis=0)
+        arrived = lax.ppermute(quarter, ("dp", "ctx"), pairs)
+        grad_dw = arrived if turn == 0 else grad_dw + arrived
+    grad_dw = grad_dw[:, :KERNEL]
     output, dframes_rows = call(
-        place_kernel, (meta,), tuple(result_blocks), [((row_count, feat_width), bf16)] * 2, cost_us=1
-    )
-    by_owner = jnp.moveaxis(part_dw.reshape(KERNEL + 1, dp_size, piece), 1, 0).reshape(dp_size, -1, 128)
-    dw_sends = [lax.dynamic_index_in_dim(by_owner, dp_index ^ k, 0, keepdims=False) for k in range(dp_size)]
-    sum_dw = dw_sends[0]
-    for k in range(1, dp_size):
-        sum_dw = sum_dw + lax.ppermute(dw_sends[k], "dp", [(i, i ^ k) for i in range(dp_size)])
-    sources = [(4 * d + 2 * (g & 1) + (g >> 1), dp_size * g + d) for d in range(dp_size) for g in range(4)]
-    all_dw = lax.ppermute(sum_dw, ("dp", "ctx"), sources)
-    (grad_kv,) = call(place_grad_kernel, (), (all_kv,), [((piece, 2 * feat_width), f32)], cost_us=1)
-    grad_dw = all_dw.reshape(KERNEL + 1, piece).T[:, :KERNEL]
+        place_kernel, (meta,), tuple(result_blocks), [((row_count, feat_width), bf16)] * 2, to_hbm=True, cost_us=1
+    )
+    (grad_kv,) = call(
+        place_grad_kernel, (), (all_kv,), [((piece, 2 * feat_width), f32)], to_hbm=True, cost_us=1
+    )
     return (output[None], dframes_rows[None], grad_kv, grad_dw)
 
 
 def on_device(frames, utt_lengths, cotangent, w_dw, w_kv):
-    if lax.axis_size("ctx") == 4 and lax.axis_size("dp") == 8:
+    if lax.axis_size("ctx") == 4 and lax.axis_size("dp") == 8 and frames.shape[1:] == (128, 1024):
         return on_device_pairs(frames, utt_lengths, cotangent, w_dw, w_kv)
     return on_device_any(frames, utt_lengths, cotangent, w_dw, w_kv)
 

time: 83.8 us -> 68.1 us (0.81)
  the two profiles are of different devices: /device:TPU:6 before, /device:TPU:0 now
where the time goes in v3:
time: 68.1 us; the launch traced here: 67.3 us
  starting transfers between devices  24.1 us (35%)
  Pallas kernels  23.3 us (34%)
  waiting for transfers between devices  14.3 us (21%)
  local copies, waits for them, and re-layouts  3.3 us (5%)
  other arithmetic  1.48 us (2%)
  between operations  0.87 us (1%)
    pallas_call x8, Pallas kernels, call(): pl.pallas_call(kernel, out_shape=[jax.ShapeDtypeStruct(*o) if to_hbm else...  23.3 us
    ppermute x9, waiting for transfers between devices, swap_ctx(): return lax.ppermute(array, 'ctx', [(i, i ^ j) for i in range(4)])  9.8 us
    ppermute x4, starting transfers between devices, on_device_pairs(): arrived = lax.ppermute(quarter, ('dp', 'ctx'), pairs)  9.63 us
    ppermute x9, starting transfers between devices, swap_ctx(): return lax.ppermute(array, 'ctx', [(i, i ^ j) for i in range(4)])  7.68 us
    all_to_all x1, starting transfers between devices, on_device_pairs(): lax.all_to_all(part_kv.reshape(4 * dp_size, piece, 2 * width), ('dp', 'ct...  4.92 us
    dynamic_slice x3, local copies, waits for them, and re-layouts, columns(): return lax.dynamic_slice_in_dim(array, owner * width, width, axis=1)  3.28 us
    ppermute x1, waiting for transfers between devices, on_device_pairs(): lax.ppermute(dw_send, 'dp', [(i, i ^ 1) for i in range(dp_size)])  2.3 us
    ppermute x4, waiting for transfers between devices, on_device_pairs(): arrived = lax.ppermute(quarter, ('dp', 'ctx'), pairs)  2.23 us
  transfers between devices with their start and end apart: 15, of which 7 were waited for; matrix products, arithmetic and copies ran while one was open for 5% of the time, Pallas kernels for 15%

profile of v3, /device:TPU:0, one launch (start us, length us, event | category | flops | bytes accessed | tf_op | source)
XLA Modules:
  0.0 67.3 jit_solution(15809479394447373706)
XLA Ops:
  0.7 1.2 %dynamic-slice_bitcast_fusion = (bf16[128,256]{1,0:T(8,128)(2,1)S(1)}, bf16[128,256]{1,0:T(8,128)(2,1)S(1)}, bf16[128,256]{1,0:T(8,128)(2,1)S(1)}, bf16[128,256]...) fusion(bf16[1,128,1024]{2,1,0:T(8,128)(2,1)} %param.7, ...), kind=kLoop, calls=%fused_computation.15 | loop fusion | bytes 1441820 | tf_op jit(solution)/shard_map/dynamic_slice | solution.py:526
  1.9 2.4 %collective-permute-start.2 = (bf16[128,768]{1,0:T(8,128)(2,1)S(1)}, bf16[128,768]{1,0:T(8,128)(2,1)S(1)}, u32[]{:S(2)}, u32[]{:S(2)}) collective-permute-start(bf16[128,768]{1,0:T(8,128)(2,1)S(1)} %pad_maximum_fusion.4), channel_id=1, source_target_pairs={{0,3},{1,2},{2,1},{3,0},{4,7},{5,6},{6,5},{7,4},{8,11},{9,10},{10,... | collective-permute-start | bytes 589832 | tf_op jit(solution)/shard_map/ppermute | solution.py:509
  4.4 0.7 %collective-permute-start = (bf16[128,768]{1,0:T(8,128)(2,1)S(1)}, bf16[128,768]{1,0:T(8,128)(2,1)S(1)}, u32[]{:S(2)}, u32[]{:S(2)}) collective-permute-start(bf16[128,768]{1,0:T(8,128)(2,1)S(1)} %pad_maximum_fusion.2), channel_id=1, source_target_pairs={{0,1},{1,0},{2,3},{3,2},{4,5},{5,4},{6,7},{7,6},{8,9},{9,8},{10,11... | collective-permute-start | bytes 589832 | tf_op jit(solution)/shard_map/ppermute | solution.py:509
  5.2 0.8 %constant_dynamic-slice_fusion.5 = (f32[31,256]{1,0:T(8,128)S(1)}, f32[31,256]{1,0:T(8,128)S(1)}) fusion(f32[31,1024]{1,0:T(8,128)} %param.8, s32[]{:T(128)S(6)} %select_n.46, s32[]{:T(128)S(6)} %select_n.47), kind=kLoop, calls=%fused_computation.34 | loop fusion | bytes 126984 | tf_op jit(solution)/shard_map/dynamic_slice | solution.py:526
  6.8 1.3 %constant_dynamic-slice_fusion.6 = (bf16[1024,256]{1,0:T(8,128)(2,1)S(1)}, bf16[1024,256]{1,0:T(8,128)(2,1)S(1)}) fusion(bf16[1024,2048]{1,0:T(8,128)(2,1)} %param.9, s32[]{:T(128)S(6)} %select_n.54, s32[]{:T(128)S(6)} %select_n.53), kind=kLoop, calls=%fused_computation.35 | loop fusion | bytes 2097160 | tf_op jit(solution)/shard_map/dynamic_slice | solution.py:526
  8.0 1.6 %collective-permute-done.2.f3 = bf16[128,768]{1,0:T(8,128)(2,1)S(1)} collective-permute-done((bf16[128,768]{1,0:T(8,128)(2,1)S(1)}, bf16[128,768]{1,0:T(8,128)(2,1)S(1)}, u32[]{:S(2)}, u32[]{:S(2)}) %collective-permute-start.2) | collective-permute-done | bytes 196640 | tf_op jit(solution)/shard_map/ppermute | solution.py:509
  9.7 4.4 %collective-permute-done.1.f2 = bf16[128,768]{1,0:T(8,128)(2,1)S(1)} collective-permute-done((bf16[128,768]{1,0:T(8,128)(2,1)S(1)}, bf16[128,768]{1,0:T(8,128)(2,1)S(1)}, u32[]{:S(2)}, u32[]{:S(2)}) %collective-permute-start.1) | collective-permute-done | bytes 196640 | tf_op jit(solution)/shard_map/ppermute | solution.py:509
  14.0 5.4 %shard_map.84 = (bf16[512,512]{1,0:T(8,128)(2,1)S(1)}, f32[108,8,256]{2,1,0:T(8,128)}, f32[78,8,256]{2,1,0:T(8,128)S(1)}) custom-call(s32[11]{0:T(128)S(1)} %pad_add_fusion.meta_ref, bf16[128,768]{1,0:T(8,128)(2,1)S(1)} %get-tuple-element.29.f0, bf16[128,768]{1,0:T(8,128)(2,1)S(1)} %collective-permute-done.f1, ...), custom_call_target="tpu_custom_call" | custom-call | flops 6000000000 | bytes 18000000 | tf_op jit(solution)/shard_map/pallas_call | solution.py:491
  19.5 1.9 %collective-permute-done.3.sib_ref = bf16[512,512]{1,0:T(8,128)(2,1)S(1)} collective-permute-done((bf16[512,512]{1,0:T(8,128)(2,1)S(1)}, bf16[512,512]{1,0:T(8,128)(2,1)S(1)}, u32[]{:S(2)}, u32[]{:S(2)}) %collective-permute-start.3) | collective-permute-done | bytes 524320 | tf_op jit(solution)/shard_map/ppermute | solution.py:509
  21.4 6.7 %shard_map.85 = (bf16[512,256]{1,0:T(8,128)(2,1)S(1)}, f32[512,512]{1,0:T(8,128)S(1)}, bf16[512,512]{1,0:T(8,128)(2,1)S(1)}, bf16[512,512]{1,0:T(8,128)(2,1)S(1)}) custom-call(s32[11]{0:T(128)S(1)} %pad_add_fusion.meta_ref, bf16[512,512]{1,0:T(8,128)(2,1)S(1)} %get-tuple-element.33.hid_ref, bf16[512,512]{1,0:T(8,128)(2,1)S(1)} %collective-permute-done.3.sib_ref, ...), custom_call_target="tpu_custom_call" | custom-call | flops 8000000000 | bytes 24000000 | tf_op jit(solution)/shard_map/pallas_call | solution.py:491
  28.3 2.0 %shard_map.87 = bf16[1024,512]{1,0:T(8,128)(2,1)} custom-call(s32[11]{0:T(128)S(1)} %pad_add_fusion.meta_ref, bf16[512,512]{1,0:T(8,128)(2,1)S(1)} %get-tuple-element.33.hid_ref, bf16[512,512]{1,0:T(8,128)(2,1)S(1)} %collective-permute-done.3.sib_ref, bf16[512,512]{1,0:T(8,128)(2,1)S(1)} %get-tuple-element.41.kvg_ref), custom_call_target="tpu_custom_call" | custom-call | flops 2000000000 | bytes 6000000 | tf_op jit(solution)/shard_map/pallas_call | solution.py:491
  30.5 2.4 %collective-permute-start.5 = (bf16[512,256]{1,0:T(8,128)(2,1)S(1)}, bf16[512,256]{1,0:T(8,128)(2,1)S(1)}, u32[]{:S(2)}, u32[]{:S(2)}) collective-permute-start(bf16[512,256]{1,0:T(8,128)(2,1)S(1)} %get-tuple-element.42), channel_id=1, source_target_pairs={{0,2},{1,3},{2,0},{3,1},{4,6},{5,7},{6,4},{7,5},{8,10},{9,11},{10,... | collective-permute-start | bytes 786440 | tf_op jit(solution)/shard_map/ppermute | solution.py:509
  32.9 4.9 %all-to-all-start = ((bf16[32,32,512]{2,1,0:T(8,128)(2,1)}), bf16[32,32,512]{2,1,0:T(8,128)(2,1)S(1)}, u32[]{:S(2)}, u32[]{:S(2)}) async-start(bf16[32,32,512]{2,1,0:T(8,128)(2,1)} %bitcast.29), calls=%async_computation | async-start | bytes 2097152 | tf_op jit(solution)/shard_map/all_to_all | solution.py:569
  37.8 1.9 %collective-permute-done.5.recv_ref = bf16[512,256]{1,0:T(8,128)(2,1)S(1)} collective-permute-done((bf16[512,256]{1,0:T(8,128)(2,1)S(1)}, bf16[512,256]{1,0:T(8,128)(2,1)S(1)}, u32[]{:S(2)}, u32[]{:S(2)}) %collective-permute-start.5) | collective-permute-done | bytes 262176 | tf_op jit(solution)/shard_map/ppermute | solution.py:509
  39.7 3.6 %shard_map.88 = (f32[78,8,256]{2,1,0:T(8,128)S(1)}, f32[108,8,256]{2,1,0:T(8,128)S(1)}, f32[128,32]{1,0:T(8,128)S(1)}, f32[128,32]{1,0:T(8,128)S(1)}) custom-call(s32[11]{0:T(128)S(1)} %pad_add_fusion.meta_ref, f32[512,256]{1,0:T(8,128)S(1)} %get-tuple-element.39.own_ref, bf16[512,256]{1,0:T(8,128)(2,1)S(1)} %collective-permute-done.5.recv_ref, ...), custom_call_target="tpu_custom_call" | custom-call | flops 99999997952 | bytes 300000000 | tf_op jit(solution)/shard_map/pallas_call | solution.py:491
  43.3 3.2 %shard_map.89 = bf16[512,256]{1,0:T(8,128)(2,1)S(1)} custom-call(s32[11]{0:T(128)S(1)} %pad_add_fusion.meta_ref, f32[78,8,256]{2,1,0:T(8,128)S(1)} %get-tuple-element.45.dh_ref, f32[108,8,256]{2,1,0:T(8,128)S(1)} %get-tuple-element.46.ext_ref, f32[31,512]{1,0:T(8,128)S(1)} %pad_maximum_fusion.5.w_ref), custom_call_target="tpu_custom_call" | custom-call | flops 20000000000 | bytes 60000000 | tf_op jit(solution)/shard_map/pallas_call | solution.py:491
  46.6 1.8 %collective-permute-start.6 = (f32[128,32]{1,0:T(8,128)S(1)}, f32[128,32]{1,0:T(8,128)S(1)}, u32[]{:S(2)}, u32[]{:S(2)}) collective-permute-start(f32[128,32]{1,0:T(8,128)S(1)} %get-tuple-element.48), channel_id=1, source_target_pairs={{0,4},{4,0},{8,12},{12,8},{16,20},{20,16},{24,28},{28,24},{1,5},{5... | collective-permute-start | bytes 49160 | tf_op jit(solution)/shard_map/ppermute | solution.py:580
  48.5 1.7 %collective-permute-start.8 = (bf16[128,512]{1,0:T(8,128)(2,1)S(1)}, bf16[128,512]{1,0:T(8,128)(2,1)S(1)}, u32[]{:S(2)}, u32[]{:S(2)}) collective-permute-start(bf16[128,512]{1,0:T(8,128)(2,1)S(1)} %get-tuple-element.58), channel_id=1, source_target_pairs={{0,2},{1,3},{2,0},{3,1},{4,6},{5,7},{6,4},{7,5},{8,10},{9,11},{10,... | collective-permute-start | bytes 393224 | tf_op jit(solution)/shard_map/ppermute | solution.py:509
  50.2 2.3 %collective-permute-done.6 = f32[128,32]{1,0:T(8,128)S(1)} collective-permute-done((f32[128,32]{1,0:T(8,128)S(1)}, f32[128,32]{1,0:T(8,128)S(1)}, u32[]{:S(2)}, u32[]{:S(2)}) %collective-permute-start.6) | collective-permute-done | bytes 16416 | tf_op jit(solution)/shard_map/ppermute | solution.py:580
  53.2 4.4 %collective-permute-start.11 = (f32[32,32]{1,0:T(8,128)S(1)}, f32[32,32]{1,0:T(8,128)S(1)}, u32[]{:S(2)}, u32[]{:S(2)}) collective-permute-start(f32[32,32]{1,0:T(8,128)S(1)} %get-tuple-element.75), channel_id=1, source_target_pairs={{0,1},{1,17},{2,9},{3,25},{4,5},{5,21},{6,13},{7,29},{8,0},{9,16},... | collective-permute-start | bytes 12296 | tf_op jit(solution)/shard_map/ppermute | solution.py:592
  57.9 4.3 %collective-permute-start.13 = (f32[32,32]{1,0:T(8,128)S(1)}, f32[32,32]{1,0:T(8,128)S(1)}, u32[]{:S(2)}, u32[]{:S(2)}) collective-permute-start(f32[32,32]{1,0:T(8,128)S(1)} %get-tuple-element.73), channel_id=1, source_target_pairs={{0,3},{1,19},{2,11},{3,27},{4,7},{5,23},{6,15},{7,31},{8,2},{9,18}... | collective-permute-start | bytes 12296 | tf_op jit(solution)/shard_map/ppermute | solution.py:592
  62.2 1.4 %shard_map.90 = (bf16[128,1024]{1,0:T(8,128)(2,1)}, bf16[128,1024]{1,0:T(8,128)(2,1)}) custom-call(s32[11]{0:T(128)S(1)} %pad_add_fusion.meta_ref, bf16[512,512]{1,0:T(8,128)(2,1)S(1)} %pad_maximum_fusion.own_ref, bf16[128,512]{1,0:T(8,128)(2,1)S(1)} %collective-permute-done.7.r1, bf16[128,512]{1,0:T(8,128)(2,1)S(1)} %collective-permute-done.8.r2, ...), custom_call_target="tpu_custom_call" | custom-call | flops 1000000000 | bytes 3000000 | tf_op jit(solution)/shard_map/pallas_call | solution.py:491
  63.6 1.6 %collective-permute-done.12 = f32[32,32]{1,0:T(8,128)S(1)} collective-permute-done((f32[32,32]{1,0:T(8,128)S(1)}, f32[32,32]{1,0:T(8,128)S(1)}, u32[]{:S(2)}, u32[]{:S(2)}) %collective-permute-start.12) | collective-permute-done | bytes 4128 | tf_op jit(solution)/shard_map/ppermute | solution.py:592
  66.5 0.8 %shard_map.91 = f32[32,2048]{1,0:T(8,128)} custom-call(bf16[32,32,512]{2,1,0:T(8,128)(2,1)S(1)} %all-to-all-done.blocks_ref), custom_call_target="tpu_custom_call" | custom-call | flops 1000000000 | bytes 3000000 | tf_op jit(solution)/shard_map/pallas_call | solution.py:491
  (27 shorter events, 3.7 us)
Async XLA Ops:
  1.9 7.7 %collective-permute-start.2 = (bf16[128,768]{1,0:T(8,128)(2,1)S(1)}, bf16[128,768]{1,0:T(8,128)(2,1)S(1)}, u32[]{:S(2)}, u32[]{:S(2)}) collective-permute-start(bf16[128,768]{1,0:T(8,128)(2,1)S(1)} %pad_maximum_fusion.4), channel_id=1, source_target_pairs={{0,3},{1,2},{2,1},{3,0},{4,7},{5,6},{6,5},{7,4},{8,11},{9,10},{10,... | collective-permute-start | bytes 589832 | tf_op jit(solution)/shard_map/ppermute | solution.py:509
  4.4 5.3 %collective-permute-start = (bf16[128,768]{1,0:T(8,128)(2,1)S(1)}, bf16[128,768]{1,0:T(8,128)(2,1)S(1)}, u32[]{:S(2)}, u32[]{:S(2)}) collective-permute-start(bf16[128,768]{1,0:T(8,128)(2,1)S(1)} %pad_maximum_fusion.2), channel_id=1, source_target_pairs={{0,1},{1,0},{2,3},{3,2},{4,5},{5,4},{6,7},{7,6},{8,9},{9,8},{10,11... | collective-permute-start | bytes 589832 | tf_op jit(solution)/shard_map/ppermute | solution.py:509
  5.1 8.9 %collective-permute-start.1 = (bf16[128,768]{1,0:T(8,128)(2,1)S(1)}, bf16[128,768]{1,0:T(8,128)(2,1)S(1)}, u32[]{:S(2)}, u32[]{:S(2)}) collective-permute-start(bf16[128,768]{1,0:T(8,128)(2,1)S(1)} %get-tuple-element.76), channel_id=1, source_target_pairs={{0,2},{1,3},{2,0},{3,1},{4,6},{5,7},{6,4},{7,5},{8,10},{9,11},{10,... | collective-permute-start | bytes 589832 | tf_op jit(solution)/shard_map/ppermute | solution.py:509
  19.4 2.0 %collective-permute-start.3 = (bf16[512,512]{1,0:T(8,128)(2,1)S(1)}, bf16[512,512]{1,0:T(8,128)(2,1)S(1)}, u32[]{:S(2)}, u32[]{:S(2)}) collective-permute-start(bf16[512,512]{1,0:T(8,128)(2,1)S(1)} %get-tuple-element.33.hid_ref), channel_id=1, source_target_pairs={{0,1},{1,0},{2,3},{3,2},{4,5},{5,4},{6,7},{7,6},{8,9},{9,8},{10,11... | collective-permute-start | bytes 1572872 | tf_op jit(solution)/shard_map/ppermute | solution.py:509
  28.1 2.2 %collective-permute-start.4 = (bf16[512,512]{1,0:T(8,128)(2,1)S(1)}, bf16[512,512]{1,0:T(8,128)(2,1)S(1)}, u32[]{:S(2)}, u32[]{:S(2)}) collective-permute-start(bf16[512,512]{1,0:T(8,128)(2,1)S(1)} %get-tuple-element.38), channel_id=1, source_target_pairs={{0,1},{1,0},{2,3},{3,2},{4,5},{5,4},{6,7},{7,6},{8,9},{9,8},{10,11... | collective-permute-start | bytes 1572872 | tf_op jit(solution)/shard_map/ppermute | solution.py:509
  30.5 9.2 %collective-permute-start.5 = (bf16[512,256]{1,0:T(8,128)(2,1)S(1)}, bf16[512,256]{1,0:T(8,128)(2,1)S(1)}, u32[]{:S(2)}, u32[]{:S(2)}) collective-permute-start(bf16[512,256]{1,0:T(8,128)(2,1)S(1)} %get-tuple-element.42), channel_id=1, source_target_pairs={{0,2},{1,3},{2,0},{3,1},{4,6},{5,7},{6,4},{7,5},{8,10},{9,11},{10,... | collective-permute-start | bytes 786440 | tf_op jit(solution)/shard_map/ppermute | solution.py:509
  32.9 33.6 %all-to-all-start = ((bf16[32,32,512]{2,1,0:T(8,128)(2,1)}), bf16[32,32,512]{2,1,0:T(8,128)(2,1)S(1)}, u32[]{:S(2)}, u32[]{:S(2)}) async-start(bf16[32,32,512]{2,1,0:T(8,128)(2,1)} %bitcast.29), calls=%async_computation | async-start | bytes 2097152 | tf_op jit(solution)/shard_map/all_to_all | solution.py:569
  46.5 6.0 %collective-permute-start.7 = (bf16[128,512]{1,0:T(8,128)(2,1)S(1)}, bf16[128,512]{1,0:T(8,128)(2,1)S(1)}, u32[]{:S(2)}, u32[]{:S(2)}) collective-permute-start(bf16[128,512]{1,0:T(8,128)(2,1)S(1)} %get-tuple-element.57), channel_id=1, source_target_pairs={{0,1},{1,0},{2,3},{3,2},{4,5},{5,4},{6,7},{7,6},{8,9},{9,8},{10,11... | collective-permute-start | bytes 393224 | tf_op jit(solution)/shard_map/ppermute | solution.py:509
  46.6 5.9 %collective-permute-start.6 = (f32[128,32]{1,0:T(8,128)S(1)}, f32[128,32]{1,0:T(8,128)S(1)}, u32[]{:S(2)}, u32[]{:S(2)}) collective-permute-start(f32[128,32]{1,0:T(8,128)S(1)} %get-tuple-element.48), channel_id=1, source_target_pairs={{0,4},{4,0},{8,12},{12,8},{16,20},{20,16},{24,28},{28,24},{1,5},{5... | collective-permute-start | bytes 49160 | tf_op jit(solution)/shard_map/ppermute | solution.py:580
  48.5 9.4 %collective-permute-start.8 = (bf16[128,512]{1,0:T(8,128)(2,1)S(1)}, bf16[128,512]{1,0:T(8,128)(2,1)S(1)}, u32[]{:S(2)}, u32[]{:S(2)}) collective-permute-start(bf16[128,512]{1,0:T(8,128)(2,1)S(1)} %get-tuple-element.58), channel_id=1, source_target_pairs={{0,2},{1,3},{2,0},{3,1},{4,6},{5,7},{6,4},{7,5},{8,10},{9,11},{10,... | collective-permute-start | bytes 393224 | tf_op jit(solution)/shard_map/ppermute | solution.py:509
  50.2 12.0 %collective-permute-start.9 = (bf16[128,512]{1,0:T(8,128)(2,1)S(1)}, bf16[128,512]{1,0:T(8,128)(2,1)S(1)}, u32[]{:S(2)}, u32[]{:S(2)}) collective-permute-start(bf16[128,512]{1,0:T(8,128)(2,1)S(1)} %get-tuple-element.56), channel_id=1, source_target_pairs={{0,3},{1,2},{2,1},{3,0},{4,7},{5,6},{6,5},{7,4},{8,11},{9,10},{10,... | collective-permute-start | bytes 393224 | tf_op jit(solution)/shard_map/ppermute | solution.py:509
  52.6 11.1 %collective-permute-start.10 = (f32[32,32]{1,0:T(8,128)S(1)}, f32[32,32]{1,0:T(8,128)S(1)}, u32[]{:S(2)}, u32[]{:S(2)}) collective-permute-start(f32[32,32]{1,0:T(8,128)S(1)} %get-tuple-element.72), channel_id=1, source_target_pairs={{0,0},{1,16},{2,8},{3,24},{4,4},{5,20},{6,12},{7,28},{8,1},{9,17},... | collective-permute-start | bytes 12296 | tf_op jit(solution)/shard_map/ppermute | solution.py:592
  53.2 10.4 %collective-permute-start.11 = (f32[32,32]{1,0:T(8,128)S(1)}, f32[32,32]{1,0:T(8,128)S(1)}, u32[]{:S(2)}, u32[]{:S(2)}) collective-permute-start(f32[32,32]{1,0:T(8,128)S(1)} %get-tuple-element.75), channel_id=1, source_target_pairs={{0,1},{1,17},{2,9},{3,25},{4,5},{5,21},{6,13},{7,29},{8,0},{9,16},... | collective-permute-start | bytes 12296 | tf_op jit(solution)/shard_map/ppermute | solution.py:592
  57.6 7.6 %collective-permute-start.12 = (f32[32,32]{1,0:T(8,128)S(1)}, f32[32,32]{1,0:T(8,128)S(1)}, u32[]{:S(2)}, u32[]{:S(2)}) collective-permute-start(f32[32,32]{1,0:T(8,128)S(1)} %get-tuple-element.74), channel_id=1, source_target_pairs={{0,2},{1,18},{2,10},{3,26},{4,6},{5,22},{6,14},{7,30},{8,3},{9,19}... | collective-permute-start | bytes 12296 | tf_op jit(solution)/shard_map/ppermute | solution.py:592
  57.9 8.0 %collective-permute-start.13 = (f32[32,32]{1,0:T(8,128)S(1)}, f32[32,32]{1,0:T(8,128)S(1)}, u32[]{:S(2)}, u32[]{:S(2)}) collective-permute-start(f32[32,32]{1,0:T(8,128)S(1)} %get-tuple-element.73), channel_id=1, source_target_pairs={{0,3},{1,19},{2,11},{3,27},{4,7},{5,23},{6,15},{7,31},{8,2},{9,18}... | collective-permute-start | bytes 12296 | tf_op jit(solution)/shard_map/ppermute | solution.py:592

commit v4 on v3

--- a/solution.py
+++ b/solution.py
@@ -13,7 +13,6 @@
 RIM = KERNEL // 2
 SUB = 8
 CHUNK = 6
-META_LENGTHS = 3
 SWAP = (0, 2, 1, 3)
 
 
@@ -182,11 +181,16 @@
     return lax.dot_general(left, right, (((0,), (0,)), ((), ())), preferred_element_type=jnp.float32)
 
 
-def utt_index(meta_ref, frame_pos):
+def device_group():
+    own_index = lax.axis_index("ctx")
+    return 2 * (own_index & 1) + (own_index >> 1)
+
+
+def utt_index(len_ref, frame_pos):
     end = jnp.int32(0)
     counted = jnp.zeros(frame_pos.shape, jnp.int32)
-    for utt in range(META_LENGTHS, meta_ref.shape[0]):
-        end = end + meta_ref[utt]
+    for utt in range(len_ref.shape[1]):
+        end = end + len_ref[0, utt]
         counted = counted + (frame_pos >= end).astype(jnp.int32)
     return counted
 
@@ -196,9 +200,9 @@
     return ((own_index ^ (row >> shift)) << shift) + (row & (row_count - 1))
 
 
-def spaced_pos(meta_ref, row, own_index, row_count):
+def spaced_pos(len_ref, row, own_index, row_count):
     frame_pos = frame_at(row, own_index, row_count)
-    return frame_pos + RIM * utt_index(meta_ref, frame_pos)
+    return frame_pos + RIM * utt_index(len_ref, frame_pos)
 
 
 def spaced_steps(seq_total, utt_count):
@@ -206,18 +210,18 @@
     return -(-rows // (SUB * CHUNK)) * CHUNK
 
 
-def spread_matrix(meta_ref, own_index, row_count, seq_total, steps):
+def spread_matrix(len_ref, own_index, row_count, seq_total, steps):
     slot = lax.broadcasted_iota(jnp.int32, (steps * SUB, seq_total), 0)
     slot_pos = (slot & (SUB - 1)) * steps + (slot >> 3)
     row = lax.broadcasted_iota(jnp.int32, (1, seq_total), 1)
-    return (slot_pos == spaced_pos(meta_ref, row, own_index, row_count)).astype(jnp.float32).astype(jnp.bfloat16)
-
-
-def gather_matrix(meta_ref, own_index, row_count, seq_total, steps):
+    return (slot_pos == spaced_pos(len_ref, row, own_index, row_count)).astype(jnp.float32).astype(jnp.bfloat16)
+
+
+def gather_matrix(len_ref, own_index, row_count, seq_total, steps):
     slot = lax.broadcasted_iota(jnp.int32, (1, steps * SUB), 1)
     slot_pos = (slot & (SUB - 1)) * steps + (slot >> 3)
     row = lax.broadcasted_iota(jnp.int32, (seq_total, 1), 0)
-    return (slot_pos == spaced_pos(meta_ref, row, own_index, row_count)).astype(jnp.float32).astype(jnp.bfloat16)
+    return (slot_pos == spaced_pos(len_ref, row, own_index, row_count)).astype(jnp.float32).astype(jnp.bfloat16)
 
 
 def write_extended(ext_ref, spaced, steps):
@@ -229,13 +233,13 @@
     ext_ref[RIM + steps :] = jnp.where(sub == SUB - 1, 0.0, pltpu.roll(blocks[:RIM], SUB - 1, 1))
 
 
-def conv_loop(ext_ref, taps_ref, lanes, tap_lanes, steps, flipped, finish):
+def conv_loop(ext_ref, taps_ref, lanes, steps, flipped, finish):
     def body(chunk, carry):
         start = chunk * CHUNK
         window = [ext_ref[start + m, :, lanes] for m in range(CHUNK + KERNEL - 1)]
         sums = [None] * CHUNK
         for tap in range(KERNEL):
-            weight = taps_ref[tap, :, tap_lanes]
+            weight = taps_ref[tap, :, lanes]
             shift = KERNEL - 1 - tap if flipped else tap
             for a in range(CHUNK):
                 term = window[a + shift] * weight
@@ -247,39 +251,103 @@
     lax.fori_loop(0, steps // CHUNK, body, 0)
 
 
-def forward_conv_kernel(
-    meta_ref, f0, f1, f2, f3, w_ref, hid_ref, ext_hbm, conv_ref, ext_ref, oth_ref, taps_ref, hid_sp_ref, sem
+def pack_kernel(rows_hbm, grads_hbm, *refs):
+    outs, sems = refs[:8], refs[8]
+    group = device_group()
+    width = outs[0].shape[1]
+    loads = []
+    for j in range(4):
+        own = pl.multiple_of((group ^ SWAP[j]) * width, width)
+        other = pl.multiple_of((group ^ SWAP[j] ^ 1) * width, width)
+        pieces = (
+            (rows_hbm, own, outs[j]),
+            (rows_hbm, other, outs[4 + j].at[:, :width]),
+            (grads_hbm, own, outs[4 + j].at[:, width:]),
+        )
+        for source, start, target in pieces:
+            loads.append(pltpu.make_async_copy(source.at[:, pl.ds(start, width)], target, sems.at[len(loads)]))
+            loads[-1].start()
+    for load in loads:
+        load.wait()
+
+
+def setup_kernel(
+    len_hbm, w_hbm, spread_ref, gather_ref, bias_ref, taps_own_ref, taps_oth_ref, len_ref, w_own_ref, w_oth_ref, sems
 ):
-    own_index = meta_ref[0]
-    row_count = f1.shape[0]
-    width = ext_ref.shape[2]
-    seq_total = 4 * row_count
-    steps = conv_ref.shape[0]
-    spread = spread_matrix(meta_ref, own_index, row_count, seq_total, steps)
-    halves = (slice(0, width), slice(width, 2 * width))
-    for lanes, ref in zip(halves, (ext_ref, oth_ref), strict=True):
-        rows = jnp.concatenate([f0[:, lanes], f1[:, lanes], f2[:, lanes], f3[:, lanes]], axis=0)
-        write_extended(ref, jnp.dot(spread, rows, preferred_element_type=jnp.float32), steps)
-    save = pltpu.make_async_copy(ext_ref, ext_hbm, sem)
-    save.start()
-    for tap in range(KERNEL):
-        taps_ref[tap] = jnp.broadcast_to(w_ref[tap : tap + 1, :], (SUB, 2 * width))
-    for part, ref in enumerate((ext_ref, oth_ref)):
-        for lane in range(0, width, 128):
-            lanes = slice(lane, lane + 128)
-            outer = slice(part * width + lane, part * width + lane + 128)
-
-            def finish(step, conv, center, part=part, lanes=lanes, outer=outer):
-                half = 0.5 * conv
-                hid_sp_ref[step, :, outer] = center + (half + half * jnp.tanh(half))
-                if part == 0:
-                    conv_ref[step, :, lanes] = conv
-
-            conv_loop(ref, taps_ref, lanes, outer, steps, False, finish)
-    hid_low = hid_sp_ref[...].reshape(steps * SUB, 2 * width).astype(jnp.bfloat16)
-    gather = gather_matrix(meta_ref, own_index, row_count, seq_total, steps)
-    hid_ref[...] = jnp.dot(gather, hid_low, preferred_element_type=jnp.float32).astype(jnp.bfloat16)
-    save.wait()
+    own_index, group = lax.axis_index("ctx"), device_group()
+    slots, seq_total = spread_ref.shape
+    row_count, steps = seq_total // 4, slots // SUB
+    width = w_own_ref.shape[1]
+    loads = [pltpu.make_async_copy(len_hbm, len_ref, sems.at[0])]
+    for part, ref in enumerate((w_own_ref, w_oth_ref)):
+        start = pl.multiple_of((group ^ part) * width, width)
+        loads.append(pltpu.make_async_copy(w_hbm.at[:, pl.ds(start, width)], ref, sems.at[1 + part]))
+    for load in loads:
+        load.start()
+    loads[0].wait()
+    spread_ref[...] = spread_matrix(len_ref, own_index, row_count, seq_total, steps)
+    gather_ref[...] = gather_matrix(len_ref, own_index, row_count, seq_total, steps)
+    key_row = lax.broadcasted_iota(jnp.int32, (seq_total, 1), 0)
+    query_row = lax.broadcasted_iota(jnp.int32, (1, seq_total), 1)
+    key_utt = utt_index(len_ref, frame_at(key_row, own_index, row_count))
+    query_utt = utt_index(len_ref, frame_at(query_row, own_index, row_count))
+    bias_ref[...] = jnp.where(key_utt == query_utt, 0.0, -jnp.inf).astype(jnp.float32)
+    for load in loads[1:]:
+        load.wait()
+    for taps_ref, w_ref in ((taps_own_ref, w_own_ref), (taps_oth_ref, w_oth_ref)):
+        for tap in range(KERNEL):
+            taps_ref[tap] = jnp.broadcast_to(w_ref[tap : tap + 1, :], taps_ref.shape[1:])
+
+
+def forward_conv(f0, f1, f2, f3, spread_ref, gather_ref, taps_ref, hid_ref, ext_ref, hid_sp_ref, conv_ref, saves):
+    width = hid_ref.shape[1]
+    steps = hid_sp_ref.shape[0]
+    rows = jnp.concatenate([f[:, :width] for f in (f0, f1, f2, f3)], axis=0)
+    write_extended(ext_ref, jnp.dot(spread_ref[...], rows, preferred_element_type=jnp.float32), steps)
+    if saves is not None:
+        saves[0].start()
+    for lane in range(0, width, 128):
+        lanes = slice(lane, lane + 128)
+
+        def finish(step, conv, center, lanes=lanes):
+            half = 0.5 * conv
+            hid_sp_ref[step, :, lanes] = center + (half + half * jnp.tanh(half))
+            if conv_ref is not None:
+                conv_ref[step, :, lanes] = conv
+
+        conv_loop(ext_ref, taps_ref, lanes, steps, False, finish)
+    if saves is not None:
+        saves[1].start()
+    hid_low = hid_sp_ref[...].reshape(steps * SUB, width).astype(jnp.bfloat16)
+    hid_ref[...] = jnp.dot(gather_ref[...], hid_low, preferred_element_type=jnp.float32).astype(jnp.bfloat16)
+
+
+def own_conv_kernel(
+    f0, f1, f2, f3, spread_ref, gather_ref, taps_ref, hid_ref, ext_hbm, conv_hbm, ext_ref, conv_ref, hid_sp_ref, sems
+):
+    saves = [
+        pltpu.make_async_copy(ext_ref, ext_hbm, sems.at[0]),
+        pltpu.make_async_copy(conv_ref, conv_hbm, sems.at[1]),
+    ]
+    forward_conv(f0, f1, f2, f3, spread_ref, gather_ref, taps_ref, hid_ref, ext_ref, hid_sp_ref, conv_ref, saves)
+    for save in saves:
+        save.wait()
+
+
+def other_conv_kernel(
+    f0, f1, f2, f3, spread_ref, gather_ref, taps_ref, w_hbm, hid_ref, wk_ref, wv_ref, ext_ref, hid_sp_ref, sems
+):
+    width = hid_ref.shape[1]
+    own = pl.multiple_of(device_group() * width, width)
+    loads = [
+        pltpu.make_async_copy(w_hbm.at[:, pl.ds(own, width)], wk_ref, sems.at[0]),
+        pltpu.make_async_copy(w_hbm.at[:, pl.ds(4 * width + own, width)], wv_ref, sems.at[1]),
+    ]
+    for load in loads:
+        load.start()
+    forward_conv(f0, f1, f2, f3, spread_ref, gather_ref, taps_ref, hid_ref, ext_ref, hid_sp_ref, None, None)
+    for load in loads:
+        load.wait()
 
 
 def swapped(array, order, row_count):
@@ -287,25 +355,21 @@
 
 
 def attention_kernel(
-    meta_ref, hid_ref, sib_ref, f0, f1, f2, f3, wk_ref, wv_ref, out_ref, keep_ref, send_ref, kvg_ref,
-    k_ref, v_ref, kt_ref, vt_ref, cot_ref, cott_ref, attt_ref, dqt_ref, dk_ref, dv_ref, bias_ref,
+    hid_ref, oth_ref, sib_ref, sib_oth_ref, f0, f1, f2, f3, wk_ref, wv_ref, bias_ref,
+    out_ref, keep_ref, send_ref, kvg_ref, k_ref, v_ref, kt_ref, vt_ref, cot_ref, cott_ref, attt_ref, dqt_ref,
+    dk_ref, dv_ref,
 ):
-    own_index, group = meta_ref[0], meta_ref[1]
+    group = device_group()
     row_count = f0.shape[0]
     seq_total, width = out_ref.shape
     head_width = 64
     scale = 1.0 / math.sqrt(head_width)
     bf16, f32 = jnp.bfloat16, jnp.float32
-    key_row = lax.broadcasted_iota(jnp.int32, (seq_total, 1), 0)
-    query_row = lax.broadcasted_iota(jnp.int32, (1, seq_total), 1)
-    key_utt = utt_index(meta_ref, frame_at(key_row, own_index, row_count))
-    query_utt = utt_index(meta_ref, frame_at(query_row, own_index, row_count))
-    bias_ref[...] = jnp.where(key_utt == query_utt, 0.0, -jnp.inf).astype(f32)
     parts = [
-        hid_ref[:, :width],
-        hid_ref[:, width:],
-        swapped(sib_ref[:, :width], (1, 0, 3, 2), row_count),
-        swapped(sib_ref[:, width:], (1, 0, 3, 2), row_count),
+        hid_ref[...],
+        oth_ref[...],
+        swapped(sib_ref[...], (1, 0, 3, 2), row_count),
+        swapped(sib_oth_ref[...], (1, 0, 3, 2), row_count),
     ]
 
     def w_rows(ref, j):
@@ -317,7 +381,7 @@
     v_ref[...] = values
     kt_ref[...] = keys.T
     vt_ref[...] = values.T
-    tail = slice(2 * width, 3 * width)
+    tail = slice(width, 2 * width)
     cot = jnp.concatenate([f0[:, tail], f1[:, tail], f2[:, tail], f3[:, tail]], axis=0)
     cot_ref[...] = cot
     cott_ref[...] = cot.T.astype(f32)
@@ -367,16 +431,16 @@
     keep_ref[:, width:] = partial(1)
 
 
-def weight_grad_kernel(meta_ref, hid_ref, sib_ref, kvg_ref, out_hbm, all_ref, sems):
-    group = meta_ref[1]
-    width = hid_ref.shape[1] // 2
+def weight_grad_kernel(hid_ref, oth_ref, sib_ref, sib_oth_ref, kvg_ref, out_hbm, all_ref, sems):
+    group = device_group()
+    width = hid_ref.shape[1]
     row_count = hid_ref.shape[0] // 4
     kvg = kvg_ref[...]
     parts = [
-        hid_ref[:, :width],
-        hid_ref[:, width:],
-        swapped(sib_ref[:, :width], (1, 0, 3, 2), row_count),
-        swapped(sib_ref[:, width:], (1, 0, 3, 2), row_count),
+        hid_ref[...],
+        oth_ref[...],
+        swapped(sib_ref[...], (1, 0, 3, 2), row_count),
+        swapped(sib_oth_ref[...], (1, 0, 3, 2), row_count),
     ]
     saves = []
     for j in range(4):
@@ -397,27 +461,35 @@
 
 
 def tap_grad_kernel(
-    meta_ref, own_ref, recv_ref, xext_hbm, conv_ref, dh_ref, ext_ref, dw_keep_ref, dw_send_ref, xext_ref, gdw_ref, sem
+    own_ref, recv_ref, xext_hbm, conv_hbm, len_hbm, dh_ref, ext_ref, dw_keep_ref, dw_send_ref,
+    xext_ref, conv_ref, len_ref, gdw_ref, sems,
 ):
-    own_index, dp_index = meta_ref[0], meta_ref[2]
+    own_index, dp_index = lax.axis_index("ctx"), lax.axis_index("dp")
     seq_total, width = own_ref.shape
     row_count = seq_total // 4
     steps = conv_ref.shape[0]
     bf16, f32 = jnp.bfloat16, jnp.float32
-    load = pltpu.make_async_copy(xext_hbm, xext_ref, sem)
-    load.start()
+    loads = [
+        pltpu.make_async_copy(len_hbm, len_ref, sems.at[0]),
+        pltpu.make_async_copy(conv_hbm, conv_ref, sems.at[1]),
+        pltpu.make_async_copy(xext_hbm, xext_ref, sems.at[2]),
+    ]
+    for load in loads:
+        load.start()
     dhidden = own_ref[...] + swapped(recv_ref[...], (2, 3, 0, 1), row_count).astype(f32)
     high = dhidden.astype(bf16)
     low = (dhidden - high.astype(f32)).astype(bf16)
-    spread = spread_matrix(meta_ref, own_index, row_count, seq_total, steps)
+    loads[0].wait()
+    spread = spread_matrix(len_ref, own_index, row_count, seq_total, steps)
     both = jnp.dot(spread, jnp.concatenate([high, low], axis=1), preferred_element_type=f32)
     spaced = both[:, :width] + both[:, width:]
     dh_ref[...] = spaced.reshape(steps, SUB, width)
+    loads[1].wait()
     conv = conv_ref[...].reshape(steps * SUB, width)
     gate = 0.5 + 0.5 * jnp.tanh(0.5 * conv)
     dconv = (spaced * (gate * (1.0 + conv * (1.0 - gate)))).astype(bf16).astype(f32)
     write_extended(ext_ref, dconv, steps)
-    load.wait()
+    loads[2].wait()
     half_taps = (KERNEL + 1) // 2
     for lane in range(0, width, 128):
         lanes = slice(lane, lane + 128)
@@ -444,26 +516,22 @@
     dw_send_ref[...] = gdw_ref[:, pl.ds(pl.multiple_of((1 - side) * half, half), half)].T
 
 
-def frame_grad_kernel(meta_ref, dh_ref, ext_ref, w_ref, dframes_ref, taps_ref, df_ref):
-    own_index = meta_ref[0]
-    seq_total, width = dframes_ref.shape
+def frame_grad_kernel(dh_ref, ext_ref, taps_ref, gather_ref, dframes_ref, df_ref):
+    width = dframes_ref.shape[1]
     steps = dh_ref.shape[0]
-    for tap in range(KERNEL):
-        taps_ref[tap] = jnp.broadcast_to(w_ref[tap : tap + 1, :width], (SUB, width))
     for lane in range(0, width, 128):
         lanes = slice(lane, lane + 128)
 
         def finish(step, conv, center, lanes=lanes):
             df_ref[step, :, lanes] = dh_ref[step, :, lanes] + conv
 
-        conv_loop(ext_ref, taps_ref, lanes, lanes, steps, True, finish)
-    gather = gather_matrix(meta_ref, own_index, seq_total // 4, seq_total, steps)
+        conv_loop(ext_ref, taps_ref, lanes, steps, True, finish)
     df_low = df_ref[...].reshape(steps * SUB, width).astype(jnp.bfloat16)
-    dframes_ref[...] = jnp.dot(gather, df_low, preferred_element_type=jnp.float32).astype(jnp.bfloat16)
-
-
-def place_kernel(meta_ref, own_ref, r1, r2, r3, out_ref, dframes_ref):
-    group = meta_ref[1]
+    dframes_ref[...] = jnp.dot(gather_ref[...], df_low, preferred_element_type=jnp.float32).astype(jnp.bfloat16)
+
+
+def place_kernel(own_ref, r1, r2, r3, out_ref, dframes_ref):
+    group = device_group()
     row_count = out_ref.shape[0]
     width = own_ref.shape[1] // 2
     for j, ref in enumerate((own_ref, r1, r2, r3)):
@@ -485,24 +553,18 @@
         out_ref[:, full + start : full + start + width] = total[:, width:]
 
 
-def call(kernel, scalars, args, outs, scratch=(), hbm_in=(), hbm_out=(), to_hbm=False, vmem_mib=16, cost_us=2):
+def call(kernel, args, outs, scratch=(), hbm_in=(), hbm_out=(), to_hbm=False, vmem_mib=8, cost_us=2):
     vmem, hbm = pl.BlockSpec(memory_space=pltpu.VMEM), pl.BlockSpec(memory_space=pltpu.HBM)
     colours = [pltpu.HBM if i in hbm_out else pltpu.VMEM for i in range(len(outs))]
     return pl.pallas_call(
         kernel,
         out_shape=[jax.ShapeDtypeStruct(*o) if to_hbm else c(*o) for c, o in zip(colours, outs, strict=True)],
-        grid_spec=pltpu.PrefetchScalarGridSpec(
-            num_scalar_prefetch=len(scalars),
-            in_specs=[hbm if i in hbm_in else vmem for i in range(len(args))],
-            out_specs=[hbm if i in hbm_out else vmem for i in range(len(outs))],
-            scratch_shapes=list(scratch),
-        ),
+        in_specs=[hbm if i in hbm_in else vmem for i in range(len(args))],
+        out_specs=[hbm if i in hbm_out else vmem for i in range(len(outs))],
+        scratch_shapes=list(scratch),
         compiler_params=pltpu.CompilerParams(vmem_limit_bytes=vmem_mib * 1024 * 1024),
         cost_estimate=pl.CostEstimate(flops=cost_us * 10**9, bytes_accessed=cost_us * 3 * 10**6, transcendentals=0),
-    )(
-        *scalars,
-        *(pltpu.with_memory_space_constraint(a, pltpu.HBM if i in hbm_in else pltpu.VMEM) for i, a in enumerate(args)),
-    )
+    )(*(pltpu.with_memory_space_constraint(a, pltpu.HBM if i in hbm_in else pltpu.VMEM) for i, a in enumerate(args)))
 
 
 def swap_ctx(array, j):
@@ -515,67 +577,82 @@
     seq_total = 4 * row_count
     steps = spaced_steps(seq_total, utt_lengths.shape[1])
     bf16, f32 = jnp.bfloat16, jnp.float32
-    ctx_index, dp_index = lax.axis_index("ctx"), lax.axis_index("dp")
+    dp_index = lax.axis_index("dp")
     dp_size = lax.axis_size("dp")
-    group = 2 * (ctx_index & 1) + (ctx_index >> 1)
-    meta = jnp.concatenate([jnp.stack([ctx_index, group, dp_index]).astype(jnp.int32), utt_lengths[0]])
-
     rows, grads = frames[0], cotangent[0]
 
-    def columns(array, owner):
-        return lax.dynamic_slice_in_dim(array, owner * width, width, axis=1)
-
-    def parcel(owner):
-        return jnp.concatenate([columns(rows, owner), columns(rows, owner ^ 1), columns(grads, owner)], axis=1)
-
-    blocks = [parcel(group)] + [swap_ctx(parcel(group ^ SWAP[j]), j) for j in (1, 2, 3)]
-    w_taps = jnp.concatenate([columns(w_dw, group), columns(w_dw, group ^ 1)], axis=1)
-    w_keys, w_values = columns(w_kv, group), columns(w_kv, group + 4)
-    blocks, w_keys, w_values = lax.optimization_barrier((blocks, w_keys, w_values))
+    packed = call(
+        pack_kernel, (rows, grads),
+        [((row_count, width), bf16)] * 4 + [((row_count, 2 * width), bf16)] * 4,
+        [pltpu.SemaphoreType.DMA((12,))], hbm_in=(0, 1), cost_us=1,
+    )
+    own_blocks = [packed[0]] + [swap_ctx(packed[j], j) for j in (1, 2, 3)]
+    parcels, own_blocks[1] = lax.optimization_barrier((packed[4:], own_blocks[1]))
+    blocks = [parcels[0]] + [swap_ctx(parcels[j], j) for j in (1, 2, 3)]
     wide = (seq_total, width)
     both = (seq_total, 2 * width)
     tall = wide[::-1]
     long = (steps + 2 * RIM, SUB, width)
     short = (steps, SUB, width)
+    taps = (KERNEL, SUB, width)
+    slots = steps * SUB
+    spread, gather, bias, taps_own, taps_oth = call(
+        setup_kernel, (utt_lengths, w_dw),
+        [
+            ((slots, seq_total), bf16), ((seq_total, slots), bf16), ((seq_total, seq_total), f32), (taps, f32),
+            (taps, f32),
+        ],
+        [
+            pltpu.SMEM(utt_lengths.shape, jnp.int32), pltpu.VMEM((KERNEL, width), f32), pltpu.VMEM((KERNEL, width), f32),
+            pltpu.SemaphoreType.DMA((3,)),
+        ],
+        hbm_in=(0, 1), cost_us=2,
+    )
     hidden, frames_ext, conv_own = call(
-        forward_conv_kernel, (meta,), (*blocks, w_taps), [(both, bf16), (long, f32), (short, f32)],
-        [
-            pltpu.VMEM(long, f32), pltpu.VMEM(long, f32), pltpu.VMEM((KERNEL, SUB, 2 * width), f32),
-            pltpu.VMEM((steps, SUB, 2 * width), f32), pltpu.SemaphoreType.DMA,
-        ],
-        hbm_out=(1,), cost_us=6,
+        own_conv_kernel, (*own_blocks, spread, gather, taps_own), [(wide, bf16), (long, f32), (short, f32)],
+        [pltpu.VMEM(long, f32), pltpu.VMEM(short, f32), pltpu.VMEM(short, f32), pltpu.SemaphoreType.DMA((2,))],
+        hbm_out=(1, 2), cost_us=20,
     )
     hidden_sib = swap_ctx(hidden, 1)
+    hidden_oth, w_keys, w_values = call(
+        other_conv_kernel, (*blocks, spread, gather, taps_oth, w_kv),
+        [(wide, bf16), ((feat_width, width), bf16), ((feat_width, width), bf16)],
+        [pltpu.VMEM(long, f32), pltpu.VMEM(short, f32), pltpu.SemaphoreType.DMA((2,))], hbm_in=(7,), cost_us=4,
+    )
+    hidden_sib_oth = swap_ctx(hidden_oth, 1)
+    hiddens = (hidden, hidden_oth, hidden_sib, hidden_sib_oth)
     out_own, keep, send, kv_grad = call(
-        attention_kernel, (meta,), (hidden, hidden_sib, *blocks, w_keys, w_values),
+        attention_kernel, (*hiddens, *blocks, w_keys, w_values, bias),
         [(wide, bf16), (both, f32), (both, bf16), (both, bf16)],
         [
             pltpu.VMEM(wide, bf16), pltpu.VMEM(wide, bf16), pltpu.VMEM(tall, bf16), pltpu.VMEM(tall, bf16),
             pltpu.VMEM(wide, bf16), pltpu.VMEM(tall, f32), pltpu.VMEM(tall, f32),
             pltpu.VMEM(tall, f32), pltpu.VMEM(wide, f32), pltpu.VMEM(wide, f32),
-            pltpu.VMEM((seq_total, seq_total), f32),
         ],
-        vmem_mib=20, cost_us=8,
+        vmem_mib=14, cost_us=8,
     )
     (part_kv,) = call(
-        weight_grad_kernel, (meta,), (hidden, hidden_sib, kv_grad), [((feat_width, 2 * width), bf16)],
+        weight_grad_kernel, (*hiddens, kv_grad), [((feat_width, 2 * width), bf16)],
         [pltpu.VMEM((4, width, 2 * width), bf16), pltpu.SemaphoreType.DMA((4,))], hbm_out=(0,), cost_us=2,
     )
     piece = feat_width // (4 * dp_size)
     from_sib = swap_ctx(send, 1)
-    part_own, part_send = call(chip_sum_kernel, (), (keep, from_sib), [(wide, f32), (wide, bf16)], cost_us=1)
+    part_own, part_send = call(chip_sum_kernel, (keep, from_sib), [(wide, f32), (wide, bf16)], cost_us=1)
     part_send, part_kv = lax.optimization_barrier((part_send, part_kv))
     from_chip = swap_ctx(part_send, 2)
     all_kv = lax.all_to_all(part_kv.reshape(4 * dp_size, piece, 2 * width), ("dp", "ctx"), 0, 0)
     dhidden, dconv_ext, dw_keep, dw_send = call(
-        tap_grad_kernel, (meta,), (part_own, from_chip, frames_ext, conv_own),
+        tap_grad_kernel, (part_own, from_chip, frames_ext, conv_own, utt_lengths),
         [(short, f32), (long, f32), ((width // 2, KERNEL + 1), f32), ((width // 2, KERNEL + 1), f32)],
-        [pltpu.VMEM(long, f32), pltpu.VMEM((KERNEL + 1, width), f32), pltpu.SemaphoreType.DMA],
-        hbm_in=(2,), cost_us=100,
+        [
+            pltpu.VMEM(long, f32), pltpu.VMEM(short, f32), pltpu.SMEM(utt_lengths.shape, jnp.int32),
+            pltpu.VMEM((KERNEL + 1, width), f32), pltpu.SemaphoreType.DMA((3,)),
+        ],
+        hbm_in=(2, 3, 4), cost_us=100,
     )
     (dframes,) = call(
-        frame_grad_kernel, (meta,), (dhidden, dconv_ext, w_taps), [(wide, bf16)],
-        [pltpu.VMEM((KERNEL, SUB, width), f32), pltpu.VMEM(short, f32)], cost_us=20,
+        frame_grad_kernel, (dhidden, dconv_ext, taps_own, gather), [(wide, bf16)], [pltpu.VMEM(short, f32)],
+        cost_us=20,
     )
     dw_half = dw_keep + lax.ppermute(dw_send, "dp", [(i, i ^ 1) for i in range(dp_size)])
     results = jnp.concatenate([out_own, dframes], axis=1)
@@ -593,10 +670,10 @@
         grad_dw = arrived if turn == 0 else grad_dw + arrived
     grad_dw = grad_dw[:, :KERNEL]
     output, dframes_rows = call(
-        place_kernel, (meta,), tuple(result_blocks), [((row_count, feat_width), bf16)] * 2, to_hbm=True, cost_us=1
+        place_kernel, tuple(result_blocks), [((row_count, feat_width), bf16)] * 2, to_hbm=True, cost_us=1
     )
     (grad_kv,) = call(
-        place_grad_kernel, (), (all_kv,), [((piece, 2 * feat_width), f32)], to_hbm=True, cost_us=1
+        place_grad_kernel, (all_kv,), [((piece, 2 * feat_width), f32)], to_hbm=True, cost_us=1
     )
     return (output[None], dframes_rows[None], grad_kv, grad_dw)
 

time: 68.1 us -> 64 us (0.940)
  local copies, waits for them, and re-layouts: 3.3 us -> 0.02 us
  waiting for transfers between devices: 14.3 us -> 11.4 us
  starting transfers between devices: 24.1 us -> 26.1 us
  Pallas kernels: 23.3 us -> 24.2 us
  other arithmetic: 1.48 us -> 0.68 us
    ppermute x9 -> x13, waiting for transfers between devices: 9.8 us -> 5.73 us  [swap_ctx(): return lax.ppermute(array, 'ctx', [(i, i ^ j) for i in range(4)])]
    dynamic_slice x3 -> x0, local copies, waits for them, and re-layouts: 3.28 us -> none  [columns(): return lax.dynamic_slice_in_dim(array, owner * width, width, axis=1)]
    ppermute x9 -> x13, starting transfers between devices: 7.68 us -> 10 us  [swap_ctx(): return lax.ppermute(array, 'ctx', [(i, i ^ j) for i in range(4)])]
    pallas_call x8 -> x11, Pallas kernels: 23.3 us -> 24.2 us  [call(): pl.pallas_call(kernel, out_shape=[jax.ShapeDtypeStruct(*o) if to_hbm else...]
    concatenate x5 -> x0, other arithmetic: 0.8 us -> none  [the longest x1 0.73 us: on_device_pairs(): jnp.concatenate([jnp.stack([ctx_index, group, dp_index]).astype(jnp.int32...]
    ppermute x4, waiting for transfers between devices: 2.23 us -> 2.99 us  [on_device_pairs(): arrived = lax.ppermute(quarter, ('dp', 'ctx'), pairs)]
  transfers between devices with their start and end apart: 15 -> 19, of which waited for: 7 -> 8; matrix products, arithmetic and copies ran while one was open for 5% -> 1% of each run, Pallas kernels for 15% -> 25%
where the time goes in v4:
time: 64 us; the launch traced here: 63.2 us
  starting transfers between devices  26.1 us (41%)
  Pallas kernels  24.2 us (38%)
  waiting for transfers between devices  11.4 us (18%)
  between operations  0.81 us (1%)
  other arithmetic  0.68 us (1%)
    pallas_call x11, Pallas kernels, call(): pl.pallas_call(kernel, out_shape=[jax.ShapeDtypeStruct(*o) if to_hbm else...  24.2 us
    ppermute x13, starting transfers between devices, swap_ctx(): return lax.ppermute(array, 'ctx', [(i, i ^ j) for i in range(4)])  10 us
    ppermute x4, starting transfers between devices, on_device_pairs(): arrived = lax.ppermute(quarter, ('dp', 'ctx'), pairs)  9.33 us
    ppermute x13, waiting for transfers between devices, swap_ctx(): return lax.ppermute(array, 'ctx', [(i, i ^ j) for i in range(4)])  5.73 us
    all_to_all x1, starting transfers between devices, on_device_pairs(): lax.all_to_all(part_kv.reshape(4 * dp_size, piece, 2 * width), ('dp', 'ct...  4.9 us
    ppermute x4, waiting for transfers between devices, on_device_pairs(): arrived = lax.ppermute(quarter, ('dp', 'ctx'), pairs)  2.99 us
    ppermute x1, waiting for transfers between devices, on_device_pairs(): lax.ppermute(dw_send, 'dp', [(i, i ^ 1) for i in range(dp_size)])  2.7 us
    ppermute x1, starting transfers between devices, on_device_pairs(): lax.ppermute(dw_send, 'dp', [(i, i ^ 1) for i in range(dp_size)])  1.82 us
  transfers between devices with their start and end apart: 19, of which 8 were waited for; matrix products, arithmetic and copies ran while one was open for 1% of the time, Pallas kernels for 25%

profile of v4, /device:TPU:0, one launch (start us, length us, event | category | flops | bytes accessed | tf_op | source)
XLA Modules:
  0.0 63.2 jit_solution(1858873434166784352)
XLA Ops:
  0.6 1.3 %shard_map.84 = (bf16[128,256]{1,0:T(8,128)(2,1)S(1)}, bf16[128,256]{1,0:T(8,128)(2,1)S(1)}, bf16[128,256]{1,0:T(8,128)(2,1)S(1)}, bf16[128,256]{1,0:T(8,128)(2,...) custom-call(bf16[128,1024]{1,0:T(8,128)(2,1)} %bitcast.6, ...), custom_call_target="tpu_custom_call" | custom-call | flops 1000000000 | bytes 3000000 | tf_op jit(solution)/shard_map/pallas_call | solution.py:559
  2.4 2.6 %collective-permute-start.1 = (bf16[128,256]{1,0:T(8,128)(2,1)S(1)}, bf16[128,256]{1,0:T(8,128)(2,1)S(1)}, u32[]{:S(2)}, u32[]{:S(2)}) collective-permute-start(bf16[128,256]{1,0:T(8,128)(2,1)S(1)} %get-tuple-element.51), channel_id=1, source_target_pairs={{0,2},{1,3},{2,0},{3,1},{4,6},{5,7},{6,4},{7,5},{8,10},{9,11},{10,... | collective-permute-start | bytes 196616 | tf_op jit(solution)/shard_map/ppermute | solution.py:571
  5.1 1.5 %shard_map.85 = (bf16[624,512]{1,0:T(8,128)(2,1)S(1)}, bf16[512,624]{1,0:T(8,128)(2,1)S(1)}, f32[512,512]{1,0:T(8,128)S(1)}, f32[31,8,256]{2,1,0:T(8,128)S(1)}, f32[31,8,256]{2,1,0:T(8,128)S(1)}) custom-call(s32[1,8]{1,0:T(1,128)} %len_hbm.3, f32[31,1024]{1,0:T(8,128)} %w_hbm.2), custom_call_target="tpu_custom_call" | custom-call | flops 2000000000 | bytes 6000000 | tf_op jit(solution)/shard_map/pallas_call | solution.py:559
  6.8 1.9 %collective-permute-start.4 = (bf16[128,512]{1,0:T(8,128)(2,1)S(1)}, bf16[128,512]{1,0:T(8,128)(2,1)S(1)}, u32[]{:S(2)}, u32[]{:S(2)}) collective-permute-start(bf16[128,512]{1,0:T(8,128)(2,1)S(1)} %get-tuple-element.59), channel_id=1, source_target_pairs={{0,2},{1,3},{2,0},{3,1},{4,6},{5,7},{6,4},{7,5},{8,10},{9,11},{10,... | collective-permute-start | bytes 393224 | tf_op jit(solution)/shard_map/ppermute | solution.py:571
  9.1 3.2 %shard_map.86 = (bf16[512,256]{1,0:T(8,128)(2,1)S(1)}, f32[108,8,256]{2,1,0:T(8,128)}, f32[78,8,256]{2,1,0:T(8,128)}) custom-call(bf16[128,256]{1,0:T(8,128)(2,1)S(1)} %get-tuple-element.44.f0, bf16[128,256]{1,0:T(8,128)(2,1)S(1)} %collective-permute-done.f1, bf16[128,256]{1,0:T(8,128)(2,1)S(1)} %collective-permute-done.1.f2, ...), custom_call_target="tpu_custom_call" | custom-call | flops 20000000000 | bytes 60000000 | tf_op jit(solution)/shard_map/pallas_call | solution.py:559
  13.2 1.7 %collective-permute-done.5.f3 = bf16[128,512]{1,0:T(8,128)(2,1)S(1)} collective-permute-done((bf16[128,512]{1,0:T(8,128)(2,1)S(1)}, bf16[128,512]{1,0:T(8,128)(2,1)S(1)}, u32[]{:S(2)}, u32[]{:S(2)}) %collective-permute-start.5) | collective-permute-done | bytes 131104 | tf_op jit(solution)/shard_map/ppermute | solution.py:571
  14.9 2.9 %shard_map.87 = (bf16[512,256]{1,0:T(8,128)(2,1)S(1)}, bf16[1024,256]{1,0:T(8,128)(2,1)S(1)}, bf16[1024,256]{1,0:T(8,128)(2,1)S(1)}) custom-call(bf16[128,512]{1,0:T(8,128)(2,1)S(1)} %get-tuple-element.57.f0, bf16[128,512]{1,0:T(8,128)(2,1)S(1)} %collective-permute-done.3.f1, bf16[128,512]{1,0:T(8,128)(2,1)S(1)} %collective-permute-done.4.f2, ...), custom_call_target="tpu_custom_call" | custom-call | flops 4000000000 | bytes 12000000 | tf_op jit(solution)/shard_map/pallas_call | solution.py:559
  18.3 1.2 %collective-permute-done.7.sib_oth_ref = bf16[512,256]{1,0:T(8,128)(2,1)S(1)} collective-permute-done((bf16[512,256]{1,0:T(8,128)(2,1)S(1)}, bf16[512,256]{1,0:T(8,128)(2,1)S(1)}, u32[]{:S(2)}, u32[]{:S(2)}) %collective-permute-start.7) | collective-permute-done | bytes 262176 | tf_op jit(solution)/shard_map/ppermute | solution.py:571
  19.4 6.0 %shard_map.88 = (bf16[512,256]{1,0:T(8,128)(2,1)S(1)}, f32[512,512]{1,0:T(8,128)S(1)}, bf16[512,512]{1,0:T(8,128)(2,1)S(1)}, bf16[512,512]{1,0:T(8,128)(2,1)S(1)}) custom-call(bf16[512,256]{1,0:T(8,128)(2,1)S(1)} %get-tuple-element.56.hid_ref, bf16[512,256]{1,0:T(8,128)(2,1)S(1)} %get-tuple-element.62.oth_ref, ...), custom_call_target="tpu_custom_call" | custom-call | flops 8000000000 | bytes 24000000 | tf_op jit(solution)/shard_map/pallas_call | solution.py:559
  25.9 1.5 %shard_map.90 = bf16[1024,512]{1,0:T(8,128)(2,1)} custom-call(bf16[512,256]{1,0:T(8,128)(2,1)S(1)} %get-tuple-element.56.hid_ref, bf16[512,256]{1,0:T(8,128)(2,1)S(1)} %get-tuple-element.62.oth_ref, bf16[512,256]{1,0:T(8,128)(2,1)S(1)} %collective-permute-done.6.sib_ref, bf16[512,256]{1,0:T(8,128)(2,1)S(1)} %collective-permute-done.7.sib_oth_ref, ...), custom_call_target="tpu_custom_call" | custom-call | flops 2000000000 | bytes 6000000 | tf_op jit(solution)/shard_map/pallas_call | solution.py:559
  27.5 1.8 %collective-permute-start.9 = (bf16[512,256]{1,0:T(8,128)(2,1)S(1)}, bf16[512,256]{1,0:T(8,128)(2,1)S(1)}, u32[]{:S(2)}, u32[]{:S(2)}) collective-permute-start(bf16[512,256]{1,0:T(8,128)(2,1)S(1)} %get-tuple-element.72), channel_id=1, source_target_pairs={{0,2},{1,3},{2,0},{3,1},{4,6},{5,7},{6,4},{7,5},{8,10},{9,11},{10,... | collective-permute-start | bytes 786440 | tf_op jit(solution)/shard_map/ppermute | solution.py:571
  29.3 4.9 %all-to-all-start = ((bf16[32,32,512]{2,1,0:T(8,128)(2,1)}), bf16[32,32,512]{2,1,0:T(8,128)(2,1)S(1)}, u32[]{:S(2)}, u32[]{:S(2)}) async-start(bf16[32,32,512]{2,1,0:T(8,128)(2,1)} %bitcast.5), calls=%async_computation | async-start | bytes 2097152 | tf_op jit(solution)/shard_map/all_to_all | solution.py:643
  34.2 1.9 %collective-permute-done.9.recv_ref = bf16[512,256]{1,0:T(8,128)(2,1)S(1)} collective-permute-done((bf16[512,256]{1,0:T(8,128)(2,1)S(1)}, bf16[512,256]{1,0:T(8,128)(2,1)S(1)}, u32[]{:S(2)}, u32[]{:S(2)}) %collective-permute-start.9) | collective-permute-done | bytes 262176 | tf_op jit(solution)/shard_map/ppermute | solution.py:571
  36.1 3.4 %shard_map.91 = (f32[78,8,256]{2,1,0:T(8,128)S(1)}, f32[108,8,256]{2,1,0:T(8,128)S(1)}, f32[128,32]{1,0:T(8,128)S(1)}, f32[128,32]{1,0:T(8,128)S(1)}) custom-call(f32[512,256]{1,0:T(8,128)S(1)} %get-tuple-element.69.own_ref, bf16[512,256]{1,0:T(8,128)(2,1)S(1)} %collective-permute-done.9.recv_ref, f32[108,8,256]{2,1,0:T(8,128)} %get-tuple-element.73.xext_hbm, ...), custom_call_target="tpu_custom_call" | custom-call | flops 99999997952 | bytes 300000000 | tf_op jit(solution)/shard_map/pallas_call | solution.py:559
  39.5 2.6 %shard_map.92 = bf16[512,256]{1,0:T(8,128)(2,1)S(1)} custom-call(f32[78,8,256]{2,1,0:T(8,128)S(1)} %get-tuple-element.75.dh_ref, f32[108,8,256]{2,1,0:T(8,128)S(1)} %get-tuple-element.76.ext_ref, f32[31,8,256]{2,1,0:T(8,128)S(1)} %get-tuple-element.55.taps_ref, bf16[512,624]{1,0:T(8,128)(2,1)S(1)} %get-tuple-element.54.gather_ref), custom_call_target="tpu_custom_call" | custom-call | flops 20000000000 | bytes 60000000 | tf_op jit(solution)/shard_map/pallas_call | solution.py:559
  42.3 1.8 %collective-permute-start.10 = (f32[128,32]{1,0:T(8,128)S(1)}, f32[128,32]{1,0:T(8,128)S(1)}, u32[]{:S(2)}, u32[]{:S(2)}) collective-permute-start(f32[128,32]{1,0:T(8,128)S(1)} %get-tuple-element.78), channel_id=1, source_target_pairs={{0,4},{4,0},{8,12},{12,8},{16,20},{20,16},{24,28},{28,24},{1,5},{5... | collective-permute-start | bytes 49160 | tf_op jit(solution)/shard_map/ppermute | solution.py:657
  44.1 1.7 %collective-permute-start.12 = (bf16[128,512]{1,0:T(8,128)(2,1)S(1)}, bf16[128,512]{1,0:T(8,128)(2,1)S(1)}, u32[]{:S(2)}, u32[]{:S(2)}) collective-permute-start(bf16[128,512]{1,0:T(8,128)(2,1)S(1)} %get-tuple-element.86), channel_id=1, source_target_pairs={{0,2},{1,3},{2,0},{3,1},{4,6},{5,7},{6,4},{7,5},{8,10},{9,11},{10,... | collective-permute-start | bytes 393224 | tf_op jit(solution)/shard_map/ppermute | solution.py:571
  45.9 2.7 %collective-permute-done.10 = f32[128,32]{1,0:T(8,128)S(1)} collective-permute-done((f32[128,32]{1,0:T(8,128)S(1)}, f32[128,32]{1,0:T(8,128)S(1)}, u32[]{:S(2)}, u32[]{:S(2)}) %collective-permute-start.10) | collective-permute-done | bytes 16416 | tf_op jit(solution)/shard_map/ppermute | solution.py:657
  49.3 3.4 %collective-permute-start.15 = (f32[32,32]{1,0:T(8,128)S(1)}, f32[32,32]{1,0:T(8,128)S(1)}, u32[]{:S(2)}, u32[]{:S(2)}) collective-permute-start(f32[32,32]{1,0:T(8,128)S(1)} %get-tuple-element.90), channel_id=1, source_target_pairs={{0,1},{1,17},{2,9},{3,25},{4,5},{5,21},{6,13},{7,29},{8,0},{9,16},... | collective-permute-start | bytes 12296 | tf_op jit(solution)/shard_map/ppermute | solution.py:669
  52.6 0.8 %collective-permute-start.16 = (f32[32,32]{1,0:T(8,128)S(1)}, f32[32,32]{1,0:T(8,128)S(1)}, u32[]{:S(2)}, u32[]{:S(2)}) collective-permute-start(f32[32,32]{1,0:T(8,128)S(1)} %get-tuple-element.89), channel_id=1, source_target_pairs={{0,2},{1,18},{2,10},{3,26},{4,6},{5,22},{6,14},{7,30},{8,3},{9,19}... | collective-permute-start | bytes 12296 | tf_op jit(solution)/shard_map/ppermute | solution.py:669
  53.5 4.5 %collective-permute-start.17 = (f32[32,32]{1,0:T(8,128)S(1)}, f32[32,32]{1,0:T(8,128)S(1)}, u32[]{:S(2)}, u32[]{:S(2)}) collective-permute-start(f32[32,32]{1,0:T(8,128)S(1)} %get-tuple-element.88), channel_id=1, source_target_pairs={{0,3},{1,19},{2,11},{3,27},{4,7},{5,23},{6,15},{7,31},{8,2},{9,18}... | collective-permute-start | bytes 12296 | tf_op jit(solution)/shard_map/ppermute | solution.py:669
  58.0 0.8 %shard_map.93 = (bf16[128,1024]{1,0:T(8,128)(2,1)}, bf16[128,1024]{1,0:T(8,128)(2,1)}) custom-call(bf16[512,512]{1,0:T(8,128)(2,1)S(1)} %pad_maximum_fusion.own_ref, bf16[128,512]{1,0:T(8,128)(2,1)S(1)} %collective-permute-done.11.r1, bf16[128,512]{1,0:T(8,128)(2,1)S(1)} %collective-permute-done.12.r2, bf16[128,512]{1,0:T(8,128)(2,1)S(1)} %collective-permute-done.13.r3), custom_call_target="tpu_custom_call" | custom-call | flops 1000000000 | bytes 3000000 | tf_op jit(solution)/shard_map/pallas_call | solution.py:559
  58.8 2.8 %collective-permute-done.16 = f32[32,32]{1,0:T(8,128)S(1)} collective-permute-done((f32[32,32]{1,0:T(8,128)S(1)}, f32[32,32]{1,0:T(8,128)S(1)}, u32[]{:S(2)}, u32[]{:S(2)}) %collective-permute-start.16) | collective-permute-done | bytes 4128 | tf_op jit(solution)/shard_map/ppermute | solution.py:669
  62.4 0.8 %shard_map.94 = f32[32,2048]{1,0:T(8,128)} custom-call(bf16[32,32,512]{2,1,0:T(8,128)(2,1)S(1)} %all-to-all-done.blocks_ref), custom_call_target="tpu_custom_call" | custom-call | flops 1000000000 | bytes 3000000 | tf_op jit(solution)/shard_map/pallas_call | solution.py:559
  (30 shorter events, 4.6 us)
Async XLA Ops:
  1.9 4.7 %collective-permute-start = (bf16[128,256]{1,0:T(8,128)(2,1)S(1)}, bf16[128,256]{1,0:T(8,128)(2,1)S(1)}, u32[]{:S(2)}, u32[]{:S(2)}) collective-permute-start(bf16[128,256]{1,0:T(8,128)(2,1)S(1)} %get-tuple-element.49), channel_id=1, source_target_pairs={{0,1},{1,0},{2,3},{3,2},{4,5},{5,4},{6,7},{7,6},{8,9},{9,8},{10,11... | collective-permute-start | bytes 196616 | tf_op jit(solution)/shard_map/ppermute | solution.py:571
  2.4 6.3 %collective-permute-start.1 = (bf16[128,256]{1,0:T(8,128)(2,1)S(1)}, bf16[128,256]{1,0:T(8,128)(2,1)S(1)}, u32[]{:S(2)}, u32[]{:S(2)}) collective-permute-start(bf16[128,256]{1,0:T(8,128)(2,1)S(1)} %get-tuple-element.51), channel_id=1, source_target_pairs={{0,2},{1,3},{2,0},{3,1},{4,6},{5,7},{6,4},{7,5},{8,10},{9,11},{10,... | collective-permute-start | bytes 196616 | tf_op jit(solution)/shard_map/ppermute | solution.py:571
  5.0 4.0 %collective-permute-start.2 = (bf16[128,256]{1,0:T(8,128)(2,1)S(1)}, bf16[128,256]{1,0:T(8,128)(2,1)S(1)}, u32[]{:S(2)}, u32[]{:S(2)}) collective-permute-start(bf16[128,256]{1,0:T(8,128)(2,1)S(1)} %get-tuple-element.52), channel_id=1, source_target_pairs={{0,3},{1,2},{2,1},{3,0},{4,7},{5,6},{6,5},{7,4},{8,11},{9,10},{10,... | collective-permute-start | bytes 196616 | tf_op jit(solution)/shard_map/ppermute | solution.py:571
  6.6 5.9 %collective-permute-start.3 = (bf16[128,512]{1,0:T(8,128)(2,1)S(1)}, bf16[128,512]{1,0:T(8,128)(2,1)S(1)}, u32[]{:S(2)}, u32[]{:S(2)}) collective-permute-start(bf16[128,512]{1,0:T(8,128)(2,1)S(1)} %get-tuple-element.58), channel_id=1, source_target_pairs={{0,1},{1,0},{2,3},{3,2},{4,5},{5,4},{6,7},{7,6},{8,9},{9,8},{10,11... | collective-permute-start | bytes 393224 | tf_op jit(solution)/shard_map/ppermute | solution.py:571
  6.8 6.3 %collective-permute-start.4 = (bf16[128,512]{1,0:T(8,128)(2,1)S(1)}, bf16[128,512]{1,0:T(8,128)(2,1)S(1)}, u32[]{:S(2)}, u32[]{:S(2)}) collective-permute-start(bf16[128,512]{1,0:T(8,128)(2,1)S(1)} %get-tuple-element.59), channel_id=1, source_target_pairs={{0,2},{1,3},{2,0},{3,1},{4,6},{5,7},{6,4},{7,5},{8,10},{9,11},{10,... | collective-permute-start | bytes 393224 | tf_op jit(solution)/shard_map/ppermute | solution.py:571
  8.8 6.1 %collective-permute-start.5 = (bf16[128,512]{1,0:T(8,128)(2,1)S(1)}, bf16[128,512]{1,0:T(8,128)(2,1)S(1)}, u32[]{:S(2)}, u32[]{:S(2)}) collective-permute-start(bf16[128,512]{1,0:T(8,128)(2,1)S(1)} %get-tuple-element.60), channel_id=1, source_target_pairs={{0,3},{1,2},{2,1},{3,0},{4,7},{5,6},{6,5},{7,4},{8,11},{9,10},{10,... | collective-permute-start | bytes 393224 | tf_op jit(solution)/shard_map/ppermute | solution.py:571
  12.3 6.0 %collective-permute-start.6 = (bf16[512,256]{1,0:T(8,128)(2,1)S(1)}, bf16[512,256]{1,0:T(8,128)(2,1)S(1)}, u32[]{:S(2)}, u32[]{:S(2)}) collective-permute-start(bf16[512,256]{1,0:T(8,128)(2,1)S(1)} %get-tuple-element.56.hid_ref), channel_id=1, source_target_pairs={{0,1},{1,0},{2,3},{3,2},{4,5},{5,4},{6,7},{7,6},{8,9},{9,8},{10,11... | collective-permute-start | bytes 786440 | tf_op jit(solution)/shard_map/ppermute | solution.py:571
  17.8 1.6 %collective-permute-start.7 = (bf16[512,256]{1,0:T(8,128)(2,1)S(1)}, bf16[512,256]{1,0:T(8,128)(2,1)S(1)}, u32[]{:S(2)}, u32[]{:S(2)}) collective-permute-start(bf16[512,256]{1,0:T(8,128)(2,1)S(1)} %get-tuple-element.62.oth_ref), channel_id=1, source_target_pairs={{0,1},{1,0},{2,3},{3,2},{4,5},{5,4},{6,7},{7,6},{8,9},{9,8},{10,11... | collective-permute-start | bytes 786440 | tf_op jit(solution)/shard_map/ppermute | solution.py:571
  25.4 2.0 %collective-permute-start.8 = (bf16[512,512]{1,0:T(8,128)(2,1)S(1)}, bf16[512,512]{1,0:T(8,128)(2,1)S(1)}, u32[]{:S(2)}, u32[]{:S(2)}) collective-permute-start(bf16[512,512]{1,0:T(8,128)(2,1)S(1)} %get-tuple-element.68), channel_id=1, source_target_pairs={{0,1},{1,0},{2,3},{3,2},{4,5},{5,4},{6,7},{7,6},{8,9},{9,8},{10,11... | collective-permute-start | bytes 1572872 | tf_op jit(solution)/shard_map/ppermute | solution.py:571
  27.5 8.7 %collective-permute-start.9 = (bf16[512,256]{1,0:T(8,128)(2,1)S(1)}, bf16[512,256]{1,0:T(8,128)(2,1)S(1)}, u32[]{:S(2)}, u32[]{:S(2)}) collective-permute-start(bf16[512,256]{1,0:T(8,128)(2,1)S(1)} %get-tuple-element.72), channel_id=1, source_target_pairs={{0,2},{1,3},{2,0},{3,1},{4,6},{5,7},{6,4},{7,5},{8,10},{9,11},{10,... | collective-permute-start | bytes 786440 | tf_op jit(solution)/shard_map/ppermute | solution.py:571
  29.3 33.1 %all-to-all-start = ((bf16[32,32,512]{2,1,0:T(8,128)(2,1)}), bf16[32,32,512]{2,1,0:T(8,128)(2,1)S(1)}, u32[]{:S(2)}, u32[]{:S(2)}) async-start(bf16[32,32,512]{2,1,0:T(8,128)(2,1)} %bitcast.5), calls=%async_computation | async-start | bytes 2097152 | tf_op jit(solution)/shard_map/all_to_all | solution.py:643
  42.2 6.4 %collective-permute-start.11 = (bf16[128,512]{1,0:T(8,128)(2,1)S(1)}, bf16[128,512]{1,0:T(8,128)(2,1)S(1)}, u32[]{:S(2)}, u32[]{:S(2)}) collective-permute-start(bf16[128,512]{1,0:T(8,128)(2,1)S(1)} %get-tuple-element.85), channel_id=1, source_target_pairs={{0,1},{1,0},{2,3},{3,2},{4,5},{5,4},{6,7},{7,6},{8,9},{9,8},{10,11... | collective-permute-start | bytes 393224 | tf_op jit(solution)/shard_map/ppermute | solution.py:571
  42.3 6.3 %collective-permute-start.10 = (f32[128,32]{1,0:T(8,128)S(1)}, f32[128,32]{1,0:T(8,128)S(1)}, u32[]{:S(2)}, u32[]{:S(2)}) collective-permute-start(f32[128,32]{1,0:T(8,128)S(1)} %get-tuple-element.78), channel_id=1, source_target_pairs={{0,4},{4,0},{8,12},{12,8},{16,20},{20,16},{24,28},{28,24},{1,5},{5... | collective-permute-start | bytes 49160 | tf_op jit(solution)/shard_map/ppermute | solution.py:657
  44.1 9.4 %collective-permute-start.12 = (bf16[128,512]{1,0:T(8,128)(2,1)S(1)}, bf16[128,512]{1,0:T(8,128)(2,1)S(1)}, u32[]{:S(2)}, u32[]{:S(2)}) collective-permute-start(bf16[128,512]{1,0:T(8,128)(2,1)S(1)} %get-tuple-element.86), channel_id=1, source_target_pairs={{0,2},{1,3},{2,0},{3,1},{4,6},{5,7},{6,4},{7,5},{8,10},{9,11},{10,... | collective-permute-start | bytes 393224 | tf_op jit(solution)/shard_map/ppermute | solution.py:571
  45.8 12.2 %collective-permute-start.13 = (bf16[128,512]{1,0:T(8,128)(2,1)S(1)}, bf16[128,512]{1,0:T(8,128)(2,1)S(1)}, u32[]{:S(2)}, u32[]{:S(2)}) collective-permute-start(bf16[128,512]{1,0:T(8,128)(2,1)S(1)} %get-tuple-element.84), channel_id=1, source_target_pairs={{0,3},{1,2},{2,1},{3,0},{4,7},{5,6},{6,5},{7,4},{8,11},{9,10},{10,... | collective-permute-start | bytes 393224 | tf_op jit(solution)/shard_map/ppermute | solution.py:571
  48.6 10.2 %collective-permute-start.14 = (f32[32,32]{1,0:T(8,128)S(1)}, f32[32,32]{1,0:T(8,128)S(1)}, u32[]{:S(2)}, u32[]{:S(2)}) collective-permute-start(f32[32,32]{1,0:T(8,128)S(1)} %get-tuple-element.87), channel_id=1, source_target_pairs={{0,0},{1,16},{2,8},{3,24},{4,4},{5,20},{6,12},{7,28},{8,1},{9,17},... | collective-permute-start | bytes 12296 | tf_op jit(solution)/shard_map/ppermute | solution.py:669
  49.3 9.5 %collective-permute-start.15 = (f32[32,32]{1,0:T(8,128)S(1)}, f32[32,32]{1,0:T(8,128)S(1)}, u32[]{:S(2)}, u32[]{:S(2)}) collective-permute-start(f32[32,32]{1,0:T(8,128)S(1)} %get-tuple-element.90), channel_id=1, source_target_pairs={{0,1},{1,17},{2,9},{3,25},{4,5},{5,21},{6,13},{7,29},{8,0},{9,16},... | collective-permute-start | bytes 12296 | tf_op jit(solution)/shard_map/ppermute | solution.py:669
  52.6 9.0 %collective-permute-start.16 = (f32[32,32]{1,0:T(8,128)S(1)}, f32[32,32]{1,0:T(8,128)S(1)}, u32[]{:S(2)}, u32[]{:S(2)}) collective-permute-start(f32[32,32]{1,0:T(8,128)S(1)} %get-tuple-element.89), channel_id=1, source_target_pairs={{0,2},{1,18},{2,10},{3,26},{4,6},{5,22},{6,14},{7,30},{8,3},{9,19}... | collective-permute-start | bytes 12296 | tf_op jit(solution)/shard_map/ppermute | solution.py:669
  53.5 8.3 %collective-permute-start.17 = (f32[32,32]{1,0:T(8,128)S(1)}, f32[32,32]{1,0:T(8,128)S(1)}, u32[]{:S(2)}, u32[]{:S(2)}) collective-permute-start(f32[32,32]{1,0:T(8,128)S(1)} %get-tuple-element.88), channel_id=1, source_target_pairs={{0,3},{1,19},{2,11},{3,27},{4,7},{5,23},{6,15},{7,31},{8,2},{9,18}... | collective-permute-start | bytes 12296 | tf_op jit(solution)/shard_map/ppermute | solution.py:669

commit v5 on v4

--- a/solution.py
+++ b/solution.py
@@ -251,28 +251,22 @@
     lax.fori_loop(0, steps // CHUNK, body, 0)
 
 
-def pack_kernel(rows_hbm, grads_hbm, *refs):
-    outs, sems = refs[:8], refs[8]
+def pack_kernel(rows_hbm, *refs):
+    outs, sems = refs[:4], refs[4]
     group = device_group()
     width = outs[0].shape[1]
     loads = []
     for j in range(4):
         own = pl.multiple_of((group ^ SWAP[j]) * width, width)
-        other = pl.multiple_of((group ^ SWAP[j] ^ 1) * width, width)
-        pieces = (
-            (rows_hbm, own, outs[j]),
-            (rows_hbm, other, outs[4 + j].at[:, :width]),
-            (grads_hbm, own, outs[4 + j].at[:, width:]),
-        )
-        for source, start, target in pieces:
-            loads.append(pltpu.make_async_copy(source.at[:, pl.ds(start, width)], target, sems.at[len(loads)]))
-            loads[-1].start()
+        loads.append(pltpu.make_async_copy(rows_hbm.at[:, pl.ds(own, width)], outs[j], sems.at[j]))
+        loads[-1].start()
     for load in loads:
         load.wait()
 
 
 def setup_kernel(
-    len_hbm, w_hbm, spread_ref, gather_ref, bias_ref, taps_own_ref, taps_oth_ref, len_ref, w_own_ref, w_oth_ref, sems
+    len_hbm, w_hbm, rows_hbm, grads_hbm, spread_ref, gather_ref, taps_own_ref, taps_oth_ref, p0, p1, p2, p3,
+    len_ref, w_own_ref, w_oth_ref, sems,
 ):
     own_index, group = lax.axis_index("ctx"), device_group()
     slots, seq_total = spread_ref.shape
@@ -282,16 +276,17 @@
     for part, ref in enumerate((w_own_ref, w_oth_ref)):
         start = pl.multiple_of((group ^ part) * width, width)
         loads.append(pltpu.make_async_copy(w_hbm.at[:, pl.ds(start, width)], ref, sems.at[1 + part]))
+    for j, parcel in enumerate((p0, p1, p2, p3)):
+        own = pl.multiple_of((group ^ SWAP[j]) * width, width)
+        other = pl.multiple_of((group ^ SWAP[j] ^ 1) * width, width)
+        for part, (source, start) in enumerate(((rows_hbm, other), (grads_hbm, own))):
+            target = parcel.at[:, part * width : (part + 1) * width]
+            loads.append(pltpu.make_async_copy(source.at[:, pl.ds(start, width)], target, sems.at[len(loads)]))
     for load in loads:
         load.start()
     loads[0].wait()
     spread_ref[...] = spread_matrix(len_ref, own_index, row_count, seq_total, steps)
     gather_ref[...] = gather_matrix(len_ref, own_index, row_count, seq_total, steps)
-    key_row = lax.broadcasted_iota(jnp.int32, (seq_total, 1), 0)
-    query_row = lax.broadcasted_iota(jnp.int32, (1, seq_total), 1)
-    key_utt = utt_index(len_ref, frame_at(key_row, own_index, row_count))
-    query_utt = utt_index(len_ref, frame_at(query_row, own_index, row_count))
-    bias_ref[...] = jnp.where(key_utt == query_utt, 0.0, -jnp.inf).astype(jnp.float32)
     for load in loads[1:]:
         load.wait()
     for taps_ref, w_ref in ((taps_own_ref, w_own_ref), (taps_oth_ref, w_oth_ref)):
@@ -354,37 +349,51 @@
     return jnp.concatenate([array[b * row_count : (b + 1) * row_count] for b in order], axis=0)
 
 
+def w_rows(ref, group, j):
+    width = ref.shape[1]
+    return ref[pl.ds(pl.multiple_of((group ^ j) * width, width), width), :]
+
+
+def ready_kernel(
+    len_hbm, hid_ref, oth_ref, sib_ref, f0, f1, f2, f3, wk_ref, wv_ref, kv_ref, cot_ref, cott_ref, bias_ref, len_ref, sem
+):
+    own_index, group = lax.axis_index("ctx"), device_group()
+    seq_total, width = hid_ref.shape
+    row_count = seq_total // 4
+    load = pltpu.make_async_copy(len_hbm, len_ref, sem)
+    load.start()
+    parts = [hid_ref[...], oth_ref[...], swapped(sib_ref[...], (1, 0, 3, 2), row_count)]
+    for n, ref in enumerate((wk_ref, wv_ref)):
+        terms = [jnp.dot(part, w_rows(ref, group, j), preferred_element_type=jnp.float32) for j, part in enumerate(parts)]
+        kv_ref[:, n * width : (n + 1) * width] = sum(terms)
+    cot = jnp.concatenate([f[:, width:] for f in (f0, f1, f2, f3)], axis=0)
+    cot_ref[...] = cot
+    cott_ref[...] = cot.T.astype(jnp.float32)
+    load.wait()
+    key_row = lax.broadcasted_iota(jnp.int32, (seq_total, 1), 0)
+    query_row = lax.broadcasted_iota(jnp.int32, (1, seq_total), 1)
+    key_utt = utt_index(len_ref, frame_at(key_row, own_index, row_count))
+    query_utt = utt_index(len_ref, frame_at(query_row, own_index, row_count))
+    bias_ref[...] = jnp.where(key_utt == query_utt, 0.0, -jnp.inf).astype(jnp.float32)
+
+
 def attention_kernel(
-    hid_ref, oth_ref, sib_ref, sib_oth_ref, f0, f1, f2, f3, wk_ref, wv_ref, bias_ref,
-    out_ref, keep_ref, send_ref, kvg_ref, k_ref, v_ref, kt_ref, vt_ref, cot_ref, cott_ref, attt_ref, dqt_ref,
-    dk_ref, dv_ref,
+    hid_ref, sib_oth_ref, kv_ref, cot_ref, cott_ref, wk_ref, wv_ref, bias_ref,
+    out_ref, keep_ref, send_ref, kvg_ref, k_ref, v_ref, kt_ref, vt_ref, attt_ref, dqt_ref, dk_ref, dv_ref,
 ):
     group = device_group()
-    row_count = f0.shape[0]
     seq_total, width = out_ref.shape
     head_width = 64
     scale = 1.0 / math.sqrt(head_width)
     bf16, f32 = jnp.bfloat16, jnp.float32
-    parts = [
-        hid_ref[...],
-        oth_ref[...],
-        swapped(sib_ref[...], (1, 0, 3, 2), row_count),
-        swapped(sib_oth_ref[...], (1, 0, 3, 2), row_count),
-    ]
-
-    def w_rows(ref, j):
-        return ref[pl.ds(pl.multiple_of((group ^ j) * width, width), width), :]
-
-    keys = sum(jnp.dot(parts[j], w_rows(wk_ref, j), preferred_element_type=f32) for j in range(4)).astype(bf16)
-    values = sum(jnp.dot(parts[j], w_rows(wv_ref, j), preferred_element_type=f32) for j in range(4)).astype(bf16)
+    part = swapped(sib_oth_ref[...], (1, 0, 3, 2), seq_total // 4)
+    keys = kv_ref[:, :width] + jnp.dot(part, w_rows(wk_ref, group, 3), preferred_element_type=f32)
+    values = kv_ref[:, width:] + jnp.dot(part, w_rows(wv_ref, group, 3), preferred_element_type=f32)
+    keys, values = keys.astype(bf16), values.astype(bf16)
     k_ref[...] = keys
     v_ref[...] = values
     kt_ref[...] = keys.T
     vt_ref[...] = values.T
-    tail = slice(width, 2 * width)
-    cot = jnp.concatenate([f0[:, tail], f1[:, tail], f2[:, tail], f3[:, tail]], axis=0)
-    cot_ref[...] = cot
-    cott_ref[...] = cot.T.astype(f32)
     lane = lax.broadcasted_iota(jnp.int32, (1, 128), 1)
     masks = [(lane < head_width).astype(f32).astype(bf16), (lane >= head_width).astype(f32).astype(bf16)]
     exp_scale = scale * math.log2(math.e)
@@ -416,18 +425,18 @@
             dv_pair = dv_head if head == 0 else dv_pair + dv_head
         dk_ref[:, lanes] = dk_pair
         dv_ref[:, lanes] = dv_pair
-    out_ref[...] = (parts[0].astype(f32) + attt_ref[...].T).astype(bf16)
+    out_ref[...] = (hid_ref[...].astype(f32) + attt_ref[...].T).astype(bf16)
     grad_k = (dk_ref[...] * scale).astype(bf16)
     grad_v = dv_ref[...].astype(bf16)
     kvg_ref[:, :width] = grad_k
     kvg_ref[:, width:] = grad_v
 
     def partial(j):
-        return nt_dot(grad_k, w_rows(wk_ref, j)) + nt_dot(grad_v, w_rows(wv_ref, j))
+        return nt_dot(grad_k, w_rows(wk_ref, group, j)) + nt_dot(grad_v, w_rows(wv_ref, group, j))
 
     send_ref[:, :width] = partial(2).astype(bf16)
     send_ref[:, width:] = partial(3).astype(bf16)
-    keep_ref[:, :width] = partial(0) + dqt_ref[...].T + cot.astype(f32)
+    keep_ref[:, :width] = partial(0) + dqt_ref[...].T + cot_ref[...].astype(f32)
     keep_ref[:, width:] = partial(1)
 
 
@@ -540,7 +549,7 @@
         dframes_ref[:, pl.ds(start, width)] = ref[:row_count, width:]
 
 
-def place_grad_kernel(blocks_ref, out_ref):
+def place_grad_kernel(blocks_ref, q0, q1, q2, q3, out_ref, dw_ref):
     piece, wide = blocks_ref.shape[1:]
     width = wide // 2
     full = out_ref.shape[1] // 2
@@ -551,6 +560,7 @@
         start = SWAP[j] * width
         out_ref[:, start : start + width] = total[:, :width]
         out_ref[:, full + start : full + start + width] = total[:, width:]
+    dw_ref[...] = ((q0[...] + q1[...]) + (q2[...] + q3[...]))[:, :KERNEL]
 
 
 def call(kernel, args, outs, scratch=(), hbm_in=(), hbm_out=(), to_hbm=False, vmem_mib=8, cost_us=2):
@@ -582,13 +592,9 @@
     rows, grads = frames[0], cotangent[0]
 
     packed = call(
-        pack_kernel, (rows, grads),
-        [((row_count, width), bf16)] * 4 + [((row_count, 2 * width), bf16)] * 4,
-        [pltpu.SemaphoreType.DMA((12,))], hbm_in=(0, 1), cost_us=1,
+        pack_kernel, (rows,), [((row_count, width), bf16)] * 4, [pltpu.SemaphoreType.DMA((4,))], hbm_in=(0,), cost_us=1
     )
     own_blocks = [packed[0]] + [swap_ctx(packed[j], j) for j in (1, 2, 3)]
-    parcels, own_blocks[1] = lax.optimization_barrier((packed[4:], own_blocks[1]))
-    blocks = [parcels[0]] + [swap_ctx(parcels[j], j) for j in (1, 2, 3)]
     wide = (seq_total, width)
     both = (seq_total, 2 * width)
     tall = wide[::-1]
@@ -596,18 +602,20 @@
     short = (steps, SUB, width)
     taps = (KERNEL, SUB, width)
     slots = steps * SUB
-    spread, gather, bias, taps_own, taps_oth = call(
-        setup_kernel, (utt_lengths, w_dw),
+    late_rows, own_blocks[1] = lax.optimization_barrier((rows, own_blocks[1]))
+    spread, gather, taps_own, taps_oth, *parcels = call(
+        setup_kernel, (utt_lengths, w_dw, late_rows, grads),
         [
-            ((slots, seq_total), bf16), ((seq_total, slots), bf16), ((seq_total, seq_total), f32), (taps, f32),
-            (taps, f32),
+            ((slots, seq_total), bf16), ((seq_total, slots), bf16), (taps, f32), (taps, f32),
+            *[((row_count, 2 * width), bf16)] * 4,
         ],
         [
             pltpu.SMEM(utt_lengths.shape, jnp.int32), pltpu.VMEM((KERNEL, width), f32), pltpu.VMEM((KERNEL, width), f32),
-            pltpu.SemaphoreType.DMA((3,)),
+            pltpu.SemaphoreType.DMA((11,)),
         ],
-        hbm_in=(0, 1), cost_us=2,
-    )
+        hbm_in=(0, 1, 2, 3), cost_us=2,
+    )
+    blocks = [parcels[0]] + [swap_ctx(parcels[j], j) for j in (1, 2, 3)]
     hidden, frames_ext, conv_own = call(
         own_conv_kernel, (*own_blocks, spread, gather, taps_own), [(wide, bf16), (long, f32), (short, f32)],
         [pltpu.VMEM(long, f32), pltpu.VMEM(short, f32), pltpu.VMEM(short, f32), pltpu.SemaphoreType.DMA((2,))],
@@ -621,13 +629,17 @@
     )
     hidden_sib_oth = swap_ctx(hidden_oth, 1)
     hiddens = (hidden, hidden_oth, hidden_sib, hidden_sib_oth)
+    kv_part, cot_own, cot_turned, bias = call(
+        ready_kernel, (utt_lengths, *hiddens[:3], *blocks, w_keys, w_values),
+        [(both, f32), (wide, bf16), (tall, f32), ((seq_total, seq_total), f32)],
+        [pltpu.SMEM(utt_lengths.shape, jnp.int32), pltpu.SemaphoreType.DMA], hbm_in=(0,), cost_us=2,
+    )
     out_own, keep, send, kv_grad = call(
-        attention_kernel, (*hiddens, *blocks, w_keys, w_values, bias),
+        attention_kernel, (hidden, hidden_sib_oth, kv_part, cot_own, cot_turned, w_keys, w_values, bias),
         [(wide, bf16), (both, f32), (both, bf16), (both, bf16)],
         [
             pltpu.VMEM(wide, bf16), pltpu.VMEM(wide, bf16), pltpu.VMEM(tall, bf16), pltpu.VMEM(tall, bf16),
-            pltpu.VMEM(wide, bf16), pltpu.VMEM(tall, f32), pltpu.VMEM(tall, f32),
-            pltpu.VMEM(tall, f32), pltpu.VMEM(wide, f32), pltpu.VMEM(wide, f32),
+            pltpu.VMEM(tall, f32), pltpu.VMEM(tall, f32), pltpu.VMEM(wide, f32), pltpu.VMEM(wide, f32),
         ],
         vmem_mib=14, cost_us=8,
     )
@@ -654,11 +666,13 @@
         frame_grad_kernel, (dhidden, dconv_ext, taps_own, gather), [(wide, bf16)], [pltpu.VMEM(short, f32)],
         cost_us=20,
     )
-    dw_half = dw_keep + lax.ppermute(dw_send, "dp", [(i, i ^ 1) for i in range(dp_size)])
+    dw_recv = lax.ppermute(dw_send, "dp", [(i, i ^ 1) for i in range(dp_size)])
+    dw_recv, dframes = lax.optimization_barrier((dw_recv, dframes))
+    dw_half = dw_keep + dw_recv
     results = jnp.concatenate([out_own, dframes], axis=1)
     result_blocks = [results] + [swap_ctx(results[j * row_count : (j + 1) * row_count], j) for j in (1, 2, 3)]
     dw_half, result_blocks[1] = lax.optimization_barrier((dw_half, result_blocks[1]))
-    grad_dw = None
+    quarters = []
     for turn in range(4):
         pairs = []
         for d in range(dp_size):
@@ -666,14 +680,13 @@
                 target = 2 * (2 * (c & 1) + (c >> 1)) + (d & 1)
                 pairs.append((4 * d + c, 4 * target + ((d >> 1) ^ turn)))
         quarter = lax.dynamic_slice_in_dim(dw_half, ((dp_index >> 1) ^ turn) * piece, piece, axis=0)
-        arrived = lax.ppermute(quarter, ("dp", "ctx"), pairs)
-        grad_dw = arrived if turn == 0 else grad_dw + arrived
-    grad_dw = grad_dw[:, :KERNEL]
+        quarters.append(lax.ppermute(quarter, ("dp", "ctx"), pairs))
     output, dframes_rows = call(
         place_kernel, tuple(result_blocks), [((row_count, feat_width), bf16)] * 2, to_hbm=True, cost_us=1
     )
-    (grad_kv,) = call(
-        place_grad_kernel, (all_kv,), [((piece, 2 * feat_width), f32)], to_hbm=True, cost_us=1
+    grad_kv, grad_dw = call(
+        place_grad_kernel, (all_kv, *quarters), [((piece, 2 * feat_width), f32), ((piece, KERNEL), f32)],
+        to_hbm=True, cost_us=1,
     )
     return (output[None], dframes_rows[None], grad_kv, grad_dw)
 

time: 64 us -> 62 us (0.969)
  waiting for transfers between devices: 11.4 us -> 9.5 us
  starting transfers between devices: 26.1 us -> 27.1 us
  other arithmetic: 0.68 us -> 0.01 us
    ppermute x13, waiting for transfers between devices: 5.73 us -> 4.66 us  [swap_ctx(): return lax.ppermute(array, 'ctx', [(i, i ^ j) for i in range(4)])]
    ppermute x5, waiting for transfers between devices: 5.7 us -> 4.84 us  [the longest x4 3.63 us: on_device_pairs(): quarters.append(lax.ppermute(quarter, ('dp', 'ctx'), pairs))]
    ppermute x5, starting transfers between devices: 11.2 us -> 12 us  [the longest x4 10.2 us: on_device_pairs(): quarters.append(lax.ppermute(quarter, ('dp', 'ctx'), pairs))]
    pallas_call x11 -> x12, Pallas kernels: 24.2 us -> 24.1 us  [call(): pl.pallas_call(kernel, out_shape=[jax.ShapeDtypeStruct(*o) if to_hbm else...]
  transfers between devices with their start and end apart: 19 -> 19, of which waited for: 8 -> 7; matrix products, arithmetic and copies ran while one was open for 1% -> 0% of each run, Pallas kernels for 25% -> 27%
where the time goes in v5:
time: 62 us; the launch traced here: 61.6 us
  starting transfers between devices  27.1 us (44%)
  Pallas kernels  24.1 us (39%)
  waiting for transfers between devices  9.5 us (15%)
  between operations  0.8 us (1%)
    pallas_call x12, Pallas kernels, call(): pl.pallas_call(kernel, out_shape=[jax.ShapeDtypeStruct(*o) if to_hbm else...  24.1 us
    ppermute x4, starting transfers between devices, on_device_pairs(): quarters.append(lax.ppermute(quarter, ('dp', 'ctx'), pairs))  10.2 us
    ppermute x13, starting transfers between devices, swap_ctx(): return lax.ppermute(array, 'ctx', [(i, i ^ j) for i in range(4)])  10.1 us
    all_to_all x1, starting transfers between devices, on_device_pairs(): lax.all_to_all(part_kv.reshape(4 * dp_size, piece, 2 * width), ('dp', 'ct...  4.93 us
    ppermute x13, waiting for transfers between devices, swap_ctx(): return lax.ppermute(array, 'ctx', [(i, i ^ j) for i in range(4)])  4.66 us
    ppermute x4, waiting for transfers between devices, on_device_pairs(): quarters.append(lax.ppermute(quarter, ('dp', 'ctx'), pairs))  3.63 us
    ppermute x1, starting transfers between devices, on_device_pairs(): dw_recv = lax.ppermute(dw_send, 'dp', [(i, i ^ 1) for i in range(dp_size)])  1.82 us
  transfers between devices with their start and end apart: 19, of which 7 were waited for; matrix products, arithmetic and copies ran while one was open for 0% of the time, Pallas kernels for 27%

profile of v5, /device:TPU:0, one launch (start us, length us, event | category | flops | bytes accessed | tf_op | source)
XLA Modules:
  0.0 61.6 jit_solution(4071541730299478072)
XLA Ops:
  0.6 1.0 %shard_map.84 = (bf16[128,256]{1,0:T(8,128)(2,1)S(1)}, bf16[128,256]{1,0:T(8,128)(2,1)S(1)}, bf16[128,256]{1,0:T(8,128)(2,1)S(1)}, bf16[128,256]{1,0:T(8,128)(2,1)S(1)}) custom-call(bf16[128,1024]{1,0:T(8,128)(2,1)} %bitcast.6), custom_call_target="tpu_custom_call" | custom-call | flops 1000000000 | bytes 3000000 | tf_op jit(solution)/shard_map/pallas_call | solution.py:569
  2.1 2.6 %collective-permute-start.1 = (bf16[128,256]{1,0:T(8,128)(2,1)S(1)}, bf16[128,256]{1,0:T(8,128)(2,1)S(1)}, u32[]{:S(2)}, u32[]{:S(2)}) collective-permute-start(bf16[128,256]{1,0:T(8,128)(2,1)S(1)} %get-tuple-element.51), channel_id=1, source_target_pairs={{0,2},{1,3},{2,0},{3,1},{4,6},{5,7},{6,4},{7,5},{8,10},{9,11},{10,... | collective-permute-start | bytes 196616 | tf_op jit(solution)/shard_map/ppermute | solution.py:581
  4.8 1.4 %shard_map.85 = (bf16[624,512]{1,0:T(8,128)(2,1)S(1)}, bf16[512,624]{1,0:T(8,128)(2,1)S(1)}, f32[31,8,256]{2,1,0:T(8,128)S(1)}, f32[31,8,256]{2,1,0:T(8,128)S(1)...) custom-call(s32[1,8]{1,0:T(1,128)} %len_hbm.5, ...), custom_call_target="tpu_custom_call" | custom-call | flops 2000000000 | bytes 6000000 | tf_op jit(solution)/shard_map/pallas_call | solution.py:569
  6.4 1.9 %collective-permute-start.4 = (bf16[128,512]{1,0:T(8,128)(2,1)S(1)}, bf16[128,512]{1,0:T(8,128)(2,1)S(1)}, u32[]{:S(2)}, u32[]{:S(2)}) collective-permute-start(bf16[128,512]{1,0:T(8,128)(2,1)S(1)} %get-tuple-element.60), channel_id=1, source_target_pairs={{0,2},{1,3},{2,0},{3,1},{4,6},{5,7},{6,4},{7,5},{8,10},{9,11},{10,... | collective-permute-start | bytes 393224 | tf_op jit(solution)/shard_map/ppermute | solution.py:581
  8.8 3.3 %shard_map.86 = (bf16[512,256]{1,0:T(8,128)(2,1)S(1)}, f32[108,8,256]{2,1,0:T(8,128)}, f32[78,8,256]{2,1,0:T(8,128)}) custom-call(bf16[128,256]{1,0:T(8,128)(2,1)S(1)} %get-tuple-element.48.f0, bf16[128,256]{1,0:T(8,128)(2,1)S(1)} %collective-permute-done.f1, bf16[128,256]{1,0:T(8,128)(2,1)S(1)} %collective-permute-done.1.f2, ...), custom_call_target="tpu_custom_call" | custom-call | flops 20000000000 | bytes 60000000 | tf_op jit(solution)/shard_map/pallas_call | solution.py:569
  12.7 1.7 %collective-permute-done.5.f3 = bf16[128,512]{1,0:T(8,128)(2,1)S(1)} collective-permute-done((bf16[128,512]{1,0:T(8,128)(2,1)S(1)}, bf16[128,512]{1,0:T(8,128)(2,1)S(1)}, u32[]{:S(2)}, u32[]{:S(2)}) %collective-permute-start.5) | collective-permute-done | bytes 131104 | tf_op jit(solution)/shard_map/ppermute | solution.py:581
  14.4 2.8 %shard_map.87 = (bf16[512,256]{1,0:T(8,128)(2,1)S(1)}, bf16[1024,256]{1,0:T(8,128)(2,1)S(1)}, bf16[1024,256]{1,0:T(8,128)(2,1)S(1)}) custom-call(bf16[128,512]{1,0:T(8,128)(2,1)S(1)} %get-tuple-element.58.f0, bf16[128,512]{1,0:T(8,128)(2,1)S(1)} %collective-permute-done.3.f1, bf16[128,512]{1,0:T(8,128)(2,1)S(1)} %collective-permute-done.4.f2, ...), custom_call_target="tpu_custom_call" | custom-call | flops 4000000000 | bytes 12000000 | tf_op jit(solution)/shard_map/pallas_call | solution.py:569
  17.7 1.0 %shard_map.88 = (f32[512,512]{1,0:T(8,128)S(1)}, bf16[512,256]{1,0:T(8,128)(2,1)S(1)}, f32[256,512]{1,0:T(8,128)S(1)}, f32[512,512]{1,0:T(8,128)S(1)}) custom-call(s32[1,8]{1,0:T(1,128)} %len_hbm.5, bf16[512,256]{1,0:T(8,128)(2,1)S(1)} %get-tuple-element.57.hid_ref, bf16[512,256]{1,0:T(8,128)(2,1)S(1)} %get-tuple-element.63.oth_ref, ...), custom_call_target="tpu_custom_call" | custom-call | flops 2000000000 | bytes 6000000 | tf_op jit(solution)/shard_map/pallas_call | solution.py:569
  18.8 5.5 %shard_map.89 = (bf16[512,256]{1,0:T(8,128)(2,1)S(1)}, f32[512,512]{1,0:T(8,128)S(1)}, bf16[512,512]{1,0:T(8,128)(2,1)S(1)}, bf16[512,512]{1,0:T(8,128)(2,1)S(1)}) custom-call(bf16[512,256]{1,0:T(8,128)(2,1)S(1)} %get-tuple-element.57.hid_ref, bf16[512,256]{1,0:T(8,128)(2,1)S(1)} %collective-permute-done.6.sib_oth_ref, ...), custom_call_target="tpu_custom_call" | custom-call | flops 8000000000 | bytes 24000000 | tf_op jit(solution)/shard_map/pallas_call | solution.py:569
  24.8 1.5 %shard_map.91 = bf16[1024,512]{1,0:T(8,128)(2,1)} custom-call(bf16[512,256]{1,0:T(8,128)(2,1)S(1)} %get-tuple-element.57.hid_ref, bf16[512,256]{1,0:T(8,128)(2,1)S(1)} %get-tuple-element.63.oth_ref, bf16[512,256]{1,0:T(8,128)(2,1)S(1)} %collective-permute-done.7.sib_ref, bf16[512,256]{1,0:T(8,128)(2,1)S(1)} %collective-permute-done.6.sib_oth_ref, ...), custom_call_target="tpu_custom_call" | custom-call | flops 2000000000 | bytes 6000000 | tf_op jit(solution)/shard_map/pallas_call | solution.py:569
  26.4 1.8 %collective-permute-start.9 = (bf16[512,256]{1,0:T(8,128)(2,1)S(1)}, bf16[512,256]{1,0:T(8,128)(2,1)S(1)}, u32[]{:S(2)}, u32[]{:S(2)}) collective-permute-start(bf16[512,256]{1,0:T(8,128)(2,1)S(1)} %get-tuple-element.76), channel_id=1, source_target_pairs={{0,2},{1,3},{2,0},{3,1},{4,6},{5,7},{6,4},{7,5},{8,10},{9,11},{10,... | collective-permute-start | bytes 786440 | tf_op jit(solution)/shard_map/ppermute | solution.py:581
  28.2 4.9 %all-to-all-start = ((bf16[32,32,512]{2,1,0:T(8,128)(2,1)}), bf16[32,32,512]{2,1,0:T(8,128)(2,1)S(1)}, u32[]{:S(2)}, u32[]{:S(2)}) async-start(bf16[32,32,512]{2,1,0:T(8,128)(2,1)} %bitcast.5), calls=%async_computation | async-start | bytes 2097152 | tf_op jit(solution)/shard_map/all_to_all | solution.py:655
  33.2 1.9 %collective-permute-done.9.recv_ref = bf16[512,256]{1,0:T(8,128)(2,1)S(1)} collective-permute-done((bf16[512,256]{1,0:T(8,128)(2,1)S(1)}, bf16[512,256]{1,0:T(8,128)(2,1)S(1)}, u32[]{:S(2)}, u32[]{:S(2)}) %collective-permute-start.9) | collective-permute-done | bytes 262176 | tf_op jit(solution)/shard_map/ppermute | solution.py:581
  35.1 3.5 %shard_map.92 = (f32[78,8,256]{2,1,0:T(8,128)S(1)}, f32[108,8,256]{2,1,0:T(8,128)S(1)}, f32[128,32]{1,0:T(8,128)S(1)}, f32[128,32]{1,0:T(8,128)S(1)}) custom-call(f32[512,256]{1,0:T(8,128)S(1)} %get-tuple-element.73.own_ref, bf16[512,256]{1,0:T(8,128)(2,1)S(1)} %collective-permute-done.9.recv_ref, f32[108,8,256]{2,1,0:T(8,128)} %get-tuple-element.77.xext_hbm, ...), custom_call_target="tpu_custom_call" | custom-call | flops 99999997952 | bytes 300000000 | tf_op jit(solution)/shard_map/pallas_call | solution.py:569
  38.6 1.8 %collective-permute-start.10 = (f32[128,32]{1,0:T(8,128)S(1)}, f32[128,32]{1,0:T(8,128)S(1)}, u32[]{:S(2)}, u32[]{:S(2)}) collective-permute-start(f32[128,32]{1,0:T(8,128)S(1)} %get-tuple-element.79), channel_id=1, source_target_pairs={{0,4},{4,0},{8,12},{12,8},{16,20},{20,16},{24,28},{28,24},{1,5},{5... | collective-permute-start | bytes 49160 | tf_op jit(solution)/shard_map/ppermute | solution.py:669
  40.4 2.4 %shard_map.93 = bf16[512,256]{1,0:T(8,128)(2,1)S(1)} custom-call(f32[78,8,256]{2,1,0:T(8,128)S(1)} %get-tuple-element.80.dh_ref, f32[108,8,256]{2,1,0:T(8,128)S(1)} %get-tuple-element.81.ext_ref, f32[31,8,256]{2,1,0:T(8,128)S(1)} %copy-done.1, bf16[512,624]{1,0:T(8,128)(2,1)S(1)} %get-tuple-element.55.gather_ref), custom_call_target="tpu_custom_call" | custom-call | flops 20000000000 | bytes 60000000 | tf_op jit(solution)/shard_map/pallas_call | solution.py:569
  42.8 1.2 %collective-permute-done.10 = f32[128,32]{1,0:T(8,128)S(1)} collective-permute-done((f32[128,32]{1,0:T(8,128)S(1)}, f32[128,32]{1,0:T(8,128)S(1)}, u32[]{:S(2)}, u32[]{:S(2)}) %collective-permute-start.10) | collective-permute-done | bytes 16416 | tf_op jit(solution)/shard_map/ppermute | solution.py:669
  44.2 1.5 %collective-permute-start.12 = (bf16[128,512]{1,0:T(8,128)(2,1)S(1)}, bf16[128,512]{1,0:T(8,128)(2,1)S(1)}, u32[]{:S(2)}, u32[]{:S(2)}) collective-permute-start(bf16[128,512]{1,0:T(8,128)(2,1)S(1)} %get-tuple-element.93), channel_id=1, source_target_pairs={{0,2},{1,3},{2,0},{3,1},{4,6},{5,7},{6,4},{7,5},{8,10},{9,11},{10,... | collective-permute-start | bytes 393224 | tf_op jit(solution)/shard_map/ppermute | solution.py:581
  46.7 4.5 %collective-permute-start.15 = (f32[32,32]{1,0:T(8,128)S(1)}, f32[32,32]{1,0:T(8,128)S(1)}, u32[]{:S(2)}, u32[]{:S(2)}) collective-permute-start(f32[32,32]{1,0:T(8,128)S(1)} %get-tuple-element.97), channel_id=1, source_target_pairs={{0,1},{1,17},{2,9},{3,25},{4,5},{5,21},{6,13},{7,29},{8,0},{9,16},... | collective-permute-start | bytes 12296 | tf_op jit(solution)/shard_map/ppermute | solution.py:683
  51.2 1.6 %collective-permute-start.16 = (f32[32,32]{1,0:T(8,128)S(1)}, f32[32,32]{1,0:T(8,128)S(1)}, u32[]{:S(2)}, u32[]{:S(2)}) collective-permute-start(f32[32,32]{1,0:T(8,128)S(1)} %get-tuple-element.96), channel_id=1, source_target_pairs={{0,2},{1,18},{2,10},{3,26},{4,6},{5,22},{6,14},{7,30},{8,3},{9,19}... | collective-permute-start | bytes 12296 | tf_op jit(solution)/shard_map/ppermute | solution.py:683
  52.8 3.5 %collective-permute-start.17 = (f32[32,32]{1,0:T(8,128)S(1)}, f32[32,32]{1,0:T(8,128)S(1)}, u32[]{:S(2)}, u32[]{:S(2)}) collective-permute-start(f32[32,32]{1,0:T(8,128)S(1)} %get-tuple-element.95), channel_id=1, source_target_pairs={{0,3},{1,19},{2,11},{3,27},{4,7},{5,23},{6,15},{7,31},{8,2},{9,18}... | collective-permute-start | bytes 12296 | tf_op jit(solution)/shard_map/ppermute | solution.py:683
  56.3 0.8 %shard_map.94 = (bf16[128,1024]{1,0:T(8,128)(2,1)}, bf16[128,1024]{1,0:T(8,128)(2,1)}) custom-call(bf16[512,512]{1,0:T(8,128)(2,1)S(1)} %constant_dynamic-update-slice_fusion.own_ref, bf16[128,512]{1,0:T(8,128)(2,1)S(1)} %collective-permute-done.11.r1, bf16[128,512]{1,0:T(8,128)(2,1)S(1)} %collective-permute-done.12.r2, ...), custom_call_target="tpu_custom_call" | custom-call | flops 1000000000 | bytes 3000000 | tf_op jit(solution)/shard_map/pallas_call | solution.py:569
  57.1 3.6 %collective-permute-done.16.q2 = f32[32,32]{1,0:T(8,128)S(1)} collective-permute-done((f32[32,32]{1,0:T(8,128)S(1)}, f32[32,32]{1,0:T(8,128)S(1)}, u32[]{:S(2)}, u32[]{:S(2)}) %collective-permute-start.16) | collective-permute-done | bytes 4128 | tf_op jit(solution)/shard_map/ppermute | solution.py:683
  60.7 0.8 %shard_map.95 = (f32[32,2048]{1,0:T(8,128)}, f32[32,31]{1,0:T(8,128)}) custom-call(bf16[32,32,512]{2,1,0:T(8,128)(2,1)S(1)} %all-to-all-done.blocks_ref, f32[32,32]{1,0:T(8,128)S(1)} %collective-permute-done.14.q0, f32[32,32]{1,0:T(8,128)S(1)} %collective-permute-done.15.q1, f32[32,32]{1,0:T(8,128)S(1)} %collective-permute-done.16.q2, ...), custom_call_target="tpu_custom_call" | custom-call | flops 1000000000 | bytes 3000000 | tf_op jit(solution)/shard_map/pallas_call | solution.py:569
  (35 shorter events, 4.3 us)
Async XLA Ops:
  1.6 3.2 %collective-permute-start = (bf16[128,256]{1,0:T(8,128)(2,1)S(1)}, bf16[128,256]{1,0:T(8,128)(2,1)S(1)}, u32[]{:S(2)}, u32[]{:S(2)}) collective-permute-start(bf16[128,256]{1,0:T(8,128)(2,1)S(1)} %get-tuple-element.49), channel_id=1, source_target_pairs={{0,1},{1,0},{2,3},{3,2},{4,5},{5,4},{6,7},{7,6},{8,9},{9,8},{10,11... | collective-permute-start | bytes 196616 | tf_op jit(solution)/shard_map/ppermute | solution.py:581
  2.1 6.2 %collective-permute-start.1 = (bf16[128,256]{1,0:T(8,128)(2,1)S(1)}, bf16[128,256]{1,0:T(8,128)(2,1)S(1)}, u32[]{:S(2)}, u32[]{:S(2)}) collective-permute-start(bf16[128,256]{1,0:T(8,128)(2,1)S(1)} %get-tuple-element.51), channel_id=1, source_target_pairs={{0,2},{1,3},{2,0},{3,1},{4,6},{5,7},{6,4},{7,5},{8,10},{9,11},{10,... | collective-permute-start | bytes 196616 | tf_op jit(solution)/shard_map/ppermute | solution.py:581
  4.7 4.0 %collective-permute-start.2 = (bf16[128,256]{1,0:T(8,128)(2,1)S(1)}, bf16[128,256]{1,0:T(8,128)(2,1)S(1)}, u32[]{:S(2)}, u32[]{:S(2)}) collective-permute-start(bf16[128,256]{1,0:T(8,128)(2,1)S(1)} %get-tuple-element.52), channel_id=1, source_target_pairs={{0,3},{1,2},{2,1},{3,0},{4,7},{5,6},{6,5},{7,4},{8,11},{9,10},{10,... | collective-permute-start | bytes 196616 | tf_op jit(solution)/shard_map/ppermute | solution.py:581
  6.1 5.9 %copy-start = (f32[31,8,256]{2,1,0:T(8,128)}, f32[31,8,256]{2,1,0:T(8,128)S(1)}, u32[]{:S(2)}) copy-start(f32[31,8,256]{2,1,0:T(8,128)S(1)} %get-tuple-element.56.taps_ref) | copy-start | bytes 761860
  6.2 6.1 %collective-permute-start.3 = (bf16[128,512]{1,0:T(8,128)(2,1)S(1)}, bf16[128,512]{1,0:T(8,128)(2,1)S(1)}, u32[]{:S(2)}, u32[]{:S(2)}) collective-permute-start(bf16[128,512]{1,0:T(8,128)(2,1)S(1)} %get-tuple-element.59), channel_id=1, source_target_pairs={{0,1},{1,0},{2,3},{3,2},{4,5},{5,4},{6,7},{7,6},{8,9},{9,8},{10,11... | collective-permute-start | bytes 393224 | tf_op jit(solution)/shard_map/ppermute | solution.py:581
  6.4 6.3 %collective-permute-start.4 = (bf16[128,512]{1,0:T(8,128)(2,1)S(1)}, bf16[128,512]{1,0:T(8,128)(2,1)S(1)}, u32[]{:S(2)}, u32[]{:S(2)}) collective-permute-start(bf16[128,512]{1,0:T(8,128)(2,1)S(1)} %get-tuple-element.60), channel_id=1, source_target_pairs={{0,2},{1,3},{2,0},{3,1},{4,6},{5,7},{6,4},{7,5},{8,10},{9,11},{10,... | collective-permute-start | bytes 393224 | tf_op jit(solution)/shard_map/ppermute | solution.py:581
  8.3 6.1 %collective-permute-start.5 = (bf16[128,512]{1,0:T(8,128)(2,1)S(1)}, bf16[128,512]{1,0:T(8,128)(2,1)S(1)}, u32[]{:S(2)}, u32[]{:S(2)}) collective-permute-start(bf16[128,512]{1,0:T(8,128)(2,1)S(1)} %get-tuple-element.61), channel_id=1, source_target_pairs={{0,3},{1,2},{2,1},{3,0},{4,7},{5,6},{6,5},{7,4},{8,11},{9,10},{10,... | collective-permute-start | bytes 393224 | tf_op jit(solution)/shard_map/ppermute | solution.py:581
  12.0 5.6 %collective-permute-start.7 = (bf16[512,256]{1,0:T(8,128)(2,1)S(1)}, bf16[512,256]{1,0:T(8,128)(2,1)S(1)}, u32[]{:S(2)}, u32[]{:S(2)}) collective-permute-start(bf16[512,256]{1,0:T(8,128)(2,1)S(1)} %get-tuple-element.57.hid_ref), channel_id=1, source_target_pairs={{0,1},{1,0},{2,3},{3,2},{4,5},{5,4},{6,7},{7,6},{8,9},{9,8},{10,11... | collective-permute-start | bytes 786440 | tf_op jit(solution)/shard_map/ppermute | solution.py:581
  17.2 1.6 %collective-permute-start.6 = (bf16[512,256]{1,0:T(8,128)(2,1)S(1)}, bf16[512,256]{1,0:T(8,128)(2,1)S(1)}, u32[]{:S(2)}, u32[]{:S(2)}) collective-permute-start(bf16[512,256]{1,0:T(8,128)(2,1)S(1)} %get-tuple-element.63.oth_ref), channel_id=1, source_target_pairs={{0,1},{1,0},{2,3},{3,2},{4,5},{5,4},{6,7},{7,6},{8,9},{9,8},{10,11... | collective-permute-start | bytes 786440 | tf_op jit(solution)/shard_map/ppermute | solution.py:581
  24.3 2.0 %collective-permute-start.8 = (bf16[512,512]{1,0:T(8,128)(2,1)S(1)}, bf16[512,512]{1,0:T(8,128)(2,1)S(1)}, u32[]{:S(2)}, u32[]{:S(2)}) collective-permute-start(bf16[512,512]{1,0:T(8,128)(2,1)S(1)} %get-tuple-element.72), channel_id=1, source_target_pairs={{0,1},{1,0},{2,3},{3,2},{4,5},{5,4},{6,7},{7,6},{8,9},{9,8},{10,11... | collective-permute-start | bytes 1572872 | tf_op jit(solution)/shard_map/ppermute | solution.py:581
  26.4 8.7 %collective-permute-start.9 = (bf16[512,256]{1,0:T(8,128)(2,1)S(1)}, bf16[512,256]{1,0:T(8,128)(2,1)S(1)}, u32[]{:S(2)}, u32[]{:S(2)}) collective-permute-start(bf16[512,256]{1,0:T(8,128)(2,1)S(1)} %get-tuple-element.76), channel_id=1, source_target_pairs={{0,2},{1,3},{2,0},{3,1},{4,6},{5,7},{6,4},{7,5},{8,10},{9,11},{10,... | collective-permute-start | bytes 786440 | tf_op jit(solution)/shard_map/ppermute | solution.py:581
  28.2 32.5 %all-to-all-start = ((bf16[32,32,512]{2,1,0:T(8,128)(2,1)}), bf16[32,32,512]{2,1,0:T(8,128)(2,1)S(1)}, u32[]{:S(2)}, u32[]{:S(2)}) async-start(bf16[32,32,512]{2,1,0:T(8,128)(2,1)} %bitcast.5), calls=%async_computation | async-start | bytes 2097152 | tf_op jit(solution)/shard_map/all_to_all | solution.py:655
  35.1 5.3 %copy-start.1 = (f32[31,8,256]{2,1,0:T(8,128)S(1)}, f32[31,8,256]{2,1,0:T(8,128)}, u32[]{:S(2)}) copy-start(f32[31,8,256]{2,1,0:T(8,128)} %copy-done) | copy-start | bytes 761860
  38.6 5.5 %collective-permute-start.10 = (f32[128,32]{1,0:T(8,128)S(1)}, f32[128,32]{1,0:T(8,128)S(1)}, u32[]{:S(2)}, u32[]{:S(2)}) collective-permute-start(f32[128,32]{1,0:T(8,128)S(1)} %get-tuple-element.79), channel_id=1, source_target_pairs={{0,4},{4,0},{8,12},{12,8},{16,20},{20,16},{24,28},{28,24},{1,5},{5... | collective-permute-start | bytes 49160 | tf_op jit(solution)/shard_map/ppermute | solution.py:669
  44.1 2.0 %collective-permute-start.11 = (bf16[128,512]{1,0:T(8,128)(2,1)S(1)}, bf16[128,512]{1,0:T(8,128)(2,1)S(1)}, u32[]{:S(2)}, u32[]{:S(2)}) collective-permute-start(bf16[128,512]{1,0:T(8,128)(2,1)S(1)} %get-tuple-element.94), channel_id=1, source_target_pairs={{0,1},{1,0},{2,3},{3,2},{4,5},{5,4},{6,7},{7,6},{8,9},{9,8},{10,11... | collective-permute-start | bytes 393224 | tf_op jit(solution)/shard_map/ppermute | solution.py:581
  44.2 8.6 %collective-permute-start.12 = (bf16[128,512]{1,0:T(8,128)(2,1)S(1)}, bf16[128,512]{1,0:T(8,128)(2,1)S(1)}, u32[]{:S(2)}, u32[]{:S(2)}) collective-permute-start(bf16[128,512]{1,0:T(8,128)(2,1)S(1)} %get-tuple-element.93), channel_id=1, source_target_pairs={{0,2},{1,3},{2,0},{3,1},{4,6},{5,7},{6,4},{7,5},{8,10},{9,11},{10,... | collective-permute-start | bytes 393224 | tf_op jit(solution)/shard_map/ppermute | solution.py:581
  45.6 10.6 %collective-permute-start.13 = (bf16[128,512]{1,0:T(8,128)(2,1)S(1)}, bf16[128,512]{1,0:T(8,128)(2,1)S(1)}, u32[]{:S(2)}, u32[]{:S(2)}) collective-permute-start(bf16[128,512]{1,0:T(8,128)(2,1)S(1)} %get-tuple-element.92), channel_id=1, source_target_pairs={{0,3},{1,2},{2,1},{3,0},{4,7},{5,6},{6,5},{7,4},{8,11},{9,10},{10,... | collective-permute-start | bytes 393224 | tf_op jit(solution)/shard_map/ppermute | solution.py:581
  46.1 11.0 %collective-permute-start.14 = (f32[32,32]{1,0:T(8,128)S(1)}, f32[32,32]{1,0:T(8,128)S(1)}, u32[]{:S(2)}, u32[]{:S(2)}) collective-permute-start(f32[32,32]{1,0:T(8,128)S(1)} %get-tuple-element.98), channel_id=1, source_target_pairs={{0,0},{1,16},{2,8},{3,24},{4,4},{5,20},{6,12},{7,28},{8,1},{9,17},... | collective-permute-start | bytes 12296 | tf_op jit(solution)/shard_map/ppermute | solution.py:683
  46.7 10.4 %collective-permute-start.15 = (f32[32,32]{1,0:T(8,128)S(1)}, f32[32,32]{1,0:T(8,128)S(1)}, u32[]{:S(2)}, u32[]{:S(2)}) collective-permute-start(f32[32,32]{1,0:T(8,128)S(1)} %get-tuple-element.97), channel_id=1, source_target_pairs={{0,1},{1,17},{2,9},{3,25},{4,5},{5,21},{6,13},{7,29},{8,0},{9,16},... | collective-permute-start | bytes 12296 | tf_op jit(solution)/shard_map/ppermute | solution.py:683
  51.2 9.5 %collective-permute-start.16 = (f32[32,32]{1,0:T(8,128)S(1)}, f32[32,32]{1,0:T(8,128)S(1)}, u32[]{:S(2)}, u32[]{:S(2)}) collective-permute-start(f32[32,32]{1,0:T(8,128)S(1)} %get-tuple-element.96), channel_id=1, source_target_pairs={{0,2},{1,18},{2,10},{3,26},{4,6},{5,22},{6,14},{7,30},{8,3},{9,19}... | collective-permute-start | bytes 12296 | tf_op jit(solution)/shard_map/ppermute | solution.py:683
  52.8 8.0 %collective-permute-start.17 = (f32[32,32]{1,0:T(8,128)S(1)}, f32[32,32]{1,0:T(8,128)S(1)}, u32[]{:S(2)}, u32[]{:S(2)}) collective-permute-start(f32[32,32]{1,0:T(8,128)S(1)} %get-tuple-element.95), channel_id=1, source_target_pairs={{0,3},{1,19},{2,11},{3,27},{4,7},{5,23},{6,15},{7,31},{8,2},{9,18}... | collective-permute-start | bytes 12296 | tf_op jit(solution)/shard_map/ppermute | solution.py:683

commit v6 on v5

--- a/solution.py
+++ b/solution.py
@@ -248,24 +248,25 @@
             finish(start + a, sums[a], window[a + RIM])
         return carry
 
-    lax.fori_loop(0, steps // CHUNK, body, 0)
+    lax.fori_loop(0, steps // CHUNK, body, 0, unroll=6)
 
 
 def pack_kernel(rows_hbm, *refs):
     outs, sems = refs[:4], refs[4]
     group = device_group()
-    width = outs[0].shape[1]
+    width = outs[0].shape[1] // 2
     loads = []
-    for j in range(4):
-        own = pl.multiple_of((group ^ SWAP[j]) * width, width)
-        loads.append(pltpu.make_async_copy(rows_hbm.at[:, pl.ds(own, width)], outs[j], sems.at[j]))
-        loads[-1].start()
+    for n in range(8):
+        start = pl.multiple_of((group ^ SWAP[n % 4] ^ (n // 4)) * width, width)
+        target = outs[n % 4].at[:, n // 4 * width : (n // 4 + 1) * width]
+        loads.append(pltpu.make_async_copy(rows_hbm.at[:, pl.ds(start, width)], target, sems.at[n]))
+        loads[n].start()
     for load in loads:
         load.wait()
 
 
 def setup_kernel(
-    len_hbm, w_hbm, rows_hbm, grads_hbm, spread_ref, gather_ref, taps_own_ref, taps_oth_ref, p0, p1, p2, p3,
+    len_hbm, w_hbm, grads_hbm, spread_ref, gather_ref, taps_own_ref, taps_oth_ref, p0, p1, p2, p3,
     len_ref, w_own_ref, w_oth_ref, sems,
 ):
     own_index, group = lax.axis_index("ctx"), device_group()
@@ -278,10 +279,7 @@
         loads.append(pltpu.make_async_copy(w_hbm.at[:, pl.ds(start, width)], ref, sems.at[1 + part]))
     for j, parcel in enumerate((p0, p1, p2, p3)):
         own = pl.multiple_of((group ^ SWAP[j]) * width, width)
-        other = pl.multiple_of((group ^ SWAP[j] ^ 1) * width, width)
-        for part, (source, start) in enumerate(((rows_hbm, other), (grads_hbm, own))):
-            target = parcel.at[:, part * width : (part + 1) * width]
-            loads.append(pltpu.make_async_copy(source.at[:, pl.ds(start, width)], target, sems.at[len(loads)]))
+        loads.append(pltpu.make_async_copy(grads_hbm.at[:, pl.ds(own, width)], parcel, sems.at[3 + j]))
     for load in loads:
         load.start()
     loads[0].wait()
@@ -294,55 +292,46 @@
             taps_ref[tap] = jnp.broadcast_to(w_ref[tap : tap + 1, :], taps_ref.shape[1:])
 
 
-def forward_conv(f0, f1, f2, f3, spread_ref, gather_ref, taps_ref, hid_ref, ext_ref, hid_sp_ref, conv_ref, saves):
-    width = hid_ref.shape[1]
-    steps = hid_sp_ref.shape[0]
-    rows = jnp.concatenate([f[:, :width] for f in (f0, f1, f2, f3)], axis=0)
-    write_extended(ext_ref, jnp.dot(spread_ref[...], rows, preferred_element_type=jnp.float32), steps)
-    if saves is not None:
-        saves[0].start()
-    for lane in range(0, width, 128):
-        lanes = slice(lane, lane + 128)
-
-        def finish(step, conv, center, lanes=lanes):
-            half = 0.5 * conv
-            hid_sp_ref[step, :, lanes] = center + (half + half * jnp.tanh(half))
-            if conv_ref is not None:
-                conv_ref[step, :, lanes] = conv
-
-        conv_loop(ext_ref, taps_ref, lanes, steps, False, finish)
-    if saves is not None:
-        saves[1].start()
-    hid_low = hid_sp_ref[...].reshape(steps * SUB, width).astype(jnp.bfloat16)
-    hid_ref[...] = jnp.dot(gather_ref[...], hid_low, preferred_element_type=jnp.float32).astype(jnp.bfloat16)
-
-
-def own_conv_kernel(
-    f0, f1, f2, f3, spread_ref, gather_ref, taps_ref, hid_ref, ext_hbm, conv_hbm, ext_ref, conv_ref, hid_sp_ref, sems
+def forward_conv_kernel(
+    f0, f1, f2, f3, spread_ref, gather_ref, taps_own_ref, taps_oth_ref, w_hbm,
+    hid_ref, wk_ref, wv_ref, ext_hbm, conv_hbm, ext_ref, oth_ref, conv_ref, hid_sp_ref, sems,
 ):
-    saves = [
-        pltpu.make_async_copy(ext_ref, ext_hbm, sems.at[0]),
-        pltpu.make_async_copy(conv_ref, conv_hbm, sems.at[1]),
-    ]
-    forward_conv(f0, f1, f2, f3, spread_ref, gather_ref, taps_ref, hid_ref, ext_ref, hid_sp_ref, conv_ref, saves)
-    for save in saves:
-        save.wait()
-
-
-def other_conv_kernel(
-    f0, f1, f2, f3, spread_ref, gather_ref, taps_ref, w_hbm, hid_ref, wk_ref, wv_ref, ext_ref, hid_sp_ref, sems
-):
-    width = hid_ref.shape[1]
+    seq_total = hid_ref.shape[0]
+    steps, _, width = conv_ref.shape
     own = pl.multiple_of(device_group() * width, width)
     loads = [
         pltpu.make_async_copy(w_hbm.at[:, pl.ds(own, width)], wk_ref, sems.at[0]),
         pltpu.make_async_copy(w_hbm.at[:, pl.ds(4 * width + own, width)], wv_ref, sems.at[1]),
     ]
+    saves = [
+        pltpu.make_async_copy(ext_ref, ext_hbm, sems.at[2]),
+        pltpu.make_async_copy(conv_ref, conv_hbm, sems.at[3]),
+    ]
     for load in loads:
         load.start()
-    forward_conv(f0, f1, f2, f3, spread_ref, gather_ref, taps_ref, hid_ref, ext_ref, hid_sp_ref, None, None)
-    for load in loads:
-        load.wait()
+    rows = jnp.concatenate([f[...] for f in (f0, f1, f2, f3)], axis=0)
+    spaced = jnp.dot(spread_ref[...], rows, preferred_element_type=jnp.float32)
+    write_extended(ext_ref, spaced[:, :width], steps)
+    write_extended(oth_ref, spaced[:, width:], steps)
+    saves[0].start()
+    for part, (source, taps_ref) in enumerate(((ext_ref, taps_own_ref), (oth_ref, taps_oth_ref))):
+        for lane in range(0, width, 128):
+            lanes = slice(lane, lane + 128)
+            outer = slice(part * width + lane, part * width + lane + 128)
+
+            def finish(step, conv, center, part=part, lanes=lanes, outer=outer):
+                half = 0.5 * conv
+                hid_sp_ref[step, :, outer] = center + (half + half * jnp.tanh(half))
+                if part == 0:
+                    conv_ref[step, :, lanes] = conv
+
+            conv_loop(source, taps_ref, lanes, steps, False, finish)
+        if part == 0:
+            saves[1].start()
+    hid_low = hid_sp_ref[...].reshape(steps * SUB, 2 * width).astype(jnp.bfloat16)
+    hid_ref[...] = jnp.dot(gather_ref[...], hid_low, preferred_element_type=jnp.float32).astype(jnp.bfloat16)
+    for copy in loads + saves:
+        copy.wait()
 
 
 def swapped(array, order, row_count):
@@ -355,18 +344,18 @@
 
 
 def ready_kernel(
-    len_hbm, hid_ref, oth_ref, sib_ref, f0, f1, f2, f3, wk_ref, wv_ref, kv_ref, cot_ref, cott_ref, bias_ref, len_ref, sem
+    len_hbm, hid_ref, f0, f1, f2, f3, wk_ref, wv_ref, kv_ref, cot_ref, cott_ref, bias_ref, len_ref, sem
 ):
     own_index, group = lax.axis_index("ctx"), device_group()
-    seq_total, width = hid_ref.shape
+    seq_total, width = cot_ref.shape
     row_count = seq_total // 4
     load = pltpu.make_async_copy(len_hbm, len_ref, sem)
     load.start()
-    parts = [hid_ref[...], oth_ref[...], swapped(sib_ref[...], (1, 0, 3, 2), row_count)]
+    parts = [hid_ref[:, :width], hid_ref[:, width:]]
     for n, ref in enumerate((wk_ref, wv_ref)):
         terms = [jnp.dot(part, w_rows(ref, group, j), preferred_element_type=jnp.float32) for j, part in enumerate(parts)]
         kv_ref[:, n * width : (n + 1) * width] = sum(terms)
-    cot = jnp.concatenate([f[:, width:] for f in (f0, f1, f2, f3)], axis=0)
+    cot = jnp.concatenate([f[...] for f in (f0, f1, f2, f3)], axis=0)
     cot_ref[...] = cot
     cott_ref[...] = cot.T.astype(jnp.float32)
     load.wait()
@@ -378,17 +367,19 @@
 
 
 def attention_kernel(
-    hid_ref, sib_oth_ref, kv_ref, cot_ref, cott_ref, wk_ref, wv_ref, bias_ref,
-    out_ref, keep_ref, send_ref, kvg_ref, k_ref, v_ref, kt_ref, vt_ref, attt_ref, dqt_ref, dk_ref, dv_ref,
+    hid_ref, sib_ref, kv_ref, cot_ref, cott_ref, wk_ref, wv_ref, bias_ref,
+    attt_ref, dqt_ref, send_ref, kvg_ref, k_ref, v_ref, kt_ref, vt_ref, dk_ref, dv_ref,
 ):
     group = device_group()
-    seq_total, width = out_ref.shape
+    seq_total, width = cot_ref.shape
     head_width = 64
     scale = 1.0 / math.sqrt(head_width)
     bf16, f32 = jnp.bfloat16, jnp.float32
-    part = swapped(sib_oth_ref[...], (1, 0, 3, 2), seq_total // 4)
-    keys = kv_ref[:, :width] + jnp.dot(part, w_rows(wk_ref, group, 3), preferred_element_type=f32)
-    values = kv_ref[:, width:] + jnp.dot(part, w_rows(wv_ref, group, 3), preferred_element_type=f32)
+    keys, values = kv_ref[:, :width], kv_ref[:, width:]
+    for j in (2, 3):
+        part = swapped(sib_ref[:, (j - 2) * width : (j - 1) * width], (1, 0, 3, 2), seq_total // 4)
+        keys = keys + jnp.dot(part, w_rows(wk_ref, group, j), preferred_element_type=f32)
+        values = values + jnp.dot(part, w_rows(wv_ref, group, j), preferred_element_type=f32)
     keys, values = keys.astype(bf16), values.astype(bf16)
     k_ref[...] = keys
     v_ref[...] = values
@@ -425,31 +416,31 @@
             dv_pair = dv_head if head == 0 else dv_pair + dv_head
         dk_ref[:, lanes] = dk_pair
         dv_ref[:, lanes] = dv_pair
-    out_ref[...] = (hid_ref[...].astype(f32) + attt_ref[...].T).astype(bf16)
     grad_k = (dk_ref[...] * scale).astype(bf16)
     grad_v = dv_ref[...].astype(bf16)
     kvg_ref[:, :width] = grad_k
     kvg_ref[:, width:] = grad_v
-
-    def partial(j):
-        return nt_dot(grad_k, w_rows(wk_ref, group, j)) + nt_dot(grad_v, w_rows(wv_ref, group, j))
-
-    send_ref[:, :width] = partial(2).astype(bf16)
-    send_ref[:, width:] = partial(3).astype(bf16)
-    keep_ref[:, :width] = partial(0) + dqt_ref[...].T + cot_ref[...].astype(f32)
-    keep_ref[:, width:] = partial(1)
-
-
-def weight_grad_kernel(hid_ref, oth_ref, sib_ref, sib_oth_ref, kvg_ref, out_hbm, all_ref, sems):
+    for j in (2, 3):
+        part = nt_dot(grad_k, w_rows(wk_ref, group, j)) + nt_dot(grad_v, w_rows(wv_ref, group, j))
+        send_ref[:, (j - 2) * width : (j - 1) * width] = part.astype(bf16)
+
+
+def output_kernel(hid_ref, attt_ref, out_ref):
+    out_ref[...] = (hid_ref[:, : out_ref.shape[1]].astype(jnp.float32) + attt_ref[...].T).astype(jnp.bfloat16)
+
+
+def weight_grad_kernel(
+    hid_ref, sib_ref, kvg_ref, dqt_ref, cot_ref, wk_ref, wv_ref, out_hbm, keep_ref, all_ref, sems
+):
     group = device_group()
-    width = hid_ref.shape[1]
+    width = cot_ref.shape[1]
     row_count = hid_ref.shape[0] // 4
     kvg = kvg_ref[...]
     parts = [
-        hid_ref[...],
-        oth_ref[...],
-        swapped(sib_ref[...], (1, 0, 3, 2), row_count),
-        swapped(sib_oth_ref[...], (1, 0, 3, 2), row_count),
+        hid_ref[:, :width],
+        hid_ref[:, width:],
+        swapped(sib_ref[:, :width], (1, 0, 3, 2), row_count),
+        swapped(sib_ref[:, width:], (1, 0, 3, 2), row_count),
     ]
     saves = []
     for j in range(4):
@@ -457,6 +448,11 @@
         start = pl.multiple_of((group ^ j) * width, width)
         saves.append(pltpu.make_async_copy(all_ref.at[j], out_hbm.at[pl.ds(start, width), :], sems.at[j]))
         saves[j].start()
+    for j in range(2):
+        part = nt_dot(kvg[:, :width], w_rows(wk_ref, group, j)) + nt_dot(kvg[:, width:], w_rows(wv_ref, group, j))
+        if j == 0:
+            part = part + dqt_ref[...].T + cot_ref[...].astype(jnp.float32)
+        keep_ref[:, j * width : (j + 1) * width] = part
     for save in saves:
         save.wait()
 
@@ -515,7 +511,7 @@
                 )
 
             zero = tuple(jnp.zeros((SUB, 128), f32) for _ in range(count))
-            sums = lax.fori_loop(0, steps // CHUNK, body, zero)
+            sums = lax.fori_loop(0, steps // CHUNK, body, zero, unroll=6)
             for t in range(count):
                 gdw_ref[first + t : first + t + 1, lanes] = jnp.sum(sums[t], axis=0, keepdims=True)
     gdw_ref[KERNEL:, :] = jnp.zeros((gdw_ref.shape[0] - KERNEL, width), f32)
@@ -592,9 +588,9 @@
     rows, grads = frames[0], cotangent[0]
 
     packed = call(
-        pack_kernel, (rows,), [((row_count, width), bf16)] * 4, [pltpu.SemaphoreType.DMA((4,))], hbm_in=(0,), cost_us=1
-    )
-    own_blocks = [packed[0]] + [swap_ctx(packed[j], j) for j in (1, 2, 3)]
+        pack_kernel, (rows,), [((row_count, 2 * width), bf16)] * 4, [pltpu.SemaphoreType.DMA((8,))], hbm_in=(0,), cost_us=1
+    )
+    blocks = [packed[0]] + [swap_ctx(packed[j], j) for j in (1, 2, 3)]
     wide = (seq_total, width)
     both = (seq_total, 2 * width)
     tall = wide[::-1]
@@ -602,49 +598,51 @@
     short = (steps, SUB, width)
     taps = (KERNEL, SUB, width)
     slots = steps * SUB
-    late_rows, own_blocks[1] = lax.optimization_barrier((rows, own_blocks[1]))
     spread, gather, taps_own, taps_oth, *parcels = call(
-        setup_kernel, (utt_lengths, w_dw, late_rows, grads),
+        setup_kernel, (utt_lengths, w_dw, grads),
         [
             ((slots, seq_total), bf16), ((seq_total, slots), bf16), (taps, f32), (taps, f32),
-            *[((row_count, 2 * width), bf16)] * 4,
+            *[((row_count, width), bf16)] * 4,
         ],
         [
             pltpu.SMEM(utt_lengths.shape, jnp.int32), pltpu.VMEM((KERNEL, width), f32), pltpu.VMEM((KERNEL, width), f32),
-            pltpu.SemaphoreType.DMA((11,)),
+            pltpu.SemaphoreType.DMA((7,)),
         ],
-        hbm_in=(0, 1, 2, 3), cost_us=2,
-    )
-    blocks = [parcels[0]] + [swap_ctx(parcels[j], j) for j in (1, 2, 3)]
-    hidden, frames_ext, conv_own = call(
-        own_conv_kernel, (*own_blocks, spread, gather, taps_own), [(wide, bf16), (long, f32), (short, f32)],
-        [pltpu.VMEM(long, f32), pltpu.VMEM(short, f32), pltpu.VMEM(short, f32), pltpu.SemaphoreType.DMA((2,))],
-        hbm_out=(1, 2), cost_us=20,
-    )
+        hbm_in=(0, 1, 2), cost_us=2,
+    )
+    parcels, blocks[1] = lax.optimization_barrier((parcels, blocks[1]))
+    cots = [parcels[0]] + [swap_ctx(parcels[j], j) for j in (1, 2, 3)]
+    hidden, w_keys, w_values, frames_ext, conv_own = call(
+        forward_conv_kernel, (*blocks, spread, gather, taps_own, taps_oth, w_kv),
+        [
+            (both, bf16), ((feat_width, width), bf16), ((feat_width, width), bf16), (long, f32), (short, f32),
+        ],
+        [
+            pltpu.VMEM(long, f32), pltpu.VMEM(long, f32), pltpu.VMEM(short, f32),
+            pltpu.VMEM((steps, SUB, 2 * width), f32), pltpu.SemaphoreType.DMA((4,)),
+        ],
+        hbm_in=(8,), hbm_out=(3, 4), vmem_mib=12, cost_us=20,
+    )
+    hidden, cots = lax.optimization_barrier((hidden, cots))
     hidden_sib = swap_ctx(hidden, 1)
-    hidden_oth, w_keys, w_values = call(
-        other_conv_kernel, (*blocks, spread, gather, taps_oth, w_kv),
-        [(wide, bf16), ((feat_width, width), bf16), ((feat_width, width), bf16)],
-        [pltpu.VMEM(long, f32), pltpu.VMEM(short, f32), pltpu.SemaphoreType.DMA((2,))], hbm_in=(7,), cost_us=4,
-    )
-    hidden_sib_oth = swap_ctx(hidden_oth, 1)
-    hiddens = (hidden, hidden_oth, hidden_sib, hidden_sib_oth)
     kv_part, cot_own, cot_turned, bias = call(
-        ready_kernel, (utt_lengths, *hiddens[:3], *blocks, w_keys, w_values),
+        ready_kernel, (utt_lengths, hidden, *cots, w_keys, w_values),
         [(both, f32), (wide, bf16), (tall, f32), ((seq_total, seq_total), f32)],
         [pltpu.SMEM(utt_lengths.shape, jnp.int32), pltpu.SemaphoreType.DMA], hbm_in=(0,), cost_us=2,
     )
-    out_own, keep, send, kv_grad = call(
-        attention_kernel, (hidden, hidden_sib_oth, kv_part, cot_own, cot_turned, w_keys, w_values, bias),
-        [(wide, bf16), (both, f32), (both, bf16), (both, bf16)],
+    att_turned, dq_turned, send, kv_grad = call(
+        attention_kernel, (hidden, hidden_sib, kv_part, cot_own, cot_turned, w_keys, w_values, bias),
+        [(tall, f32), (tall, f32), (both, bf16), (both, bf16)],
         [
             pltpu.VMEM(wide, bf16), pltpu.VMEM(wide, bf16), pltpu.VMEM(tall, bf16), pltpu.VMEM(tall, bf16),
-            pltpu.VMEM(tall, f32), pltpu.VMEM(tall, f32), pltpu.VMEM(wide, f32), pltpu.VMEM(wide, f32),
+            pltpu.VMEM(wide, f32), pltpu.VMEM(wide, f32),
         ],
         vmem_mib=14, cost_us=8,
     )
-    (part_kv,) = call(
-        weight_grad_kernel, (*hiddens, kv_grad), [((feat_width, 2 * width), bf16)],
+    (out_own,) = call(output_kernel, (hidden, att_turned), [(wide, bf16)], cost_us=1)
+    part_kv, keep = call(
+        weight_grad_kernel, (hidden, hidden_sib, kv_grad, dq_turned, cot_own, w_keys, w_values),
+        [((feat_width, 2 * width), bf16), (both, f32)],
         [pltpu.VMEM((4, width, 2 * width), bf16), pltpu.SemaphoreType.DMA((4,))], hbm_out=(0,), cost_us=2,
     )
     piece = feat_width // (4 * dp_size)

time: 62 us -> 60.8 us (0.981)
  Pallas kernels: 24.1 us -> 21.1 us
  waiting for transfers between devices: 9.5 us -> 11 us
    pallas_call x12, Pallas kernels: 24.1 us -> 21.1 us  [call(): pl.pallas_call(kernel, out_shape=[jax.ShapeDtypeStruct(*o) if to_hbm else...]
    ppermute x1, waiting for transfers between devices: 1.21 us -> 1.89 us  [on_device_pairs(): dw_recv = lax.ppermute(dw_send, 'dp', [(i, i ^ 1) for i in range(dp_size)])]
    ppermute x13 -> x12, waiting for transfers between devices: 4.66 us -> 5.06 us  [swap_ctx(): return lax.ppermute(array, 'ctx', [(i, i ^ j) for i in range(4)])]
    ppermute x13 -> x12, starting transfers between devices: 10.1 us -> 10.3 us  [swap_ctx(): return lax.ppermute(array, 'ctx', [(i, i ^ j) for i in range(4)])]
  transfers between devices with their start and end apart: 19 -> 18, of which waited for: 7 -> 6; matrix products, arithmetic and copies ran while one was open for 0% -> 0% of each run, Pallas kernels for 27% -> 23%
where the time goes in v6:
time: 60.8 us; the launch traced here: 60.5 us
  starting transfers between devices  27.4 us (45%)
  Pallas kernels  21.1 us (35%)
  waiting for transfers between devices  11 us (18%)
  between operations  0.85 us (1%)
    pallas_call x12, Pallas kernels, call(): pl.pallas_call(kernel, out_shape=[jax.ShapeDtypeStruct(*o) if to_hbm else...  21.1 us
    ppermute x12, starting transfers between devices, swap_ctx(): return lax.ppermute(array, 'ctx', [(i, i ^ j) for i in range(4)])  10.3 us
    ppermute x4, starting transfers between devices, on_device_pairs(): quarters.append(lax.ppermute(quarter, ('dp', 'ctx'), pairs))  10.2 us
    all_to_all x1, starting transfers between devices, on_device_pairs(): lax.all_to_all(part_kv.reshape(4 * dp_size, piece, 2 * width), ('dp', 'ct...  5.11 us
    ppermute x12, waiting for transfers between devices, swap_ctx(): return lax.ppermute(array, 'ctx', [(i, i ^ j) for i in range(4)])  5.06 us
    ppermute x4, waiting for transfers between devices, on_device_pairs(): quarters.append(lax.ppermute(quarter, ('dp', 'ctx'), pairs))  4.04 us
    ppermute x1, waiting for transfers between devices, on_device_pairs(): dw_recv = lax.ppermute(dw_send, 'dp', [(i, i ^ 1) for i in range(dp_size)])  1.89 us
    ppermute x1, starting transfers between devices, on_device_pairs(): dw_recv = lax.ppermute(dw_send, 'dp', [(i, i ^ 1) for i in range(dp_size)])  1.84 us
  transfers between devices with their start and end apart: 18, of which 6 were waited for; matrix products, arithmetic and copies ran while one was open for 0% of the time, Pallas kernels for 23%

profile of v6, /device:TPU:0, one launch (start us, length us, event | category | flops | bytes accessed | tf_op | source)
XLA Modules:
  0.0 60.5 jit_solution(8096259004504525990)
XLA Ops:
  0.6 1.1 %shard_map.84 = (bf16[128,512]{1,0:T(8,128)(2,1)S(1)}, bf16[128,512]{1,0:T(8,128)(2,1)S(1)}, bf16[128,512]{1,0:T(8,128)(2,1)S(1)}, bf16[128,512]{1,0:T(8,128)(2,1)S(1)}) custom-call(bf16[128,1024]{1,0:T(8,128)(2,1)} %bitcast.6), custom_call_target="tpu_custom_call" | custom-call | flops 1000000000 | bytes 3000000 | tf_op jit(solution)/shard_map/pallas_call | solution.py:565
  2.3 2.6 %collective-permute-start.1 = (bf16[128,512]{1,0:T(8,128)(2,1)S(1)}, bf16[128,512]{1,0:T(8,128)(2,1)S(1)}, u32[]{:S(2)}, u32[]{:S(2)}) collective-permute-start(bf16[128,512]{1,0:T(8,128)(2,1)S(1)} %get-tuple-element.64), channel_id=1, source_target_pairs={{0,2},{1,3},{2,0},{3,1},{4,6},{5,7},{6,4},{7,5},{8,10},{9,11},{10,... | collective-permute-start | bytes 393224 | tf_op jit(solution)/shard_map/ppermute | solution.py:577
  4.9 1.3 %shard_map.85 = (bf16[624,512]{1,0:T(8,128)(2,1)S(1)}, bf16[512,624]{1,0:T(8,128)(2,1)S(1)}, f32[31,8,256]{2,1,0:T(8,128)S(1)}, f32[31,8,256]{2,1,0:T(8,128)S(1)...) custom-call(s32[1,8]{1,0:T(1,128)} %len_hbm.5, ...), custom_call_target="tpu_custom_call" | custom-call | flops 2000000000 | bytes 6000000 | tf_op jit(solution)/shard_map/pallas_call | solution.py:565
  6.5 1.9 %collective-permute-start.4 = (bf16[128,256]{1,0:T(8,128)(2,1)S(1)}, bf16[128,256]{1,0:T(8,128)(2,1)S(1)}, u32[]{:S(2)}, u32[]{:S(2)}) collective-permute-start(bf16[128,256]{1,0:T(8,128)(2,1)S(1)} %get-tuple-element.73), channel_id=1, source_target_pairs={{0,2},{1,3},{2,0},{3,1},{4,6},{5,7},{6,4},{7,5},{8,10},{9,11},{10,... | collective-permute-start | bytes 196616 | tf_op jit(solution)/shard_map/ppermute | solution.py:577
  8.4 0.8 %collective-permute-done.1.f2 = bf16[128,512]{1,0:T(8,128)(2,1)S(1)} collective-permute-done((bf16[128,512]{1,0:T(8,128)(2,1)S(1)}, bf16[128,512]{1,0:T(8,128)(2,1)S(1)}, u32[]{:S(2)}, u32[]{:S(2)}) %collective-permute-start.1) | collective-permute-done | bytes 131104 | tf_op jit(solution)/shard_map/ppermute | solution.py:577
  9.2 2.3 %collective-permute-done.2.f3 = bf16[128,512]{1,0:T(8,128)(2,1)S(1)} collective-permute-done((bf16[128,512]{1,0:T(8,128)(2,1)S(1)}, bf16[128,512]{1,0:T(8,128)(2,1)S(1)}, u32[]{:S(2)}, u32[]{:S(2)}) %collective-permute-start.2) | collective-permute-done | bytes 131104 | tf_op jit(solution)/shard_map/ppermute | solution.py:577
  11.5 4.0 %shard_map.86 = (bf16[512,512]{1,0:T(8,128)(2,1)S(1)}, bf16[1024,256]{1,0:T(8,128)(2,1)S(1)}, bf16[1024,256]{1,0:T(8,128)(2,1)S(1)}, f32[108,8,256]{2,1,0:T(8,128)}, f32[78,8,256]{2,1,0:T(8,128)}) custom-call(bf16[128,512]{1,0:T(8,128)(2,1)S(1)} %get-tuple-element.57.f0, bf16[128,512]{1,0:T(8,128)(2,1)S(1)} %collective-permute-done.f1, ...), custom_call_target="tpu_custom_call" | custom-call | flops 20000000000 | bytes 60000000 | tf_op jit(solution)/shard_map/pallas_call | solution.py:565
  16.0 1.0 %shard_map.87 = (f32[512,512]{1,0:T(8,128)S(1)}, bf16[512,256]{1,0:T(8,128)(2,1)S(1)}, f32[256,512]{1,0:T(8,128)S(1)}, f32[512,512]{1,0:T(8,128)S(1)}) custom-call(s32[1,8]{1,0:T(1,128)} %len_hbm.5, bf16[512,512]{1,0:T(8,128)(2,1)S(1)} %get-tuple-element.75.hid_ref, bf16[128,256]{1,0:T(8,128)(2,1)S(1)} %get-tuple-element.76.f0, ...), custom_call_target="tpu_custom_call" | custom-call | flops 2000000000 | bytes 6000000 | tf_op jit(solution)/shard_map/pallas_call | solution.py:565
  17.5 5.3 %shard_map.88 = (f32[256,512]{1,0:T(8,128)S(1)}, f32[256,512]{1,0:T(8,128)S(1)}, bf16[512,512]{1,0:T(8,128)(2,1)S(1)}, bf16[512,512]{1,0:T(8,128)(2,1)S(1)}) custom-call(bf16[512,512]{1,0:T(8,128)(2,1)S(1)} %get-tuple-element.75.hid_ref, bf16[512,512]{1,0:T(8,128)(2,1)S(1)} %collective-permute-done.6.sib_ref, f32[512,512]{1,0:T(8,128)S(1)} %get-tuple-element.82.kv_ref, ...), custom_call_target="tpu_custom_call" | custom-call | flops 8000000000 | bytes 24000000 | tf_op jit(solution)/shard_map/pallas_call | solution.py:565
  23.3 1.6 %shard_map.90 = (bf16[1024,512]{1,0:T(8,128)(2,1)}, f32[512,512]{1,0:T(8,128)S(1)}) custom-call(bf16[512,512]{1,0:T(8,128)(2,1)S(1)} %get-tuple-element.75.hid_ref, bf16[512,512]{1,0:T(8,128)(2,1)S(1)} %collective-permute-done.6.sib_ref, bf16[512,512]{1,0:T(8,128)(2,1)S(1)} %get-tuple-element.87.kvg_ref, f32[256,512]{1,0:T(8,128)S(1)} %get-tuple-element.88.dqt_ref, ...), custom_call_target="tpu_custom_call" | custom-call | flops 2000000000 | bytes 6000000 | tf_op jit(solution)/shard_map/pallas_call | solution.py:565
  25.0 2.0 %collective-permute-start.8 = (bf16[512,256]{1,0:T(8,128)(2,1)S(1)}, bf16[512,256]{1,0:T(8,128)(2,1)S(1)}, u32[]{:S(2)}, u32[]{:S(2)}) collective-permute-start(bf16[512,256]{1,0:T(8,128)(2,1)S(1)} %get-tuple-element.94), channel_id=1, source_target_pairs={{0,2},{1,3},{2,0},{3,1},{4,6},{5,7},{6,4},{7,5},{8,10},{9,11},{10,... | collective-permute-start | bytes 786440 | tf_op jit(solution)/shard_map/ppermute | solution.py:577
  27.2 5.1 %all-to-all-start = ((bf16[32,32,512]{2,1,0:T(8,128)(2,1)}), bf16[32,32,512]{2,1,0:T(8,128)(2,1)S(1)}, u32[]{:S(2)}, u32[]{:S(2)}) async-start(bf16[32,32,512]{2,1,0:T(8,128)(2,1)} %bitcast.5), calls=%async_computation | async-start | bytes 2097152 | tf_op jit(solution)/shard_map/all_to_all | solution.py:653
  32.4 1.4 %collective-permute-done.8.recv_ref = bf16[512,256]{1,0:T(8,128)(2,1)S(1)} collective-permute-done((bf16[512,256]{1,0:T(8,128)(2,1)S(1)}, bf16[512,256]{1,0:T(8,128)(2,1)S(1)}, u32[]{:S(2)}, u32[]{:S(2)}) %collective-permute-start.8) | collective-permute-done | bytes 262176 | tf_op jit(solution)/shard_map/ppermute | solution.py:577
  33.8 2.9 %shard_map.92 = (f32[78,8,256]{2,1,0:T(8,128)S(1)}, f32[108,8,256]{2,1,0:T(8,128)S(1)}, f32[128,32]{1,0:T(8,128)S(1)}, f32[128,32]{1,0:T(8,128)S(1)}) custom-call(f32[512,256]{1,0:T(8,128)S(1)} %get-tuple-element.91.own_ref, bf16[512,256]{1,0:T(8,128)(2,1)S(1)} %collective-permute-done.8.recv_ref, f32[108,8,256]{2,1,0:T(8,128)} %get-tuple-element.95.xext_hbm, ...), custom_call_target="tpu_custom_call" | custom-call | flops 99999997952 | bytes 300000000 | tf_op jit(solution)/shard_map/pallas_call | solution.py:565
  36.7 1.8 %collective-permute-start.9 = (f32[128,32]{1,0:T(8,128)S(1)}, f32[128,32]{1,0:T(8,128)S(1)}, u32[]{:S(2)}, u32[]{:S(2)}) collective-permute-start(f32[128,32]{1,0:T(8,128)S(1)} %get-tuple-element.97), channel_id=1, source_target_pairs={{0,4},{4,0},{8,12},{12,8},{16,20},{20,16},{24,28},{28,24},{1,5},{5... | collective-permute-start | bytes 49160 | tf_op jit(solution)/shard_map/ppermute | solution.py:667
  38.6 1.8 %shard_map.93 = bf16[512,256]{1,0:T(8,128)(2,1)S(1)} custom-call(f32[78,8,256]{2,1,0:T(8,128)S(1)} %get-tuple-element.98.dh_ref, f32[108,8,256]{2,1,0:T(8,128)S(1)} %get-tuple-element.99.ext_ref, f32[31,8,256]{2,1,0:T(8,128)S(1)} %get-tuple-element.68.taps_own_ref.taps_ref, bf16[512,624]{1,0:T(8,128)(2,1)S(1)} %get-tuple-element.67.gather_ref), custom_call_target="tpu_custom_call" | custom-call | flops 20000000000 | bytes 60000000 | tf_op jit(solution)/shard_map/pallas_call | solution.py:565
  40.3 1.9 %collective-permute-done.9 = f32[128,32]{1,0:T(8,128)S(1)} collective-permute-done((f32[128,32]{1,0:T(8,128)S(1)}, f32[128,32]{1,0:T(8,128)S(1)}, u32[]{:S(2)}, u32[]{:S(2)}) %collective-permute-start.9) | collective-permute-done | bytes 16416 | tf_op jit(solution)/shard_map/ppermute | solution.py:667
  42.4 2.1 %collective-permute-start.11 = (bf16[128,512]{1,0:T(8,128)(2,1)S(1)}, bf16[128,512]{1,0:T(8,128)(2,1)S(1)}, u32[]{:S(2)}, u32[]{:S(2)}) collective-permute-start(bf16[128,512]{1,0:T(8,128)(2,1)S(1)} %get-tuple-element.112), channel_id=1, source_target_pairs={{0,2},{1,3},{2,0},{3,1},{4,6},{5,7},{6,4},{7,5},{8,10},{9,11},{10,... | collective-permute-start | bytes 393224 | tf_op jit(solution)/shard_map/ppermute | solution.py:577
  45.2 3.9 %collective-permute-start.14 = (f32[32,32]{1,0:T(8,128)S(1)}, f32[32,32]{1,0:T(8,128)S(1)}, u32[]{:S(2)}, u32[]{:S(2)}) collective-permute-start(f32[32,32]{1,0:T(8,128)S(1)} %get-tuple-element.115), channel_id=1, source_target_pairs={{0,1},{1,17},{2,9},{3,25},{4,5},{5,21},{6,13},{7,29},{8,0},{9,16},... | collective-permute-start | bytes 12296 | tf_op jit(solution)/shard_map/ppermute | solution.py:681
  49.1 1.6 %collective-permute-start.15 = (f32[32,32]{1,0:T(8,128)S(1)}, f32[32,32]{1,0:T(8,128)S(1)}, u32[]{:S(2)}, u32[]{:S(2)}) collective-permute-start(f32[32,32]{1,0:T(8,128)S(1)} %get-tuple-element.114), channel_id=1, source_target_pairs={{0,2},{1,18},{2,10},{3,26},{4,6},{5,22},{6,14},{7,30},{8,3},{9,19}... | collective-permute-start | bytes 12296 | tf_op jit(solution)/shard_map/ppermute | solution.py:681
  50.7 4.0 %collective-permute-start.16 = (f32[32,32]{1,0:T(8,128)S(1)}, f32[32,32]{1,0:T(8,128)S(1)}, u32[]{:S(2)}, u32[]{:S(2)}) collective-permute-start(f32[32,32]{1,0:T(8,128)S(1)} %get-tuple-element.113), channel_id=1, source_target_pairs={{0,3},{1,19},{2,11},{3,27},{4,7},{5,23},{6,15},{7,31},{8,2},{9,18}... | collective-permute-start | bytes 12296 | tf_op jit(solution)/shard_map/ppermute | solution.py:681
  54.8 0.8 %shard_map.94 = (bf16[128,1024]{1,0:T(8,128)(2,1)}, bf16[128,1024]{1,0:T(8,128)(2,1)}) custom-call(bf16[512,512]{1,0:T(8,128)(2,1)S(1)} %pad_maximum_fusion.own_ref, bf16[128,512]{1,0:T(8,128)(2,1)S(1)} %collective-permute-done.10.r1, bf16[128,512]{1,0:T(8,128)(2,1)S(1)} %collective-permute-done.11.r2, bf16[128,512]{1,0:T(8,128)(2,1)S(1)} %collective-permute-done.12.r3), custom_call_target="tpu_custom_call" | custom-call | flops 1000000000 | bytes 3000000 | tf_op jit(solution)/shard_map/pallas_call | solution.py:565
  55.6 4.0 %collective-permute-done.15.q2 = f32[32,32]{1,0:T(8,128)S(1)} collective-permute-done((f32[32,32]{1,0:T(8,128)S(1)}, f32[32,32]{1,0:T(8,128)S(1)}, u32[]{:S(2)}, u32[]{:S(2)}) %collective-permute-start.15) | collective-permute-done | bytes 4128 | tf_op jit(solution)/shard_map/ppermute | solution.py:681
  59.6 0.8 %shard_map.95 = (f32[32,2048]{1,0:T(8,128)}, f32[32,31]{1,0:T(8,128)}) custom-call(bf16[32,32,512]{2,1,0:T(8,128)(2,1)S(1)} %all-to-all-done.blocks_ref, f32[32,32]{1,0:T(8,128)S(1)} %collective-permute-done.13.q0, f32[32,32]{1,0:T(8,128)S(1)} %collective-permute-done.14.q1, f32[32,32]{1,0:T(8,128)S(1)} %collective-permute-done.15.q2, ...), custom_call_target="tpu_custom_call" | custom-call | flops 1000000000 | bytes 3000000 | tf_op jit(solution)/shard_map/pallas_call | solution.py:565
  (28 shorter events, 3.4 us)
Async XLA Ops:
  1.8 4.5 %collective-permute-start = (bf16[128,512]{1,0:T(8,128)(2,1)S(1)}, bf16[128,512]{1,0:T(8,128)(2,1)S(1)}, u32[]{:S(2)}, u32[]{:S(2)}) collective-permute-start(bf16[128,512]{1,0:T(8,128)(2,1)S(1)} %get-tuple-element.62), channel_id=1, source_target_pairs={{0,1},{1,0},{2,3},{3,2},{4,5},{5,4},{6,7},{7,6},{8,9},{9,8},{10,11... | collective-permute-start | bytes 393224 | tf_op jit(solution)/shard_map/ppermute | solution.py:577
  2.3 6.9 %collective-permute-start.1 = (bf16[128,512]{1,0:T(8,128)(2,1)S(1)}, bf16[128,512]{1,0:T(8,128)(2,1)S(1)}, u32[]{:S(2)}, u32[]{:S(2)}) collective-permute-start(bf16[128,512]{1,0:T(8,128)(2,1)S(1)} %get-tuple-element.64), channel_id=1, source_target_pairs={{0,2},{1,3},{2,0},{3,1},{4,6},{5,7},{6,4},{7,5},{8,10},{9,11},{10,... | collective-permute-start | bytes 393224 | tf_op jit(solution)/shard_map/ppermute | solution.py:577
  4.9 6.6 %collective-permute-start.2 = (bf16[128,512]{1,0:T(8,128)(2,1)S(1)}, bf16[128,512]{1,0:T(8,128)(2,1)S(1)}, u32[]{:S(2)}, u32[]{:S(2)}) collective-permute-start(bf16[128,512]{1,0:T(8,128)(2,1)S(1)} %get-tuple-element.65), channel_id=1, source_target_pairs={{0,3},{1,2},{2,1},{3,0},{4,7},{5,6},{6,5},{7,4},{8,11},{9,10},{10,... | collective-permute-start | bytes 393224 | tf_op jit(solution)/shard_map/ppermute | solution.py:577
  6.3 9.2 %collective-permute-start.3 = (bf16[128,256]{1,0:T(8,128)(2,1)S(1)}, bf16[128,256]{1,0:T(8,128)(2,1)S(1)}, u32[]{:S(2)}, u32[]{:S(2)}) collective-permute-start(bf16[128,256]{1,0:T(8,128)(2,1)S(1)} %get-tuple-element.72), channel_id=1, source_target_pairs={{0,1},{1,0},{2,3},{3,2},{4,5},{5,4},{6,7},{7,6},{8,9},{9,8},{10,11... | collective-permute-start | bytes 196616 | tf_op jit(solution)/shard_map/ppermute | solution.py:577
  6.5 9.1 %collective-permute-start.4 = (bf16[128,256]{1,0:T(8,128)(2,1)S(1)}, bf16[128,256]{1,0:T(8,128)(2,1)S(1)}, u32[]{:S(2)}, u32[]{:S(2)}) collective-permute-start(bf16[128,256]{1,0:T(8,128)(2,1)S(1)} %get-tuple-element.73), channel_id=1, source_target_pairs={{0,2},{1,3},{2,0},{3,1},{4,6},{5,7},{6,4},{7,5},{8,10},{9,11},{10,... | collective-permute-start | bytes 196616 | tf_op jit(solution)/shard_map/ppermute | solution.py:577
  8.4 7.1 %collective-permute-start.5 = (bf16[128,256]{1,0:T(8,128)(2,1)S(1)}, bf16[128,256]{1,0:T(8,128)(2,1)S(1)}, u32[]{:S(2)}, u32[]{:S(2)}) collective-permute-start(bf16[128,256]{1,0:T(8,128)(2,1)S(1)} %get-tuple-element.74), channel_id=1, source_target_pairs={{0,3},{1,2},{2,1},{3,0},{4,7},{5,6},{6,5},{7,4},{8,11},{9,10},{10,... | collective-permute-start | bytes 196616 | tf_op jit(solution)/shard_map/ppermute | solution.py:577
  15.5 2.0 %collective-permute-start.6 = (bf16[512,512]{1,0:T(8,128)(2,1)S(1)}, bf16[512,512]{1,0:T(8,128)(2,1)S(1)}, u32[]{:S(2)}, u32[]{:S(2)}) collective-permute-start(bf16[512,512]{1,0:T(8,128)(2,1)S(1)} %get-tuple-element.75.hid_ref), channel_id=1, source_target_pairs={{0,1},{1,0},{2,3},{3,2},{4,5},{5,4},{6,7},{7,6},{8,9},{9,8},{10,11... | collective-permute-start | bytes 1572872 | tf_op jit(solution)/shard_map/ppermute | solution.py:577
  22.9 2.0 %collective-permute-start.7 = (bf16[512,512]{1,0:T(8,128)(2,1)S(1)}, bf16[512,512]{1,0:T(8,128)(2,1)S(1)}, u32[]{:S(2)}, u32[]{:S(2)}) collective-permute-start(bf16[512,512]{1,0:T(8,128)(2,1)S(1)} %get-tuple-element.90), channel_id=1, source_target_pairs={{0,1},{1,0},{2,3},{3,2},{4,5},{5,4},{6,7},{7,6},{8,9},{9,8},{10,11... | collective-permute-start | bytes 1572872 | tf_op jit(solution)/shard_map/ppermute | solution.py:577
  25.0 8.8 %collective-permute-start.8 = (bf16[512,256]{1,0:T(8,128)(2,1)S(1)}, bf16[512,256]{1,0:T(8,128)(2,1)S(1)}, u32[]{:S(2)}, u32[]{:S(2)}) collective-permute-start(bf16[512,256]{1,0:T(8,128)(2,1)S(1)} %get-tuple-element.94), channel_id=1, source_target_pairs={{0,2},{1,3},{2,0},{3,1},{4,6},{5,7},{6,4},{7,5},{8,10},{9,11},{10,... | collective-permute-start | bytes 786440 | tf_op jit(solution)/shard_map/ppermute | solution.py:577
  27.2 32.4 %all-to-all-start = ((bf16[32,32,512]{2,1,0:T(8,128)(2,1)}), bf16[32,32,512]{2,1,0:T(8,128)(2,1)S(1)}, u32[]{:S(2)}, u32[]{:S(2)}) async-start(bf16[32,32,512]{2,1,0:T(8,128)(2,1)} %bitcast.5), calls=%async_computation | async-start | bytes 2097152 | tf_op jit(solution)/shard_map/all_to_all | solution.py:653
  36.7 5.5 %collective-permute-start.9 = (f32[128,32]{1,0:T(8,128)S(1)}, f32[128,32]{1,0:T(8,128)S(1)}, u32[]{:S(2)}, u32[]{:S(2)}) collective-permute-start(f32[128,32]{1,0:T(8,128)S(1)} %get-tuple-element.97), channel_id=1, source_target_pairs={{0,4},{4,0},{8,12},{12,8},{16,20},{20,16},{24,28},{28,24},{1,5},{5... | collective-permute-start | bytes 49160 | tf_op jit(solution)/shard_map/ppermute | solution.py:667
  42.2 2.3 %collective-permute-start.10 = (bf16[128,512]{1,0:T(8,128)(2,1)S(1)}, bf16[128,512]{1,0:T(8,128)(2,1)S(1)}, u32[]{:S(2)}, u32[]{:S(2)}) collective-permute-start(bf16[128,512]{1,0:T(8,128)(2,1)S(1)} %get-tuple-element.111), channel_id=1, source_target_pairs={{0,1},{1,0},{2,3},{3,2},{4,5},{5,4},{6,7},{7,6},{8,9},{9,8},{10,11... | collective-permute-start | bytes 393224 | tf_op jit(solution)/shard_map/ppermute | solution.py:577
  42.4 8.4 %collective-permute-start.11 = (bf16[128,512]{1,0:T(8,128)(2,1)S(1)}, bf16[128,512]{1,0:T(8,128)(2,1)S(1)}, u32[]{:S(2)}, u32[]{:S(2)}) collective-permute-start(bf16[128,512]{1,0:T(8,128)(2,1)S(1)} %get-tuple-element.112), channel_id=1, source_target_pairs={{0,2},{1,3},{2,0},{3,1},{4,6},{5,7},{6,4},{7,5},{8,10},{9,11},{10,... | collective-permute-start | bytes 393224 | tf_op jit(solution)/shard_map/ppermute | solution.py:577
  44.4 10.3 %collective-permute-start.12 = (bf16[128,512]{1,0:T(8,128)(2,1)S(1)}, bf16[128,512]{1,0:T(8,128)(2,1)S(1)}, u32[]{:S(2)}, u32[]{:S(2)}) collective-permute-start(bf16[128,512]{1,0:T(8,128)(2,1)S(1)} %get-tuple-element.110), channel_id=1, source_target_pairs={{0,3},{1,2},{2,1},{3,0},{4,7},{5,6},{6,5},{7,4},{8,11},{9,10},{10,... | collective-permute-start | bytes 393224 | tf_op jit(solution)/shard_map/ppermute | solution.py:577
  44.6 11.0 %collective-permute-start.13 = (f32[32,32]{1,0:T(8,128)S(1)}, f32[32,32]{1,0:T(8,128)S(1)}, u32[]{:S(2)}, u32[]{:S(2)}) collective-permute-start(f32[32,32]{1,0:T(8,128)S(1)} %get-tuple-element.116), channel_id=1, source_target_pairs={{0,0},{1,16},{2,8},{3,24},{4,4},{5,20},{6,12},{7,28},{8,1},{9,17},... | collective-permute-start | bytes 12296 | tf_op jit(solution)/shard_map/ppermute | solution.py:681
  45.2 10.4 %collective-permute-start.14 = (f32[32,32]{1,0:T(8,128)S(1)}, f32[32,32]{1,0:T(8,128)S(1)}, u32[]{:S(2)}, u32[]{:S(2)}) collective-permute-start(f32[32,32]{1,0:T(8,128)S(1)} %get-tuple-element.115), channel_id=1, source_target_pairs={{0,1},{1,17},{2,9},{3,25},{4,5},{5,21},{6,13},{7,29},{8,0},{9,16},... | collective-permute-start | bytes 12296 | tf_op jit(solution)/shard_map/ppermute | solution.py:681
  49.1 10.5 %collective-permute-start.15 = (f32[32,32]{1,0:T(8,128)S(1)}, f32[32,32]{1,0:T(8,128)S(1)}, u32[]{:S(2)}, u32[]{:S(2)}) collective-permute-start(f32[32,32]{1,0:T(8,128)S(1)} %get-tuple-element.114), channel_id=1, source_target_pairs={{0,2},{1,18},{2,10},{3,26},{4,6},{5,22},{6,14},{7,30},{8,3},{9,19}... | collective-permute-start | bytes 12296 | tf_op jit(solution)/shard_map/ppermute | solution.py:681
  50.7 8.9 %collective-permute-start.16 = (f32[32,32]{1,0:T(8,128)S(1)}, f32[32,32]{1,0:T(8,128)S(1)}, u32[]{:S(2)}, u32[]{:S(2)}) collective-permute-start(f32[32,32]{1,0:T(8,128)S(1)} %get-tuple-element.113), channel_id=1, source_target_pairs={{0,3},{1,19},{2,11},{3,27},{4,7},{5,23},{6,15},{7,31},{8,2},{9,18}... | collective-permute-start | bytes 12296 | tf_op jit(solution)/shard_map/ppermute | solution.py:681

commit v7 on v6

--- a/solution.py
+++ b/solution.py
@@ -13,6 +13,7 @@
 RIM = KERNEL // 2
 SUB = 8
 CHUNK = 6
+LONGEST = 384
 SWAP = (0, 2, 1, 3)
 
 
@@ -200,8 +201,17 @@
     return ((own_index ^ (row >> shift)) << shift) + (row & (row_count - 1))
 
 
-def spaced_pos(len_ref, row, own_index, row_count):
-    frame_pos = frame_at(row, own_index, row_count)
+def sorted_frame(len_ref, row):
+    first, longest, start = jnp.int32(0), jnp.int32(0), jnp.int32(0)
+    for utt in range(len_ref.shape[1]):
+        length = len_ref[0, utt]
+        first = jnp.where(length > longest, start, first)
+        longest = jnp.maximum(length, longest)
+        start = start + length
+    return jnp.where(row < LONGEST, row + first, jnp.where(row < LONGEST + first, row - LONGEST, row))
+
+
+def spaced_pos(len_ref, frame_pos):
     return frame_pos + RIM * utt_index(len_ref, frame_pos)
 
 
@@ -210,18 +220,22 @@
     return -(-rows // (SUB * CHUNK)) * CHUNK
 
 
-def spread_matrix(len_ref, own_index, row_count, seq_total, steps):
-    slot = lax.broadcasted_iota(jnp.int32, (steps * SUB, seq_total), 0)
-    slot_pos = (slot & (SUB - 1)) * steps + (slot >> 3)
-    row = lax.broadcasted_iota(jnp.int32, (1, seq_total), 1)
-    return (slot_pos == spaced_pos(len_ref, row, own_index, row_count)).astype(jnp.float32).astype(jnp.bfloat16)
-
-
-def gather_matrix(len_ref, own_index, row_count, seq_total, steps):
+def one_hot(left, right):
+    return (left == right).astype(jnp.float32).astype(jnp.bfloat16)
+
+
+def spread_matrix(len_ref, frame_pos, steps):
+    slot = lax.broadcasted_iota(jnp.int32, (steps * SUB, frame_pos.shape[1]), 0)
+    return one_hot((slot & (SUB - 1)) * steps + (slot >> 3), spaced_pos(len_ref, frame_pos))
+
+
+def gather_matrix(len_ref, frame_pos, steps):
     slot = lax.broadcasted_iota(jnp.int32, (1, steps * SUB), 1)
-    slot_pos = (slot & (SUB - 1)) * steps + (slot >> 3)
-    row = lax.broadcasted_iota(jnp.int32, (seq_total, 1), 0)
-    return (slot_pos == spaced_pos(len_ref, row, own_index, row_count)).astype(jnp.float32).astype(jnp.bfloat16)
+    return one_hot((slot & (SUB - 1)) * steps + (slot >> 3), spaced_pos(len_ref, frame_pos))
+
+
+def row_and_column(size):
+    return lax.broadcasted_iota(jnp.int32, (size, 1), 0), lax.broadcasted_iota(jnp.int32, (1, size), 1)
 
 
 def write_extended(ext_ref, spaced, steps):
@@ -283,8 +297,9 @@
     for load in loads:
         load.start()
     loads[0].wait()
-    spread_ref[...] = spread_matrix(len_ref, own_index, row_count, seq_total, steps)
-    gather_ref[...] = gather_matrix(len_ref, own_index, row_count, seq_total, steps)
+    row, column = row_and_column(seq_total)
+    spread_ref[...] = spread_matrix(len_ref, frame_at(column, own_index, row_count), steps)
+    gather_ref[...] = gather_matrix(len_ref, sorted_frame(len_ref, row), steps)
     for load in loads[1:]:
         load.wait()
     for taps_ref, w_ref in ((taps_own_ref, w_own_ref), (taps_oth_ref, w_oth_ref)):
@@ -334,10 +349,6 @@
         copy.wait()
 
 
-def swapped(array, order, row_count):
-    return jnp.concatenate([array[b * row_count : (b + 1) * row_count] for b in order], axis=0)
-
-
 def w_rows(ref, group, j):
     width = ref.shape[1]
     return ref[pl.ds(pl.multiple_of((group ^ j) * width, width), width), :]
@@ -356,14 +367,16 @@
         terms = [jnp.dot(part, w_rows(ref, group, j), preferred_element_type=jnp.float32) for j, part in enumerate(parts)]
         kv_ref[:, n * width : (n + 1) * width] = sum(terms)
     cot = jnp.concatenate([f[...] for f in (f0, f1, f2, f3)], axis=0)
-    cot_ref[...] = cot
-    cott_ref[...] = cot.T.astype(jnp.float32)
     load.wait()
-    key_row = lax.broadcasted_iota(jnp.int32, (seq_total, 1), 0)
-    query_row = lax.broadcasted_iota(jnp.int32, (1, seq_total), 1)
-    key_utt = utt_index(len_ref, frame_at(key_row, own_index, row_count))
-    query_utt = utt_index(len_ref, frame_at(query_row, own_index, row_count))
-    bias_ref[...] = jnp.where(key_utt == query_utt, 0.0, -jnp.inf).astype(jnp.float32)
+    row, column = row_and_column(seq_total)
+    order = one_hot(sorted_frame(len_ref, row), frame_at(column, own_index, row_count))
+    cot = jnp.dot(order, cot, preferred_element_type=jnp.float32)
+    cot_ref[...] = cot.astype(jnp.bfloat16)
+    cott_ref[...] = cot.T
+    row, column = row_and_column(seq_total - LONGEST)
+    row_utt = utt_index(len_ref, sorted_frame(len_ref, row + LONGEST))
+    column_utt = utt_index(len_ref, sorted_frame(len_ref, column + LONGEST))
+    bias_ref[...] = jnp.where(row_utt == column_utt, 0.0, -jnp.inf).astype(jnp.float32)
 
 
 def attention_kernel(
@@ -377,7 +390,7 @@
     bf16, f32 = jnp.bfloat16, jnp.float32
     keys, values = kv_ref[:, :width], kv_ref[:, width:]
     for j in (2, 3):
-        part = swapped(sib_ref[:, (j - 2) * width : (j - 1) * width], (1, 0, 3, 2), seq_total // 4)
+        part = sib_ref[:, (j - 2) * width : (j - 1) * width]
         keys = keys + jnp.dot(part, w_rows(wk_ref, group, j), preferred_element_type=f32)
         values = values + jnp.dot(part, w_rows(wv_ref, group, j), preferred_element_type=f32)
     keys, values = keys.astype(bf16), values.astype(bf16)
@@ -388,34 +401,72 @@
     lane = lax.broadcasted_iota(jnp.int32, (1, 128), 1)
     masks = [(lane < head_width).astype(f32).astype(bf16), (lane >= head_width).astype(f32).astype(bf16)]
     exp_scale = scale * math.log2(math.e)
+    rows = slice(0, LONGEST)
     for first in range(0, width, 128):
         lanes = slice(first, first + 128)
-        query = hid_ref[:, lanes]
-        grad = cot_ref[:, lanes]
-        k_pair = k_ref[:, lanes]
-        v_pair = v_ref[:, lanes]
-        dk_pair = None
-        dv_pair = None
+        queries = jnp.concatenate([hid_ref[rows, lanes] * mask for mask in masks], axis=0)
+        grads = jnp.concatenate([cot_ref[rows, lanes] * mask for mask in masks], axis=0)
+        scores = nt_dot(k_ref[rows, lanes], queries)
+        top = jnp.max(scores, axis=0, keepdims=True)
+        expd = jnp.exp2((scores - top) * exp_scale)
+        probs = expd * (1.0 / jnp.sum(expd, axis=0, keepdims=True))
+        probs_low = probs.astype(bf16)
+        dprobs = nt_dot(v_ref[rows, lanes], grads)
+        rowdots = []
         for head in range(2):
-            mask = masks[head]
             hrows = slice(first + head * head_width, first + (head + 1) * head_width)
-            scores = nt_dot(k_pair * mask, query) + bias_ref[...]
-            top = jnp.max(scores, axis=0, keepdims=True)
-            expd = jnp.exp2((scores - top) * exp_scale)
-            probs = expd * (1.0 / jnp.sum(expd, axis=0, keepdims=True))
-            probs_low = probs.astype(bf16)
-            attended = jnp.dot(vt_ref[hrows, :], probs_low, preferred_element_type=f32)
-            dprobs = nt_dot(v_pair * mask, grad)
-            rowdot = jnp.sum(cott_ref[hrows, :] * attended, axis=0, keepdims=True)
-            dscores = (probs * (dprobs - rowdot)).astype(bf16)
-            attt_ref[hrows, :] = attended
-            dqt_ref[hrows, :] = jnp.dot(kt_ref[hrows, :], dscores, preferred_element_type=f32) * scale
-            dk_head = jnp.dot(dscores, query * mask, preferred_element_type=f32)
-            dv_head = jnp.dot(probs_low, grad * mask, preferred_element_type=f32)
-            dk_pair = dk_head if head == 0 else dk_pair + dk_head
-            dv_pair = dv_head if head == 0 else dv_pair + dv_head
-        dk_ref[:, lanes] = dk_pair
-        dv_ref[:, lanes] = dv_pair
+            part = slice(head * LONGEST, (head + 1) * LONGEST)
+            attended = jnp.dot(vt_ref[hrows, rows], probs_low[:, part], preferred_element_type=f32)
+            attt_ref[hrows, rows] = attended
+            rowdots.append(jnp.sum(cott_ref[hrows, rows] * attended, axis=0, keepdims=True))
+        dscores = (probs * (dprobs - jnp.concatenate(rowdots, axis=1))).astype(bf16)
+        for head in range(2):
+            hrows = slice(first + head * head_width, first + (head + 1) * head_width)
+            part = slice(head * LONGEST, (head + 1) * LONGEST)
+            dqt_ref[hrows, rows] = jnp.dot(kt_ref[hrows, rows], dscores[:, part], preferred_element_type=f32) * scale
+        dk_ref[rows, lanes] = jnp.dot(dscores, queries, preferred_element_type=f32)
+        dv_ref[rows, lanes] = jnp.dot(probs_low, grads, preferred_element_type=f32)
+    heads = [(first, head) for first in range(0, width, 128) for head in range(2)]
+    rows = slice(LONGEST, seq_total)
+    size = seq_total - LONGEST
+
+    def all_heads(left_ref, right_ref):
+        return jnp.concatenate(
+            [
+                nt_dot(left_ref[rows, f : f + 128] * masks[h], right_ref[rows, f : f + 128])
+                for f, h in heads
+            ],
+            axis=1,
+        )
+
+    bias = jnp.concatenate([bias_ref[...]] * len(heads), axis=1)
+    scores = all_heads(k_ref, hid_ref) + bias
+    dprobs = all_heads(v_ref, cot_ref)
+    top = jnp.max(scores, axis=0, keepdims=True)
+    expd = jnp.exp2((scores - top) * exp_scale)
+    probs = expd * (1.0 / jnp.sum(expd, axis=0, keepdims=True))
+    probs_low = probs.astype(bf16)
+    rowdots = []
+    for n, (first, head) in enumerate(heads):
+        hrows = slice(first + head * head_width, first + (head + 1) * head_width)
+        attended = jnp.dot(vt_ref[hrows, rows], probs_low[:, n * size : (n + 1) * size], preferred_element_type=f32)
+        attt_ref[hrows, rows] = attended
+        rowdots.append(jnp.sum(cott_ref[hrows, rows] * attended, axis=0, keepdims=True))
+    dscores = (probs * (dprobs - jnp.concatenate(rowdots, axis=1))).astype(bf16)
+    for first in range(0, width, 128):
+        lanes = slice(first, first + 128)
+        sums = [None, None]
+        for head in range(2):
+            n = 2 * (first // 128) + head
+            part = slice(n * size, (n + 1) * size)
+            hrows = slice(first + head * head_width, first + (head + 1) * head_width)
+            dqt_ref[hrows, rows] = jnp.dot(kt_ref[hrows, rows], dscores[:, part], preferred_element_type=f32) * scale
+            terms = [
+                jnp.dot(dscores[:, part], hid_ref[rows, lanes] * masks[head], preferred_element_type=f32),
+                jnp.dot(probs_low[:, part], cot_ref[rows, lanes] * masks[head], preferred_element_type=f32),
+            ]
+            sums = terms if head == 0 else [x + y for x, y in zip(sums, terms, strict=True)]
+        dk_ref[rows, lanes], dv_ref[rows, lanes] = sums
     grad_k = (dk_ref[...] * scale).astype(bf16)
     grad_v = dv_ref[...].astype(bf16)
     kvg_ref[:, :width] = grad_k
@@ -425,22 +476,17 @@
         send_ref[:, (j - 2) * width : (j - 1) * width] = part.astype(bf16)
 
 
-def output_kernel(hid_ref, attt_ref, out_ref):
-    out_ref[...] = (hid_ref[:, : out_ref.shape[1]].astype(jnp.float32) + attt_ref[...].T).astype(jnp.bfloat16)
-
-
 def weight_grad_kernel(
     hid_ref, sib_ref, kvg_ref, dqt_ref, cot_ref, wk_ref, wv_ref, out_hbm, keep_ref, all_ref, sems
 ):
     group = device_group()
     width = cot_ref.shape[1]
-    row_count = hid_ref.shape[0] // 4
     kvg = kvg_ref[...]
     parts = [
         hid_ref[:, :width],
         hid_ref[:, width:],
-        swapped(sib_ref[:, :width], (1, 0, 3, 2), row_count),
-        swapped(sib_ref[:, width:], (1, 0, 3, 2), row_count),
+        sib_ref[:, :width],
+        sib_ref[:, width:],
     ]
     saves = []
     for j in range(4):
@@ -459,8 +505,7 @@
 
 def chip_sum_kernel(keep_ref, recv_ref, own_ref, send_ref):
     width = keep_ref.shape[1] // 2
-    row_count = keep_ref.shape[0] // 4
-    total = keep_ref[...] + swapped(recv_ref[...], (1, 0, 3, 2), row_count).astype(jnp.float32)
+    total = keep_ref[...] + recv_ref[...].astype(jnp.float32)
     own_ref[...] = total[:, :width]
     send_ref[...] = total[:, width:].astype(jnp.bfloat16)
 
@@ -469,9 +514,8 @@
     own_ref, recv_ref, xext_hbm, conv_hbm, len_hbm, dh_ref, ext_ref, dw_keep_ref, dw_send_ref,
     xext_ref, conv_ref, len_ref, gdw_ref, sems,
 ):
-    own_index, dp_index = lax.axis_index("ctx"), lax.axis_index("dp")
+    dp_index = lax.axis_index("dp")
     seq_total, width = own_ref.shape
-    row_count = seq_total // 4
     steps = conv_ref.shape[0]
     bf16, f32 = jnp.bfloat16, jnp.float32
     loads = [
@@ -481,11 +525,12 @@
     ]
     for load in loads:
         load.start()
-    dhidden = own_ref[...] + swapped(recv_ref[...], (2, 3, 0, 1), row_count).astype(f32)
+    dhidden = own_ref[...] + recv_ref[...].astype(f32)
     high = dhidden.astype(bf16)
     low = (dhidden - high.astype(f32)).astype(bf16)
     loads[0].wait()
-    spread = spread_matrix(len_ref, own_index, row_count, seq_total, steps)
+    _, column = row_and_column(seq_total)
+    spread = spread_matrix(len_ref, sorted_frame(len_ref, column), steps)
     both = jnp.dot(spread, jnp.concatenate([high, low], axis=1), preferred_element_type=f32)
     spaced = both[:, :width] + both[:, width:]
     dh_ref[...] = spaced.reshape(steps, SUB, width)
@@ -521,7 +566,11 @@
     dw_send_ref[...] = gdw_ref[:, pl.ds(pl.multiple_of((1 - side) * half, half), half)].T
 
 
-def frame_grad_kernel(dh_ref, ext_ref, taps_ref, gather_ref, dframes_ref, df_ref):
+def frame_grad_kernel(
+    dh_ref, ext_ref, taps_ref, hid_ref, attt_ref, len_hbm, dframes_ref, out_ref, df_ref, len_ref, sem
+):
+    load = pltpu.make_async_copy(len_hbm, len_ref, sem)
+    load.start()
     width = dframes_ref.shape[1]
     steps = dh_ref.shape[0]
     for lane in range(0, width, 128):
@@ -532,7 +581,15 @@
 
         conv_loop(ext_ref, taps_ref, lanes, steps, True, finish)
     df_low = df_ref[...].reshape(steps * SUB, width).astype(jnp.bfloat16)
-    dframes_ref[...] = jnp.dot(gather_ref[...], df_low, preferred_element_type=jnp.float32).astype(jnp.bfloat16)
+    output = (hid_ref[:, :width].astype(jnp.float32) + attt_ref[...].T).astype(jnp.bfloat16)
+    load.wait()
+    seq_total = dframes_ref.shape[0]
+    row, column = row_and_column(seq_total)
+    own_rows = frame_at(row, lax.axis_index("ctx"), seq_total // 4)
+    gather = gather_matrix(len_ref, own_rows, steps)
+    dframes_ref[...] = jnp.dot(gather, df_low, preferred_element_type=jnp.float32).astype(jnp.bfloat16)
+    order = one_hot(own_rows, sorted_frame(len_ref, column))
+    out_ref[...] = jnp.dot(order, output, preferred_element_type=jnp.float32).astype(jnp.bfloat16)
 
 
 def place_kernel(own_ref, r1, r2, r3, out_ref, dframes_ref):
@@ -627,7 +684,7 @@
     hidden_sib = swap_ctx(hidden, 1)
     kv_part, cot_own, cot_turned, bias = call(
         ready_kernel, (utt_lengths, hidden, *cots, w_keys, w_values),
-        [(both, f32), (wide, bf16), (tall, f32), ((seq_total, seq_total), f32)],
+        [(both, f32), (wide, bf16), (tall, f32), ((seq_total - LONGEST,) * 2, f32)],
         [pltpu.SMEM(utt_lengths.shape, jnp.int32), pltpu.SemaphoreType.DMA], hbm_in=(0,), cost_us=2,
     )
     att_turned, dq_turned, send, kv_grad = call(
@@ -639,7 +696,6 @@
         ],
         vmem_mib=14, cost_us=8,
     )
-    (out_own,) = call(output_kernel, (hidden, att_turned), [(wide, bf16)], cost_us=1)
     part_kv, keep = call(
         weight_grad_kernel, (hidden, hidden_sib, kv_grad, dq_turned, cot_own, w_keys, w_values),
         [((feat_width, 2 * width), bf16), (both, f32)],
@@ -660,9 +716,10 @@
         ],
         hbm_in=(2, 3, 4), cost_us=100,
     )
-    (dframes,) = call(
-        frame_grad_kernel, (dhidden, dconv_ext, taps_own, gather), [(wide, bf16)], [pltpu.VMEM(short, f32)],
-        cost_us=20,
+    dframes, out_own = call(
+        frame_grad_kernel, (dhidden, dconv_ext, taps_own, hidden, att_turned, utt_lengths), [(wide, bf16), (wide, bf16)],
+        [pltpu.VMEM(short, f32), pltpu.SMEM(utt_lengths.shape, jnp.int32), pltpu.SemaphoreType.DMA],
+        hbm_in=(5,), cost_us=20,
     )
     dw_recv = lax.ppermute(dw_send, "dp", [(i, i ^ 1) for i in range(dp_size)])
     dw_recv, dframes = lax.optimization_barrier((dw_recv, dframes))

time: 60.8 us -> 59 us (0.970)
  Pallas kernels: 21.1 us -> 20 us
    pallas_call x12 -> x11, Pallas kernels: 21.1 us -> 20 us  [call(): pl.pallas_call(kernel, out_shape=[jax.ShapeDtypeStruct(*o) if to_hbm else...]
  transfers between devices with their start and end apart: 18 -> 18, of which waited for: 6 -> 6; matrix products, arithmetic and copies ran while one was open for 0% -> 0% of each run, Pallas kernels for 23% -> 24%
where the time goes in v7:
time: 59 us; the launch traced here: 58.6 us
  starting transfers between devices  27.3 us (46%)
  Pallas kernels  20 us (34%)
  waiting for transfers between devices  10.5 us (18%)
  between operations  0.83 us (1%)
    pallas_call x11, Pallas kernels, call(): pl.pallas_call(kernel, out_shape=[jax.ShapeDtypeStruct(*o) if to_hbm else...  20 us
    ppermute x12, starting transfers between devices, swap_ctx(): return lax.ppermute(array, 'ctx', [(i, i ^ j) for i in range(4)])  10.2 us
    ppermute x4, starting transfers between devices, on_device_pairs(): quarters.append(lax.ppermute(quarter, ('dp', 'ctx'), pairs))  10.2 us
    ppermute x12, waiting for transfers between devices, swap_ctx(): return lax.ppermute(array, 'ctx', [(i, i ^ j) for i in range(4)])  5.13 us
    all_to_all x1, starting transfers between devices, on_device_pairs(): lax.all_to_all(part_kv.reshape(4 * dp_size, piece, 2 * width), ('dp', 'ct...  5.1 us
    ppermute x4, waiting for transfers between devices, on_device_pairs(): quarters.append(lax.ppermute(quarter, ('dp', 'ctx'), pairs))  3.98 us
    ppermute x1, starting transfers between devices, on_device_pairs(): dw_recv = lax.ppermute(dw_send, 'dp', [(i, i ^ 1) for i in range(dp_size)])  1.84 us
    ppermute x1, waiting for transfers between devices, on_device_pairs(): dw_recv = lax.ppermute(dw_send, 'dp', [(i, i ^ 1) for i in range(dp_size)])  1.33 us
  transfers between devices with their start and end apart: 18, of which 6 were waited for; matrix products, arithmetic and copies ran while one was open for 0% of the time, Pallas kernels for 24%

profile of v7, /device:TPU:0, one launch (start us, length us, event | category | flops | bytes accessed | tf_op | source)
XLA Modules:
  0.0 58.6 jit_solution(17264081727534484246)
XLA Ops:
  0.6 1.1 %shard_map.84 = (bf16[128,512]{1,0:T(8,128)(2,1)S(1)}, bf16[128,512]{1,0:T(8,128)(2,1)S(1)}, bf16[128,512]{1,0:T(8,128)(2,1)S(1)}, bf16[128,512]{1,0:T(8,128)(2,1)S(1)}) custom-call(bf16[128,1024]{1,0:T(8,128)(2,1)} %bitcast.6), custom_call_target="tpu_custom_call" | custom-call | flops 1000000000 | bytes 3000000 | tf_op jit(solution)/shard_map/pallas_call | solution.py:622
  2.3 2.6 %collective-permute-start.1 = (bf16[128,512]{1,0:T(8,128)(2,1)S(1)}, bf16[128,512]{1,0:T(8,128)(2,1)S(1)}, u32[]{:S(2)}, u32[]{:S(2)}) collective-permute-start(bf16[128,512]{1,0:T(8,128)(2,1)S(1)} %get-tuple-element.66), channel_id=1, source_target_pairs={{0,2},{1,3},{2,0},{3,1},{4,6},{5,7},{6,4},{7,5},{8,10},{9,11},{10,... | collective-permute-start | bytes 393224 | tf_op jit(solution)/shard_map/ppermute | solution.py:634
  4.9 1.3 %shard_map.85 = (bf16[624,512]{1,0:T(8,128)(2,1)S(1)}, bf16[512,624]{1,0:T(8,128)(2,1)S(1)}, f32[31,8,256]{2,1,0:T(8,128)S(1)}, f32[31,8,256]{2,1,0:T(8,128)S(1)...) custom-call(s32[1,8]{1,0:T(1,128)} %len_hbm.7, ...), custom_call_target="tpu_custom_call" | custom-call | flops 2000000000 | bytes 6000000 | tf_op jit(solution)/shard_map/pallas_call | solution.py:622
  6.5 1.9 %collective-permute-start.4 = (bf16[128,256]{1,0:T(8,128)(2,1)S(1)}, bf16[128,256]{1,0:T(8,128)(2,1)S(1)}, u32[]{:S(2)}, u32[]{:S(2)}) collective-permute-start(bf16[128,256]{1,0:T(8,128)(2,1)S(1)} %get-tuple-element.75), channel_id=1, source_target_pairs={{0,2},{1,3},{2,0},{3,1},{4,6},{5,7},{6,4},{7,5},{8,10},{9,11},{10,... | collective-permute-start | bytes 196616 | tf_op jit(solution)/shard_map/ppermute | solution.py:634
  8.4 0.8 %collective-permute-done.1.f2 = bf16[128,512]{1,0:T(8,128)(2,1)S(1)} collective-permute-done((bf16[128,512]{1,0:T(8,128)(2,1)S(1)}, bf16[128,512]{1,0:T(8,128)(2,1)S(1)}, u32[]{:S(2)}, u32[]{:S(2)}) %collective-permute-start.1) | collective-permute-done | bytes 131104 | tf_op jit(solution)/shard_map/ppermute | solution.py:634
  9.2 2.3 %collective-permute-done.2.f3 = bf16[128,512]{1,0:T(8,128)(2,1)S(1)} collective-permute-done((bf16[128,512]{1,0:T(8,128)(2,1)S(1)}, bf16[128,512]{1,0:T(8,128)(2,1)S(1)}, u32[]{:S(2)}, u32[]{:S(2)}) %collective-permute-start.2) | collective-permute-done | bytes 131104 | tf_op jit(solution)/shard_map/ppermute | solution.py:634
  11.5 4.0 %shard_map.86 = (bf16[512,512]{1,0:T(8,128)(2,1)S(1)}, bf16[1024,256]{1,0:T(8,128)(2,1)S(1)}, bf16[1024,256]{1,0:T(8,128)(2,1)S(1)}, f32[108,8,256]{2,1,0:T(8,128)}, f32[78,8,256]{2,1,0:T(8,128)}) custom-call(bf16[128,512]{1,0:T(8,128)(2,1)S(1)} %get-tuple-element.59.f0, bf16[128,512]{1,0:T(8,128)(2,1)S(1)} %collective-permute-done.f1, ...), custom_call_target="tpu_custom_call" | custom-call | flops 20000000000 | bytes 60000000 | tf_op jit(solution)/shard_map/pallas_call | solution.py:622
  16.0 1.2 %shard_map.87 = (f32[512,512]{1,0:T(8,128)S(1)}, bf16[512,256]{1,0:T(8,128)(2,1)S(1)}, f32[256,512]{1,0:T(8,128)S(1)}, f32[128,128]{1,0:T(8,128)S(1)}) custom-call(s32[1,8]{1,0:T(1,128)} %len_hbm.7, bf16[512,512]{1,0:T(8,128)(2,1)S(1)} %get-tuple-element.77.hid_ref, bf16[128,256]{1,0:T(8,128)(2,1)S(1)} %get-tuple-element.78.f0, ...), custom_call_target="tpu_custom_call" | custom-call | flops 2000000000 | bytes 6000000 | tf_op jit(solution)/shard_map/pallas_call | solution.py:622
  17.5 3.7 %shard_map.88 = (f32[256,512]{1,0:T(8,128)S(1)}, f32[256,512]{1,0:T(8,128)S(1)}, bf16[512,512]{1,0:T(8,128)(2,1)S(1)}, bf16[512,512]{1,0:T(8,128)(2,1)S(1)}) custom-call(bf16[512,512]{1,0:T(8,128)(2,1)S(1)} %get-tuple-element.77.hid_ref, bf16[512,512]{1,0:T(8,128)(2,1)S(1)} %collective-permute-done.6.sib_ref, f32[512,512]{1,0:T(8,128)S(1)} %get-tuple-element.84.kv_ref, ...), custom_call_target="tpu_custom_call" | custom-call | flops 8000000000 | bytes 24000000 | tf_op jit(solution)/shard_map/pallas_call | solution.py:622
  21.6 1.6 %shard_map.89 = (bf16[1024,512]{1,0:T(8,128)(2,1)}, f32[512,512]{1,0:T(8,128)S(1)}) custom-call(bf16[512,512]{1,0:T(8,128)(2,1)S(1)} %get-tuple-element.77.hid_ref, bf16[512,512]{1,0:T(8,128)(2,1)S(1)} %collective-permute-done.6.sib_ref, bf16[512,512]{1,0:T(8,128)(2,1)S(1)} %get-tuple-element.88.kvg_ref, f32[256,512]{1,0:T(8,128)S(1)} %get-tuple-element.89.dqt_ref, ...), custom_call_target="tpu_custom_call" | custom-call | flops 2000000000 | bytes 6000000 | tf_op jit(solution)/shard_map/pallas_call | solution.py:622
  23.4 2.0 %collective-permute-start.8 = (bf16[512,256]{1,0:T(8,128)(2,1)S(1)}, bf16[512,256]{1,0:T(8,128)(2,1)S(1)}, u32[]{:S(2)}, u32[]{:S(2)}) collective-permute-start(bf16[512,256]{1,0:T(8,128)(2,1)S(1)} %get-tuple-element.95), channel_id=1, source_target_pairs={{0,2},{1,3},{2,0},{3,1},{4,6},{5,7},{6,4},{7,5},{8,10},{9,11},{10,... | collective-permute-start | bytes 786440 | tf_op jit(solution)/shard_map/ppermute | solution.py:634
  25.4 5.1 %all-to-all-start = ((bf16[32,32,512]{2,1,0:T(8,128)(2,1)}), bf16[32,32,512]{2,1,0:T(8,128)(2,1)S(1)}, u32[]{:S(2)}, u32[]{:S(2)}) async-start(bf16[32,32,512]{2,1,0:T(8,128)(2,1)} %bitcast.5), calls=%async_computation | async-start | bytes 2097152 | tf_op jit(solution)/shard_map/all_to_all | solution.py:709
  30.5 1.6 %collective-permute-done.8.recv_ref = bf16[512,256]{1,0:T(8,128)(2,1)S(1)} collective-permute-done((bf16[512,256]{1,0:T(8,128)(2,1)S(1)}, bf16[512,256]{1,0:T(8,128)(2,1)S(1)}, u32[]{:S(2)}, u32[]{:S(2)}) %collective-permute-start.8) | collective-permute-done | bytes 262176 | tf_op jit(solution)/shard_map/ppermute | solution.py:634
  32.1 2.9 %shard_map.91 = (f32[78,8,256]{2,1,0:T(8,128)S(1)}, f32[108,8,256]{2,1,0:T(8,128)S(1)}, f32[128,32]{1,0:T(8,128)S(1)}, f32[128,32]{1,0:T(8,128)S(1)}) custom-call(f32[512,256]{1,0:T(8,128)S(1)} %get-tuple-element.92.own_ref, bf16[512,256]{1,0:T(8,128)(2,1)S(1)} %collective-permute-done.8.recv_ref, f32[108,8,256]{2,1,0:T(8,128)} %get-tuple-element.96.xext_hbm, ...), custom_call_target="tpu_custom_call" | custom-call | flops 99999997952 | bytes 300000000 | tf_op jit(solution)/shard_map/pallas_call | solution.py:622
  35.1 1.8 %collective-permute-start.9 = (f32[128,32]{1,0:T(8,128)S(1)}, f32[128,32]{1,0:T(8,128)S(1)}, u32[]{:S(2)}, u32[]{:S(2)}) collective-permute-start(f32[128,32]{1,0:T(8,128)S(1)} %get-tuple-element.102), channel_id=1, source_target_pairs={{0,4},{4,0},{8,12},{12,8},{16,20},{20,16},{24,28},{28,24},{1,5},{5... | collective-permute-start | bytes 49160 | tf_op jit(solution)/shard_map/ppermute | solution.py:724
  36.9 2.3 %shard_map.92 = (bf16[512,256]{1,0:T(8,128)(2,1)S(1)}, bf16[512,256]{1,0:T(8,128)(2,1)S(1)}) custom-call(f32[78,8,256]{2,1,0:T(8,128)S(1)} %get-tuple-element.98.dh_ref, f32[108,8,256]{2,1,0:T(8,128)S(1)} %get-tuple-element.99.ext_ref, f32[31,8,256]{2,1,0:T(8,128)S(1)} %get-tuple-element.70.taps_own_ref.taps_ref, ...), custom_call_target="tpu_custom_call" | custom-call | flops 20000000000 | bytes 60000000 | tf_op jit(solution)/shard_map/pallas_call | solution.py:622
  39.2 1.3 %collective-permute-done.9 = f32[128,32]{1,0:T(8,128)S(1)} collective-permute-done((f32[128,32]{1,0:T(8,128)S(1)}, f32[128,32]{1,0:T(8,128)S(1)}, u32[]{:S(2)}, u32[]{:S(2)}) %collective-permute-start.9) | collective-permute-done | bytes 16416 | tf_op jit(solution)/shard_map/ppermute | solution.py:724
  40.7 1.9 %collective-permute-start.11 = (bf16[128,512]{1,0:T(8,128)(2,1)S(1)}, bf16[128,512]{1,0:T(8,128)(2,1)S(1)}, u32[]{:S(2)}, u32[]{:S(2)}) collective-permute-start(bf16[128,512]{1,0:T(8,128)(2,1)S(1)} %get-tuple-element.115), channel_id=1, source_target_pairs={{0,2},{1,3},{2,0},{3,1},{4,6},{5,7},{6,4},{7,5},{8,10},{9,11},{10,... | collective-permute-start | bytes 393224 | tf_op jit(solution)/shard_map/ppermute | solution.py:634
  43.4 4.1 %collective-permute-start.14 = (f32[32,32]{1,0:T(8,128)S(1)}, f32[32,32]{1,0:T(8,128)S(1)}, u32[]{:S(2)}, u32[]{:S(2)}) collective-permute-start(f32[32,32]{1,0:T(8,128)S(1)} %get-tuple-element.119), channel_id=1, source_target_pairs={{0,1},{1,17},{2,9},{3,25},{4,5},{5,21},{6,13},{7,29},{8,0},{9,16},... | collective-permute-start | bytes 12296 | tf_op jit(solution)/shard_map/ppermute | solution.py:738
  47.5 1.5 %collective-permute-start.15 = (f32[32,32]{1,0:T(8,128)S(1)}, f32[32,32]{1,0:T(8,128)S(1)}, u32[]{:S(2)}, u32[]{:S(2)}) collective-permute-start(f32[32,32]{1,0:T(8,128)S(1)} %get-tuple-element.118), channel_id=1, source_target_pairs={{0,2},{1,18},{2,10},{3,26},{4,6},{5,22},{6,14},{7,30},{8,3},{9,19}... | collective-permute-start | bytes 12296 | tf_op jit(solution)/shard_map/ppermute | solution.py:738
  49.1 3.9 %collective-permute-start.16 = (f32[32,32]{1,0:T(8,128)S(1)}, f32[32,32]{1,0:T(8,128)S(1)}, u32[]{:S(2)}, u32[]{:S(2)}) collective-permute-start(f32[32,32]{1,0:T(8,128)S(1)} %get-tuple-element.117), channel_id=1, source_target_pairs={{0,3},{1,19},{2,11},{3,27},{4,7},{5,23},{6,15},{7,31},{8,2},{9,18}... | collective-permute-start | bytes 12296 | tf_op jit(solution)/shard_map/ppermute | solution.py:738
  52.9 0.8 %shard_map.93 = (bf16[128,1024]{1,0:T(8,128)(2,1)}, bf16[128,1024]{1,0:T(8,128)(2,1)}) custom-call(bf16[512,512]{1,0:T(8,128)(2,1)S(1)} %constant_dynamic-update-slice_fusion.own_ref, bf16[128,512]{1,0:T(8,128)(2,1)S(1)} %collective-permute-done.10.r1, bf16[128,512]{1,0:T(8,128)(2,1)S(1)} %collective-permute-done.11.r2, ...), custom_call_target="tpu_custom_call" | custom-call | flops 1000000000 | bytes 3000000 | tf_op jit(solution)/shard_map/pallas_call | solution.py:622
  53.8 4.0 %collective-permute-done.15.q2 = f32[32,32]{1,0:T(8,128)S(1)} collective-permute-done((f32[32,32]{1,0:T(8,128)S(1)}, f32[32,32]{1,0:T(8,128)S(1)}, u32[]{:S(2)}, u32[]{:S(2)}) %collective-permute-start.15) | collective-permute-done | bytes 4128 | tf_op jit(solution)/shard_map/ppermute | solution.py:738
  57.8 0.8 %shard_map.94 = (f32[32,2048]{1,0:T(8,128)}, f32[32,31]{1,0:T(8,128)}) custom-call(bf16[32,32,512]{2,1,0:T(8,128)(2,1)S(1)} %all-to-all-done.blocks_ref, f32[32,32]{1,0:T(8,128)S(1)} %collective-permute-done.13.q0, f32[32,32]{1,0:T(8,128)S(1)} %collective-permute-done.14.q1, f32[32,32]{1,0:T(8,128)S(1)} %collective-permute-done.15.q2, ...), custom_call_target="tpu_custom_call" | custom-call | flops 1000000000 | bytes 3000000 | tf_op jit(solution)/shard_map/pallas_call | solution.py:622
  (28 shorter events, 3.0 us)
Async XLA Ops:
  1.8 4.5 %collective-permute-start = (bf16[128,512]{1,0:T(8,128)(2,1)S(1)}, bf16[128,512]{1,0:T(8,128)(2,1)S(1)}, u32[]{:S(2)}, u32[]{:S(2)}) collective-permute-start(bf16[128,512]{1,0:T(8,128)(2,1)S(1)} %get-tuple-element.64), channel_id=1, source_target_pairs={{0,1},{1,0},{2,3},{3,2},{4,5},{5,4},{6,7},{7,6},{8,9},{9,8},{10,11... | collective-permute-start | bytes 393224 | tf_op jit(solution)/shard_map/ppermute | solution.py:634
  2.3 6.9 %collective-permute-start.1 = (bf16[128,512]{1,0:T(8,128)(2,1)S(1)}, bf16[128,512]{1,0:T(8,128)(2,1)S(1)}, u32[]{:S(2)}, u32[]{:S(2)}) collective-permute-start(bf16[128,512]{1,0:T(8,128)(2,1)S(1)} %get-tuple-element.66), channel_id=1, source_target_pairs={{0,2},{1,3},{2,0},{3,1},{4,6},{5,7},{6,4},{7,5},{8,10},{9,11},{10,... | collective-permute-start | bytes 393224 | tf_op jit(solution)/shard_map/ppermute | solution.py:634
  4.9 6.6 %collective-permute-start.2 = (bf16[128,512]{1,0:T(8,128)(2,1)S(1)}, bf16[128,512]{1,0:T(8,128)(2,1)S(1)}, u32[]{:S(2)}, u32[]{:S(2)}) collective-permute-start(bf16[128,512]{1,0:T(8,128)(2,1)S(1)} %get-tuple-element.67), channel_id=1, source_target_pairs={{0,3},{1,2},{2,1},{3,0},{4,7},{5,6},{6,5},{7,4},{8,11},{9,10},{10,... | collective-permute-start | bytes 393224 | tf_op jit(solution)/shard_map/ppermute | solution.py:634
  6.2 9.3 %collective-permute-start.3 = (bf16[128,256]{1,0:T(8,128)(2,1)S(1)}, bf16[128,256]{1,0:T(8,128)(2,1)S(1)}, u32[]{:S(2)}, u32[]{:S(2)}) collective-permute-start(bf16[128,256]{1,0:T(8,128)(2,1)S(1)} %get-tuple-element.74), channel_id=1, source_target_pairs={{0,1},{1,0},{2,3},{3,2},{4,5},{5,4},{6,7},{7,6},{8,9},{9,8},{10,11... | collective-permute-start | bytes 196616 | tf_op jit(solution)/shard_map/ppermute | solution.py:634
  6.5 9.1 %collective-permute-start.4 = (bf16[128,256]{1,0:T(8,128)(2,1)S(1)}, bf16[128,256]{1,0:T(8,128)(2,1)S(1)}, u32[]{:S(2)}, u32[]{:S(2)}) collective-permute-start(bf16[128,256]{1,0:T(8,128)(2,1)S(1)} %get-tuple-element.75), channel_id=1, source_target_pairs={{0,2},{1,3},{2,0},{3,1},{4,6},{5,7},{6,4},{7,5},{8,10},{9,11},{10,... | collective-permute-start | bytes 196616 | tf_op jit(solution)/shard_map/ppermute | solution.py:634
  8.4 7.2 %collective-permute-start.5 = (bf16[128,256]{1,0:T(8,128)(2,1)S(1)}, bf16[128,256]{1,0:T(8,128)(2,1)S(1)}, u32[]{:S(2)}, u32[]{:S(2)}) collective-permute-start(bf16[128,256]{1,0:T(8,128)(2,1)S(1)} %get-tuple-element.76), channel_id=1, source_target_pairs={{0,3},{1,2},{2,1},{3,0},{4,7},{5,6},{6,5},{7,4},{8,11},{9,10},{10,... | collective-permute-start | bytes 196616 | tf_op jit(solution)/shard_map/ppermute | solution.py:634
  15.5 2.0 %collective-permute-start.6 = (bf16[512,512]{1,0:T(8,128)(2,1)S(1)}, bf16[512,512]{1,0:T(8,128)(2,1)S(1)}, u32[]{:S(2)}, u32[]{:S(2)}) collective-permute-start(bf16[512,512]{1,0:T(8,128)(2,1)S(1)} %get-tuple-element.77.hid_ref), channel_id=1, source_target_pairs={{0,1},{1,0},{2,3},{3,2},{4,5},{5,4},{6,7},{7,6},{8,9},{9,8},{10,11... | collective-permute-start | bytes 1572872 | tf_op jit(solution)/shard_map/ppermute | solution.py:634
  21.2 2.0 %collective-permute-start.7 = (bf16[512,512]{1,0:T(8,128)(2,1)S(1)}, bf16[512,512]{1,0:T(8,128)(2,1)S(1)}, u32[]{:S(2)}, u32[]{:S(2)}) collective-permute-start(bf16[512,512]{1,0:T(8,128)(2,1)S(1)} %get-tuple-element.91), channel_id=1, source_target_pairs={{0,1},{1,0},{2,3},{3,2},{4,5},{5,4},{6,7},{7,6},{8,9},{9,8},{10,11... | collective-permute-start | bytes 1572872 | tf_op jit(solution)/shard_map/ppermute | solution.py:634
  23.4 8.8 %collective-permute-start.8 = (bf16[512,256]{1,0:T(8,128)(2,1)S(1)}, bf16[512,256]{1,0:T(8,128)(2,1)S(1)}, u32[]{:S(2)}, u32[]{:S(2)}) collective-permute-start(bf16[512,256]{1,0:T(8,128)(2,1)S(1)} %get-tuple-element.95), channel_id=1, source_target_pairs={{0,2},{1,3},{2,0},{3,1},{4,6},{5,7},{6,4},{7,5},{8,10},{9,11},{10,... | collective-permute-start | bytes 786440 | tf_op jit(solution)/shard_map/ppermute | solution.py:634
  25.4 32.4 %all-to-all-start = ((bf16[32,32,512]{2,1,0:T(8,128)(2,1)}), bf16[32,32,512]{2,1,0:T(8,128)(2,1)S(1)}, u32[]{:S(2)}, u32[]{:S(2)}) async-start(bf16[32,32,512]{2,1,0:T(8,128)(2,1)} %bitcast.5), calls=%async_computation | async-start | bytes 2097152 | tf_op jit(solution)/shard_map/all_to_all | solution.py:709
  35.1 5.5 %collective-permute-start.9 = (f32[128,32]{1,0:T(8,128)S(1)}, f32[128,32]{1,0:T(8,128)S(1)}, u32[]{:S(2)}, u32[]{:S(2)}) collective-permute-start(f32[128,32]{1,0:T(8,128)S(1)} %get-tuple-element.102), channel_id=1, source_target_pairs={{0,4},{4,0},{8,12},{12,8},{16,20},{20,16},{24,28},{28,24},{1,5},{5... | collective-permute-start | bytes 49160 | tf_op jit(solution)/shard_map/ppermute | solution.py:724
  40.6 2.1 %collective-permute-start.10 = (bf16[128,512]{1,0:T(8,128)(2,1)S(1)}, bf16[128,512]{1,0:T(8,128)(2,1)S(1)}, u32[]{:S(2)}, u32[]{:S(2)}) collective-permute-start(bf16[128,512]{1,0:T(8,128)(2,1)S(1)} %get-tuple-element.116), channel_id=1, source_target_pairs={{0,1},{1,0},{2,3},{3,2},{4,5},{5,4},{6,7},{7,6},{8,9},{9,8},{10,11... | collective-permute-start | bytes 393224 | tf_op jit(solution)/shard_map/ppermute | solution.py:634
  40.7 8.3 %collective-permute-start.11 = (bf16[128,512]{1,0:T(8,128)(2,1)S(1)}, bf16[128,512]{1,0:T(8,128)(2,1)S(1)}, u32[]{:S(2)}, u32[]{:S(2)}) collective-permute-start(bf16[128,512]{1,0:T(8,128)(2,1)S(1)} %get-tuple-element.115), channel_id=1, source_target_pairs={{0,2},{1,3},{2,0},{3,1},{4,6},{5,7},{6,4},{7,5},{8,10},{9,11},{10,... | collective-permute-start | bytes 393224 | tf_op jit(solution)/shard_map/ppermute | solution.py:634
  42.6 10.3 %collective-permute-start.12 = (bf16[128,512]{1,0:T(8,128)(2,1)S(1)}, bf16[128,512]{1,0:T(8,128)(2,1)S(1)}, u32[]{:S(2)}, u32[]{:S(2)}) collective-permute-start(bf16[128,512]{1,0:T(8,128)(2,1)S(1)} %get-tuple-element.114), channel_id=1, source_target_pairs={{0,3},{1,2},{2,1},{3,0},{4,7},{5,6},{6,5},{7,4},{8,11},{9,10},{10,... | collective-permute-start | bytes 393224 | tf_op jit(solution)/shard_map/ppermute | solution.py:634
  42.8 11.0 %collective-permute-start.13 = (f32[32,32]{1,0:T(8,128)S(1)}, f32[32,32]{1,0:T(8,128)S(1)}, u32[]{:S(2)}, u32[]{:S(2)}) collective-permute-start(f32[32,32]{1,0:T(8,128)S(1)} %get-tuple-element.120), channel_id=1, source_target_pairs={{0,0},{1,16},{2,8},{3,24},{4,4},{5,20},{6,12},{7,28},{8,1},{9,17},... | collective-permute-start | bytes 12296 | tf_op jit(solution)/shard_map/ppermute | solution.py:738
  43.4 10.4 %collective-permute-start.14 = (f32[32,32]{1,0:T(8,128)S(1)}, f32[32,32]{1,0:T(8,128)S(1)}, u32[]{:S(2)}, u32[]{:S(2)}) collective-permute-start(f32[32,32]{1,0:T(8,128)S(1)} %get-tuple-element.119), channel_id=1, source_target_pairs={{0,1},{1,17},{2,9},{3,25},{4,5},{5,21},{6,13},{7,29},{8,0},{9,16},... | collective-permute-start | bytes 12296 | tf_op jit(solution)/shard_map/ppermute | solution.py:738
  47.5 10.2 %collective-permute-start.15 = (f32[32,32]{1,0:T(8,128)S(1)}, f32[32,32]{1,0:T(8,128)S(1)}, u32[]{:S(2)}, u32[]{:S(2)}) collective-permute-start(f32[32,32]{1,0:T(8,128)S(1)} %get-tuple-element.118), channel_id=1, source_target_pairs={{0,2},{1,18},{2,10},{3,26},{4,6},{5,22},{6,14},{7,30},{8,3},{9,19}... | collective-permute-start | bytes 12296 | tf_op jit(solution)/shard_map/ppermute | solution.py:738
  49.1 8.7 %collective-permute-start.16 = (f32[32,32]{1,0:T(8,128)S(1)}, f32[32,32]{1,0:T(8,128)S(1)}, u32[]{:S(2)}, u32[]{:S(2)}) collective-permute-start(f32[32,32]{1,0:T(8,128)S(1)} %get-tuple-element.117), channel_id=1, source_target_pairs={{0,3},{1,19},{2,11},{3,27},{4,7},{5,23},{6,15},{7,31},{8,2},{9,18}... | collective-permute-start | bytes 12296 | tf_op jit(solution)/shard_map/ppermute | solution.py:738

commit v8 on v7

--- a/solution.py
+++ b/solution.py
@@ -562,8 +562,8 @@
     gdw_ref[KERNEL:, :] = jnp.zeros((gdw_ref.shape[0] - KERNEL, width), f32)
     half = width // 2
     side = dp_index & 1
-    dw_keep_ref[...] = gdw_ref[:, pl.ds(pl.multiple_of(side * half, half), half)].T
-    dw_send_ref[...] = gdw_ref[:, pl.ds(pl.multiple_of((1 - side) * half, half), half)].T
+    dw_keep_ref[...] = gdw_ref[:, pl.ds(pl.multiple_of(side * half, half), half)]
+    dw_send_ref[...] = gdw_ref[:, pl.ds(pl.multiple_of((1 - side) * half, half), half)]
 
 
 def frame_grad_kernel(
@@ -602,10 +602,13 @@
         dframes_ref[:, pl.ds(start, width)] = ref[:row_count, width:]
 
 
-def place_grad_kernel(blocks_ref, q0, q1, q2, q3, out_ref, dw_ref):
+def place_grad_kernel(blocks_ref, q0, q1, q2, q3, out_ref, dw_ref, sum_ref):
     piece, wide = blocks_ref.shape[1:]
     width = wide // 2
     full = out_ref.shape[1] // 2
+    quarters = [q[...].astype(jnp.float32) for q in (q0, q1, q2, q3)]
+    sum_ref[...] = ((quarters[0] + quarters[1]) + (quarters[2] + quarters[3])).T
+    dw_ref[...] = sum_ref[pl.ds(pl.multiple_of(lax.axis_index("ctx") * piece, piece), piece), :KERNEL]
     for j in range(4):
         total = blocks_ref[j].astype(jnp.float32)
         for d in range(1, blocks_ref.shape[0] // 4):
@@ -613,7 +616,6 @@
         start = SWAP[j] * width
         out_ref[:, start : start + width] = total[:, :width]
         out_ref[:, full + start : full + start + width] = total[:, width:]
-    dw_ref[...] = ((q0[...] + q1[...]) + (q2[...] + q3[...]))[:, :KERNEL]
 
 
 def call(kernel, args, outs, scratch=(), hbm_in=(), hbm_out=(), to_hbm=False, vmem_mib=8, cost_us=2):
@@ -709,7 +711,7 @@
     all_kv = lax.all_to_all(part_kv.reshape(4 * dp_size, piece, 2 * width), ("dp", "ctx"), 0, 0)
     dhidden, dconv_ext, dw_keep, dw_send = call(
         tap_grad_kernel, (part_own, from_chip, frames_ext, conv_own, utt_lengths),
-        [(short, f32), (long, f32), ((width // 2, KERNEL + 1), f32), ((width // 2, KERNEL + 1), f32)],
+        [(short, f32), (long, f32), ((KERNEL + 1, width // 2), f32), ((KERNEL + 1, width // 2), f32)],
         [
             pltpu.VMEM(long, f32), pltpu.VMEM(short, f32), pltpu.SMEM(utt_lengths.shape, jnp.int32),
             pltpu.VMEM((KERNEL + 1, width), f32), pltpu.SemaphoreType.DMA((3,)),
@@ -723,24 +725,24 @@
     )
     dw_recv = lax.ppermute(dw_send, "dp", [(i, i ^ 1) for i in range(dp_size)])
     dw_recv, dframes = lax.optimization_barrier((dw_recv, dframes))
-    dw_half = dw_keep + dw_recv
+    dw_half = (dw_keep + dw_recv).astype(bf16)
     results = jnp.concatenate([out_own, dframes], axis=1)
     result_blocks = [results] + [swap_ctx(results[j * row_count : (j + 1) * row_count], j) for j in (1, 2, 3)]
     dw_half, result_blocks[1] = lax.optimization_barrier((dw_half, result_blocks[1]))
-    quarters = []
+    arrived = []
     for turn in range(4):
         pairs = []
         for d in range(dp_size):
             for c in range(4):
                 target = 2 * (2 * (c & 1) + (c >> 1)) + (d & 1)
                 pairs.append((4 * d + c, 4 * target + ((d >> 1) ^ turn)))
-        quarter = lax.dynamic_slice_in_dim(dw_half, ((dp_index >> 1) ^ turn) * piece, piece, axis=0)
-        quarters.append(lax.ppermute(quarter, ("dp", "ctx"), pairs))
+        arrived.append(lax.ppermute(dw_half, ("dp", "ctx"), pairs))
     output, dframes_rows = call(
         place_kernel, tuple(result_blocks), [((row_count, feat_width), bf16)] * 2, to_hbm=True, cost_us=1
     )
     grad_kv, grad_dw = call(
-        place_grad_kernel, (all_kv, *quarters), [((piece, 2 * feat_width), f32), ((piece, KERNEL), f32)],
+        place_grad_kernel, (all_kv, *arrived),
+        [((piece, 2 * feat_width), f32), ((piece, KERNEL), f32)], [pltpu.VMEM((width // 2, KERNEL + 1), f32)],
         to_hbm=True, cost_us=1,
     )
     return (output[None], dframes_rows[None], grad_kv, grad_dw)

time: 59 us -> 58.2 us (0.986)
  starting transfers between devices: 27.3 us -> 23.5 us
  waiting for transfers between devices: 10.5 us -> 13.3 us
    ppermute x4, starting transfers between devices: 10.2 us -> 6.54 us  [on_device_pairs(): arrived.append(lax.ppermute(dw_half, ('dp', 'ctx'), pairs))]
    ppermute x12, waiting for transfers between devices: 5.13 us -> 7.98 us  [swap_ctx(): return lax.ppermute(array, 'ctx', [(i, i ^ j) for i in range(4)])]
    ppermute x4, waiting for transfers between devices: 3.98 us -> 5.36 us  [on_device_pairs(): arrived.append(lax.ppermute(dw_half, ('dp', 'ctx'), pairs))]
    ppermute x1, waiting for transfers between devices: 1.33 us -> 0.01 us  [on_device_pairs(): dw_recv = lax.ppermute(dw_send, 'dp', [(i, i ^ 1) for i in range(dp_size)])]
  transfers between devices with their start and end apart: 18 -> 18, of which waited for: 6 -> 8; matrix products, arithmetic and copies ran while one was open for 0% -> 0% of each run, Pallas kernels for 24% -> 25%
where the time goes in v8:
time: 58.2 us; the launch traced here: 57.9 us
  starting transfers between devices  23.5 us (40%)
  Pallas kernels  20.1 us (35%)
  waiting for transfers between devices  13.3 us (23%)
  between operations  0.81 us (1%)
    pallas_call x11, Pallas kernels, call(): pl.pallas_call(kernel, out_shape=[jax.ShapeDtypeStruct(*o) if to_hbm else...  20.1 us
    ppermute x12, starting transfers between devices, swap_ctx(): return lax.ppermute(array, 'ctx', [(i, i ^ j) for i in range(4)])  10.1 us
    ppermute x12, waiting for transfers between devices, swap_ctx(): return lax.ppermute(array, 'ctx', [(i, i ^ j) for i in range(4)])  7.98 us
    ppermute x4, starting transfers between devices, on_device_pairs(): arrived.append(lax.ppermute(dw_half, ('dp', 'ctx'), pairs))  6.54 us
    ppermute x4, waiting for transfers between devices, on_device_pairs(): arrived.append(lax.ppermute(dw_half, ('dp', 'ctx'), pairs))  5.36 us
    all_to_all x1, starting transfers between devices, on_device_pairs(): lax.all_to_all(part_kv.reshape(4 * dp_size, piece, 2 * width), ('dp', 'ct...  5.1 us
    ppermute x1, starting transfers between devices, on_device_pairs(): dw_recv = lax.ppermute(dw_send, 'dp', [(i, i ^ 1) for i in range(dp_size)])  1.84 us
  transfers between devices with their start and end apart: 18, of which 8 were waited for; matrix products, arithmetic and copies ran while one was open for 0% of the time, Pallas kernels for 25%

profile of v8, /device:TPU:0, one launch (start us, length us, event | category | flops | bytes accessed | tf_op | source)
XLA Modules:
  0.0 57.9 jit_solution(4941102322609253251)
XLA Ops:
  0.6 1.1 %shard_map.84 = (bf16[128,512]{1,0:T(8,128)(2,1)S(1)}, bf16[128,512]{1,0:T(8,128)(2,1)S(1)}, bf16[128,512]{1,0:T(8,128)(2,1)S(1)}, bf16[128,512]{1,0:T(8,128)(2,1)S(1)}) custom-call(bf16[128,1024]{1,0:T(8,128)(2,1)} %bitcast.6), custom_call_target="tpu_custom_call" | custom-call | flops 1000000000 | bytes 3000000 | tf_op jit(solution)/shard_map/pallas_call | solution.py:624
  2.3 2.6 %collective-permute-start.1 = (bf16[128,512]{1,0:T(8,128)(2,1)S(1)}, bf16[128,512]{1,0:T(8,128)(2,1)S(1)}, u32[]{:S(2)}, u32[]{:S(2)}) collective-permute-start(bf16[128,512]{1,0:T(8,128)(2,1)S(1)} %get-tuple-element.66), channel_id=1, source_target_pairs={{0,2},{1,3},{2,0},{3,1},{4,6},{5,7},{6,4},{7,5},{8,10},{9,11},{10,... | collective-permute-start | bytes 393224 | tf_op jit(solution)/shard_map/ppermute | solution.py:636
  4.9 1.3 %shard_map.85 = (bf16[624,512]{1,0:T(8,128)(2,1)S(1)}, bf16[512,624]{1,0:T(8,128)(2,1)S(1)}, f32[31,8,256]{2,1,0:T(8,128)S(1)}, f32[31,8,256]{2,1,0:T(8,128)S(1)...) custom-call(s32[1,8]{1,0:T(1,128)} %len_hbm.7, ...), custom_call_target="tpu_custom_call" | custom-call | flops 2000000000 | bytes 6000000 | tf_op jit(solution)/shard_map/pallas_call | solution.py:624
  6.5 1.9 %collective-permute-start.4 = (bf16[128,256]{1,0:T(8,128)(2,1)S(1)}, bf16[128,256]{1,0:T(8,128)(2,1)S(1)}, u32[]{:S(2)}, u32[]{:S(2)}) collective-permute-start(bf16[128,256]{1,0:T(8,128)(2,1)S(1)} %get-tuple-element.75), channel_id=1, source_target_pairs={{0,2},{1,3},{2,0},{3,1},{4,6},{5,7},{6,4},{7,5},{8,10},{9,11},{10,... | collective-permute-start | bytes 196616 | tf_op jit(solution)/shard_map/ppermute | solution.py:636
  9.2 2.3 %collective-permute-done.2.f3 = bf16[128,512]{1,0:T(8,128)(2,1)S(1)} collective-permute-done((bf16[128,512]{1,0:T(8,128)(2,1)S(1)}, bf16[128,512]{1,0:T(8,128)(2,1)S(1)}, u32[]{:S(2)}, u32[]{:S(2)}) %collective-permute-start.2) | collective-permute-done | bytes 131104 | tf_op jit(solution)/shard_map/ppermute | solution.py:636
  11.5 4.0 %shard_map.86 = (bf16[512,512]{1,0:T(8,128)(2,1)S(1)}, bf16[1024,256]{1,0:T(8,128)(2,1)S(1)}, bf16[1024,256]{1,0:T(8,128)(2,1)S(1)}, f32[108,8,256]{2,1,0:T(8,128)}, f32[78,8,256]{2,1,0:T(8,128)}) custom-call(bf16[128,512]{1,0:T(8,128)(2,1)S(1)} %get-tuple-element.59.f0, bf16[128,512]{1,0:T(8,128)(2,1)S(1)} %collective-permute-done.f1, ...), custom_call_target="tpu_custom_call" | custom-call | flops 20000000000 | bytes 60000000 | tf_op jit(solution)/shard_map/pallas_call | solution.py:624
  16.0 1.2 %shard_map.87 = (f32[512,512]{1,0:T(8,128)S(1)}, bf16[512,256]{1,0:T(8,128)(2,1)S(1)}, f32[256,512]{1,0:T(8,128)S(1)}, f32[128,128]{1,0:T(8,128)S(1)}) custom-call(s32[1,8]{1,0:T(1,128)} %len_hbm.7, bf16[512,512]{1,0:T(8,128)(2,1)S(1)} %get-tuple-element.77.hid_ref, bf16[128,256]{1,0:T(8,128)(2,1)S(1)} %get-tuple-element.78.f0, ...), custom_call_target="tpu_custom_call" | custom-call | flops 2000000000 | bytes 6000000 | tf_op jit(solution)/shard_map/pallas_call | solution.py:624
  17.5 3.7 %shard_map.88 = (f32[256,512]{1,0:T(8,128)S(1)}, f32[256,512]{1,0:T(8,128)S(1)}, bf16[512,512]{1,0:T(8,128)(2,1)S(1)}, bf16[512,512]{1,0:T(8,128)(2,1)S(1)}) custom-call(bf16[512,512]{1,0:T(8,128)(2,1)S(1)} %get-tuple-element.77.hid_ref, bf16[512,512]{1,0:T(8,128)(2,1)S(1)} %collective-permute-done.6.sib_ref, f32[512,512]{1,0:T(8,128)S(1)} %get-tuple-element.84.kv_ref, ...), custom_call_target="tpu_custom_call" | custom-call | flops 8000000000 | bytes 24000000 | tf_op jit(solution)/shard_map/pallas_call | solution.py:624
  21.6 1.6 %shard_map.89 = (bf16[1024,512]{1,0:T(8,128)(2,1)}, f32[512,512]{1,0:T(8,128)S(1)}) custom-call(bf16[512,512]{1,0:T(8,128)(2,1)S(1)} %get-tuple-element.77.hid_ref, bf16[512,512]{1,0:T(8,128)(2,1)S(1)} %collective-permute-done.6.sib_ref, bf16[512,512]{1,0:T(8,128)(2,1)S(1)} %get-tuple-element.88.kvg_ref, f32[256,512]{1,0:T(8,128)S(1)} %get-tuple-element.89.dqt_ref, ...), custom_call_target="tpu_custom_call" | custom-call | flops 2000000000 | bytes 6000000 | tf_op jit(solution)/shard_map/pallas_call | solution.py:624
  23.4 2.0 %collective-permute-start.8 = (bf16[512,256]{1,0:T(8,128)(2,1)S(1)}, bf16[512,256]{1,0:T(8,128)(2,1)S(1)}, u32[]{:S(2)}, u32[]{:S(2)}) collective-permute-start(bf16[512,256]{1,0:T(8,128)(2,1)S(1)} %get-tuple-element.95), channel_id=1, source_target_pairs={{0,2},{1,3},{2,0},{3,1},{4,6},{5,7},{6,4},{7,5},{8,10},{9,11},{10,... | collective-permute-start | bytes 786440 | tf_op jit(solution)/shard_map/ppermute | solution.py:636
  25.4 5.1 %all-to-all-start = ((bf16[32,32,512]{2,1,0:T(8,128)(2,1)}), bf16[32,32,512]{2,1,0:T(8,128)(2,1)S(1)}, u32[]{:S(2)}, u32[]{:S(2)}) async-start(bf16[32,32,512]{2,1,0:T(8,128)(2,1)} %bitcast.5), calls=%async_computation | async-start | bytes 2097152 | tf_op jit(solution)/shard_map/all_to_all | solution.py:711
  30.5 1.6 %collective-permute-done.8.recv_ref = bf16[512,256]{1,0:T(8,128)(2,1)S(1)} collective-permute-done((bf16[512,256]{1,0:T(8,128)(2,1)S(1)}, bf16[512,256]{1,0:T(8,128)(2,1)S(1)}, u32[]{:S(2)}, u32[]{:S(2)}) %collective-permute-start.8) | collective-permute-done | bytes 262176 | tf_op jit(solution)/shard_map/ppermute | solution.py:636
  32.1 2.9 %shard_map.91 = (f32[78,8,256]{2,1,0:T(8,128)S(1)}, f32[108,8,256]{2,1,0:T(8,128)S(1)}, f32[32,128]{1,0:T(8,128)S(1)}, f32[32,128]{1,0:T(8,128)S(1)}) custom-call(f32[512,256]{1,0:T(8,128)S(1)} %get-tuple-element.92.own_ref, bf16[512,256]{1,0:T(8,128)(2,1)S(1)} %collective-permute-done.8.recv_ref, f32[108,8,256]{2,1,0:T(8,128)} %get-tuple-element.96.xext_hbm, ...), custom_call_target="tpu_custom_call" | custom-call | flops 99999997952 | bytes 300000000 | tf_op jit(solution)/shard_map/pallas_call | solution.py:624
  35.0 1.8 %collective-permute-start.9 = (f32[32,128]{1,0:T(8,128)S(1)}, f32[32,128]{1,0:T(8,128)S(1)}, u32[]{:S(2)}, u32[]{:S(2)}) collective-permute-start(f32[32,128]{1,0:T(8,128)S(1)} %get-tuple-element.102), channel_id=1, source_target_pairs={{0,4},{4,0},{8,12},{12,8},{16,20},{20,16},{24,28},{28,24},{1,5},{5... | collective-permute-start | bytes 49160 | tf_op jit(solution)/shard_map/ppermute | solution.py:726
  36.8 2.5 %shard_map.92 = (bf16[512,256]{1,0:T(8,128)(2,1)S(1)}, bf16[512,256]{1,0:T(8,128)(2,1)S(1)}) custom-call(f32[78,8,256]{2,1,0:T(8,128)S(1)} %get-tuple-element.98.dh_ref, f32[108,8,256]{2,1,0:T(8,128)S(1)} %get-tuple-element.99.ext_ref, f32[31,8,256]{2,1,0:T(8,128)S(1)} %get-tuple-element.70.taps_own_ref.taps_ref, ...), custom_call_target="tpu_custom_call" | custom-call | flops 20000000000 | bytes 60000000 | tf_op jit(solution)/shard_map/pallas_call | solution.py:624
  40.0 1.1 %collective-permute-start.11 = (bf16[128,512]{1,0:T(8,128)(2,1)S(1)}, bf16[128,512]{1,0:T(8,128)(2,1)S(1)}, u32[]{:S(2)}, u32[]{:S(2)}) collective-permute-start(bf16[128,512]{1,0:T(8,128)(2,1)S(1)} %get-tuple-element.115), channel_id=1, source_target_pairs={{0,2},{1,3},{2,0},{3,1},{4,6},{5,7},{6,4},{7,5},{8,10},{9,11},{10,... | collective-permute-start | bytes 393224 | tf_op jit(solution)/shard_map/ppermute | solution.py:636
  41.4 1.2 %collective-permute-done.10.r1 = bf16[128,512]{1,0:T(8,128)(2,1)S(1)} collective-permute-done((bf16[128,512]{1,0:T(8,128)(2,1)S(1)}, bf16[128,512]{1,0:T(8,128)(2,1)S(1)}, u32[]{:S(2)}, u32[]{:S(2)}) %collective-permute-start.10) | collective-permute-done | bytes 131104 | tf_op jit(solution)/shard_map/ppermute | solution.py:636
  42.5 3.3 %collective-permute-start.16 = (bf16[32,128]{1,0:T(8,128)(2,1)S(1)}, bf16[32,128]{1,0:T(8,128)(2,1)S(1)}, u32[]{:S(2)}, u32[]{:S(2)}) collective-permute-start(bf16[32,128]{1,0:T(8,128)(2,1)S(1)} %add_convert_fusion), channel_id=1, source_target_pairs={{0,3},{1,19},{2,11},{3,27},{4,7},{5,23},{6,15},{7,31},{8,2},{9,18}... | collective-permute-start | bytes 24584 | tf_op jit(solution)/shard_map/ppermute | solution.py:739
  45.8 1.8 %collective-permute-start.15 = (bf16[32,128]{1,0:T(8,128)(2,1)S(1)}, bf16[32,128]{1,0:T(8,128)(2,1)S(1)}, u32[]{:S(2)}, u32[]{:S(2)}) collective-permute-start(bf16[32,128]{1,0:T(8,128)(2,1)S(1)} %add_convert_fusion), channel_id=1, source_target_pairs={{0,2},{1,18},{2,10},{3,26},{4,6},{5,22},{6,14},{7,30},{8,3},{9,19}... | collective-permute-start | bytes 24584 | tf_op jit(solution)/shard_map/ppermute | solution.py:739
  47.6 0.8 %collective-permute-start.14 = (bf16[32,128]{1,0:T(8,128)(2,1)S(1)}, bf16[32,128]{1,0:T(8,128)(2,1)S(1)}, u32[]{:S(2)}, u32[]{:S(2)}) collective-permute-start(bf16[32,128]{1,0:T(8,128)(2,1)S(1)} %add_convert_fusion), channel_id=1, source_target_pairs={{0,1},{1,17},{2,9},{3,25},{4,5},{5,21},{6,13},{7,29},{8,0},{9,16},... | collective-permute-start | bytes 24584 | tf_op jit(solution)/shard_map/ppermute | solution.py:739
  49.1 1.7 %collective-permute-done.11.r2 = bf16[128,512]{1,0:T(8,128)(2,1)S(1)} collective-permute-done((bf16[128,512]{1,0:T(8,128)(2,1)S(1)}, bf16[128,512]{1,0:T(8,128)(2,1)S(1)}, u32[]{:S(2)}, u32[]{:S(2)}) %collective-permute-start.11) | collective-permute-done | bytes 131104 | tf_op jit(solution)/shard_map/ppermute | solution.py:636
  50.8 0.8 %shard_map.93 = (bf16[128,1024]{1,0:T(8,128)(2,1)}, bf16[128,1024]{1,0:T(8,128)(2,1)}) custom-call(bf16[512,512]{1,0:T(8,128)(2,1)S(1)} %constant_dynamic-update-slice_fusion.own_ref, bf16[128,512]{1,0:T(8,128)(2,1)S(1)} %collective-permute-done.10.r1, bf16[128,512]{1,0:T(8,128)(2,1)S(1)} %collective-permute-done.11.r2, ...), custom_call_target="tpu_custom_call" | custom-call | flops 1000000000 | bytes 3000000 | tf_op jit(solution)/shard_map/pallas_call | solution.py:624
  52.1 4.8 %collective-permute-done.15.q2 = bf16[32,128]{1,0:T(8,128)(2,1)S(1)} collective-permute-done((bf16[32,128]{1,0:T(8,128)(2,1)S(1)}, bf16[32,128]{1,0:T(8,128)(2,1)S(1)}, u32[]{:S(2)}, u32[]{:S(2)}) %collective-permute-start.15) | collective-permute-done | bytes 8224 | tf_op jit(solution)/shard_map/ppermute | solution.py:739
  57.0 0.9 %shard_map.94 = (f32[32,2048]{1,0:T(8,128)}, f32[32,31]{1,0:T(8,128)}) custom-call(bf16[32,32,512]{2,1,0:T(8,128)(2,1)S(1)} %all-to-all-done.blocks_ref, bf16[32,128]{1,0:T(8,128)(2,1)S(1)} %collective-permute-done.13.q0, bf16[32,128]{1,0:T(8,128)(2,1)S(1)} %collective-permute-done.14.q1, bf16[32,128]{1,0:T(8,128)(2,1)S(1)} %collective-permute-done.15.q2, ...), custom_call_target="tpu_custom_call" | custom-call | flops 1000000000 | bytes 3000000 | tf_op jit(solution)/shard_map/pallas_call | solution.py:624
  (27 shorter events, 4.9 us)
Async XLA Ops:
  1.8 4.5 %collective-permute-start = (bf16[128,512]{1,0:T(8,128)(2,1)S(1)}, bf16[128,512]{1,0:T(8,128)(2,1)S(1)}, u32[]{:S(2)}, u32[]{:S(2)}) collective-permute-start(bf16[128,512]{1,0:T(8,128)(2,1)S(1)} %get-tuple-element.64), channel_id=1, source_target_pairs={{0,1},{1,0},{2,3},{3,2},{4,5},{5,4},{6,7},{7,6},{8,9},{9,8},{10,11... | collective-permute-start | bytes 393224 | tf_op jit(solution)/shard_map/ppermute | solution.py:636
  2.3 6.9 %collective-permute-start.1 = (bf16[128,512]{1,0:T(8,128)(2,1)S(1)}, bf16[128,512]{1,0:T(8,128)(2,1)S(1)}, u32[]{:S(2)}, u32[]{:S(2)}) collective-permute-start(bf16[128,512]{1,0:T(8,128)(2,1)S(1)} %get-tuple-element.66), channel_id=1, source_target_pairs={{0,2},{1,3},{2,0},{3,1},{4,6},{5,7},{6,4},{7,5},{8,10},{9,11},{10,... | collective-permute-start | bytes 393224 | tf_op jit(solution)/shard_map/ppermute | solution.py:636
  4.9 6.6 %collective-permute-start.2 = (bf16[128,512]{1,0:T(8,128)(2,1)S(1)}, bf16[128,512]{1,0:T(8,128)(2,1)S(1)}, u32[]{:S(2)}, u32[]{:S(2)}) collective-permute-start(bf16[128,512]{1,0:T(8,128)(2,1)S(1)} %get-tuple-element.67), channel_id=1, source_target_pairs={{0,3},{1,2},{2,1},{3,0},{4,7},{5,6},{6,5},{7,4},{8,11},{9,10},{10,... | collective-permute-start | bytes 393224 | tf_op jit(solution)/shard_map/ppermute | solution.py:636
  6.2 9.3 %collective-permute-start.3 = (bf16[128,256]{1,0:T(8,128)(2,1)S(1)}, bf16[128,256]{1,0:T(8,128)(2,1)S(1)}, u32[]{:S(2)}, u32[]{:S(2)}) collective-permute-start(bf16[128,256]{1,0:T(8,128)(2,1)S(1)} %get-tuple-element.74), channel_id=1, source_target_pairs={{0,1},{1,0},{2,3},{3,2},{4,5},{5,4},{6,7},{7,6},{8,9},{9,8},{10,11... | collective-permute-start | bytes 196616 | tf_op jit(solution)/shard_map/ppermute | solution.py:636
  6.5 9.1 %collective-permute-start.4 = (bf16[128,256]{1,0:T(8,128)(2,1)S(1)}, bf16[128,256]{1,0:T(8,128)(2,1)S(1)}, u32[]{:S(2)}, u32[]{:S(2)}) collective-permute-start(bf16[128,256]{1,0:T(8,128)(2,1)S(1)} %get-tuple-element.75), channel_id=1, source_target_pairs={{0,2},{1,3},{2,0},{3,1},{4,6},{5,7},{6,4},{7,5},{8,10},{9,11},{10,... | collective-permute-start | bytes 196616 | tf_op jit(solution)/shard_map/ppermute | solution.py:636
  8.4 7.2 %collective-permute-start.5 = (bf16[128,256]{1,0:T(8,128)(2,1)S(1)}, bf16[128,256]{1,0:T(8,128)(2,1)S(1)}, u32[]{:S(2)}, u32[]{:S(2)}) collective-permute-start(bf16[128,256]{1,0:T(8,128)(2,1)S(1)} %get-tuple-element.76), channel_id=1, source_target_pairs={{0,3},{1,2},{2,1},{3,0},{4,7},{5,6},{6,5},{7,4},{8,11},{9,10},{10,... | collective-permute-start | bytes 196616 | tf_op jit(solution)/shard_map/ppermute | solution.py:636
  15.5 2.0 %collective-permute-start.6 = (bf16[512,512]{1,0:T(8,128)(2,1)S(1)}, bf16[512,512]{1,0:T(8,128)(2,1)S(1)}, u32[]{:S(2)}, u32[]{:S(2)}) collective-permute-start(bf16[512,512]{1,0:T(8,128)(2,1)S(1)} %get-tuple-element.77.hid_ref), channel_id=1, source_target_pairs={{0,1},{1,0},{2,3},{3,2},{4,5},{5,4},{6,7},{7,6},{8,9},{9,8},{10,11... | collective-permute-start | bytes 1572872 | tf_op jit(solution)/shard_map/ppermute | solution.py:636
  21.2 2.0 %collective-permute-start.7 = (bf16[512,512]{1,0:T(8,128)(2,1)S(1)}, bf16[512,512]{1,0:T(8,128)(2,1)S(1)}, u32[]{:S(2)}, u32[]{:S(2)}) collective-permute-start(bf16[512,512]{1,0:T(8,128)(2,1)S(1)} %get-tuple-element.91), channel_id=1, source_target_pairs={{0,1},{1,0},{2,3},{3,2},{4,5},{5,4},{6,7},{7,6},{8,9},{9,8},{10,11... | collective-permute-start | bytes 1572872 | tf_op jit(solution)/shard_map/ppermute | solution.py:636
  23.4 8.8 %collective-permute-start.8 = (bf16[512,256]{1,0:T(8,128)(2,1)S(1)}, bf16[512,256]{1,0:T(8,128)(2,1)S(1)}, u32[]{:S(2)}, u32[]{:S(2)}) collective-permute-start(bf16[512,256]{1,0:T(8,128)(2,1)S(1)} %get-tuple-element.95), channel_id=1, source_target_pairs={{0,2},{1,3},{2,0},{3,1},{4,6},{5,7},{6,4},{7,5},{8,10},{9,11},{10,... | collective-permute-start | bytes 786440 | tf_op jit(solution)/shard_map/ppermute | solution.py:636
  25.4 31.6 %all-to-all-start = ((bf16[32,32,512]{2,1,0:T(8,128)(2,1)}), bf16[32,32,512]{2,1,0:T(8,128)(2,1)S(1)}, u32[]{:S(2)}, u32[]{:S(2)}) async-start(bf16[32,32,512]{2,1,0:T(8,128)(2,1)} %bitcast.5), calls=%async_computation | async-start | bytes 2097152 | tf_op jit(solution)/shard_map/all_to_all | solution.py:711
  35.0 4.4 %collective-permute-start.9 = (f32[32,128]{1,0:T(8,128)S(1)}, f32[32,128]{1,0:T(8,128)S(1)}, u32[]{:S(2)}, u32[]{:S(2)}) collective-permute-start(f32[32,128]{1,0:T(8,128)S(1)} %get-tuple-element.102), channel_id=1, source_target_pairs={{0,4},{4,0},{8,12},{12,8},{16,20},{20,16},{24,28},{28,24},{1,5},{5... | collective-permute-start | bytes 49160 | tf_op jit(solution)/shard_map/ppermute | solution.py:726
  39.4 9.0 %collective-permute-start.12 = (bf16[128,512]{1,0:T(8,128)(2,1)S(1)}, bf16[128,512]{1,0:T(8,128)(2,1)S(1)}, u32[]{:S(2)}, u32[]{:S(2)}) collective-permute-start(bf16[128,512]{1,0:T(8,128)(2,1)S(1)} %get-tuple-element.114), channel_id=1, source_target_pairs={{0,3},{1,2},{2,1},{3,0},{4,7},{5,6},{6,5},{7,4},{8,11},{9,10},{10,... | collective-permute-start | bytes 393224 | tf_op jit(solution)/shard_map/ppermute | solution.py:636
  40.0 10.8 %collective-permute-start.11 = (bf16[128,512]{1,0:T(8,128)(2,1)S(1)}, bf16[128,512]{1,0:T(8,128)(2,1)S(1)}, u32[]{:S(2)}, u32[]{:S(2)}) collective-permute-start(bf16[128,512]{1,0:T(8,128)(2,1)S(1)} %get-tuple-element.115), channel_id=1, source_target_pairs={{0,2},{1,3},{2,0},{3,1},{4,6},{5,7},{6,4},{7,5},{8,10},{9,11},{10,... | collective-permute-start | bytes 393224 | tf_op jit(solution)/shard_map/ppermute | solution.py:636
  41.2 1.3 %collective-permute-start.10 = (bf16[128,512]{1,0:T(8,128)(2,1)S(1)}, bf16[128,512]{1,0:T(8,128)(2,1)S(1)}, u32[]{:S(2)}, u32[]{:S(2)}) collective-permute-start(bf16[128,512]{1,0:T(8,128)(2,1)S(1)} %get-tuple-element.116), channel_id=1, source_target_pairs={{0,1},{1,0},{2,3},{3,2},{4,5},{5,4},{6,7},{7,6},{8,9},{9,8},{10,11... | collective-permute-start | bytes 393224 | tf_op jit(solution)/shard_map/ppermute | solution.py:636
  42.5 9.6 %collective-permute-start.16 = (bf16[32,128]{1,0:T(8,128)(2,1)S(1)}, bf16[32,128]{1,0:T(8,128)(2,1)S(1)}, u32[]{:S(2)}, u32[]{:S(2)}) collective-permute-start(bf16[32,128]{1,0:T(8,128)(2,1)S(1)} %add_convert_fusion), channel_id=1, source_target_pairs={{0,3},{1,19},{2,11},{3,27},{4,7},{5,23},{6,15},{7,31},{8,2},{9,18}... | collective-permute-start | bytes 24584 | tf_op jit(solution)/shard_map/ppermute | solution.py:739
  45.8 11.2 %collective-permute-start.15 = (bf16[32,128]{1,0:T(8,128)(2,1)S(1)}, bf16[32,128]{1,0:T(8,128)(2,1)S(1)}, u32[]{:S(2)}, u32[]{:S(2)}) collective-permute-start(bf16[32,128]{1,0:T(8,128)(2,1)S(1)} %add_convert_fusion), channel_id=1, source_target_pairs={{0,2},{1,18},{2,10},{3,26},{4,6},{5,22},{6,14},{7,30},{8,3},{9,19}... | collective-permute-start | bytes 24584 | tf_op jit(solution)/shard_map/ppermute | solution.py:739
  47.6 9.4 %collective-permute-start.14 = (bf16[32,128]{1,0:T(8,128)(2,1)S(1)}, bf16[32,128]{1,0:T(8,128)(2,1)S(1)}, u32[]{:S(2)}, u32[]{:S(2)}) collective-permute-start(bf16[32,128]{1,0:T(8,128)(2,1)S(1)} %add_convert_fusion), channel_id=1, source_target_pairs={{0,1},{1,17},{2,9},{3,25},{4,5},{5,21},{6,13},{7,29},{8,0},{9,16},... | collective-permute-start | bytes 24584 | tf_op jit(solution)/shard_map/ppermute | solution.py:739
  48.4 8.6 %collective-permute-start.13 = (bf16[32,128]{1,0:T(8,128)(2,1)S(1)}, bf16[32,128]{1,0:T(8,128)(2,1)S(1)}, u32[]{:S(2)}, u32[]{:S(2)}) collective-permute-start(bf16[32,128]{1,0:T(8,128)(2,1)S(1)} %add_convert_fusion), channel_id=1, source_target_pairs={{0,0},{1,16},{2,8},{3,24},{4,4},{5,20},{6,12},{7,28},{8,1},{9,17},... | collective-permute-start | bytes 24584 | tf_op jit(solution)/shard_map/ppermute | solution.py:739

commit v9 on v8

--- a/solution.py
+++ b/solution.py
@@ -412,6 +412,7 @@
         probs = expd * (1.0 / jnp.sum(expd, axis=0, keepdims=True))
         probs_low = probs.astype(bf16)
         dprobs = nt_dot(v_ref[rows, lanes], grads)
+        dv_ref[rows, lanes] = jnp.dot(probs_low, grads, preferred_element_type=f32)
         rowdots = []
         for head in range(2):
             hrows = slice(first + head * head_width, first + (head + 1) * head_width)
@@ -425,7 +426,6 @@
             part = slice(head * LONGEST, (head + 1) * LONGEST)
             dqt_ref[hrows, rows] = jnp.dot(kt_ref[hrows, rows], dscores[:, part], preferred_element_type=f32) * scale
         dk_ref[rows, lanes] = jnp.dot(dscores, queries, preferred_element_type=f32)
-        dv_ref[rows, lanes] = jnp.dot(probs_low, grads, preferred_element_type=f32)
     heads = [(first, head) for first in range(0, width, 128) for head in range(2)]
     rows = slice(LONGEST, seq_total)
     size = seq_total - LONGEST

time: 58.2 us -> 57.8 us (level)
  no operation moved by 1% of the time
where the time goes in v9:
time: 57.8 us; the launch traced here: 57.4 us
  starting transfers between devices  23.5 us (41%)
  Pallas kernels  19.6 us (34%)
  waiting for transfers between devices  13.4 us (23%)
  between operations  0.81 us (1%)
    pallas_call x11, Pallas kernels, call(): pl.pallas_call(kernel, out_shape=[jax.ShapeDtypeStruct(*o) if to_hbm else...  19.6 us
    ppermute x12, starting transfers between devices, swap_ctx(): return lax.ppermute(array, 'ctx', [(i, i ^ j) for i in range(4)])  10 us
    ppermute x12, waiting for transfers between devices, swap_ctx(): return lax.ppermute(array, 'ctx', [(i, i ^ j) for i in range(4)])  7.98 us
    ppermute x4, starting transfers between devices, on_device_pairs(): arrived.append(lax.ppermute(dw_half, ('dp', 'ctx'), pairs))  6.53 us
    ppermute x4, waiting for transfers between devices, on_device_pairs(): arrived.append(lax.ppermute(dw_half, ('dp', 'ctx'), pairs))  5.36 us
    all_to_all x1, starting transfers between devices, on_device_pairs(): lax.all_to_all(part_kv.reshape(4 * dp_size, piece, 2 * width), ('dp', 'ct...  5.1 us
    ppermute x1, starting transfers between devices, on_device_pairs(): dw_recv = lax.ppermute(dw_send, 'dp', [(i, i ^ 1) for i in range(dp_size)])  1.84 us
  transfers between devices with their start and end apart: 18, of which 8 were waited for; matrix products, arithmetic and copies ran while one was open for 0% of the time, Pallas kernels for 25%

profile of v9, /device:TPU:0, one launch (start us, length us, event | category | flops | bytes accessed | tf_op | source)
XLA Modules:
  0.0 57.4 jit_solution(9609558905503788264)
XLA Ops:
  0.6 1.1 %shard_map.84 = (bf16[128,512]{1,0:T(8,128)(2,1)S(1)}, bf16[128,512]{1,0:T(8,128)(2,1)S(1)}, bf16[128,512]{1,0:T(8,128)(2,1)S(1)}, bf16[128,512]{1,0:T(8,128)(2,1)S(1)}) custom-call(bf16[128,1024]{1,0:T(8,128)(2,1)} %bitcast.6), custom_call_target="tpu_custom_call" | custom-call | flops 1000000000 | bytes 3000000 | tf_op jit(solution)/shard_map/pallas_call | solution.py:624
  2.3 2.6 %collective-permute-start.1 = (bf16[128,512]{1,0:T(8,128)(2,1)S(1)}, bf16[128,512]{1,0:T(8,128)(2,1)S(1)}, u32[]{:S(2)}, u32[]{:S(2)}) collective-permute-start(bf16[128,512]{1,0:T(8,128)(2,1)S(1)} %get-tuple-element.66), channel_id=1, source_target_pairs={{0,2},{1,3},{2,0},{3,1},{4,6},{5,7},{6,4},{7,5},{8,10},{9,11},{10,... | collective-permute-start | bytes 393224 | tf_op jit(solution)/shard_map/ppermute | solution.py:636
  4.9 1.3 %shard_map.85 = (bf16[624,512]{1,0:T(8,128)(2,1)S(1)}, bf16[512,624]{1,0:T(8,128)(2,1)S(1)}, f32[31,8,256]{2,1,0:T(8,128)S(1)}, f32[31,8,256]{2,1,0:T(8,128)S(1)...) custom-call(s32[1,8]{1,0:T(1,128)} %len_hbm.7, ...), custom_call_target="tpu_custom_call" | custom-call | flops 2000000000 | bytes 6000000 | tf_op jit(solution)/shard_map/pallas_call | solution.py:624
  6.5 1.9 %collective-permute-start.4 = (bf16[128,256]{1,0:T(8,128)(2,1)S(1)}, bf16[128,256]{1,0:T(8,128)(2,1)S(1)}, u32[]{:S(2)}, u32[]{:S(2)}) collective-permute-start(bf16[128,256]{1,0:T(8,128)(2,1)S(1)} %get-tuple-element.75), channel_id=1, source_target_pairs={{0,2},{1,3},{2,0},{3,1},{4,6},{5,7},{6,4},{7,5},{8,10},{9,11},{10,... | collective-permute-start | bytes 196616 | tf_op jit(solution)/shard_map/ppermute | solution.py:636
  9.2 2.3 %collective-permute-done.2.f3 = bf16[128,512]{1,0:T(8,128)(2,1)S(1)} collective-permute-done((bf16[128,512]{1,0:T(8,128)(2,1)S(1)}, bf16[128,512]{1,0:T(8,128)(2,1)S(1)}, u32[]{:S(2)}, u32[]{:S(2)}) %collective-permute-start.2) | collective-permute-done | bytes 131104 | tf_op jit(solution)/shard_map/ppermute | solution.py:636
  11.5 4.0 %shard_map.86 = (bf16[512,512]{1,0:T(8,128)(2,1)S(1)}, bf16[1024,256]{1,0:T(8,128)(2,1)S(1)}, bf16[1024,256]{1,0:T(8,128)(2,1)S(1)}, f32[108,8,256]{2,1,0:T(8,128)}, f32[78,8,256]{2,1,0:T(8,128)}) custom-call(bf16[128,512]{1,0:T(8,128)(2,1)S(1)} %get-tuple-element.59.f0, bf16[128,512]{1,0:T(8,128)(2,1)S(1)} %collective-permute-done.f1, ...), custom_call_target="tpu_custom_call" | custom-call | flops 20000000000 | bytes 60000000 | tf_op jit(solution)/shard_map/pallas_call | solution.py:624
  16.0 1.2 %shard_map.87 = (f32[512,512]{1,0:T(8,128)S(1)}, bf16[512,256]{1,0:T(8,128)(2,1)S(1)}, f32[256,512]{1,0:T(8,128)S(1)}, f32[128,128]{1,0:T(8,128)S(1)}) custom-call(s32[1,8]{1,0:T(1,128)} %len_hbm.7, bf16[512,512]{1,0:T(8,128)(2,1)S(1)} %get-tuple-element.77.hid_ref, bf16[128,256]{1,0:T(8,128)(2,1)S(1)} %get-tuple-element.78.f0, ...), custom_call_target="tpu_custom_call" | custom-call | flops 2000000000 | bytes 6000000 | tf_op jit(solution)/shard_map/pallas_call | solution.py:624
  17.5 3.2 %shard_map.88 = (f32[256,512]{1,0:T(8,128)S(1)}, f32[256,512]{1,0:T(8,128)S(1)}, bf16[512,512]{1,0:T(8,128)(2,1)S(1)}, bf16[512,512]{1,0:T(8,128)(2,1)S(1)}) custom-call(bf16[512,512]{1,0:T(8,128)(2,1)S(1)} %get-tuple-element.77.hid_ref, bf16[512,512]{1,0:T(8,128)(2,1)S(1)} %collective-permute-done.6.sib_ref, f32[512,512]{1,0:T(8,128)S(1)} %get-tuple-element.84.kv_ref, ...), custom_call_target="tpu_custom_call" | custom-call | flops 8000000000 | bytes 24000000 | tf_op jit(solution)/shard_map/pallas_call | solution.py:624
  21.2 1.6 %shard_map.89 = (bf16[1024,512]{1,0:T(8,128)(2,1)}, f32[512,512]{1,0:T(8,128)S(1)}) custom-call(bf16[512,512]{1,0:T(8,128)(2,1)S(1)} %get-tuple-element.77.hid_ref, bf16[512,512]{1,0:T(8,128)(2,1)S(1)} %collective-permute-done.6.sib_ref, bf16[512,512]{1,0:T(8,128)(2,1)S(1)} %get-tuple-element.88.kvg_ref, f32[256,512]{1,0:T(8,128)S(1)} %get-tuple-element.89.dqt_ref, ...), custom_call_target="tpu_custom_call" | custom-call | flops 2000000000 | bytes 6000000 | tf_op jit(solution)/shard_map/pallas_call | solution.py:624
  22.9 2.0 %collective-permute-start.8 = (bf16[512,256]{1,0:T(8,128)(2,1)S(1)}, bf16[512,256]{1,0:T(8,128)(2,1)S(1)}, u32[]{:S(2)}, u32[]{:S(2)}) collective-permute-start(bf16[512,256]{1,0:T(8,128)(2,1)S(1)} %get-tuple-element.95), channel_id=1, source_target_pairs={{0,2},{1,3},{2,0},{3,1},{4,6},{5,7},{6,4},{7,5},{8,10},{9,11},{10,... | collective-permute-start | bytes 786440 | tf_op jit(solution)/shard_map/ppermute | solution.py:636
  24.9 5.1 %all-to-all-start = ((bf16[32,32,512]{2,1,0:T(8,128)(2,1)}), bf16[32,32,512]{2,1,0:T(8,128)(2,1)S(1)}, u32[]{:S(2)}, u32[]{:S(2)}) async-start(bf16[32,32,512]{2,1,0:T(8,128)(2,1)} %bitcast.5), calls=%async_computation | async-start | bytes 2097152 | tf_op jit(solution)/shard_map/all_to_all | solution.py:711
  30.0 1.6 %collective-permute-done.8.recv_ref = bf16[512,256]{1,0:T(8,128)(2,1)S(1)} collective-permute-done((bf16[512,256]{1,0:T(8,128)(2,1)S(1)}, bf16[512,256]{1,0:T(8,128)(2,1)S(1)}, u32[]{:S(2)}, u32[]{:S(2)}) %collective-permute-start.8) | collective-permute-done | bytes 262176 | tf_op jit(solution)/shard_map/ppermute | solution.py:636
  31.7 2.9 %shard_map.91 = (f32[78,8,256]{2,1,0:T(8,128)S(1)}, f32[108,8,256]{2,1,0:T(8,128)S(1)}, f32[32,128]{1,0:T(8,128)S(1)}, f32[32,128]{1,0:T(8,128)S(1)}) custom-call(f32[512,256]{1,0:T(8,128)S(1)} %get-tuple-element.92.own_ref, bf16[512,256]{1,0:T(8,128)(2,1)S(1)} %collective-permute-done.8.recv_ref, f32[108,8,256]{2,1,0:T(8,128)} %get-tuple-element.96.xext_hbm, ...), custom_call_target="tpu_custom_call" | custom-call | flops 99999997952 | bytes 300000000 | tf_op jit(solution)/shard_map/pallas_call | solution.py:624
  34.5 1.8 %collective-permute-start.9 = (f32[32,128]{1,0:T(8,128)S(1)}, f32[32,128]{1,0:T(8,128)S(1)}, u32[]{:S(2)}, u32[]{:S(2)}) collective-permute-start(f32[32,128]{1,0:T(8,128)S(1)} %get-tuple-element.102), channel_id=1, source_target_pairs={{0,4},{4,0},{8,12},{12,8},{16,20},{20,16},{24,28},{28,24},{1,5},{5... | collective-permute-start | bytes 49160 | tf_op jit(solution)/shard_map/ppermute | solution.py:726
  36.4 2.5 %shard_map.92 = (bf16[512,256]{1,0:T(8,128)(2,1)S(1)}, bf16[512,256]{1,0:T(8,128)(2,1)S(1)}) custom-call(f32[78,8,256]{2,1,0:T(8,128)S(1)} %get-tuple-element.98.dh_ref, f32[108,8,256]{2,1,0:T(8,128)S(1)} %get-tuple-element.99.ext_ref, f32[31,8,256]{2,1,0:T(8,128)S(1)} %get-tuple-element.70.taps_own_ref.taps_ref, ...), custom_call_target="tpu_custom_call" | custom-call | flops 20000000000 | bytes 60000000 | tf_op jit(solution)/shard_map/pallas_call | solution.py:624
  39.6 1.2 %collective-permute-start.11 = (bf16[128,512]{1,0:T(8,128)(2,1)S(1)}, bf16[128,512]{1,0:T(8,128)(2,1)S(1)}, u32[]{:S(2)}, u32[]{:S(2)}) collective-permute-start(bf16[128,512]{1,0:T(8,128)(2,1)S(1)} %get-tuple-element.115), channel_id=1, source_target_pairs={{0,2},{1,3},{2,0},{3,1},{4,6},{5,7},{6,4},{7,5},{8,10},{9,11},{10,... | collective-permute-start | bytes 393224 | tf_op jit(solution)/shard_map/ppermute | solution.py:636
  40.9 1.2 %collective-permute-done.10.r1 = bf16[128,512]{1,0:T(8,128)(2,1)S(1)} collective-permute-done((bf16[128,512]{1,0:T(8,128)(2,1)S(1)}, bf16[128,512]{1,0:T(8,128)(2,1)S(1)}, u32[]{:S(2)}, u32[]{:S(2)}) %collective-permute-start.10) | collective-permute-done | bytes 131104 | tf_op jit(solution)/shard_map/ppermute | solution.py:636
  42.1 3.3 %collective-permute-start.16 = (bf16[32,128]{1,0:T(8,128)(2,1)S(1)}, bf16[32,128]{1,0:T(8,128)(2,1)S(1)}, u32[]{:S(2)}, u32[]{:S(2)}) collective-permute-start(bf16[32,128]{1,0:T(8,128)(2,1)S(1)} %add_convert_fusion), channel_id=1, source_target_pairs={{0,3},{1,19},{2,11},{3,27},{4,7},{5,23},{6,15},{7,31},{8,2},{9,18}... | collective-permute-start | bytes 24584 | tf_op jit(solution)/shard_map/ppermute | solution.py:739
  45.4 1.8 %collective-permute-start.15 = (bf16[32,128]{1,0:T(8,128)(2,1)S(1)}, bf16[32,128]{1,0:T(8,128)(2,1)S(1)}, u32[]{:S(2)}, u32[]{:S(2)}) collective-permute-start(bf16[32,128]{1,0:T(8,128)(2,1)S(1)} %add_convert_fusion), channel_id=1, source_target_pairs={{0,2},{1,18},{2,10},{3,26},{4,6},{5,22},{6,14},{7,30},{8,3},{9,19}... | collective-permute-start | bytes 24584 | tf_op jit(solution)/shard_map/ppermute | solution.py:739
  47.1 0.8 %collective-permute-start.14 = (bf16[32,128]{1,0:T(8,128)(2,1)S(1)}, bf16[32,128]{1,0:T(8,128)(2,1)S(1)}, u32[]{:S(2)}, u32[]{:S(2)}) collective-permute-start(bf16[32,128]{1,0:T(8,128)(2,1)S(1)} %add_convert_fusion), channel_id=1, source_target_pairs={{0,1},{1,17},{2,9},{3,25},{4,5},{5,21},{6,13},{7,29},{8,0},{9,16},... | collective-permute-start | bytes 24584 | tf_op jit(solution)/shard_map/ppermute | solution.py:739
  48.6 1.7 %collective-permute-done.11.r2 = bf16[128,512]{1,0:T(8,128)(2,1)S(1)} collective-permute-done((bf16[128,512]{1,0:T(8,128)(2,1)S(1)}, bf16[128,512]{1,0:T(8,128)(2,1)S(1)}, u32[]{:S(2)}, u32[]{:S(2)}) %collective-permute-start.11) | collective-permute-done | bytes 131104 | tf_op jit(solution)/shard_map/ppermute | solution.py:636
  50.3 0.8 %shard_map.93 = (bf16[128,1024]{1,0:T(8,128)(2,1)}, bf16[128,1024]{1,0:T(8,128)(2,1)}) custom-call(bf16[512,512]{1,0:T(8,128)(2,1)S(1)} %constant_dynamic-update-slice_fusion.own_ref, bf16[128,512]{1,0:T(8,128)(2,1)S(1)} %collective-permute-done.10.r1, bf16[128,512]{1,0:T(8,128)(2,1)S(1)} %collective-permute-done.11.r2, ...), custom_call_target="tpu_custom_call" | custom-call | flops 1000000000 | bytes 3000000 | tf_op jit(solution)/shard_map/pallas_call | solution.py:624
  51.7 4.8 %collective-permute-done.15.q2 = bf16[32,128]{1,0:T(8,128)(2,1)S(1)} collective-permute-done((bf16[32,128]{1,0:T(8,128)(2,1)S(1)}, bf16[32,128]{1,0:T(8,128)(2,1)S(1)}, u32[]{:S(2)}, u32[]{:S(2)}) %collective-permute-start.15) | collective-permute-done | bytes 8224 | tf_op jit(solution)/shard_map/ppermute | solution.py:739
  56.5 0.9 %shard_map.94 = (f32[32,2048]{1,0:T(8,128)}, f32[32,31]{1,0:T(8,128)}) custom-call(bf16[32,32,512]{2,1,0:T(8,128)(2,1)S(1)} %all-to-all-done.blocks_ref, bf16[32,128]{1,0:T(8,128)(2,1)S(1)} %collective-permute-done.13.q0, bf16[32,128]{1,0:T(8,128)(2,1)S(1)} %collective-permute-done.14.q1, bf16[32,128]{1,0:T(8,128)(2,1)S(1)} %collective-permute-done.15.q2, ...), custom_call_target="tpu_custom_call" | custom-call | flops 1000000000 | bytes 3000000 | tf_op jit(solution)/shard_map/pallas_call | solution.py:624
  (27 shorter events, 4.9 us)
Async XLA Ops:
  1.8 4.5 %collective-permute-start = (bf16[128,512]{1,0:T(8,128)(2,1)S(1)}, bf16[128,512]{1,0:T(8,128)(2,1)S(1)}, u32[]{:S(2)}, u32[]{:S(2)}) collective-permute-start(bf16[128,512]{1,0:T(8,128)(2,1)S(1)} %get-tuple-element.64), channel_id=1, source_target_pairs={{0,1},{1,0},{2,3},{3,2},{4,5},{5,4},{6,7},{7,6},{8,9},{9,8},{10,11... | collective-permute-start | bytes 393224 | tf_op jit(solution)/shard_map/ppermute | solution.py:636
  2.3 6.9 %collective-permute-start.1 = (bf16[128,512]{1,0:T(8,128)(2,1)S(1)}, bf16[128,512]{1,0:T(8,128)(2,1)S(1)}, u32[]{:S(2)}, u32[]{:S(2)}) collective-permute-start(bf16[128,512]{1,0:T(8,128)(2,1)S(1)} %get-tuple-element.66), channel_id=1, source_target_pairs={{0,2},{1,3},{2,0},{3,1},{4,6},{5,7},{6,4},{7,5},{8,10},{9,11},{10,... | collective-permute-start | bytes 393224 | tf_op jit(solution)/shard_map/ppermute | solution.py:636
  4.9 6.6 %collective-permute-start.2 = (bf16[128,512]{1,0:T(8,128)(2,1)S(1)}, bf16[128,512]{1,0:T(8,128)(2,1)S(1)}, u32[]{:S(2)}, u32[]{:S(2)}) collective-permute-start(bf16[128,512]{1,0:T(8,128)(2,1)S(1)} %get-tuple-element.67), channel_id=1, source_target_pairs={{0,3},{1,2},{2,1},{3,0},{4,7},{5,6},{6,5},{7,4},{8,11},{9,10},{10,... | collective-permute-start | bytes 393224 | tf_op jit(solution)/shard_map/ppermute | solution.py:636
  6.2 9.3 %collective-permute-start.3 = (bf16[128,256]{1,0:T(8,128)(2,1)S(1)}, bf16[128,256]{1,0:T(8,128)(2,1)S(1)}, u32[]{:S(2)}, u32[]{:S(2)}) collective-permute-start(bf16[128,256]{1,0:T(8,128)(2,1)S(1)} %get-tuple-element.74), channel_id=1, source_target_pairs={{0,1},{1,0},{2,3},{3,2},{4,5},{5,4},{6,7},{7,6},{8,9},{9,8},{10,11... | collective-permute-start | bytes 196616 | tf_op jit(solution)/shard_map/ppermute | solution.py:636
  6.5 9.1 %collective-permute-start.4 = (bf16[128,256]{1,0:T(8,128)(2,1)S(1)}, bf16[128,256]{1,0:T(8,128)(2,1)S(1)}, u32[]{:S(2)}, u32[]{:S(2)}) collective-permute-start(bf16[128,256]{1,0:T(8,128)(2,1)S(1)} %get-tuple-element.75), channel_id=1, source_target_pairs={{0,2},{1,3},{2,0},{3,1},{4,6},{5,7},{6,4},{7,5},{8,10},{9,11},{10,... | collective-permute-start | bytes 196616 | tf_op jit(solution)/shard_map/ppermute | solution.py:636
  8.4 7.2 %collective-permute-start.5 = (bf16[128,256]{1,0:T(8,128)(2,1)S(1)}, bf16[128,256]{1,0:T(8,128)(2,1)S(1)}, u32[]{:S(2)}, u32[]{:S(2)}) collective-permute-start(bf16[128,256]{1,0:T(8,128)(2,1)S(1)} %get-tuple-element.76), channel_id=1, source_target_pairs={{0,3},{1,2},{2,1},{3,0},{4,7},{5,6},{6,5},{7,4},{8,11},{9,10},{10,... | collective-permute-start | bytes 196616 | tf_op jit(solution)/shard_map/ppermute | solution.py:636
  15.5 2.0 %collective-permute-start.6 = (bf16[512,512]{1,0:T(8,128)(2,1)S(1)}, bf16[512,512]{1,0:T(8,128)(2,1)S(1)}, u32[]{:S(2)}, u32[]{:S(2)}) collective-permute-start(bf16[512,512]{1,0:T(8,128)(2,1)S(1)} %get-tuple-element.77.hid_ref), channel_id=1, source_target_pairs={{0,1},{1,0},{2,3},{3,2},{4,5},{5,4},{6,7},{7,6},{8,9},{9,8},{10,11... | collective-permute-start | bytes 1572872 | tf_op jit(solution)/shard_map/ppermute | solution.py:636
  20.8 2.0 %collective-permute-start.7 = (bf16[512,512]{1,0:T(8,128)(2,1)S(1)}, bf16[512,512]{1,0:T(8,128)(2,1)S(1)}, u32[]{:S(2)}, u32[]{:S(2)}) collective-permute-start(bf16[512,512]{1,0:T(8,128)(2,1)S(1)} %get-tuple-element.91), channel_id=1, source_target_pairs={{0,1},{1,0},{2,3},{3,2},{4,5},{5,4},{6,7},{7,6},{8,9},{9,8},{10,11... | collective-permute-start | bytes 1572872 | tf_op jit(solution)/shard_map/ppermute | solution.py:636
  22.9 8.8 %collective-permute-start.8 = (bf16[512,256]{1,0:T(8,128)(2,1)S(1)}, bf16[512,256]{1,0:T(8,128)(2,1)S(1)}, u32[]{:S(2)}, u32[]{:S(2)}) collective-permute-start(bf16[512,256]{1,0:T(8,128)(2,1)S(1)} %get-tuple-element.95), channel_id=1, source_target_pairs={{0,2},{1,3},{2,0},{3,1},{4,6},{5,7},{6,4},{7,5},{8,10},{9,11},{10,... | collective-permute-start | bytes 786440 | tf_op jit(solution)/shard_map/ppermute | solution.py:636
  24.9 31.6 %all-to-all-start = ((bf16[32,32,512]{2,1,0:T(8,128)(2,1)}), bf16[32,32,512]{2,1,0:T(8,128)(2,1)S(1)}, u32[]{:S(2)}, u32[]{:S(2)}) async-start(bf16[32,32,512]{2,1,0:T(8,128)(2,1)} %bitcast.5), calls=%async_computation | async-start | bytes 2097152 | tf_op jit(solution)/shard_map/all_to_all | solution.py:711
  34.5 4.4 %collective-permute-start.9 = (f32[32,128]{1,0:T(8,128)S(1)}, f32[32,128]{1,0:T(8,128)S(1)}, u32[]{:S(2)}, u32[]{:S(2)}) collective-permute-start(f32[32,128]{1,0:T(8,128)S(1)} %get-tuple-element.102), channel_id=1, source_target_pairs={{0,4},{4,0},{8,12},{12,8},{16,20},{20,16},{24,28},{28,24},{1,5},{5... | collective-permute-start | bytes 49160 | tf_op jit(solution)/shard_map/ppermute | solution.py:726
  39.0 9.0 %collective-permute-start.12 = (bf16[128,512]{1,0:T(8,128)(2,1)S(1)}, bf16[128,512]{1,0:T(8,128)(2,1)S(1)}, u32[]{:S(2)}, u32[]{:S(2)}) collective-permute-start(bf16[128,512]{1,0:T(8,128)(2,1)S(1)} %get-tuple-element.114), channel_id=1, source_target_pairs={{0,3},{1,2},{2,1},{3,0},{4,7},{5,6},{6,5},{7,4},{8,11},{9,10},{10,... | collective-permute-start | bytes 393224 | tf_op jit(solution)/shard_map/ppermute | solution.py:636
  39.6 10.8 %collective-permute-start.11 = (bf16[128,512]{1,0:T(8,128)(2,1)S(1)}, bf16[128,512]{1,0:T(8,128)(2,1)S(1)}, u32[]{:S(2)}, u32[]{:S(2)}) collective-permute-start(bf16[128,512]{1,0:T(8,128)(2,1)S(1)} %get-tuple-element.115), channel_id=1, source_target_pairs={{0,2},{1,3},{2,0},{3,1},{4,6},{5,7},{6,4},{7,5},{8,10},{9,11},{10,... | collective-permute-start | bytes 393224 | tf_op jit(solution)/shard_map/ppermute | solution.py:636
  40.7 1.3 %collective-permute-start.10 = (bf16[128,512]{1,0:T(8,128)(2,1)S(1)}, bf16[128,512]{1,0:T(8,128)(2,1)S(1)}, u32[]{:S(2)}, u32[]{:S(2)}) collective-permute-start(bf16[128,512]{1,0:T(8,128)(2,1)S(1)} %get-tuple-element.116), channel_id=1, source_target_pairs={{0,1},{1,0},{2,3},{3,2},{4,5},{5,4},{6,7},{7,6},{8,9},{9,8},{10,11... | collective-permute-start | bytes 393224 | tf_op jit(solution)/shard_map/ppermute | solution.py:636
  42.1 9.6 %collective-permute-start.16 = (bf16[32,128]{1,0:T(8,128)(2,1)S(1)}, bf16[32,128]{1,0:T(8,128)(2,1)S(1)}, u32[]{:S(2)}, u32[]{:S(2)}) collective-permute-start(bf16[32,128]{1,0:T(8,128)(2,1)S(1)} %add_convert_fusion), channel_id=1, source_target_pairs={{0,3},{1,19},{2,11},{3,27},{4,7},{5,23},{6,15},{7,31},{8,2},{9,18}... | collective-permute-start | bytes 24584 | tf_op jit(solution)/shard_map/ppermute | solution.py:739
  45.4 11.2 %collective-permute-start.15 = (bf16[32,128]{1,0:T(8,128)(2,1)S(1)}, bf16[32,128]{1,0:T(8,128)(2,1)S(1)}, u32[]{:S(2)}, u32[]{:S(2)}) collective-permute-start(bf16[32,128]{1,0:T(8,128)(2,1)S(1)} %add_convert_fusion), channel_id=1, source_target_pairs={{0,2},{1,18},{2,10},{3,26},{4,6},{5,22},{6,14},{7,30},{8,3},{9,19}... | collective-permute-start | bytes 24584 | tf_op jit(solution)/shard_map/ppermute | solution.py:739
  47.1 9.4 %collective-permute-start.14 = (bf16[32,128]{1,0:T(8,128)(2,1)S(1)}, bf16[32,128]{1,0:T(8,128)(2,1)S(1)}, u32[]{:S(2)}, u32[]{:S(2)}) collective-permute-start(bf16[32,128]{1,0:T(8,128)(2,1)S(1)} %add_convert_fusion), channel_id=1, source_target_pairs={{0,1},{1,17},{2,9},{3,25},{4,5},{5,21},{6,13},{7,29},{8,0},{9,16},... | collective-permute-start | bytes 24584 | tf_op jit(solution)/shard_map/ppermute | solution.py:739
  48.0 8.6 %collective-permute-start.13 = (bf16[32,128]{1,0:T(8,128)(2,1)S(1)}, bf16[32,128]{1,0:T(8,128)(2,1)S(1)}, u32[]{:S(2)}, u32[]{:S(2)}) collective-permute-start(bf16[32,128]{1,0:T(8,128)(2,1)S(1)} %add_convert_fusion), channel_id=1, source_target_pairs={{0,0},{1,16},{2,8},{3,24},{4,4},{5,20},{6,12},{7,28},{8,1},{9,17},... | collective-permute-start | bytes 24584 | tf_op jit(solution)/shard_map/ppermute | solution.py:739

commit v10 on v9

--- a/solution.py
+++ b/solution.py
@@ -602,13 +602,29 @@
         dframes_ref[:, pl.ds(start, width)] = ref[:row_count, width:]
 
 
-def place_grad_kernel(blocks_ref, q0, q1, q2, q3, out_ref, dw_ref, sum_ref):
+def pack_taps_kernel(keep_ref, recv_ref, *refs):
+    outs, all_ref = refs[:4], refs[4]
+    total = keep_ref[...] + recv_ref[...]
+    taps, channels = total.shape
+    piece = channels // 4
+    for n in range(4):
+        quarter = total[:, n * piece : (n + 1) * piece]
+        packed = jnp.concatenate([quarter[t : t + SUB] for t in range(0, taps, SUB)], axis=1)
+        high = packed.astype(jnp.bfloat16).astype(jnp.float32)
+        all_ref[n] = jnp.concatenate([high, packed - high], axis=0).astype(jnp.bfloat16)
+    z_index = lax.axis_index("dp") >> 1
+    for turn in range(4):
+        outs[turn][...] = all_ref[z_index ^ turn]
+
+
+def place_grad_kernel(blocks_ref, q0, q1, q2, q3, out_ref, dw_ref):
     piece, wide = blocks_ref.shape[1:]
     width = wide // 2
     full = out_ref.shape[1] // 2
     quarters = [q[...].astype(jnp.float32) for q in (q0, q1, q2, q3)]
-    sum_ref[...] = ((quarters[0] + quarters[1]) + (quarters[2] + quarters[3])).T
-    dw_ref[...] = sum_ref[pl.ds(pl.multiple_of(lax.axis_index("ctx") * piece, piece), piece), :KERNEL]
+    packed = (quarters[0] + quarters[1]) + (quarters[2] + quarters[3])
+    packed = packed[:SUB] + packed[SUB:]
+    dw_ref[...] = jnp.concatenate([packed[:, t : t + piece] for t in range(0, 4 * piece, piece)], axis=0).T[:, :KERNEL]
     for j in range(4):
         total = blocks_ref[j].astype(jnp.float32)
         for d in range(1, blocks_ref.shape[0] // 4):
@@ -725,10 +741,12 @@
     )
     dw_recv = lax.ppermute(dw_send, "dp", [(i, i ^ 1) for i in range(dp_size)])
     dw_recv, dframes = lax.optimization_barrier((dw_recv, dframes))
-    dw_half = (dw_keep + dw_recv).astype(bf16)
+    quarters = call(
+        pack_taps_kernel, (dw_keep, dw_recv), [((2 * SUB, 128), bf16)] * 4, [pltpu.VMEM((4, 2 * SUB, 128), bf16)], cost_us=1
+    )
     results = jnp.concatenate([out_own, dframes], axis=1)
     result_blocks = [results] + [swap_ctx(results[j * row_count : (j + 1) * row_count], j) for j in (1, 2, 3)]
-    dw_half, result_blocks[1] = lax.optimization_barrier((dw_half, result_blocks[1]))
+    quarters, result_blocks[1] = lax.optimization_barrier((quarters, result_blocks[1]))
     arrived = []
     for turn in range(4):
         pairs = []
@@ -736,13 +754,13 @@
             for c in range(4):
                 target = 2 * (2 * (c & 1) + (c >> 1)) + (d & 1)
                 pairs.append((4 * d + c, 4 * target + ((d >> 1) ^ turn)))
-        arrived.append(lax.ppermute(dw_half, ("dp", "ctx"), pairs))
+        arrived.append(lax.ppermute(quarters[turn], ("dp", "ctx"), pairs))
     output, dframes_rows = call(
         place_kernel, tuple(result_blocks), [((row_count, feat_width), bf16)] * 2, to_hbm=True, cost_us=1
     )
     grad_kv, grad_dw = call(
         place_grad_kernel, (all_kv, *arrived),
-        [((piece, 2 * feat_width), f32), ((piece, KERNEL), f32)], [pltpu.VMEM((width // 2, KERNEL + 1), f32)],
+        [((piece, 2 * feat_width), f32), ((piece, KERNEL), f32)],
         to_hbm=True, cost_us=1,
     )
     return (output[None], dframes_rows[None], grad_kv, grad_dw)

time: 57.8 us -> 57.8 us (level)
  waiting for transfers between devices: 13.4 us -> 9.11 us
  starting transfers between devices: 23.5 us -> 27.7 us
    ppermute x4, starting transfers between devices: 6.53 us -> 10.4 us  [on_device_pairs(): arrived.append(lax.ppermute(quarters[turn], ('dp', 'ctx'), pairs))]
    ppermute x12, waiting for transfers between devices: 7.98 us -> 5.13 us  [swap_ctx(): return lax.ppermute(array, 'ctx', [(i, i ^ j) for i in range(4)])]
    ppermute x4, waiting for transfers between devices: 5.36 us -> 3.97 us  [on_device_pairs(): arrived.append(lax.ppermute(quarters[turn], ('dp', 'ctx'), pairs))]
    pallas_call x11 -> x12, Pallas kernels: 19.6 us -> 19.8 us  [call(): pl.pallas_call(kernel, out_shape=[jax.ShapeDtypeStruct(*o) if to_hbm else...]
  transfers between devices with their start and end apart: 18 -> 18, of which waited for: 8 -> 5; matrix products, arithmetic and copies ran while one was open for 0% -> 0% of each run, Pallas kernels for 25% -> 25%
where the time goes in v10:
time: 57.8 us; the launch traced here: 57.4 us
  starting transfers between devices  27.7 us (48%)
  Pallas kernels  19.8 us (34%)
  waiting for transfers between devices  9.11 us (16%)
  between operations  0.84 us (1%)
    pallas_call x12, Pallas kernels, call(): pl.pallas_call(kernel, out_shape=[jax.ShapeDtypeStruct(*o) if to_hbm else...  19.8 us
    ppermute x4, starting transfers between devices, on_device_pairs(): arrived.append(lax.ppermute(quarters[turn], ('dp', 'ctx'), pairs))  10.4 us
    ppermute x12, starting transfers between devices, swap_ctx(): return lax.ppermute(array, 'ctx', [(i, i ^ j) for i in range(4)])  10.3 us
    ppermute x12, waiting for transfers between devices, swap_ctx(): return lax.ppermute(array, 'ctx', [(i, i ^ j) for i in range(4)])  5.13 us
    all_to_all x1, starting transfers between devices, on_device_pairs(): lax.all_to_all(part_kv.reshape(4 * dp_size, piece, 2 * width), ('dp', 'ct...  5.1 us
    ppermute x4, waiting for transfers between devices, on_device_pairs(): arrived.append(lax.ppermute(quarters[turn], ('dp', 'ctx'), pairs))  3.97 us
    ppermute x1, starting transfers between devices, on_device_pairs(): dw_recv = lax.ppermute(dw_send, 'dp', [(i, i ^ 1) for i in range(dp_size)])  1.84 us
  transfers between devices with their start and end apart: 18, of which 5 were waited for; matrix products, arithmetic and copies ran while one was open for 0% of the time, Pallas kernels for 25%

profile of v10, /device:TPU:0, one launch (start us, length us, event | category | flops | bytes accessed | tf_op | source)
XLA Modules:
  0.0 57.4 jit_solution(15604759721384405556)
XLA Ops:
  0.6 1.1 %shard_map.84 = (bf16[128,512]{1,0:T(8,128)(2,1)S(1)}, bf16[128,512]{1,0:T(8,128)(2,1)S(1)}, bf16[128,512]{1,0:T(8,128)(2,1)S(1)}, bf16[128,512]{1,0:T(8,128)(2,1)S(1)}) custom-call(bf16[128,1024]{1,0:T(8,128)(2,1)} %bitcast.6), custom_call_target="tpu_custom_call" | custom-call | flops 1000000000 | bytes 3000000 | tf_op jit(solution)/shard_map/pallas_call | solution.py:640
  2.3 2.6 %collective-permute-start.1 = (bf16[128,512]{1,0:T(8,128)(2,1)S(1)}, bf16[128,512]{1,0:T(8,128)(2,1)S(1)}, u32[]{:S(2)}, u32[]{:S(2)}) collective-permute-start(bf16[128,512]{1,0:T(8,128)(2,1)S(1)} %get-tuple-element.73), channel_id=1, source_target_pairs={{0,2},{1,3},{2,0},{3,1},{4,6},{5,7},{6,4},{7,5},{8,10},{9,11},{10,... | collective-permute-start | bytes 393224 | tf_op jit(solution)/shard_map/ppermute | solution.py:652
  4.9 1.3 %shard_map.85 = (bf16[624,512]{1,0:T(8,128)(2,1)S(1)}, bf16[512,624]{1,0:T(8,128)(2,1)S(1)}, f32[31,8,256]{2,1,0:T(8,128)S(1)}, f32[31,8,256]{2,1,0:T(8,128)S(1)...) custom-call(s32[1,8]{1,0:T(1,128)} %len_hbm.7, ...), custom_call_target="tpu_custom_call" | custom-call | flops 2000000000 | bytes 6000000 | tf_op jit(solution)/shard_map/pallas_call | solution.py:640
  6.5 1.9 %collective-permute-start.4 = (bf16[128,256]{1,0:T(8,128)(2,1)S(1)}, bf16[128,256]{1,0:T(8,128)(2,1)S(1)}, u32[]{:S(2)}, u32[]{:S(2)}) collective-permute-start(bf16[128,256]{1,0:T(8,128)(2,1)S(1)} %get-tuple-element.82), channel_id=1, source_target_pairs={{0,2},{1,3},{2,0},{3,1},{4,6},{5,7},{6,4},{7,5},{8,10},{9,11},{10,... | collective-permute-start | bytes 196616 | tf_op jit(solution)/shard_map/ppermute | solution.py:652
  8.4 0.8 %collective-permute-done.1.f2 = bf16[128,512]{1,0:T(8,128)(2,1)S(1)} collective-permute-done((bf16[128,512]{1,0:T(8,128)(2,1)S(1)}, bf16[128,512]{1,0:T(8,128)(2,1)S(1)}, u32[]{:S(2)}, u32[]{:S(2)}) %collective-permute-start.1) | collective-permute-done | bytes 131104 | tf_op jit(solution)/shard_map/ppermute | solution.py:652
  9.2 2.3 %collective-permute-done.2.f3 = bf16[128,512]{1,0:T(8,128)(2,1)S(1)} collective-permute-done((bf16[128,512]{1,0:T(8,128)(2,1)S(1)}, bf16[128,512]{1,0:T(8,128)(2,1)S(1)}, u32[]{:S(2)}, u32[]{:S(2)}) %collective-permute-start.2) | collective-permute-done | bytes 131104 | tf_op jit(solution)/shard_map/ppermute | solution.py:652
  11.5 4.1 %shard_map.86 = (bf16[512,512]{1,0:T(8,128)(2,1)S(1)}, bf16[1024,256]{1,0:T(8,128)(2,1)S(1)}, bf16[1024,256]{1,0:T(8,128)(2,1)S(1)}, f32[108,8,256]{2,1,0:T(8,128)}, f32[78,8,256]{2,1,0:T(8,128)}) custom-call(bf16[128,512]{1,0:T(8,128)(2,1)S(1)} %get-tuple-element.66.f0, bf16[128,512]{1,0:T(8,128)(2,1)S(1)} %collective-permute-done.f1, ...), custom_call_target="tpu_custom_call" | custom-call | flops 20000000000 | bytes 60000000 | tf_op jit(solution)/shard_map/pallas_call | solution.py:640
  16.0 1.2 %shard_map.87 = (f32[512,512]{1,0:T(8,128)S(1)}, bf16[512,256]{1,0:T(8,128)(2,1)S(1)}, f32[256,512]{1,0:T(8,128)S(1)}, f32[128,128]{1,0:T(8,128)S(1)}) custom-call(s32[1,8]{1,0:T(1,128)} %len_hbm.7, bf16[512,512]{1,0:T(8,128)(2,1)S(1)} %get-tuple-element.84.hid_ref, bf16[128,256]{1,0:T(8,128)(2,1)S(1)} %get-tuple-element.85.f0, ...), custom_call_target="tpu_custom_call" | custom-call | flops 2000000000 | bytes 6000000 | tf_op jit(solution)/shard_map/pallas_call | solution.py:640
  17.6 3.3 %shard_map.88 = (f32[256,512]{1,0:T(8,128)S(1)}, f32[256,512]{1,0:T(8,128)S(1)}, bf16[512,512]{1,0:T(8,128)(2,1)S(1)}, bf16[512,512]{1,0:T(8,128)(2,1)S(1)}) custom-call(bf16[512,512]{1,0:T(8,128)(2,1)S(1)} %get-tuple-element.84.hid_ref, bf16[512,512]{1,0:T(8,128)(2,1)S(1)} %collective-permute-done.6.sib_ref, f32[512,512]{1,0:T(8,128)S(1)} %get-tuple-element.91.kv_ref, ...), custom_call_target="tpu_custom_call" | custom-call | flops 8000000000 | bytes 24000000 | tf_op jit(solution)/shard_map/pallas_call | solution.py:640
  21.3 1.6 %shard_map.89 = (bf16[1024,512]{1,0:T(8,128)(2,1)}, f32[512,512]{1,0:T(8,128)S(1)}) custom-call(bf16[512,512]{1,0:T(8,128)(2,1)S(1)} %get-tuple-element.84.hid_ref, bf16[512,512]{1,0:T(8,128)(2,1)S(1)} %collective-permute-done.6.sib_ref, bf16[512,512]{1,0:T(8,128)(2,1)S(1)} %get-tuple-element.95.kvg_ref, f32[256,512]{1,0:T(8,128)S(1)} %get-tuple-element.96.dqt_ref, ...), custom_call_target="tpu_custom_call" | custom-call | flops 2000000000 | bytes 6000000 | tf_op jit(solution)/shard_map/pallas_call | solution.py:640
  23.0 2.0 %collective-permute-start.8 = (bf16[512,256]{1,0:T(8,128)(2,1)S(1)}, bf16[512,256]{1,0:T(8,128)(2,1)S(1)}, u32[]{:S(2)}, u32[]{:S(2)}) collective-permute-start(bf16[512,256]{1,0:T(8,128)(2,1)S(1)} %get-tuple-element.102), channel_id=1, source_target_pairs={{0,2},{1,3},{2,0},{3,1},{4,6},{5,7},{6,4},{7,5},{8,10},{9,11},{10,... | collective-permute-start | bytes 786440 | tf_op jit(solution)/shard_map/ppermute | solution.py:652
  25.0 5.1 %all-to-all-start = ((bf16[32,32,512]{2,1,0:T(8,128)(2,1)}), bf16[32,32,512]{2,1,0:T(8,128)(2,1)S(1)}, u32[]{:S(2)}, u32[]{:S(2)}) async-start(bf16[32,32,512]{2,1,0:T(8,128)(2,1)} %bitcast.5), calls=%async_computation | async-start | bytes 2097152 | tf_op jit(solution)/shard_map/all_to_all | solution.py:727
  30.2 1.6 %collective-permute-done.8.recv_ref = bf16[512,256]{1,0:T(8,128)(2,1)S(1)} collective-permute-done((bf16[512,256]{1,0:T(8,128)(2,1)S(1)}, bf16[512,256]{1,0:T(8,128)(2,1)S(1)}, u32[]{:S(2)}, u32[]{:S(2)}) %collective-permute-start.8) | collective-permute-done | bytes 262176 | tf_op jit(solution)/shard_map/ppermute | solution.py:652
  31.8 2.9 %shard_map.91 = (f32[78,8,256]{2,1,0:T(8,128)S(1)}, f32[108,8,256]{2,1,0:T(8,128)S(1)}, f32[32,128]{1,0:T(8,128)S(1)}, f32[32,128]{1,0:T(8,128)S(1)}) custom-call(f32[512,256]{1,0:T(8,128)S(1)} %get-tuple-element.99.own_ref, bf16[512,256]{1,0:T(8,128)(2,1)S(1)} %collective-permute-done.8.recv_ref, f32[108,8,256]{2,1,0:T(8,128)} %get-tuple-element.103.xext_hbm, ...), custom_call_target="tpu_custom_call" | custom-call | flops 99999997952 | bytes 300000000 | tf_op jit(solution)/shard_map/pallas_call | solution.py:640
  34.6 1.8 %collective-permute-start.9 = (f32[32,128]{1,0:T(8,128)S(1)}, f32[32,128]{1,0:T(8,128)S(1)}, u32[]{:S(2)}, u32[]{:S(2)}) collective-permute-start(f32[32,128]{1,0:T(8,128)S(1)} %get-tuple-element.109), channel_id=1, source_target_pairs={{0,4},{4,0},{8,12},{12,8},{16,20},{20,16},{24,28},{28,24},{1,5},{5... | collective-permute-start | bytes 49160 | tf_op jit(solution)/shard_map/ppermute | solution.py:742
  36.5 2.4 %shard_map.92 = (bf16[512,256]{1,0:T(8,128)(2,1)S(1)}, bf16[512,256]{1,0:T(8,128)(2,1)S(1)}) custom-call(f32[78,8,256]{2,1,0:T(8,128)S(1)} %get-tuple-element.105.dh_ref, f32[108,8,256]{2,1,0:T(8,128)S(1)} %get-tuple-element.106.ext_ref, f32[31,8,256]{2,1,0:T(8,128)S(1)} %get-tuple-element.77.taps_own_ref.taps_ref, ...), custom_call_target="tpu_custom_call" | custom-call | flops 20000000000 | bytes 60000000 | tf_op jit(solution)/shard_map/pallas_call | solution.py:640
  39.0 1.7 %collective-permute-start.12 = (bf16[128,512]{1,0:T(8,128)(2,1)S(1)}, bf16[128,512]{1,0:T(8,128)(2,1)S(1)}, u32[]{:S(2)}, u32[]{:S(2)}) collective-permute-start(bf16[128,512]{1,0:T(8,128)(2,1)S(1)} %get-tuple-element.128), channel_id=1, source_target_pairs={{0,3},{1,2},{2,1},{3,0},{4,7},{5,6},{6,5},{7,4},{8,11},{9,10},{10,... | collective-permute-start | bytes 393224 | tf_op jit(solution)/shard_map/ppermute | solution.py:652
  41.3 0.7 %collective-permute-start.13 = (bf16[16,128]{1,0:T(8,128)(2,1)S(1)}, bf16[16,128]{1,0:T(8,128)(2,1)S(1)}, u32[]{:S(2)}, u32[]{:S(2)}) collective-permute-start(bf16[16,128]{1,0:T(8,128)(2,1)S(1)} %get-tuple-element.122), channel_id=1, source_target_pairs={{0,0},{1,16},{2,8},{3,24},{4,4},{5,20},{6,12},{7,28},{8,1},{9,17},... | collective-permute-start | bytes 12296 | tf_op jit(solution)/shard_map/ppermute | solution.py:757
  42.0 4.8 %collective-permute-start.14 = (bf16[16,128]{1,0:T(8,128)(2,1)S(1)}, bf16[16,128]{1,0:T(8,128)(2,1)S(1)}, u32[]{:S(2)}, u32[]{:S(2)}) collective-permute-start(bf16[16,128]{1,0:T(8,128)(2,1)S(1)} %get-tuple-element.123), channel_id=1, source_target_pairs={{0,1},{1,17},{2,9},{3,25},{4,5},{5,21},{6,13},{7,29},{8,0},{9,16},... | collective-permute-start | bytes 12296 | tf_op jit(solution)/shard_map/ppermute | solution.py:757
  46.7 1.0 %collective-permute-start.15 = (bf16[16,128]{1,0:T(8,128)(2,1)S(1)}, bf16[16,128]{1,0:T(8,128)(2,1)S(1)}, u32[]{:S(2)}, u32[]{:S(2)}) collective-permute-start(bf16[16,128]{1,0:T(8,128)(2,1)S(1)} %get-tuple-element.124), channel_id=1, source_target_pairs={{0,2},{1,18},{2,10},{3,26},{4,6},{5,22},{6,14},{7,30},{8,3},{9,19}... | collective-permute-start | bytes 12296 | tf_op jit(solution)/shard_map/ppermute | solution.py:757
  47.8 3.9 %collective-permute-start.16 = (bf16[16,128]{1,0:T(8,128)(2,1)S(1)}, bf16[16,128]{1,0:T(8,128)(2,1)S(1)}, u32[]{:S(2)}, u32[]{:S(2)}) collective-permute-start(bf16[16,128]{1,0:T(8,128)(2,1)S(1)} %get-tuple-element.125), channel_id=1, source_target_pairs={{0,3},{1,19},{2,11},{3,27},{4,7},{5,23},{6,15},{7,31},{8,2},{9,18}... | collective-permute-start | bytes 12296 | tf_op jit(solution)/shard_map/ppermute | solution.py:757
  51.7 0.8 %shard_map.94 = (bf16[128,1024]{1,0:T(8,128)(2,1)}, bf16[128,1024]{1,0:T(8,128)(2,1)}) custom-call(bf16[512,512]{1,0:T(8,128)(2,1)S(1)} %constant_dynamic-update-slice_fusion.own_ref, bf16[128,512]{1,0:T(8,128)(2,1)S(1)} %collective-permute-done.10.r1, bf16[128,512]{1,0:T(8,128)(2,1)S(1)} %collective-permute-done.11.r2, ...), custom_call_target="tpu_custom_call" | custom-call | flops 1000000000 | bytes 3000000 | tf_op jit(solution)/shard_map/pallas_call | solution.py:640
  52.6 4.0 %collective-permute-done.15.q2 = bf16[16,128]{1,0:T(8,128)(2,1)S(1)} collective-permute-done((bf16[16,128]{1,0:T(8,128)(2,1)S(1)}, bf16[16,128]{1,0:T(8,128)(2,1)S(1)}, u32[]{:S(2)}, u32[]{:S(2)}) %collective-permute-start.15) | collective-permute-done | bytes 4128 | tf_op jit(solution)/shard_map/ppermute | solution.py:757
  56.5 0.9 %shard_map.95 = (f32[32,2048]{1,0:T(8,128)}, f32[32,31]{1,0:T(8,128)}) custom-call(bf16[32,32,512]{2,1,0:T(8,128)(2,1)S(1)} %all-to-all-done.blocks_ref, bf16[16,128]{1,0:T(8,128)(2,1)S(1)} %collective-permute-done.13.q0, bf16[16,128]{1,0:T(8,128)(2,1)S(1)} %collective-permute-done.14.q1, bf16[16,128]{1,0:T(8,128)(2,1)S(1)} %collective-permute-done.15.q2, ...), custom_call_target="tpu_custom_call" | custom-call | flops 1000000000 | bytes 3000000 | tf_op jit(solution)/shard_map/pallas_call | solution.py:640
  (27 shorter events, 2.7 us)
Async XLA Ops:
  1.8 4.5 %collective-permute-start = (bf16[128,512]{1,0:T(8,128)(2,1)S(1)}, bf16[128,512]{1,0:T(8,128)(2,1)S(1)}, u32[]{:S(2)}, u32[]{:S(2)}) collective-permute-start(bf16[128,512]{1,0:T(8,128)(2,1)S(1)} %get-tuple-element.71), channel_id=1, source_target_pairs={{0,1},{1,0},{2,3},{3,2},{4,5},{5,4},{6,7},{7,6},{8,9},{9,8},{10,11... | collective-permute-start | bytes 393224 | tf_op jit(solution)/shard_map/ppermute | solution.py:652
  2.3 6.9 %collective-permute-start.1 = (bf16[128,512]{1,0:T(8,128)(2,1)S(1)}, bf16[128,512]{1,0:T(8,128)(2,1)S(1)}, u32[]{:S(2)}, u32[]{:S(2)}) collective-permute-start(bf16[128,512]{1,0:T(8,128)(2,1)S(1)} %get-tuple-element.73), channel_id=1, source_target_pairs={{0,2},{1,3},{2,0},{3,1},{4,6},{5,7},{6,4},{7,5},{8,10},{9,11},{10,... | collective-permute-start | bytes 393224 | tf_op jit(solution)/shard_map/ppermute | solution.py:652
  4.9 6.6 %collective-permute-start.2 = (bf16[128,512]{1,0:T(8,128)(2,1)S(1)}, bf16[128,512]{1,0:T(8,128)(2,1)S(1)}, u32[]{:S(2)}, u32[]{:S(2)}) collective-permute-start(bf16[128,512]{1,0:T(8,128)(2,1)S(1)} %get-tuple-element.74), channel_id=1, source_target_pairs={{0,3},{1,2},{2,1},{3,0},{4,7},{5,6},{6,5},{7,4},{8,11},{9,10},{10,... | collective-permute-start | bytes 393224 | tf_op jit(solution)/shard_map/ppermute | solution.py:652
  6.2 9.4 %collective-permute-start.3 = (bf16[128,256]{1,0:T(8,128)(2,1)S(1)}, bf16[128,256]{1,0:T(8,128)(2,1)S(1)}, u32[]{:S(2)}, u32[]{:S(2)}) collective-permute-start(bf16[128,256]{1,0:T(8,128)(2,1)S(1)} %get-tuple-element.81), channel_id=1, source_target_pairs={{0,1},{1,0},{2,3},{3,2},{4,5},{5,4},{6,7},{7,6},{8,9},{9,8},{10,11... | collective-permute-start | bytes 196616 | tf_op jit(solution)/shard_map/ppermute | solution.py:652
  6.5 9.2 %collective-permute-start.4 = (bf16[128,256]{1,0:T(8,128)(2,1)S(1)}, bf16[128,256]{1,0:T(8,128)(2,1)S(1)}, u32[]{:S(2)}, u32[]{:S(2)}) collective-permute-start(bf16[128,256]{1,0:T(8,128)(2,1)S(1)} %get-tuple-element.82), channel_id=1, source_target_pairs={{0,2},{1,3},{2,0},{3,1},{4,6},{5,7},{6,4},{7,5},{8,10},{9,11},{10,... | collective-permute-start | bytes 196616 | tf_op jit(solution)/shard_map/ppermute | solution.py:652
  8.4 7.2 %collective-permute-start.5 = (bf16[128,256]{1,0:T(8,128)(2,1)S(1)}, bf16[128,256]{1,0:T(8,128)(2,1)S(1)}, u32[]{:S(2)}, u32[]{:S(2)}) collective-permute-start(bf16[128,256]{1,0:T(8,128)(2,1)S(1)} %get-tuple-element.83), channel_id=1, source_target_pairs={{0,3},{1,2},{2,1},{3,0},{4,7},{5,6},{6,5},{7,4},{8,11},{9,10},{10,... | collective-permute-start | bytes 196616 | tf_op jit(solution)/shard_map/ppermute | solution.py:652
  15.6 2.0 %collective-permute-start.6 = (bf16[512,512]{1,0:T(8,128)(2,1)S(1)}, bf16[512,512]{1,0:T(8,128)(2,1)S(1)}, u32[]{:S(2)}, u32[]{:S(2)}) collective-permute-start(bf16[512,512]{1,0:T(8,128)(2,1)S(1)} %get-tuple-element.84.hid_ref), channel_id=1, source_target_pairs={{0,1},{1,0},{2,3},{3,2},{4,5},{5,4},{6,7},{7,6},{8,9},{9,8},{10,11... | collective-permute-start | bytes 1572872 | tf_op jit(solution)/shard_map/ppermute | solution.py:652
  20.9 2.0 %collective-permute-start.7 = (bf16[512,512]{1,0:T(8,128)(2,1)S(1)}, bf16[512,512]{1,0:T(8,128)(2,1)S(1)}, u32[]{:S(2)}, u32[]{:S(2)}) collective-permute-start(bf16[512,512]{1,0:T(8,128)(2,1)S(1)} %get-tuple-element.98), channel_id=1, source_target_pairs={{0,1},{1,0},{2,3},{3,2},{4,5},{5,4},{6,7},{7,6},{8,9},{9,8},{10,11... | collective-permute-start | bytes 1572872 | tf_op jit(solution)/shard_map/ppermute | solution.py:652
  23.0 8.8 %collective-permute-start.8 = (bf16[512,256]{1,0:T(8,128)(2,1)S(1)}, bf16[512,256]{1,0:T(8,128)(2,1)S(1)}, u32[]{:S(2)}, u32[]{:S(2)}) collective-permute-start(bf16[512,256]{1,0:T(8,128)(2,1)S(1)} %get-tuple-element.102), channel_id=1, source_target_pairs={{0,2},{1,3},{2,0},{3,1},{4,6},{5,7},{6,4},{7,5},{8,10},{9,11},{10,... | collective-permute-start | bytes 786440 | tf_op jit(solution)/shard_map/ppermute | solution.py:652
  25.0 31.5 %all-to-all-start = ((bf16[32,32,512]{2,1,0:T(8,128)(2,1)}), bf16[32,32,512]{2,1,0:T(8,128)(2,1)S(1)}, u32[]{:S(2)}, u32[]{:S(2)}) async-start(bf16[32,32,512]{2,1,0:T(8,128)(2,1)} %bitcast.5), calls=%async_computation | async-start | bytes 2097152 | tf_op jit(solution)/shard_map/all_to_all | solution.py:727
  34.6 4.2 %collective-permute-start.9 = (f32[32,128]{1,0:T(8,128)S(1)}, f32[32,128]{1,0:T(8,128)S(1)}, u32[]{:S(2)}, u32[]{:S(2)}) collective-permute-start(f32[32,128]{1,0:T(8,128)S(1)} %get-tuple-element.109), channel_id=1, source_target_pairs={{0,4},{4,0},{8,12},{12,8},{16,20},{20,16},{24,28},{28,24},{1,5},{5... | collective-permute-start | bytes 49160 | tf_op jit(solution)/shard_map/ppermute | solution.py:742
  39.0 2.3 %collective-permute-start.10 = (bf16[128,512]{1,0:T(8,128)(2,1)S(1)}, bf16[128,512]{1,0:T(8,128)(2,1)S(1)}, u32[]{:S(2)}, u32[]{:S(2)}) collective-permute-start(bf16[128,512]{1,0:T(8,128)(2,1)S(1)} %get-tuple-element.130), channel_id=1, source_target_pairs={{0,1},{1,0},{2,3},{3,2},{4,5},{5,4},{6,7},{7,6},{8,9},{9,8},{10,11... | collective-permute-start | bytes 393224 | tf_op jit(solution)/shard_map/ppermute | solution.py:652
  39.0 8.7 %collective-permute-start.12 = (bf16[128,512]{1,0:T(8,128)(2,1)S(1)}, bf16[128,512]{1,0:T(8,128)(2,1)S(1)}, u32[]{:S(2)}, u32[]{:S(2)}) collective-permute-start(bf16[128,512]{1,0:T(8,128)(2,1)S(1)} %get-tuple-element.128), channel_id=1, source_target_pairs={{0,3},{1,2},{2,1},{3,0},{4,7},{5,6},{6,5},{7,4},{8,11},{9,10},{10,... | collective-permute-start | bytes 393224 | tf_op jit(solution)/shard_map/ppermute | solution.py:652
  40.8 10.9 %collective-permute-start.11 = (bf16[128,512]{1,0:T(8,128)(2,1)S(1)}, bf16[128,512]{1,0:T(8,128)(2,1)S(1)}, u32[]{:S(2)}, u32[]{:S(2)}) collective-permute-start(bf16[128,512]{1,0:T(8,128)(2,1)S(1)} %get-tuple-element.129), channel_id=1, source_target_pairs={{0,2},{1,3},{2,0},{3,1},{4,6},{5,7},{6,4},{7,5},{8,10},{9,11},{10,... | collective-permute-start | bytes 393224 | tf_op jit(solution)/shard_map/ppermute | solution.py:652
  41.3 11.3 %collective-permute-start.13 = (bf16[16,128]{1,0:T(8,128)(2,1)S(1)}, bf16[16,128]{1,0:T(8,128)(2,1)S(1)}, u32[]{:S(2)}, u32[]{:S(2)}) collective-permute-start(bf16[16,128]{1,0:T(8,128)(2,1)S(1)} %get-tuple-element.122), channel_id=1, source_target_pairs={{0,0},{1,16},{2,8},{3,24},{4,4},{5,20},{6,12},{7,28},{8,1},{9,17},... | collective-permute-start | bytes 12296 | tf_op jit(solution)/shard_map/ppermute | solution.py:757
  42.0 10.6 %collective-permute-start.14 = (bf16[16,128]{1,0:T(8,128)(2,1)S(1)}, bf16[16,128]{1,0:T(8,128)(2,1)S(1)}, u32[]{:S(2)}, u32[]{:S(2)}) collective-permute-start(bf16[16,128]{1,0:T(8,128)(2,1)S(1)} %get-tuple-element.123), channel_id=1, source_target_pairs={{0,1},{1,17},{2,9},{3,25},{4,5},{5,21},{6,13},{7,29},{8,0},{9,16},... | collective-permute-start | bytes 12296 | tf_op jit(solution)/shard_map/ppermute | solution.py:757
  46.7 9.8 %collective-permute-start.15 = (bf16[16,128]{1,0:T(8,128)(2,1)S(1)}, bf16[16,128]{1,0:T(8,128)(2,1)S(1)}, u32[]{:S(2)}, u32[]{:S(2)}) collective-permute-start(bf16[16,128]{1,0:T(8,128)(2,1)S(1)} %get-tuple-element.124), channel_id=1, source_target_pairs={{0,2},{1,18},{2,10},{3,26},{4,6},{5,22},{6,14},{7,30},{8,3},{9,19}... | collective-permute-start | bytes 12296 | tf_op jit(solution)/shard_map/ppermute | solution.py:757
  47.8 8.8 %collective-permute-start.16 = (bf16[16,128]{1,0:T(8,128)(2,1)S(1)}, bf16[16,128]{1,0:T(8,128)(2,1)S(1)}, u32[]{:S(2)}, u32[]{:S(2)}) collective-permute-start(bf16[16,128]{1,0:T(8,128)(2,1)S(1)} %get-tuple-element.125), channel_id=1, source_target_pairs={{0,3},{1,19},{2,11},{3,27},{4,7},{5,23},{6,15},{7,31},{8,2},{9,18}... | collective-permute-start | bytes 12296 | tf_op jit(solution)/shard_map/ppermute | solution.py:757
